TPU v7x, 32 devices: a whole 2x2x4 slice. The times are simulated.
32 devices in a mesh: tm: 4 (over y, core), seq: 8 (over z, x).
Axes of the slice: x: 2, y: 2, z: 4, core: 2. Of those that a mesh axis runs over, the one named last changes fastest.
Arguments:
- queries: bfloat16 [4, 192, 4096], P('tm', 'seq'), may hold values from -144 to 144
- keys_proj: bfloat16 [4, 192, 4096], P('tm', 'seq'), may hold values from -12 to 12
- values: bfloat16 [4, 192, 4096], P('tm', 'seq'), may hold values from -4 to 4
- hidden: bfloat16 [4, 192, 4096], P('tm', 'seq'), may hold values from -4 to 4
- fresh_latent: bfloat16 [192, 4096], P('seq'), may hold values from -4 to 4
- gate_table: float32 [50, 4096], replicated, may hold values from 0.5 to 2.5
- noise_step: int32 [4], P('tm'), may hold values from 0 to 49, as said below
- pattern: int32 [4, 4], replicated, may hold values from 0 to 1, as said below
Outputs:
- advanced: bfloat16 [4, 192, 4096], P('tm', 'seq')
- next_cache: bfloat16 [4, 2, 192, 4096], P('tm', None, None, 'seq')
Inputs may be any that keep to these rules, and one draw needn't show every extreme that they name: pattern[i][0] is 1 for every i, and pattern[i][j] is 0 where j > i. noise_step[0] is 0, noise_step[3] is 49, and all 4 values are distinct.
All inputs are finite; a program needn't handle non-finite values.
Results may differ from a plain program's by a relative error of at most 0.0036.
Values may be sent and summed in bfloat16 or wider, within the bound.
No kernel may reach another device: no remote copies, remote signals or barrier semaphores. Data moves between devices by JAX's collectives and lax.ppermute only.
A program may use at most 64 MiB of HBM per device.

v0:
```python
import functools
import math

import jax
import jax.numpy as jnp
from jax import lax
from jax.experimental import pallas as pl
from jax.experimental.pallas import tpu as pltpu
from jax.sharding import PartitionSpec as P

HD = 128
BOTH = ("tm", "seq")
VMEM = pltpu.VMEM
SMEM = pltpu.SMEM


def shifted(block, axis, distance):
    devices = range(lax.axis_size(axis))
    route = [(i - distance, i) for i in devices if i - distance in devices]
    return lax.ppermute(block, axis, route)


def pack_kernel(seq_count, noise_ref, q_ref, k_ref, v_ref, h_ref, gate_ref, out_ref, moved_ref):
    tok = q_ref.shape[1]
    wide = out_ref.shape[1] // 3
    count = out_ref.shape[0] // tok
    tm_count = count // seq_count
    for pair in range(count // 2):
        for place, ref in enumerate((q_ref, k_ref, v_ref)):
            rows = []
            for dest in (2 * pair, 2 * pair + 1):
                start = ((dest % seq_count) * tm_count + dest // seq_count) * wide
                rows.append(ref[0, :, start : start + wide].astype(jnp.float32))
            both = jnp.concatenate(rows, axis=0).astype(jnp.bfloat16)
            out_ref[2 * pair * tok : 2 * (pair + 1) * tok, place * wide : (place + 1) * wide] = both
    gate = gate_ref[pl.ds(noise_ref[0], 1), :]
    high = gate.astype(jnp.bfloat16).astype(jnp.float32)
    middle = (gate - high).astype(jnp.bfloat16).astype(jnp.float32)
    low = gate - high - middle
    parts = jnp.concatenate([high, middle, low, jnp.zeros((5, gate.shape[1]), jnp.float32)], axis=0)
    moved_ref[...] = jnp.concatenate([h_ref[0].astype(jnp.float32), parts], axis=0).astype(jnp.bfloat16)


def attend_kernel(tok, pattern_ref, x_ref, out_ref, cache_ref):
    groups = cache_ref.shape[0]
    wide = out_ref.shape[1]
    rows = x_ref.shape[0] // groups
    factor = math.log2(math.e) / math.sqrt(HD)
    for group in range(1, groups):
        span = (group + 1) * rows
        column = lax.broadcasted_iota(jnp.int32, (1, span), 1)
        kept = jnp.zeros((1, span), jnp.int32)
        for source in range(group + 1):
            inside = (column >= source * rows) & (column < (source + 1) * rows)
            kept = jnp.where(inside, pattern_ref[group, source], kept)
        for head in range(0, wide, HD):
            query = x_ref[group * rows : span, head : head + HD]
            key = x_ref[:span, wide + head : wide + head + HD]
            value = x_ref[:span, 2 * wide + head : 2 * wide + head + HD]
            scores = lax.dot_general(
                query, key, (((1,), (1,)), ((), ())), preferred_element_type=jnp.float32
            )
            scores = jnp.where(kept > 0, scores, -1e30)
            highest = jnp.max(scores, axis=-1, keepdims=True)
            raised = jnp.exp2((scores - highest) * factor)
            total = jnp.sum(raised, axis=-1, keepdims=True)
            numer = jnp.dot(raised.astype(jnp.bfloat16), value, preferred_element_type=jnp.float32)
            out_ref[(group - 1) * rows : group * rows, head : head + HD] = (numer / total).astype(
                jnp.bfloat16
            )
        cache_ref[group - 1] = x_ref[group * rows : span, wide:]
    out_ref[(groups - 1) * rows :, :] = jnp.zeros((rows, wide), jnp.bfloat16)
    cache_ref[groups - 1] = jnp.zeros((rows, 2 * wide), jnp.bfloat16)


def cache_kernel(in_ref, out_ref):
    wide = in_ref.shape[2] // 2
    for part in range(in_ref.shape[0]):
        for kind in range(2):
            out_ref[0, kind, :, part * wide : (part + 1) * wide] = in_ref[
                part, :, kind * wide : (kind + 1) * wide
            ]


def update_kernel(seq_count, tm_count, att_ref, moved_ref, fresh_ref, out_ref):
    tok = out_ref.shape[1]
    wide = att_ref.shape[1]
    count = att_ref.shape[0] // tok
    last = lax.axis_index("tm") == tm_count - 1

    @pl.when(last)
    def take_fresh():
        out_ref[0] = fresh_ref[...]

    @pl.when(jnp.logical_not(last))
    def take_update():
        for pair in range(count // 2):
            rows = att_ref[2 * pair * tok : 2 * (pair + 1) * tok, :].astype(jnp.float32)
            for half in range(2):
                source = 2 * pair + half
                start = ((source % seq_count) * tm_count + source // seq_count) * wide
                moved = moved_ref[:, start : start + wide].astype(jnp.float32)
                gate = (moved[tok : tok + 1] + moved[tok + 1 : tok + 2]) + moved[tok + 2 : tok + 3]
                result = moved[:tok] + gate * rows[half * tok : (half + 1) * tok]
                out_ref[0, :, start : start + wide] = result.astype(jnp.bfloat16)


def whole(space=VMEM):
    return pl.BlockSpec(memory_space=space)


def spread_body(queries, keys_proj, values, hidden, fresh_latent, gate_table, noise_step, pattern):
    tm_count, seq_count = lax.axis_size("tm"), lax.axis_size("seq")
    count = tm_count * seq_count
    _, tok, width = queries.shape
    wide = width // count
    group_tok = tok * seq_count
    kind = queries.dtype

    packed, residual = pl.pallas_call(
        functools.partial(pack_kernel, seq_count),
        out_shape=(
            jax.ShapeDtypeStruct((count * tok, 3 * wide), kind),
            jax.ShapeDtypeStruct((tok + 8, width), kind),
        ),
        in_specs=[whole(SMEM)] + [whole()] * 5,
        out_specs=(whole(), whole()),
        name="pack",
    )(noise_step, queries, keys_proj, values, hidden, gate_table)

    exchanged = lax.all_to_all(packed, BOTH, split_axis=0, concat_axis=0, tiled=True)
    moved = shifted(residual, "tm", -1)

    attended, handed = pl.pallas_call(
        functools.partial(attend_kernel, tok),
        out_shape=(
            jax.ShapeDtypeStruct((count * tok, wide), kind),
            jax.ShapeDtypeStruct((tm_count, group_tok, 2 * wide), kind),
        ),
        in_specs=[whole(SMEM), whole()],
        out_specs=(whole(), whole()),
        name="attend",
    )(pattern, exchanged)

    returned = lax.all_to_all(attended, BOTH, split_axis=0, concat_axis=0, tiled=True)
    handed = lax.all_to_all(handed, "tm", split_axis=0, concat_axis=0, tiled=True)

    next_cache = pl.pallas_call(
        cache_kernel,
        out_shape=jax.ShapeDtypeStruct((1, 2, group_tok, tm_count * wide), kind),
        in_specs=[whole()],
        out_specs=whole(),
        name="cache",
    )(handed)
    advanced = pl.pallas_call(
        functools.partial(update_kernel, seq_count, tm_count),
        out_shape=jax.ShapeDtypeStruct((1, tok, width), kind),
        in_specs=[whole()] * 3,
        out_specs=whole(),
        name="update",
    )(returned, moved, fresh_latent)
    return (advanced, next_cache)


def absorb(state, query_heads, key_piece, value_piece, scale_factor):
    accum, totals, highest = state
    row_count, head_count, head_dim = query_heads.shape
    key_heads = key_piece.reshape(key_piece.shape[0], head_count, head_dim)
    value_heads = value_piece.reshape(value_piece.shape[0], head_count, head_dim)
    scores = (
        jnp.einsum("qhd,khd->qhk", query_heads, key_heads, preferred_element_type=jnp.float32)
        * scale_factor
    )
    raised = jnp.maximum(highest, jnp.max(scores, axis=-1))
    fade = jnp.exp(highest - raised)
    weights = jnp.exp(scores - raised[..., None])
    totals = totals * fade + jnp.sum(weights, axis=-1)
    accum = accum * fade[..., None] + jnp.einsum(
        "qhk,khd->qhd",
        weights.astype(jnp.bfloat16),
        value_heads,
        preferred_element_type=jnp.float32,
    )
    return (accum, totals, raised)


def gather_body(queries, keys_proj, values, hidden, fresh_latent, gate_table, noise_step, pattern):
    group_index = lax.axis_index("tm")
    final_index = lax.axis_size("tm") - 1
    query_tok, key_tok, value_tok = (
        lax.all_to_all(queries[0], "seq", split_axis=1, concat_axis=0, tiled=True),
        lax.all_to_all(keys_proj[0], "seq", split_axis=1, concat_axis=0, tiled=True),
        lax.all_to_all(values[0], "seq", split_axis=1, concat_axis=0, tiled=True),
    )
    row_count, local_width = query_tok.shape
    head_count = local_width // HD
    query_heads = query_tok.reshape(row_count, head_count, HD)
    scale_factor = 1.0 / math.sqrt(HD)
    reach = lax.dynamic_index_in_dim(pattern, group_index, 0, keepdims=False)
    start_state = (
        jnp.zeros((row_count, head_count, HD), jnp.float32),
        jnp.zeros((row_count, head_count), jnp.float32),
        jnp.full((row_count, head_count), -1e30, jnp.float32),
    )

    def one_block(current, inputs):
        key_block, value_block, flag = inputs
        return (
            lax.cond(
                flag > 0,
                lambda state: absorb(state, query_heads, key_block, value_block, scale_factor),
                lambda state: state,
                current,
            ),
            None,
        )

    key_piece = lax.all_gather(key_tok, "tm", axis=0, tiled=False)
    value_piece = lax.all_gather(value_tok, "tm", axis=0, tiled=False)
    state, unused = lax.scan(one_block, start_state, (key_piece, value_piece, reach))
    cache_keys, cache_values = shifted((key_tok, value_tok), "tm", -1)
    accum, totals, highest = state
    attended_head = (accum / totals[..., None]).reshape(row_count, local_width).astype(jnp.bfloat16)
    attended = lax.all_to_all(attended_head, "seq", split_axis=0, concat_axis=1, tiled=True)
    gate_row = lax.dynamic_index_in_dim(gate_table, noise_step[0], 0, keepdims=False)
    updated = (
        hidden[0].astype(jnp.float32) + gate_row[None, :] * attended.astype(jnp.float32)
    ).astype(jnp.bfloat16)
    moved = shifted(updated, "tm", -1)
    advanced = jnp.where(group_index == final_index, fresh_latent, moved)[None]
    next_cache = jnp.stack([cache_keys, cache_values], axis=0)[None]
    return (advanced, next_cache)


def body(queries, *others):
    tm_count, seq_count = lax.axis_size("tm"), lax.axis_size("seq")
    _, tok, width = queries.shape
    count = tm_count * seq_count
    even = width % (count * HD) == 0 and tok % 8 == 0 and seq_count % 2 == 0
    return (spread_body if even else gather_body)(queries, *others)


def solution(mesh):
    placed = (
        P("tm", "seq", None),
        P("tm", "seq", None),
        P("tm", "seq", None),
        P("tm", "seq", None),
        P("seq", None),
        P(),
        P("tm"),
        P(),
    )
    return jax.shard_map(
        body,
        mesh=mesh,
        in_specs=placed,
        out_specs=(P("tm", "seq", None), P("tm", None, None, "seq")),
        check_vma=False,
    )
```

profile of v0, /device:TPU:0, one launch (start us, length us, event | category | flops | bytes accessed | tf_op | source)
XLA Modules:
  0.0 57.4 jit_solution(9269565663910788281)
XLA Ops:
  1.3 2.5 %pack.1 = (bf16[768,384]{1,0:T(8,128)(2,1)}, bf16[32,4096]{1,0:T(8,128)(2,1)}) custom-call(s32[1]{0:T(128)S(6)} %copy.10.noise_ref, bf16[1,24,4096]{2,1,0:T(8,128)(2,1)} %q_ref.1, bf16[1,24,4096]{2,1,0:T(8,128)(2,1)} %k_ref.1, bf16[1,24,4096]{2,1,0:T(8,128)(2,1)} %v_ref.1, bf16[1,24,4096]{2,1,0:T(8,128)(2,1)} %h_ref.1, f32[50,4096]{1,0:T(8,128)} %gate_ref.1), custom_call_target="tpu_custom_call" | custom-call | tf_op jit(solution)/shard_map/pack/pallas_call | solution.py:120
  3.8 25.2 %all_to_all.27 = bf16[32,24,384]{2,1,0:T(8,128)(2,1)} all-to-all(bf16[32,24,384]{2,1,0:T(8,128)(2,1)} %bitcast.6), channel_id=1, replica_groups=mesh['tm'=4,'seq'=8] {'tm','seq'}, dimensions={0} | all-to-all | bytes 1179648 | tf_op jit(solution)/shard_map/all_to_all | solution.py:131
  29.0 3.0 %attend.1 = (bf16[768,128]{1,0:T(8,128)(2,1)}, bf16[4,192,256]{2,1,0:T(8,128)(2,1)}) custom-call(s32[4,4]{1,0:T(4,128)} %pattern_ref.1, bf16[768,384]{1,0:T(8,128)(2,1)} %bitcast.4), custom_call_target="tpu_custom_call" | custom-call | tf_op jit(solution)/shard_map/attend/pallas_call | solution.py:134
  32.0 11.6 %all_to_all.28.in_ref = bf16[4,192,256]{2,1,0:T(8,128)(2,1)} all-to-all(bf16[4,192,256]{2,1,0:T(8,128)(2,1)} %get-tuple-element.9), channel_id=1, replica_groups=mesh['tm'=4,'seq'=8] {'tm'}, dimensions={0} | all-to-all | bytes 786432 | tf_op jit(solution)/shard_map/all_to_all | solution.py:146
  43.6 0.0 copy-start.2
  43.6 2.7 %all-to-all-start.1 = ((bf16[32,24,128]{2,1,0:T(8,128)(2,1)}), bf16[32,24,128]{2,1,0:T(8,128)(2,1)S(1)}, u32[]{:S(2)}, u32[]{:S(2)}) async-start(bf16[32,24,128]{2,1,0:T(8,128)(2,1)} %bitcast.2), calls=%async_computation.1 | async-start | bytes 393216 | tf_op jit(solution)/shard_map/all_to_all | solution.py:145
  46.3 0.0 copy-done.2
  46.3 1.3 %collective-permute-start = (bf16[32,4096]{1,0:T(8,128)(2,1)S(1)}, bf16[32,4096]{1,0:T(8,128)(2,1)S(1)}, u32[]{:S(2)}, u32[]{:S(2)}) collective-permute-start(bf16[32,4096]{1,0:T(8,128)(2,1)S(1)} %copy-done.2), channel_id=1, source_target_pairs={{8,0},{16,8},{24,16},{9,1},{17,9},{25,17},{10,2},{18,10},{26,18},{... | collective-permute-start | bytes 786440 | tf_op jit(solution)/shard_map/ppermute | solution.py:20
  47.6 1.8 %cache.1 = bf16[1,2,192,512]{3,2,1,0:T(8,128)(2,1)} custom-call(bf16[4,192,256]{2,1,0:T(8,128)(2,1)} %all_to_all.28.in_ref), custom_call_target="tpu_custom_call" | custom-call | tf_op jit(solution)/shard_map/cache/pallas_call | solution.py:148
  49.4 0.3 collective-permute-done.moved_ref
  49.7 0.0 copy-start.1
  49.7 5.1 %all-to-all-done.1 = bf16[32,24,128]{2,1,0:T(8,128)(2,1)S(1)} async-done(((bf16[32,24,128]{2,1,0:T(8,128)(2,1)}), bf16[32,24,128]{2,1,0:T(8,128)(2,1)S(1)}, u32[]{:S(2)}, u32[]{:S(2)}) %all-to-all-start.1) | async-done | bytes 196640 | tf_op jit(solution)/shard_map/all_to_all | solution.py:145
  54.9 0.0 copy-start
  54.9 0.0 copy-done.1
  54.9 0.7 %copy-done = bf16[32,24,128]{2,1,0:T(8,128)(2,1)} copy-done((bf16[32,24,128]{2,1,0:T(8,128)(2,1)}, bf16[32,24,128]{2,1,0:T(8,128)(2,1)S(1)}, u32[]{:S(2)}) %copy-start) | copy-done | bytes 196632
  55.5 1.9 %update.1 = bf16[1,24,4096]{2,1,0:T(8,128)(2,1)} custom-call(bf16[768,128]{1,0:T(8,128)(2,1)} %bitcast.5, bf16[32,4096]{1,0:T(8,128)(2,1)} %copy-done.1, bf16[24,4096]{1,0:T(8,128)(2,1)} %fresh_ref.1), custom_call_target="tpu_custom_call" | custom-call | tf_op jit(solution)/shard_map/update/pallas_call | solution.py:155
Async XLA Ops:
  43.6 2.7 %copy-start.2 = (bf16[32,4096]{1,0:T(8,128)(2,1)S(1)}, bf16[32,4096]{1,0:T(8,128)(2,1)}, u32[]{:S(2)}) copy-start(bf16[32,4096]{1,0:T(8,128)(2,1)} %get-tuple-element.8) | copy-start | bytes 786436
  43.6 11.3 %all-to-all-start.1 = ((bf16[32,24,128]{2,1,0:T(8,128)(2,1)}), bf16[32,24,128]{2,1,0:T(8,128)(2,1)S(1)}, u32[]{:S(2)}, u32[]{:S(2)}) async-start(bf16[32,24,128]{2,1,0:T(8,128)(2,1)} %bitcast.2), calls=%async_computation.1 | async-start | bytes 393216 | tf_op jit(solution)/shard_map/all_to_all | solution.py:145
  46.3 3.4 %collective-permute-start = (bf16[32,4096]{1,0:T(8,128)(2,1)S(1)}, bf16[32,4096]{1,0:T(8,128)(2,1)S(1)}, u32[]{:S(2)}, u32[]{:S(2)}) collective-permute-start(bf16[32,4096]{1,0:T(8,128)(2,1)S(1)} %copy-done.2), channel_id=1, source_target_pairs={{8,0},{16,8},{24,16},{9,1},{17,9},{25,17},{10,2},{18,10},{26,18},{... | collective-permute-start | bytes 786440 | tf_op jit(solution)/shard_map/ppermute | solution.py:20
  49.7 5.1 %copy-start.1 = (bf16[32,4096]{1,0:T(8,128)(2,1)}, bf16[32,4096]{1,0:T(8,128)(2,1)S(1)}, u32[]{:S(2)}) copy-start(bf16[32,4096]{1,0:T(8,128)(2,1)S(1)} %collective-permute-done.moved_ref) | copy-start | bytes 786436
  54.9 0.7 %copy-start = (bf16[32,24,128]{2,1,0:T(8,128)(2,1)}, bf16[32,24,128]{2,1,0:T(8,128)(2,1)S(1)}, u32[]{:S(2)}) copy-start(bf16[32,24,128]{2,1,0:T(8,128)(2,1)S(1)} %all-to-all-done.1) | copy-start | bytes 589828
where the time goes:
time: 57.9 us; the launch traced here: 57.4 us
  blocking collectives  36.8 us (64%)
  Pallas kernels  9.2 us (16%)
  waiting for transfers between devices  5.44 us (9%)
  starting transfers between devices  4 us (7%)
  between operations  1.31 us (2%)
  local copies, waits for them, and re-layouts  0.67 us (1%)
    all_to_all x1, blocking collectives, spread_body(): lax.all_to_all(packed, BOTH, split_axis=0, concat_axis=0, tiled=True)  25.2 us
    all_to_all x1, blocking collectives, spread_body(): lax.all_to_all(handed, 'tm', split_axis=0, concat_axis=0, tiled=True)  11.6 us
    all_to_all x1, waiting for transfers between devices, spread_body(): lax.all_to_all(attended, BOTH, split_axis=0, concat_axis=0, tiled=True)  5.12 us
    pallas_call x1, Pallas kernels, spread_body(): pl.pallas_call(functools.partial(attend_kernel, tok), out_shape=(jax.Shap...  2.98 us
    all_to_all x1, starting transfers between devices, spread_body(): lax.all_to_all(attended, BOTH, split_axis=0, concat_axis=0, tiled=True)  2.71 us
    pallas_call x1, Pallas kernels, spread_body(): pl.pallas_call(functools.partial(pack_kernel, seq_count), out_shape=(jax....  2.55 us
    pallas_call x1, Pallas kernels, spread_body(): pl.pallas_call(functools.partial(update_kernel, seq_count, tm_count), out...  1.87 us
    pallas_call x1, Pallas kernels, spread_body(): pl.pallas_call(cache_kernel, out_shape=jax.ShapeDtypeStruct((1, 2, group_...  1.81 us
  transfers between devices with their start and end apart: 2, of which 2 were waited for; matrix products, arithmetic and copies ran while one was open for 0% of the time, Pallas kernels for 3%

commit v1 on v0

--- a/solution.py
+++ b/solution.py
@@ -20,32 +20,38 @@
     return lax.ppermute(block, axis, route)
 
 
-def pack_kernel(seq_count, noise_ref, q_ref, k_ref, v_ref, h_ref, gate_ref, out_ref, moved_ref):
+def pack_kernel(seq_count, q_ref, k_ref, v_ref, out_ref):
     tok = q_ref.shape[1]
     wide = out_ref.shape[1] // 3
     count = out_ref.shape[0] // tok
     tm_count = count // seq_count
-    for pair in range(count // 2):
-        for place, ref in enumerate((q_ref, k_ref, v_ref)):
+    for place, ref in enumerate((q_ref, k_ref, v_ref)):
+        for pair in range(count // 2):
             rows = []
             for dest in (2 * pair, 2 * pair + 1):
                 start = ((dest % seq_count) * tm_count + dest // seq_count) * wide
                 rows.append(ref[0, :, start : start + wide].astype(jnp.float32))
             both = jnp.concatenate(rows, axis=0).astype(jnp.bfloat16)
             out_ref[2 * pair * tok : 2 * (pair + 1) * tok, place * wide : (place + 1) * wide] = both
+
+
+def residual_kernel(noise_ref, h_ref, gate_ref, out_ref):
     gate = gate_ref[pl.ds(noise_ref[0], 1), :]
     high = gate.astype(jnp.bfloat16).astype(jnp.float32)
     middle = (gate - high).astype(jnp.bfloat16).astype(jnp.float32)
     low = gate - high - middle
     parts = jnp.concatenate([high, middle, low, jnp.zeros((5, gate.shape[1]), jnp.float32)], axis=0)
-    moved_ref[...] = jnp.concatenate([h_ref[0].astype(jnp.float32), parts], axis=0).astype(jnp.bfloat16)
-
-
-def attend_kernel(tok, pattern_ref, x_ref, out_ref, cache_ref):
-    groups = cache_ref.shape[0]
+    out_ref[...] = jnp.concatenate([h_ref[0].astype(jnp.float32), parts], axis=0).astype(jnp.bfloat16)
+
+
+def attend_kernel(groups, pattern_ref, x_ref, out_ref, *hand_refs):
     wide = out_ref.shape[1]
     rows = x_ref.shape[0] // groups
     factor = math.log2(math.e) / math.sqrt(HD)
+    here = lax.axis_index("tm")
+    for distance, hand_ref in enumerate(hand_refs, 1):
+        group = lax.rem(here + groups - distance + 1, groups)
+        hand_ref[...] = x_ref[pl.ds(pl.multiple_of(group * rows, rows), rows), wide:]
     for group in range(1, groups):
         span = (group + 1) * rows
         column = lax.broadcasted_iota(jnp.int32, (1, span), 1)
@@ -68,18 +74,28 @@
             out_ref[(group - 1) * rows : group * rows, head : head + HD] = (numer / total).astype(
                 jnp.bfloat16
             )
-        cache_ref[group - 1] = x_ref[group * rows : span, wide:]
     out_ref[(groups - 1) * rows :, :] = jnp.zeros((rows, wide), jnp.bfloat16)
-    cache_ref[groups - 1] = jnp.zeros((rows, 2 * wide), jnp.bfloat16)
-
-
-def cache_kernel(in_ref, out_ref):
-    wide = in_ref.shape[2] // 2
-    for part in range(in_ref.shape[0]):
-        for kind in range(2):
-            out_ref[0, kind, :, part * wide : (part + 1) * wide] = in_ref[
-                part, :, kind * wide : (kind + 1) * wide
-            ]
+
+
+def cache_kernel(x_ref, *refs):
+    hand_refs, out_ref = refs[:-1], refs[-1]
+    groups = len(refs)
+    wide = x_ref.shape[1] // 3
+    rows = out_ref.shape[2]
+    here = lax.axis_index("tm")
+
+    @pl.when(here == groups - 1)
+    def clear():
+        out_ref[...] = jnp.zeros_like(out_ref)
+
+    @pl.when(here < groups - 1)
+    def place():
+        own = x_ref[pl.ds(pl.multiple_of((here + 1) * rows, rows), rows), wide:]
+        for distance, block in enumerate((own,) + hand_refs):
+            source = lax.rem(here + distance, groups)
+            lanes = pl.ds(pl.multiple_of(source * wide, wide), wide)
+            for kind in range(2):
+                out_ref[0, kind, :, lanes] = block[:, kind * wide : (kind + 1) * wide]
 
 
 def update_kernel(seq_count, tm_count, att_ref, moved_ref, fresh_ref, out_ref):
@@ -109,56 +125,77 @@
     return pl.BlockSpec(memory_space=space)
 
 
+def run(kernel, name, out_shape, specs, operands, flops=0):
+    def size(a):
+        return math.prod(a.shape) * a.dtype.itemsize
+
+    outs = jax.tree.leaves(out_shape)
+    moved = sum(map(size, operands)) + sum(map(size, outs))
+    return pl.pallas_call(
+        kernel,
+        out_shape=out_shape,
+        in_specs=specs,
+        out_specs=jax.tree.map(lambda a: whole(), out_shape),
+        compiler_params=pltpu.CompilerParams(vmem_limit_bytes=4 * moved + (4 << 20)),
+        cost_estimate=pl.CostEstimate(flops=flops, bytes_accessed=moved, transcendentals=0),
+        name=name,
+    )(*operands)
+
+
 def spread_body(queries, keys_proj, values, hidden, fresh_latent, gate_table, noise_step, pattern):
     tm_count, seq_count = lax.axis_size("tm"), lax.axis_size("seq")
     count = tm_count * seq_count
     _, tok, width = queries.shape
     wide = width // count
     group_tok = tok * seq_count
-    kind = queries.dtype
-
-    packed, residual = pl.pallas_call(
+    shape = functools.partial(jax.ShapeDtypeStruct, dtype=queries.dtype)
+
+    packed = run(
         functools.partial(pack_kernel, seq_count),
-        out_shape=(
-            jax.ShapeDtypeStruct((count * tok, 3 * wide), kind),
-            jax.ShapeDtypeStruct((tok + 8, width), kind),
-        ),
-        in_specs=[whole(SMEM)] + [whole()] * 5,
-        out_specs=(whole(), whole()),
-        name="pack",
-    )(noise_step, queries, keys_proj, values, hidden, gate_table)
-
+        "pack",
+        shape((count * tok, 3 * wide)),
+        [whole()] * 3,
+        (queries, keys_proj, values),
+    )
     exchanged = lax.all_to_all(packed, BOTH, split_axis=0, concat_axis=0, tiled=True)
+
+    residual = run(
+        residual_kernel,
+        "residual",
+        shape((tok + 8, width)),
+        [whole(SMEM)] + [whole()] * 2,
+        (noise_step, hidden, gate_table),
+    )
     moved = shifted(residual, "tm", -1)
 
-    attended, handed = pl.pallas_call(
-        functools.partial(attend_kernel, tok),
-        out_shape=(
-            jax.ShapeDtypeStruct((count * tok, wide), kind),
-            jax.ShapeDtypeStruct((tm_count, group_tok, 2 * wide), kind),
-        ),
-        in_specs=[whole(SMEM), whole()],
-        out_specs=(whole(), whole()),
-        name="attend",
-    )(pattern, exchanged)
-
+    attended, *hands = run(
+        functools.partial(attend_kernel, tm_count),
+        "attend",
+        [shape((count * tok, wide))] + [shape((group_tok, 2 * wide))] * (tm_count - 1),
+        [whole(SMEM), whole()],
+        (pattern, exchanged),
+        flops=2 * count * tok * count * tok * wide,
+    )
     returned = lax.all_to_all(attended, BOTH, split_axis=0, concat_axis=0, tiled=True)
-    handed = lax.all_to_all(handed, "tm", split_axis=0, concat_axis=0, tiled=True)
-
-    next_cache = pl.pallas_call(
+    handed = []
+    for distance, hand in enumerate(hands, 1):
+        route = [(i, (i - distance) % tm_count) for i in range(tm_count)]
+        handed.append(lax.ppermute(hand, "tm", [(i, j) for i, j in route if j < tm_count - 1]))
+
+    next_cache = run(
         cache_kernel,
-        out_shape=jax.ShapeDtypeStruct((1, 2, group_tok, tm_count * wide), kind),
-        in_specs=[whole()],
-        out_specs=whole(),
-        name="cache",
-    )(handed)
-    advanced = pl.pallas_call(
+        "cache",
+        shape((1, 2, group_tok, tm_count * wide)),
+        [whole()] * tm_count,
+        (exchanged, *handed),
+    )
+    advanced = run(
         functools.partial(update_kernel, seq_count, tm_count),
-        out_shape=jax.ShapeDtypeStruct((1, tok, width), kind),
-        in_specs=[whole()] * 3,
-        out_specs=whole(),
-        name="update",
-    )(returned, moved, fresh_latent)
+        "update",
+        shape((1, tok, width)),
+        [whole()] * 3,
+        (returned, moved, fresh_latent),
+    )
     return (advanced, next_cache)
 
 

time: 57.9 us -> 50.3 us (0.87)
  blocking collectives: 36.8 us -> 24.9 us
  starting transfers between devices: 4 us -> 12.6 us
  Pallas kernels: 9.2 us -> 4.24 us
  local copies, waits for them, and re-layouts: 0.67 us -> 2.8 us
  waiting for transfers between devices: 5.44 us -> 4 us
    all_to_all x1 -> x0, blocking collectives: 11.6 us -> none  [spread_body(): lax.all_to_all(handed, 'tm', split_axis=0, concat_axis=0, tiled=True)]
    ppermute x0 -> x3, starting transfers between devices: none -> 8.63 us  [spread_body(): lax.ppermute(hand, 'tm', [(i, j) for i, j in route if j < tm_count - 1])]
    all_to_all x1, waiting for transfers between devices: 5.12 us -> 0.01 us  [spread_body(): lax.all_to_all(attended, BOTH, split_axis=0, concat_axis=0, tiled=True)]
    pallas_call x4 -> x5, Pallas kernels: 9.2 us -> 4.24 us  [run(): pl.pallas_call(kernel, out_shape=out_shape, in_specs=specs, out_specs=jax...]
    ppermute x0 -> x3, waiting for transfers between devices: none -> 4 us  [spread_body(): lax.ppermute(hand, 'tm', [(i, j) for i, j in route if j < tm_count - 1])]
    unnamed x6 -> x14, local copies, waits for them, and re-layouts: 0.67 us -> 2.8 us
  transfers between devices with their start and end apart: 2 -> 5, of which waited for: 2 -> 2; matrix products, arithmetic and copies ran while one was open for 0% -> 0% of each run, Pallas kernels for 3% -> 2%
where the time goes in v1:
time: 50.3 us; the launch traced here: 49.9 us
  blocking collectives  24.9 us (50%)
  starting transfers between devices  12.6 us (25%)
  Pallas kernels  4.24 us (8%)
  waiting for transfers between devices  4 us (8%)
  local copies, waits for them, and re-layouts  2.8 us (6%)
  between operations  1.39 us (3%)
    all_to_all x1, blocking collectives, spread_body(): lax.all_to_all(packed, BOTH, split_axis=0, concat_axis=0, tiled=True)  24.9 us
    ppermute x3, starting transfers between devices, spread_body(): lax.ppermute(hand, 'tm', [(i, j) for i, j in route if j < tm_count - 1])  8.63 us
    pallas_call x5, Pallas kernels, run(): pl.pallas_call(kernel, out_shape=out_shape, in_specs=specs, out_specs=jax...  4.24 us
    ppermute x3, waiting for transfers between devices, spread_body(): lax.ppermute(hand, 'tm', [(i, j) for i, j in route if j < tm_count - 1])  4 us
    unnamed x14, local copies, waits for them, and re-layouts  2.8 us
    all_to_all x1, starting transfers between devices, spread_body(): lax.all_to_all(attended, BOTH, split_axis=0, concat_axis=0, tiled=True)  2.71 us
    ppermute x1, starting transfers between devices, shifted(): return lax.ppermute(block, axis, route)  1.29 us
  transfers between devices with their start and end apart: 5, of which 2 were waited for; matrix products, arithmetic and copies ran while one was open for 0% of the time, Pallas kernels for 2%

profile of v1, /device:TPU:0, one launch (start us, length us, event | category | flops | bytes accessed | tf_op | source)
XLA Modules:
  0.0 49.9 jit_solution(16135811259229696168)
XLA Ops:
  0.6 0.0 copy-start.1
  0.6 0.9 %copy-done.1 = bf16[1,24,4096]{2,1,0:T(8,128)(2,1)S(1)} copy-done((bf16[1,24,4096]{2,1,0:T(8,128)(2,1)S(1)}, bf16[1,24,4096]{2,1,0:T(8,128)(2,1)}, u32[]{:S(2)}) %copy-start.1) | copy-done | bytes 196632
  1.6 0.0 copy-start.2
  1.6 0.9 %copy-done.2 = bf16[1,24,4096]{2,1,0:T(8,128)(2,1)S(1)} copy-done((bf16[1,24,4096]{2,1,0:T(8,128)(2,1)S(1)}, bf16[1,24,4096]{2,1,0:T(8,128)(2,1)}, u32[]{:S(2)}) %copy-start.2) | copy-done | bytes 196632
  2.5 0.0 copy-start.3
  2.5 0.9 %copy-done.3 = bf16[1,24,4096]{2,1,0:T(8,128)(2,1)S(1)} copy-done((bf16[1,24,4096]{2,1,0:T(8,128)(2,1)S(1)}, bf16[1,24,4096]{2,1,0:T(8,128)(2,1)}, u32[]{:S(2)}) %copy-start.3) | copy-done | bytes 196632
  3.4 0.1 pack.1
  3.5 0.0 copy-start.6
  3.5 0.0 copy-start
  3.5 24.9 %all_to_all.22 = bf16[32,24,384]{2,1,0:T(8,128)(2,1)S(1)} all-to-all(bf16[32,24,384]{2,1,0:T(8,128)(2,1)S(1)} %bitcast.6), channel_id=1, replica_groups=mesh['tm'=4,'seq'=8] {'tm','seq'}, dimensions={0} | all-to-all | bytes 1179648 | tf_op jit(solution)/shard_map/all_to_all | solution.py:160
  28.4 0.0 copy-done.6
  28.4 2.4 %attend.1 = (bf16[768,128]{1,0:T(8,128)(2,1)}, bf16[192,256]{1,0:T(8,128)(2,1)S(1)}, bf16[192,256]{1,0:T(8,128)(2,1)S(1)}, bf16[192,256]{1,0:T(8,128)(2,1)S(1)}) custom-call(s32[4,4]{1,0:T(4,128)S(1)} %copy-done.6, bf16[768,384]{1,0:T(8,128)(2,1)S(1)} %bitcast.4), custom_call_target="tpu_custom_call" | custom-call | flops 150994944 | bytes 1081408 | tf_op jit(solution)/shard_map/attend/pallas_call | solution.py:134
  30.8 0.0 copy-start.4
  30.8 2.7 %all-to-all-start.1 = ((bf16[32,24,128]{2,1,0:T(8,128)(2,1)}), bf16[32,24,128]{2,1,0:T(8,128)(2,1)S(1)}, u32[]{:S(2)}, u32[]{:S(2)}) async-start(bf16[32,24,128]{2,1,0:T(8,128)(2,1)} %bitcast.2), calls=%async_computation.1 | async-start | bytes 393216 | tf_op jit(solution)/shard_map/all_to_all | solution.py:179
  34.2 0.0 copy-done
  34.2 0.0 copy-done.4
  34.2 0.1 residual.1
  34.3 1.3 %collective-permute-start = (bf16[32,4096]{1,0:T(8,128)(2,1)S(1)}, bf16[32,4096]{1,0:T(8,128)(2,1)S(1)}, u32[]{:S(2)}, u32[]{:S(2)}) collective-permute-start(bf16[32,4096]{1,0:T(8,128)(2,1)S(1)} %residual.1), channel_id=1, source_target_pairs={{8,0},{16,8},{24,16},{9,1},{17,9},{25,17},{10,2},{18,10},{26,18},{... | collective-permute-start | bytes 786440 | tf_op jit(solution)/shard_map/ppermute | solution.py:20
  35.6 1.3 %collective-permute-start.1 = (bf16[192,256]{1,0:T(8,128)(2,1)S(1)}, bf16[192,256]{1,0:T(8,128)(2,1)S(1)}, u32[]{:S(2)}, u32[]{:S(2)}) collective-permute-start(bf16[192,256]{1,0:T(8,128)(2,1)S(1)} %get-tuple-element.7), channel_id=1, source_target_pairs={{8,0},{16,8},{24,16},{9,1},{17,9},{25,17},{10,2},{18,10},{26,18},{... | collective-permute-start | bytes 294920 | tf_op jit(solution)/shard_map/ppermute | solution.py:183
  36.9 5.3 %collective-permute-start.2 = (bf16[192,256]{1,0:T(8,128)(2,1)S(1)}, bf16[192,256]{1,0:T(8,128)(2,1)S(1)}, u32[]{:S(2)}, u32[]{:S(2)}) collective-permute-start(bf16[192,256]{1,0:T(8,128)(2,1)S(1)} %get-tuple-element.8), channel_id=1, source_target_pairs={{0,16},{16,0},{24,8},{1,17},{17,1},{25,9},{2,18},{18,2},{26,10},{3... | collective-permute-start | bytes 294920 | tf_op jit(solution)/shard_map/ppermute | solution.py:183
  42.2 0.0 copy-start.5
  42.2 2.1 %collective-permute-start.3 = (bf16[192,256]{1,0:T(8,128)(2,1)S(1)}, bf16[192,256]{1,0:T(8,128)(2,1)S(1)}, u32[]{:S(2)}, u32[]{:S(2)}) collective-permute-start(bf16[192,256]{1,0:T(8,128)(2,1)S(1)} %get-tuple-element.9), channel_id=1, source_target_pairs={{0,8},{8,16},{24,0},{1,9},{9,17},{25,1},{2,10},{10,18},{26,2},{3,1... | collective-permute-start | bytes 294920 | tf_op jit(solution)/shard_map/ppermute | solution.py:183
  44.3 0.0 collective-permute-done.1.refs_0_
  44.3 2.0 %collective-permute-done.2.refs_1_ = bf16[192,256]{1,0:T(8,128)(2,1)S(1)} collective-permute-done((bf16[192,256]{1,0:T(8,128)(2,1)S(1)}, bf16[192,256]{1,0:T(8,128)(2,1)S(1)}, u32[]{:S(2)}, u32[]{:S(2)}) %collective-permute-start.2) | collective-permute-done | bytes 98336 | tf_op jit(solution)/shard_map/ppermute | solution.py:183
  46.3 2.0 %collective-permute-done.3.refs_2_ = bf16[192,256]{1,0:T(8,128)(2,1)S(1)} collective-permute-done((bf16[192,256]{1,0:T(8,128)(2,1)S(1)}, bf16[192,256]{1,0:T(8,128)(2,1)S(1)}, u32[]{:S(2)}, u32[]{:S(2)}) %collective-permute-start.3) | collective-permute-done | bytes 98336 | tf_op jit(solution)/shard_map/ppermute | solution.py:183
  48.3 0.9 %cache.1 = bf16[1,2,192,512]{3,2,1,0:T(8,128)(2,1)} custom-call(bf16[768,384]{1,0:T(8,128)(2,1)S(1)} %bitcast.5, bf16[192,256]{1,0:T(8,128)(2,1)S(1)} %collective-permute-done.1.refs_0_, bf16[192,256]{1,0:T(8,128)(2,1)S(1)} %collective-permute-done.2.refs_1_, bf16[192,256]{1,0:T(8,128)(2,1)S(1)} %collective-permute-done.3.refs_2_), custom_call_target="tpu_custom_call" | custom-call | bytes 1277952 | tf_op jit(solution)/shard_map/cache/pallas_call | solution.py:134
  49.1 0.0 collective-permute-done.moved_ref
  49.1 0.0 all-to-all-done.1
  49.1 0.0 copy-done.5
  49.1 0.8 %update.1 = bf16[1,24,4096]{2,1,0:T(8,128)(2,1)} custom-call(bf16[768,128]{1,0:T(8,128)(2,1)S(1)} %bitcast.7, bf16[32,4096]{1,0:T(8,128)(2,1)S(1)} %collective-permute-done.moved_ref, bf16[24,4096]{1,0:T(8,128)(2,1)S(1)} %copy-done.5), custom_call_target="tpu_custom_call" | custom-call | bytes 851968 | tf_op jit(solution)/shard_map/update/pallas_call | solution.py:134
Async XLA Ops:
  0.6 0.9 %copy-start.1 = (bf16[1,24,4096]{2,1,0:T(8,128)(2,1)S(1)}, bf16[1,24,4096]{2,1,0:T(8,128)(2,1)}, u32[]{:S(2)}) copy-start(bf16[1,24,4096]{2,1,0:T(8,128)(2,1)} %q_ref.1) | copy-start | bytes 589828
  1.6 0.9 %copy-start.2 = (bf16[1,24,4096]{2,1,0:T(8,128)(2,1)S(1)}, bf16[1,24,4096]{2,1,0:T(8,128)(2,1)}, u32[]{:S(2)}) copy-start(bf16[1,24,4096]{2,1,0:T(8,128)(2,1)} %k_ref.1) | copy-start | bytes 589828
  2.5 0.9 %copy-start.3 = (bf16[1,24,4096]{2,1,0:T(8,128)(2,1)S(1)}, bf16[1,24,4096]{2,1,0:T(8,128)(2,1)}, u32[]{:S(2)}) copy-start(bf16[1,24,4096]{2,1,0:T(8,128)(2,1)} %v_ref.1) | copy-start | bytes 589828
  3.5 24.9 %copy-start.6 = (s32[4,4]{1,0:T(4,128)S(1)}, s32[4,4]{1,0:T(4,128)}, u32[]{:S(2)}) copy-start(s32[4,4]{1,0:T(4,128)} %pattern_ref.1) | copy-start | bytes 196
  3.5 30.7 %copy-start = (f32[50,4096]{1,0:T(8,128)S(1)}, f32[50,4096]{1,0:T(8,128)}, u32[]{:S(2)}) copy-start(f32[50,4096]{1,0:T(8,128)} %gate_ref.1) | copy-start | bytes 2457604
  30.8 3.4 %copy-start.4 = (bf16[1,24,4096]{2,1,0:T(8,128)(2,1)S(1)}, bf16[1,24,4096]{2,1,0:T(8,128)(2,1)}, u32[]{:S(2)}) copy-start(bf16[1,24,4096]{2,1,0:T(8,128)(2,1)} %h_ref.1) | copy-start | bytes 589828
  30.8 18.3 %all-to-all-start.1 = ((bf16[32,24,128]{2,1,0:T(8,128)(2,1)}), bf16[32,24,128]{2,1,0:T(8,128)(2,1)S(1)}, u32[]{:S(2)}, u32[]{:S(2)}) async-start(bf16[32,24,128]{2,1,0:T(8,128)(2,1)} %bitcast.2), calls=%async_computation.1 | async-start | bytes 393216 | tf_op jit(solution)/shard_map/all_to_all | solution.py:179
  34.3 14.8 %collective-permute-start = (bf16[32,4096]{1,0:T(8,128)(2,1)S(1)}, bf16[32,4096]{1,0:T(8,128)(2,1)S(1)}, u32[]{:S(2)}, u32[]{:S(2)}) collective-permute-start(bf16[32,4096]{1,0:T(8,128)(2,1)S(1)} %residual.1), channel_id=1, source_target_pairs={{8,0},{16,8},{24,16},{9,1},{17,9},{25,17},{10,2},{18,10},{26,18},{... | collective-permute-start | bytes 786440 | tf_op jit(solution)/shard_map/ppermute | solution.py:20
  35.6 8.7 %collective-permute-start.1 = (bf16[192,256]{1,0:T(8,128)(2,1)S(1)}, bf16[192,256]{1,0:T(8,128)(2,1)S(1)}, u32[]{:S(2)}, u32[]{:S(2)}) collective-permute-start(bf16[192,256]{1,0:T(8,128)(2,1)S(1)} %get-tuple-element.7), channel_id=1, source_target_pairs={{8,0},{16,8},{24,16},{9,1},{17,9},{25,17},{10,2},{18,10},{26,18},{... | collective-permute-start | bytes 294920 | tf_op jit(solution)/shard_map/ppermute | solution.py:183
  36.9 9.4 %collective-permute-start.2 = (bf16[192,256]{1,0:T(8,128)(2,1)S(1)}, bf16[192,256]{1,0:T(8,128)(2,1)S(1)}, u32[]{:S(2)}, u32[]{:S(2)}) collective-permute-start(bf16[192,256]{1,0:T(8,128)(2,1)S(1)} %get-tuple-element.8), channel_id=1, source_target_pairs={{0,16},{16,0},{24,8},{1,17},{17,1},{25,9},{2,18},{18,2},{26,10},{3... | collective-permute-start | bytes 294920 | tf_op jit(solution)/shard_map/ppermute | solution.py:183
  42.2 6.9 %copy-start.5 = (bf16[24,4096]{1,0:T(8,128)(2,1)S(1)}, bf16[24,4096]{1,0:T(8,128)(2,1)}, u32[]{:S(2)}) copy-start(bf16[24,4096]{1,0:T(8,128)(2,1)} %fresh_ref.1) | copy-start | bytes 589828
  42.2 6.1 %collective-permute-start.3 = (bf16[192,256]{1,0:T(8,128)(2,1)S(1)}, bf16[192,256]{1,0:T(8,128)(2,1)S(1)}, u32[]{:S(2)}, u32[]{:S(2)}) collective-permute-start(bf16[192,256]{1,0:T(8,128)(2,1)S(1)} %get-tuple-element.9), channel_id=1, source_target_pairs={{0,8},{8,16},{24,0},{1,9},{9,17},{25,1},{2,10},{10,18},{26,2},{3,1... | collective-permute-start | bytes 294920 | tf_op jit(solution)/shard_map/ppermute | solution.py:183

commit v2 on v1

--- a/solution.py
+++ b/solution.py
@@ -20,22 +20,30 @@
     return lax.ppermute(block, axis, route)
 
 
-def pack_kernel(seq_count, q_ref, k_ref, v_ref, out_ref):
-    tok = q_ref.shape[1]
+def pack_kernel(seq_count, q_hbm, k_hbm, v_hbm, out_ref, *scratch):
+    held, sems = scratch
+    tok = held.shape[1]
     wide = out_ref.shape[1] // 3
     count = out_ref.shape[0] // tok
     tm_count = count // seq_count
-    for place, ref in enumerate((q_ref, k_ref, v_ref)):
+    copies = [
+        pltpu.make_async_copy(ref.at[0], held.at[place], sems.at[place])
+        for place, ref in enumerate((q_hbm, k_hbm, v_hbm))
+    ]
+    for copy in copies:
+        copy.start()
+    for place, copy in enumerate(copies):
+        copy.wait()
         for pair in range(count // 2):
             rows = []
             for dest in (2 * pair, 2 * pair + 1):
                 start = ((dest % seq_count) * tm_count + dest // seq_count) * wide
-                rows.append(ref[0, :, start : start + wide].astype(jnp.float32))
+                rows.append(held[place, :, start : start + wide].astype(jnp.float32))
             both = jnp.concatenate(rows, axis=0).astype(jnp.bfloat16)
             out_ref[2 * pair * tok : 2 * (pair + 1) * tok, place * wide : (place + 1) * wide] = both
 
 
-def residual_kernel(noise_ref, h_ref, gate_ref, out_ref):
+def residual_kernel(noise_ref, h_ref, gate_ref, after_ref, out_ref):
     gate = gate_ref[pl.ds(noise_ref[0], 1), :]
     high = gate.astype(jnp.bfloat16).astype(jnp.float32)
     middle = (gate - high).astype(jnp.bfloat16).astype(jnp.float32)
@@ -44,13 +52,17 @@
     out_ref[...] = jnp.concatenate([h_ref[0].astype(jnp.float32), parts], axis=0).astype(jnp.bfloat16)
 
 
-def attend_kernel(groups, pattern_ref, x_ref, out_ref, *hand_refs):
+def partner(here, distance, groups):
+    return here ^ distance if groups & (groups - 1) == 0 else (here + groups - distance) % groups
+
+
+def attend_kernel(groups, pattern_ref, x_ref, after_ref, out_ref, *hand_refs):
     wide = out_ref.shape[1]
     rows = x_ref.shape[0] // groups
     factor = math.log2(math.e) / math.sqrt(HD)
     here = lax.axis_index("tm")
     for distance, hand_ref in enumerate(hand_refs, 1):
-        group = lax.rem(here + groups - distance + 1, groups)
+        group = lax.rem(partner(here, distance, groups) + 1, groups)
         hand_ref[...] = x_ref[pl.ds(pl.multiple_of(group * rows, rows), rows), wide:]
     for group in range(1, groups):
         span = (group + 1) * rows
@@ -92,7 +104,7 @@
     def place():
         own = x_ref[pl.ds(pl.multiple_of((here + 1) * rows, rows), rows), wide:]
         for distance, block in enumerate((own,) + hand_refs):
-            source = lax.rem(here + distance, groups)
+            source = partner(here, groups - distance if groups & (groups - 1) else distance, groups)
             lanes = pl.ds(pl.multiple_of(source * wide, wide), wide)
             for kind in range(2):
                 out_ref[0, kind, :, lanes] = block[:, kind * wide : (kind + 1) * wide]
@@ -125,7 +137,7 @@
     return pl.BlockSpec(memory_space=space)
 
 
-def run(kernel, name, out_shape, specs, operands, flops=0):
+def run(kernel, name, out_shape, specs, operands, flops=0, scratch=()):
     def size(a):
         return math.prod(a.shape) * a.dtype.itemsize
 
@@ -136,6 +148,7 @@
         out_shape=out_shape,
         in_specs=specs,
         out_specs=jax.tree.map(lambda a: whole(), out_shape),
+        scratch_shapes=scratch,
         compiler_params=pltpu.CompilerParams(vmem_limit_bytes=4 * moved + (4 << 20)),
         cost_estimate=pl.CostEstimate(flops=flops, bytes_accessed=moved, transcendentals=0),
         name=name,
@@ -154,8 +167,9 @@
         functools.partial(pack_kernel, seq_count),
         "pack",
         shape((count * tok, 3 * wide)),
-        [whole()] * 3,
-        (queries, keys_proj, values),
+        [whole(pltpu.HBM)] * 3,
+        [pltpu.with_memory_space_constraint(a, pltpu.HBM) for a in (queries, keys_proj, values)],
+        scratch=[VMEM((3, tok, width), queries.dtype), pltpu.SemaphoreType.DMA((3,))],
     )
     exchanged = lax.all_to_all(packed, BOTH, split_axis=0, concat_axis=0, tiled=True)
 
@@ -163,8 +177,8 @@
         residual_kernel,
         "residual",
         shape((tok + 8, width)),
-        [whole(SMEM)] + [whole()] * 2,
-        (noise_step, hidden, gate_table),
+        [whole(SMEM), whole(), whole(), whole(pl.ANY)],
+        (noise_step, hidden, gate_table, packed),
     )
     moved = shifted(residual, "tm", -1)
 
@@ -172,14 +186,14 @@
         functools.partial(attend_kernel, tm_count),
         "attend",
         [shape((count * tok, wide))] + [shape((group_tok, 2 * wide))] * (tm_count - 1),
-        [whole(SMEM), whole()],
-        (pattern, exchanged),
+        [whole(SMEM), whole(), whole(pl.ANY)],
+        (pattern, exchanged, moved),
         flops=2 * count * tok * count * tok * wide,
     )
     returned = lax.all_to_all(attended, BOTH, split_axis=0, concat_axis=0, tiled=True)
     handed = []
     for distance, hand in enumerate(hands, 1):
-        route = [(i, (i - distance) % tm_count) for i in range(tm_count)]
+        route = [(i, partner(i, distance, tm_count)) for i in range(tm_count)]
         handed.append(lax.ppermute(hand, "tm", [(i, j) for i, j in route if j < tm_count - 1]))
 
     next_cache = run(

time: 50.3 us -> 46.5 us (0.924)
  blocking collectives: 24.9 us -> 0 us
  waiting for transfers between devices: 4 us -> 21 us
  starting transfers between devices: 12.6 us -> 17.5 us
  local copies, waits for them, and re-layouts: 2.8 us -> 0.02 us
  Pallas kernels: 4.24 us -> 6.18 us
    all_to_all x1 -> x0, blocking collectives: 24.9 us -> none  [spread_body(): lax.all_to_all(packed, BOTH, split_axis=0, concat_axis=0, tiled=True)]
    all_to_all x0 -> x1, waiting for transfers between devices: none -> 13.6 us  [spread_body(): lax.all_to_all(packed, BOTH, split_axis=0, concat_axis=0, tiled=True)]
    all_to_all x0 -> x1, starting transfers between devices: none -> 7.3 us  [spread_body(): lax.all_to_all(packed, BOTH, split_axis=0, concat_axis=0, tiled=True)]
    unnamed x14 -> x8, local copies, waits for them, and re-layouts: 2.8 us -> 0.02 us
    ppermute x3, starting transfers between devices: 8.63 us -> 6.28 us  [spread_body(): lax.ppermute(hand, 'tm', [(i, j) for i, j in route if j < tm_count - 1])]
    ppermute x1, waiting for transfers between devices: 0.01 us -> 2.13 us  [shifted(): return lax.ppermute(block, axis, route)]
    pallas_call x5, Pallas kernels: 4.24 us -> 6.18 us  [run(): pl.pallas_call(kernel, out_shape=out_shape, in_specs=specs, out_specs=jax...]
    ppermute x3, waiting for transfers between devices: 4 us -> 5.36 us  [spread_body(): lax.ppermute(hand, 'tm', [(i, j) for i, j in route if j < tm_count - 1])]
  transfers between devices with their start and end apart: 5 -> 6, of which waited for: 2 -> 4; matrix products, arithmetic and copies ran while one was open for 0% -> 0% of each run, Pallas kernels for 2% -> 2%
where the time goes in v2:
time: 46.5 us; the launch traced here: 46.1 us
  waiting for transfers between devices  21 us (45%)
  starting transfers between devices  17.5 us (38%)
  Pallas kernels  6.18 us (13%)
  between operations  1.4 us (3%)
    all_to_all x1, waiting for transfers between devices, spread_body(): lax.all_to_all(packed, BOTH, split_axis=0, concat_axis=0, tiled=True)  13.6 us
    all_to_all x1, starting transfers between devices, spread_body(): lax.all_to_all(packed, BOTH, split_axis=0, concat_axis=0, tiled=True)  7.3 us
    ppermute x3, starting transfers between devices, spread_body(): lax.ppermute(hand, 'tm', [(i, j) for i, j in route if j < tm_count - 1])  6.28 us
    pallas_call x5, Pallas kernels, run(): pl.pallas_call(kernel, out_shape=out_shape, in_specs=specs, out_specs=jax...  6.18 us
    ppermute x3, waiting for transfers between devices, spread_body(): lax.ppermute(hand, 'tm', [(i, j) for i, j in route if j < tm_count - 1])  5.36 us
    all_to_all x1, starting transfers between devices, spread_body(): lax.all_to_all(attended, BOTH, split_axis=0, concat_axis=0, tiled=True)  2.58 us
    ppermute x1, waiting for transfers between devices, shifted(): return lax.ppermute(block, axis, route)  2.13 us
    ppermute x1, starting transfers between devices, shifted(): return lax.ppermute(block, axis, route)  1.29 us
  transfers between devices with their start and end apart: 6, of which 4 were waited for; matrix products, arithmetic and copies ran while one was open for 0% of the time, Pallas kernels for 2%

profile of v2, /device:TPU:0, one launch (start us, length us, event | category | flops | bytes accessed | tf_op | source)
XLA Modules:
  0.0 46.1 jit_solution(7420353820113328880)
XLA Ops:
  0.6 0.0 copy-start
  0.6 2.1 %pack.1.after_ref = bf16[768,384]{1,0:T(8,128)(2,1)} custom-call(bf16[1,24,4096]{2,1,0:T(8,128)(2,1)} %q_hbm.1, bf16[1,24,4096]{2,1,0:T(8,128)(2,1)} %k_hbm.1, bf16[1,24,4096]{2,1,0:T(8,128)(2,1)} %v_hbm.1), custom_call_target="tpu_custom_call" | custom-call | bytes 1179648 | tf_op jit(solution)/shard_map/pack/pallas_call | solution.py:146
  2.7 0.0 copy-start.1
  2.7 7.3 %all-to-all-start = ((bf16[32,24,384]{2,1,0:T(8,128)(2,1)}), bf16[32,24,384]{2,1,0:T(8,128)(2,1)S(1)}, u32[]{:S(2)}, u32[]{:S(2)}) async-start(bf16[32,24,384]{2,1,0:T(8,128)(2,1)} %bitcast), calls=%async_computation | async-start | bytes 1179648 | tf_op jit(solution)/shard_map/all_to_all | solution.py:174
  10.7 0.0 copy-done
  10.7 0.0 copy-done.1
  10.7 0.0 copy-start.3
  10.7 0.1 residual.1
  10.8 1.3 %collective-permute-start = (bf16[32,4096]{1,0:T(8,128)(2,1)S(1)}, bf16[32,4096]{1,0:T(8,128)(2,1)S(1)}, u32[]{:S(2)}, u32[]{:S(2)}) collective-permute-start(bf16[32,4096]{1,0:T(8,128)(2,1)S(1)} %residual.1), channel_id=1, source_target_pairs={{8,0},{16,8},{24,16},{9,1},{17,9},{25,17},{10,2},{18,10},{26,18},{... | collective-permute-start | bytes 786440 | tf_op jit(solution)/shard_map/ppermute | solution.py:20
  12.1 2.1 %collective-permute-done.after_ref.moved_ref = bf16[32,4096]{1,0:T(8,128)(2,1)S(1)} collective-permute-done((bf16[32,4096]{1,0:T(8,128)(2,1)S(1)}, bf16[32,4096]{1,0:T(8,128)(2,1)S(1)}, u32[]{:S(2)}, u32[]{:S(2)}) %collective-permute-start) | collective-permute-done | bytes 262176 | tf_op jit(solution)/shard_map/ppermute | solution.py:20
  14.3 13.6 %all-to-all-done = bf16[32,24,384]{2,1,0:T(8,128)(2,1)S(1)} async-done(((bf16[32,24,384]{2,1,0:T(8,128)(2,1)}), bf16[32,24,384]{2,1,0:T(8,128)(2,1)S(1)}, u32[]{:S(2)}, u32[]{:S(2)}) %all-to-all-start) | async-done | bytes 589856 | tf_op jit(solution)/shard_map/all_to_all | solution.py:174
  27.8 0.0 copy-done.3
  27.8 2.4 %attend.1 = (bf16[768,128]{1,0:T(8,128)(2,1)}, bf16[192,256]{1,0:T(8,128)(2,1)S(1)}, bf16[192,256]{1,0:T(8,128)(2,1)S(1)}, bf16[192,256]{1,0:T(8,128)(2,1)S(1)}) custom-call(s32[4,4]{1,0:T(4,128)S(1)} %copy-done.3, bf16[768,384]{1,0:T(8,128)(2,1)S(1)} %bitcast.4, bf16[32,4096]{1,0:T(8,128)(2,1)S(1)} %collective-permute-done.after_ref.moved_ref), custom_call_target="tpu_custom_call" | custom-call | flops 150994944 | bytes 1343552 | tf_op jit(solution)/shard_map/attend/pallas_call | solution.py:146
  30.2 2.6 %all-to-all-start.1 = ((bf16[32,24,128]{2,1,0:T(8,128)(2,1)}), bf16[32,24,128]{2,1,0:T(8,128)(2,1)S(1)}, u32[]{:S(2)}, u32[]{:S(2)}) async-start(bf16[32,24,128]{2,1,0:T(8,128)(2,1)} %bitcast.2), calls=%async_computation.1 | async-start | bytes 393216 | tf_op jit(solution)/shard_map/all_to_all | solution.py:193
  32.8 2.0 %collective-permute-start.1 = (bf16[192,256]{1,0:T(8,128)(2,1)S(1)}, bf16[192,256]{1,0:T(8,128)(2,1)S(1)}, u32[]{:S(2)}, u32[]{:S(2)}) collective-permute-start(bf16[192,256]{1,0:T(8,128)(2,1)S(1)} %get-tuple-element.7), channel_id=1, source_target_pairs={{0,8},{8,0},{24,16},{1,9},{9,1},{25,17},{2,10},{10,2},{26,18},{3,1... | collective-permute-start | bytes 294920 | tf_op jit(solution)/shard_map/ppermute | solution.py:197
  34.8 2.8 %collective-permute-start.2 = (bf16[192,256]{1,0:T(8,128)(2,1)S(1)}, bf16[192,256]{1,0:T(8,128)(2,1)S(1)}, u32[]{:S(2)}, u32[]{:S(2)}) collective-permute-start(bf16[192,256]{1,0:T(8,128)(2,1)S(1)} %get-tuple-element.8), channel_id=1, source_target_pairs={{0,16},{16,0},{24,8},{1,17},{17,1},{25,9},{2,18},{18,2},{26,10},{3... | collective-permute-start | bytes 294920 | tf_op jit(solution)/shard_map/ppermute | solution.py:197
  37.7 0.0 copy-start.2
  37.7 1.4 %collective-permute-start.3 = (bf16[192,256]{1,0:T(8,128)(2,1)S(1)}, bf16[192,256]{1,0:T(8,128)(2,1)S(1)}, u32[]{:S(2)}, u32[]{:S(2)}) collective-permute-start(bf16[192,256]{1,0:T(8,128)(2,1)S(1)} %get-tuple-element.9), channel_id=1, source_target_pairs={{8,16},{16,8},{24,0},{9,17},{17,9},{25,1},{10,18},{18,10},{26,2},{... | collective-permute-start | bytes 294920 | tf_op jit(solution)/shard_map/ppermute | solution.py:197
  39.1 0.0 collective-permute-done.1.refs_0_
  39.1 3.3 %collective-permute-done.2.refs_1_ = bf16[192,256]{1,0:T(8,128)(2,1)S(1)} collective-permute-done((bf16[192,256]{1,0:T(8,128)(2,1)S(1)}, bf16[192,256]{1,0:T(8,128)(2,1)S(1)}, u32[]{:S(2)}, u32[]{:S(2)}) %collective-permute-start.2) | collective-permute-done | bytes 98336 | tf_op jit(solution)/shard_map/ppermute | solution.py:197
  42.4 2.1 %collective-permute-done.3.refs_2_ = bf16[192,256]{1,0:T(8,128)(2,1)S(1)} collective-permute-done((bf16[192,256]{1,0:T(8,128)(2,1)S(1)}, bf16[192,256]{1,0:T(8,128)(2,1)S(1)}, u32[]{:S(2)}, u32[]{:S(2)}) %collective-permute-start.3) | collective-permute-done | bytes 98336 | tf_op jit(solution)/shard_map/ppermute | solution.py:197
  44.5 0.8 %cache.1 = bf16[1,2,192,512]{3,2,1,0:T(8,128)(2,1)} custom-call(bf16[768,384]{1,0:T(8,128)(2,1)S(1)} %bitcast.5, bf16[192,256]{1,0:T(8,128)(2,1)S(1)} %collective-permute-done.1.refs_0_, bf16[192,256]{1,0:T(8,128)(2,1)S(1)} %collective-permute-done.2.refs_1_, bf16[192,256]{1,0:T(8,128)(2,1)S(1)} %collective-permute-done.3.refs_2_), custom_call_target="tpu_custom_call" | custom-call | bytes 1277952 | tf_op jit(solution)/shard_map/cache/pallas_call | solution.py:146
  45.3 0.0 all-to-all-done.1
  45.3 0.0 copy-done.2
  45.3 0.8 %update.1 = bf16[1,24,4096]{2,1,0:T(8,128)(2,1)} custom-call(bf16[768,128]{1,0:T(8,128)(2,1)S(1)} %bitcast.6, bf16[32,4096]{1,0:T(8,128)(2,1)S(1)} %collective-permute-done.after_ref.moved_ref, bf16[24,4096]{1,0:T(8,128)(2,1)S(1)} %copy-done.2), custom_call_target="tpu_custom_call" | custom-call | bytes 851968 | tf_op jit(solution)/shard_map/update/pallas_call | solution.py:146
Async XLA Ops:
  0.6 10.1 %copy-start = (f32[50,4096]{1,0:T(8,128)S(1)}, f32[50,4096]{1,0:T(8,128)}, u32[]{:S(2)}) copy-start(f32[50,4096]{1,0:T(8,128)} %gate_ref.1) | copy-start | bytes 2457604
  2.7 8.0 %copy-start.1 = (bf16[1,24,4096]{2,1,0:T(8,128)(2,1)S(1)}, bf16[1,24,4096]{2,1,0:T(8,128)(2,1)}, u32[]{:S(2)}) copy-start(bf16[1,24,4096]{2,1,0:T(8,128)(2,1)} %h_ref.1) | copy-start | bytes 589828
  2.7 25.1 %all-to-all-start = ((bf16[32,24,384]{2,1,0:T(8,128)(2,1)}), bf16[32,24,384]{2,1,0:T(8,128)(2,1)S(1)}, u32[]{:S(2)}, u32[]{:S(2)}) async-start(bf16[32,24,384]{2,1,0:T(8,128)(2,1)} %bitcast), calls=%async_computation | async-start | bytes 1179648 | tf_op jit(solution)/shard_map/all_to_all | solution.py:174
  10.7 17.1 %copy-start.3 = (s32[4,4]{1,0:T(4,128)S(1)}, s32[4,4]{1,0:T(4,128)}, u32[]{:S(2)}) copy-start(s32[4,4]{1,0:T(4,128)} %pattern_ref.1) | copy-start | bytes 196
  10.8 3.4 %collective-permute-start = (bf16[32,4096]{1,0:T(8,128)(2,1)S(1)}, bf16[32,4096]{1,0:T(8,128)(2,1)S(1)}, u32[]{:S(2)}, u32[]{:S(2)}) collective-permute-start(bf16[32,4096]{1,0:T(8,128)(2,1)S(1)} %residual.1), channel_id=1, source_target_pairs={{8,0},{16,8},{24,16},{9,1},{17,9},{25,17},{10,2},{18,10},{26,18},{... | collective-permute-start | bytes 786440 | tf_op jit(solution)/shard_map/ppermute | solution.py:20
  30.2 15.1 %all-to-all-start.1 = ((bf16[32,24,128]{2,1,0:T(8,128)(2,1)}), bf16[32,24,128]{2,1,0:T(8,128)(2,1)S(1)}, u32[]{:S(2)}, u32[]{:S(2)}) async-start(bf16[32,24,128]{2,1,0:T(8,128)(2,1)} %bitcast.2), calls=%async_computation.1 | async-start | bytes 393216 | tf_op jit(solution)/shard_map/all_to_all | solution.py:193
  32.8 6.3 %collective-permute-start.1 = (bf16[192,256]{1,0:T(8,128)(2,1)S(1)}, bf16[192,256]{1,0:T(8,128)(2,1)S(1)}, u32[]{:S(2)}, u32[]{:S(2)}) collective-permute-start(bf16[192,256]{1,0:T(8,128)(2,1)S(1)} %get-tuple-element.7), channel_id=1, source_target_pairs={{0,8},{8,0},{24,16},{1,9},{9,1},{25,17},{2,10},{10,2},{26,18},{3,1... | collective-permute-start | bytes 294920 | tf_op jit(solution)/shard_map/ppermute | solution.py:197
  34.8 7.5 %collective-permute-start.2 = (bf16[192,256]{1,0:T(8,128)(2,1)S(1)}, bf16[192,256]{1,0:T(8,128)(2,1)S(1)}, u32[]{:S(2)}, u32[]{:S(2)}) collective-permute-start(bf16[192,256]{1,0:T(8,128)(2,1)S(1)} %get-tuple-element.8), channel_id=1, source_target_pairs={{0,16},{16,0},{24,8},{1,17},{17,1},{25,9},{2,18},{18,2},{26,10},{3... | collective-permute-start | bytes 294920 | tf_op jit(solution)/shard_map/ppermute | solution.py:197
  37.7 7.6 %copy-start.2 = (bf16[24,4096]{1,0:T(8,128)(2,1)S(1)}, bf16[24,4096]{1,0:T(8,128)(2,1)}, u32[]{:S(2)}) copy-start(bf16[24,4096]{1,0:T(8,128)(2,1)} %fresh_ref.1) | copy-start | bytes 589828
  37.7 6.8 %collective-permute-start.3 = (bf16[192,256]{1,0:T(8,128)(2,1)S(1)}, bf16[192,256]{1,0:T(8,128)(2,1)S(1)}, u32[]{:S(2)}, u32[]{:S(2)}) collective-permute-start(bf16[192,256]{1,0:T(8,128)(2,1)S(1)} %get-tuple-element.9), channel_id=1, source_target_pairs={{8,16},{16,8},{24,0},{9,17},{17,9},{25,1},{10,18},{18,10},{26,2},{... | collective-permute-start | bytes 294920 | tf_op jit(solution)/shard_map/ppermute | solution.py:197

commit v3 on v2

--- a/solution.py
+++ b/solution.py
@@ -90,8 +90,8 @@
 
 
 def cache_kernel(x_ref, *refs):
-    hand_refs, out_ref = refs[:-1], refs[-1]
-    groups = len(refs)
+    hand_refs, out_ref = refs[:-2], refs[-1]
+    groups = len(hand_refs) + 1
     wide = x_ref.shape[1] // 3
     rows = out_ref.shape[2]
     here = lax.axis_index("tm")
@@ -137,7 +137,7 @@
     return pl.BlockSpec(memory_space=space)
 
 
-def run(kernel, name, out_shape, specs, operands, flops=0, scratch=()):
+def run(kernel, name, out_shape, specs, operands, flops=0, scratch=(), space=VMEM):
     def size(a):
         return math.prod(a.shape) * a.dtype.itemsize
 
@@ -145,7 +145,7 @@
     moved = sum(map(size, operands)) + sum(map(size, outs))
     return pl.pallas_call(
         kernel,
-        out_shape=out_shape,
+        out_shape=jax.tree.map(lambda a: space(a.shape, a.dtype), out_shape),
         in_specs=specs,
         out_specs=jax.tree.map(lambda a: whole(), out_shape),
         scratch_shapes=scratch,
@@ -191,24 +191,28 @@
         flops=2 * count * tok * count * tok * wide,
     )
     returned = lax.all_to_all(attended, BOTH, split_axis=0, concat_axis=0, tiled=True)
-    handed = []
-    for distance, hand in enumerate(hands, 1):
+    handed = [None] * len(hands)
+    for distance in range(tm_count - 1, 0, -1):
         route = [(i, partner(i, distance, tm_count)) for i in range(tm_count)]
-        handed.append(lax.ppermute(hand, "tm", [(i, j) for i, j in route if j < tm_count - 1]))
-
-    next_cache = run(
-        cache_kernel,
-        "cache",
-        shape((1, 2, group_tok, tm_count * wide)),
-        [whole()] * tm_count,
-        (exchanged, *handed),
-    )
+        handed[distance - 1] = lax.ppermute(
+            hands[distance - 1], "tm", [(i, j) for i, j in route if j < tm_count - 1]
+        )
+
     advanced = run(
         functools.partial(update_kernel, seq_count, tm_count),
         "update",
         shape((1, tok, width)),
         [whole()] * 3,
         (returned, moved, fresh_latent),
+        space=pltpu.HBM,
+    )
+    next_cache = run(
+        cache_kernel,
+        "cache",
+        shape((1, 2, group_tok, tm_count * wide)),
+        [whole()] * tm_count + [whole(pltpu.HBM)],
+        (exchanged, *handed, pltpu.with_memory_space_constraint(advanced, pltpu.HBM)),
+        space=pltpu.HBM,
     )
     return (advanced, next_cache)
 

time: 46.5 us -> 45.8 us (0.985)
  waiting for transfers between devices: 21 us -> 20.4 us
    ppermute x3, waiting for transfers between devices: 5.36 us -> 2.35 us  [spread_body(): lax.ppermute(hands[distance - 1], 'tm', [(i, j) for i, j in route if j <...]
    all_to_all x1, waiting for transfers between devices: 0.01 us -> 2.39 us  [spread_body(): lax.all_to_all(attended, BOTH, split_axis=0, concat_axis=0, tiled=True)]
  transfers between devices with their start and end apart: 6 -> 6, of which waited for: 4 -> 5; matrix products, arithmetic and copies ran while one was open for 0% -> 0% of each run, Pallas kernels for 2% -> 2%
where the time goes in v3:
time: 45.8 us; the launch traced here: 45.5 us
  waiting for transfers between devices  20.4 us (45%)
  starting transfers between devices  17.5 us (38%)
  Pallas kernels  6.18 us (13%)
  between operations  1.38 us (3%)
    all_to_all x1, waiting for transfers between devices, spread_body(): lax.all_to_all(packed, BOTH, split_axis=0, concat_axis=0, tiled=True)  13.6 us
    all_to_all x1, starting transfers between devices, spread_body(): lax.all_to_all(packed, BOTH, split_axis=0, concat_axis=0, tiled=True)  7.3 us
    pallas_call x5, Pallas kernels, run(): pl.pallas_call(kernel, out_shape=jax.tree.map(lambda a: space(a.shape, a....  6.18 us
    ppermute x3, starting transfers between devices, spread_body(): lax.ppermute(hands[distance - 1], 'tm', [(i, j) for i, j in route if j <...  6.15 us
    all_to_all x1, starting transfers between devices, spread_body(): lax.all_to_all(attended, BOTH, split_axis=0, concat_axis=0, tiled=True)  2.71 us
    all_to_all x1, waiting for transfers between devices, spread_body(): lax.all_to_all(attended, BOTH, split_axis=0, concat_axis=0, tiled=True)  2.39 us
    ppermute x3, waiting for transfers between devices, spread_body(): lax.ppermute(hands[distance - 1], 'tm', [(i, j) for i, j in route if j <...  2.35 us
    ppermute x1, waiting for transfers between devices, shifted(): return lax.ppermute(block, axis, route)  2.13 us
  transfers between devices with their start and end apart: 6, of which 5 were waited for; matrix products, arithmetic and copies ran while one was open for 0% of the time, Pallas kernels for 2%

profile of v3, /device:TPU:0, one launch (start us, length us, event | category | flops | bytes accessed | tf_op | source)
XLA Modules:
  0.0 45.5 jit_solution(8472277131190093483)
XLA Ops:
  0.6 0.0 copy-start
  0.6 2.1 %pack.1.after_ref = bf16[768,384]{1,0:T(8,128)(2,1)} custom-call(bf16[1,24,4096]{2,1,0:T(8,128)(2,1)} %q_hbm.1, bf16[1,24,4096]{2,1,0:T(8,128)(2,1)} %k_hbm.1, bf16[1,24,4096]{2,1,0:T(8,128)(2,1)} %v_hbm.1), custom_call_target="tpu_custom_call" | custom-call | bytes 1179648 | tf_op jit(solution)/shard_map/pack/pallas_call | solution.py:146
  2.7 0.0 copy-start.1
  2.7 7.3 %all-to-all-start = ((bf16[32,24,384]{2,1,0:T(8,128)(2,1)}), bf16[32,24,384]{2,1,0:T(8,128)(2,1)S(1)}, u32[]{:S(2)}, u32[]{:S(2)}) async-start(bf16[32,24,384]{2,1,0:T(8,128)(2,1)} %bitcast), calls=%async_computation | async-start | bytes 1179648 | tf_op jit(solution)/shard_map/all_to_all | solution.py:174
  10.7 0.0 copy-done
  10.7 0.0 copy-done.1
  10.7 0.0 copy-start.3
  10.7 0.1 residual.1
  10.8 1.3 %collective-permute-start = (bf16[32,4096]{1,0:T(8,128)(2,1)S(1)}, bf16[32,4096]{1,0:T(8,128)(2,1)S(1)}, u32[]{:S(2)}, u32[]{:S(2)}) collective-permute-start(bf16[32,4096]{1,0:T(8,128)(2,1)S(1)} %residual.1), channel_id=1, source_target_pairs={{8,0},{16,8},{24,16},{9,1},{17,9},{25,17},{10,2},{18,10},{26,18},{... | collective-permute-start | bytes 786440 | tf_op jit(solution)/shard_map/ppermute | solution.py:20
  12.1 2.1 %collective-permute-done.after_ref.moved_ref = bf16[32,4096]{1,0:T(8,128)(2,1)S(1)} collective-permute-done((bf16[32,4096]{1,0:T(8,128)(2,1)S(1)}, bf16[32,4096]{1,0:T(8,128)(2,1)S(1)}, u32[]{:S(2)}, u32[]{:S(2)}) %collective-permute-start) | collective-permute-done | bytes 262176 | tf_op jit(solution)/shard_map/ppermute | solution.py:20
  14.3 13.6 %all-to-all-done = bf16[32,24,384]{2,1,0:T(8,128)(2,1)S(1)} async-done(((bf16[32,24,384]{2,1,0:T(8,128)(2,1)}), bf16[32,24,384]{2,1,0:T(8,128)(2,1)S(1)}, u32[]{:S(2)}, u32[]{:S(2)}) %all-to-all-start) | async-done | bytes 589856 | tf_op jit(solution)/shard_map/all_to_all | solution.py:174
  27.8 0.0 copy-done.3
  27.8 2.4 %attend.1 = (bf16[768,128]{1,0:T(8,128)(2,1)}, bf16[192,256]{1,0:T(8,128)(2,1)S(1)}, bf16[192,256]{1,0:T(8,128)(2,1)S(1)}, bf16[192,256]{1,0:T(8,128)(2,1)S(1)}) custom-call(s32[4,4]{1,0:T(4,128)S(1)} %copy-done.3, bf16[768,384]{1,0:T(8,128)(2,1)S(1)} %bitcast.4, bf16[32,4096]{1,0:T(8,128)(2,1)S(1)} %collective-permute-done.after_ref.moved_ref), custom_call_target="tpu_custom_call" | custom-call | flops 150994944 | bytes 1343552 | tf_op jit(solution)/shard_map/attend/pallas_call | solution.py:146
  30.2 0.0 copy-start.2
  30.2 2.7 %all-to-all-start.1 = ((bf16[32,24,128]{2,1,0:T(8,128)(2,1)}), bf16[32,24,128]{2,1,0:T(8,128)(2,1)S(1)}, u32[]{:S(2)}, u32[]{:S(2)}) async-start(bf16[32,24,128]{2,1,0:T(8,128)(2,1)} %bitcast.2), calls=%async_computation.1 | async-start | bytes 393216 | tf_op jit(solution)/shard_map/all_to_all | solution.py:193
  32.9 2.0 %collective-permute-start.1 = (bf16[192,256]{1,0:T(8,128)(2,1)S(1)}, bf16[192,256]{1,0:T(8,128)(2,1)S(1)}, u32[]{:S(2)}, u32[]{:S(2)}) collective-permute-start(bf16[192,256]{1,0:T(8,128)(2,1)S(1)} %get-tuple-element.7), channel_id=1, source_target_pairs={{0,8},{8,0},{24,16},{1,9},{9,1},{25,17},{2,10},{10,2},{26,18},{3,1... | collective-permute-start | bytes 294920 | tf_op jit(solution)/shard_map/ppermute | solution.py:197
  35.0 2.8 %collective-permute-start.2 = (bf16[192,256]{1,0:T(8,128)(2,1)S(1)}, bf16[192,256]{1,0:T(8,128)(2,1)S(1)}, u32[]{:S(2)}, u32[]{:S(2)}) collective-permute-start(bf16[192,256]{1,0:T(8,128)(2,1)S(1)} %get-tuple-element.8), channel_id=1, source_target_pairs={{0,16},{16,0},{24,8},{1,17},{17,1},{25,9},{2,18},{18,2},{26,10},{3... | collective-permute-start | bytes 294920 | tf_op jit(solution)/shard_map/ppermute | solution.py:197
  37.8 1.3 %collective-permute-start.3 = (bf16[192,256]{1,0:T(8,128)(2,1)S(1)}, bf16[192,256]{1,0:T(8,128)(2,1)S(1)}, u32[]{:S(2)}, u32[]{:S(2)}) collective-permute-start(bf16[192,256]{1,0:T(8,128)(2,1)S(1)} %get-tuple-element.9), channel_id=1, source_target_pairs={{8,16},{16,8},{24,0},{9,17},{17,9},{25,1},{10,18},{18,10},{26,2},{... | collective-permute-start | bytes 294920 | tf_op jit(solution)/shard_map/ppermute | solution.py:197
  39.1 2.4 %all-to-all-done.1 = bf16[32,24,128]{2,1,0:T(8,128)(2,1)S(1)} async-done(((bf16[32,24,128]{2,1,0:T(8,128)(2,1)}), bf16[32,24,128]{2,1,0:T(8,128)(2,1)S(1)}, u32[]{:S(2)}, u32[]{:S(2)}) %all-to-all-start.1) | async-done | bytes 196640 | tf_op jit(solution)/shard_map/all_to_all | solution.py:193
  41.5 0.0 copy-done.2
  41.5 0.8 %update.1.refs_3_ = bf16[1,24,4096]{2,1,0:T(8,128)(2,1)} custom-call(bf16[768,128]{1,0:T(8,128)(2,1)S(1)} %bitcast.6, bf16[32,4096]{1,0:T(8,128)(2,1)S(1)} %collective-permute-done.after_ref.moved_ref, bf16[24,4096]{1,0:T(8,128)(2,1)S(1)} %copy-done.2), custom_call_target="tpu_custom_call" | custom-call | bytes 851968 | tf_op jit(solution)/shard_map/update/pallas_call | solution.py:146
  42.3 0.0 collective-permute-done.1.refs_0_
  42.3 0.2 collective-permute-done.2.refs_1_
  42.5 2.1 %collective-permute-done.3.refs_2_ = bf16[192,256]{1,0:T(8,128)(2,1)S(1)} collective-permute-done((bf16[192,256]{1,0:T(8,128)(2,1)S(1)}, bf16[192,256]{1,0:T(8,128)(2,1)S(1)}, u32[]{:S(2)}, u32[]{:S(2)}) %collective-permute-start.3) | collective-permute-done | bytes 98336 | tf_op jit(solution)/shard_map/ppermute | solution.py:197
  44.6 0.8 %cache.1 = bf16[1,2,192,512]{3,2,1,0:T(8,128)(2,1)} custom-call(bf16[768,384]{1,0:T(8,128)(2,1)S(1)} %bitcast.5, bf16[192,256]{1,0:T(8,128)(2,1)S(1)} %collective-permute-done.1.refs_0_, bf16[192,256]{1,0:T(8,128)(2,1)S(1)} %collective-permute-done.2.refs_1_, bf16[192,256]{1,0:T(8,128)(2,1)S(1)} %collective-permute-done.3.refs_2_, ...), custom_call_target="tpu_custom_call" | custom-call | bytes 1474560 | tf_op jit(solution)/shard_map/cache/pallas_call | solution.py:146
Async XLA Ops:
  0.6 10.1 %copy-start = (f32[50,4096]{1,0:T(8,128)S(1)}, f32[50,4096]{1,0:T(8,128)}, u32[]{:S(2)}) copy-start(f32[50,4096]{1,0:T(8,128)} %gate_ref.1) | copy-start | bytes 2457604
  2.7 8.0 %copy-start.1 = (bf16[1,24,4096]{2,1,0:T(8,128)(2,1)S(1)}, bf16[1,24,4096]{2,1,0:T(8,128)(2,1)}, u32[]{:S(2)}) copy-start(bf16[1,24,4096]{2,1,0:T(8,128)(2,1)} %h_ref.1) | copy-start | bytes 589828
  2.7 25.1 %all-to-all-start = ((bf16[32,24,384]{2,1,0:T(8,128)(2,1)}), bf16[32,24,384]{2,1,0:T(8,128)(2,1)S(1)}, u32[]{:S(2)}, u32[]{:S(2)}) async-start(bf16[32,24,384]{2,1,0:T(8,128)(2,1)} %bitcast), calls=%async_computation | async-start | bytes 1179648 | tf_op jit(solution)/shard_map/all_to_all | solution.py:174
  10.7 17.1 %copy-start.3 = (s32[4,4]{1,0:T(4,128)S(1)}, s32[4,4]{1,0:T(4,128)}, u32[]{:S(2)}) copy-start(s32[4,4]{1,0:T(4,128)} %pattern_ref.1) | copy-start | bytes 196
  10.8 3.4 %collective-permute-start = (bf16[32,4096]{1,0:T(8,128)(2,1)S(1)}, bf16[32,4096]{1,0:T(8,128)(2,1)S(1)}, u32[]{:S(2)}, u32[]{:S(2)}) collective-permute-start(bf16[32,4096]{1,0:T(8,128)(2,1)S(1)} %residual.1), channel_id=1, source_target_pairs={{8,0},{16,8},{24,16},{9,1},{17,9},{25,17},{10,2},{18,10},{26,18},{... | collective-permute-start | bytes 786440 | tf_op jit(solution)/shard_map/ppermute | solution.py:20
  30.2 11.3 %copy-start.2 = (bf16[24,4096]{1,0:T(8,128)(2,1)S(1)}, bf16[24,4096]{1,0:T(8,128)(2,1)}, u32[]{:S(2)}) copy-start(bf16[24,4096]{1,0:T(8,128)(2,1)} %fresh_ref.1) | copy-start | bytes 589828
  30.2 11.3 %all-to-all-start.1 = ((bf16[32,24,128]{2,1,0:T(8,128)(2,1)}), bf16[32,24,128]{2,1,0:T(8,128)(2,1)S(1)}, u32[]{:S(2)}, u32[]{:S(2)}) async-start(bf16[32,24,128]{2,1,0:T(8,128)(2,1)} %bitcast.2), calls=%async_computation.1 | async-start | bytes 393216 | tf_op jit(solution)/shard_map/all_to_all | solution.py:193
  32.9 9.3 %collective-permute-start.1 = (bf16[192,256]{1,0:T(8,128)(2,1)S(1)}, bf16[192,256]{1,0:T(8,128)(2,1)S(1)}, u32[]{:S(2)}, u32[]{:S(2)}) collective-permute-start(bf16[192,256]{1,0:T(8,128)(2,1)S(1)} %get-tuple-element.7), channel_id=1, source_target_pairs={{0,8},{8,0},{24,16},{1,9},{9,1},{25,17},{2,10},{10,2},{26,18},{3,1... | collective-permute-start | bytes 294920 | tf_op jit(solution)/shard_map/ppermute | solution.py:197
  35.0 7.5 %collective-permute-start.2 = (bf16[192,256]{1,0:T(8,128)(2,1)S(1)}, bf16[192,256]{1,0:T(8,128)(2,1)S(1)}, u32[]{:S(2)}, u32[]{:S(2)}) collective-permute-start(bf16[192,256]{1,0:T(8,128)(2,1)S(1)} %get-tuple-element.8), channel_id=1, source_target_pairs={{0,16},{16,0},{24,8},{1,17},{17,1},{25,9},{2,18},{18,2},{26,10},{3... | collective-permute-start | bytes 294920 | tf_op jit(solution)/shard_map/ppermute | solution.py:197
  37.8 6.8 %collective-permute-start.3 = (bf16[192,256]{1,0:T(8,128)(2,1)S(1)}, bf16[192,256]{1,0:T(8,128)(2,1)S(1)}, u32[]{:S(2)}, u32[]{:S(2)}) collective-permute-start(bf16[192,256]{1,0:T(8,128)(2,1)S(1)} %get-tuple-element.9), channel_id=1, source_target_pairs={{8,16},{16,8},{24,0},{9,17},{17,9},{25,1},{10,18},{18,10},{26,2},{... | collective-permute-start | bytes 294920 | tf_op jit(solution)/shard_map/ppermute | solution.py:197

commit v4 on v3

--- a/solution.py
+++ b/solution.py
@@ -56,12 +56,16 @@
     return here ^ distance if groups & (groups - 1) == 0 else (here + groups - distance) % groups
 
 
+def distances(groups):
+    return range(groups - 1, 0, -1)
+
+
 def attend_kernel(groups, pattern_ref, x_ref, after_ref, out_ref, *hand_refs):
     wide = out_ref.shape[1]
     rows = x_ref.shape[0] // groups
     factor = math.log2(math.e) / math.sqrt(HD)
     here = lax.axis_index("tm")
-    for distance, hand_ref in enumerate(hand_refs, 1):
+    for distance, hand_ref in zip(distances(groups), hand_refs):
         group = lax.rem(partner(here, distance, groups) + 1, groups)
         hand_ref[...] = x_ref[pl.ds(pl.multiple_of(group * rows, rows), rows), wide:]
     for group in range(1, groups):
@@ -103,7 +107,7 @@
     @pl.when(here < groups - 1)
     def place():
         own = x_ref[pl.ds(pl.multiple_of((here + 1) * rows, rows), rows), wide:]
-        for distance, block in enumerate((own,) + hand_refs):
+        for distance, block in zip((0, *distances(groups)), (own,) + hand_refs):
             source = partner(here, groups - distance if groups & (groups - 1) else distance, groups)
             lanes = pl.ds(pl.multiple_of(source * wide, wide), wide)
             for kind in range(2):
@@ -191,12 +195,10 @@
         flops=2 * count * tok * count * tok * wide,
     )
     returned = lax.all_to_all(attended, BOTH, split_axis=0, concat_axis=0, tiled=True)
-    handed = [None] * len(hands)
-    for distance in range(tm_count - 1, 0, -1):
+    handed = []
+    for distance, hand in zip(distances(tm_count), hands):
         route = [(i, partner(i, distance, tm_count)) for i in range(tm_count)]
-        handed[distance - 1] = lax.ppermute(
-            hands[distance - 1], "tm", [(i, j) for i, j in route if j < tm_count - 1]
-        )
+        handed.append(lax.ppermute(hand, "tm", [(i, j) for i, j in route if j < tm_count - 1]))
 
     advanced = run(
         functools.partial(update_kernel, seq_count, tm_count),

time: 45.8 us -> 44.4 us (0.969)
  waiting for transfers between devices: 20.4 us -> 17.6 us
  starting transfers between devices: 17.5 us -> 18.8 us
    ppermute x3, waiting for transfers between devices: 2.35 us -> 0.89 us  [spread_body(): lax.ppermute(hand, 'tm', [(i, j) for i, j in route if j < tm_count - 1])]
    ppermute x3, starting transfers between devices: 6.15 us -> 7.48 us  [spread_body(): lax.ppermute(hand, 'tm', [(i, j) for i, j in route if j < tm_count - 1])]
    all_to_all x1, waiting for transfers between devices: 2.39 us -> 1.06 us  [spread_body(): lax.all_to_all(attended, BOTH, split_axis=0, concat_axis=0, tiled=True)]
  transfers between devices with their start and end apart: 6 -> 6, of which waited for: 5 -> 4; matrix products, arithmetic and copies ran while one was open for 0% -> 0% of each run, Pallas kernels for 2% -> 2%
where the time goes in v4:
time: 44.4 us; the launch traced here: 44 us
  starting transfers between devices  18.8 us (42%)
  waiting for transfers between devices  17.6 us (40%)
  Pallas kernels  6.18 us (14%)
  between operations  1.38 us (3%)
    all_to_all x1, waiting for transfers between devices, spread_body(): lax.all_to_all(packed, BOTH, split_axis=0, concat_axis=0, tiled=True)  13.6 us
    ppermute x3, starting transfers between devices, spread_body(): lax.ppermute(hand, 'tm', [(i, j) for i, j in route if j < tm_count - 1])  7.48 us
    all_to_all x1, starting transfers between devices, spread_body(): lax.all_to_all(packed, BOTH, split_axis=0, concat_axis=0, tiled=True)  7.3 us
    pallas_call x5, Pallas kernels, run(): pl.pallas_call(kernel, out_shape=jax.tree.map(lambda a: space(a.shape, a....  6.18 us
    all_to_all x1, starting transfers between devices, spread_body(): lax.all_to_all(attended, BOTH, split_axis=0, concat_axis=0, tiled=True)  2.71 us
    ppermute x1, waiting for transfers between devices, shifted(): return lax.ppermute(block, axis, route)  2.13 us
    ppermute x1, starting transfers between devices, shifted(): return lax.ppermute(block, axis, route)  1.29 us
    all_to_all x1, waiting for transfers between devices, spread_body(): lax.all_to_all(attended, BOTH, split_axis=0, concat_axis=0, tiled=True)  1.06 us
  transfers between devices with their start and end apart: 6, of which 4 were waited for; matrix products, arithmetic and copies ran while one was open for 0% of the time, Pallas kernels for 2%

profile of v4, /device:TPU:0, one launch (start us, length us, event | category | flops | bytes accessed | tf_op | source)
XLA Modules:
  0.0 44.0 jit_solution(17490325373940274136)
XLA Ops:
  0.6 0.0 copy-start
  0.6 2.1 %pack.1.after_ref = bf16[768,384]{1,0:T(8,128)(2,1)} custom-call(bf16[1,24,4096]{2,1,0:T(8,128)(2,1)} %q_hbm.1, bf16[1,24,4096]{2,1,0:T(8,128)(2,1)} %k_hbm.1, bf16[1,24,4096]{2,1,0:T(8,128)(2,1)} %v_hbm.1), custom_call_target="tpu_custom_call" | custom-call | bytes 1179648 | tf_op jit(solution)/shard_map/pack/pallas_call | solution.py:150
  2.7 0.0 copy-start.1
  2.7 7.3 %all-to-all-start = ((bf16[32,24,384]{2,1,0:T(8,128)(2,1)}), bf16[32,24,384]{2,1,0:T(8,128)(2,1)S(1)}, u32[]{:S(2)}, u32[]{:S(2)}) async-start(bf16[32,24,384]{2,1,0:T(8,128)(2,1)} %bitcast), calls=%async_computation | async-start | bytes 1179648 | tf_op jit(solution)/shard_map/all_to_all | solution.py:178
  10.7 0.0 copy-done
  10.7 0.0 copy-done.1
  10.7 0.0 copy-start.3
  10.7 0.1 residual.1
  10.8 1.3 %collective-permute-start = (bf16[32,4096]{1,0:T(8,128)(2,1)S(1)}, bf16[32,4096]{1,0:T(8,128)(2,1)S(1)}, u32[]{:S(2)}, u32[]{:S(2)}) collective-permute-start(bf16[32,4096]{1,0:T(8,128)(2,1)S(1)} %residual.1), channel_id=1, source_target_pairs={{8,0},{16,8},{24,16},{9,1},{17,9},{25,17},{10,2},{18,10},{26,18},{... | collective-permute-start | bytes 786440 | tf_op jit(solution)/shard_map/ppermute | solution.py:20
  12.1 2.1 %collective-permute-done.after_ref.moved_ref = bf16[32,4096]{1,0:T(8,128)(2,1)S(1)} collective-permute-done((bf16[32,4096]{1,0:T(8,128)(2,1)S(1)}, bf16[32,4096]{1,0:T(8,128)(2,1)S(1)}, u32[]{:S(2)}, u32[]{:S(2)}) %collective-permute-start) | collective-permute-done | bytes 262176 | tf_op jit(solution)/shard_map/ppermute | solution.py:20
  14.3 13.6 %all-to-all-done = bf16[32,24,384]{2,1,0:T(8,128)(2,1)S(1)} async-done(((bf16[32,24,384]{2,1,0:T(8,128)(2,1)}), bf16[32,24,384]{2,1,0:T(8,128)(2,1)S(1)}, u32[]{:S(2)}, u32[]{:S(2)}) %all-to-all-start) | async-done | bytes 589856 | tf_op jit(solution)/shard_map/all_to_all | solution.py:178
  27.8 0.0 copy-done.3
  27.8 2.4 %attend.1 = (bf16[768,128]{1,0:T(8,128)(2,1)}, bf16[192,256]{1,0:T(8,128)(2,1)S(1)}, bf16[192,256]{1,0:T(8,128)(2,1)S(1)}, bf16[192,256]{1,0:T(8,128)(2,1)S(1)}) custom-call(s32[4,4]{1,0:T(4,128)S(1)} %copy-done.3, bf16[768,384]{1,0:T(8,128)(2,1)S(1)} %bitcast.4, bf16[32,4096]{1,0:T(8,128)(2,1)S(1)} %collective-permute-done.after_ref.moved_ref), custom_call_target="tpu_custom_call" | custom-call | flops 150994944 | bytes 1343552 | tf_op jit(solution)/shard_map/attend/pallas_call | solution.py:150
  30.2 0.0 copy-start.2
  30.2 2.7 %all-to-all-start.1 = ((bf16[32,24,128]{2,1,0:T(8,128)(2,1)}), bf16[32,24,128]{2,1,0:T(8,128)(2,1)S(1)}, u32[]{:S(2)}, u32[]{:S(2)}) async-start(bf16[32,24,128]{2,1,0:T(8,128)(2,1)} %bitcast.2), calls=%async_computation.1 | async-start | bytes 393216 | tf_op jit(solution)/shard_map/all_to_all | solution.py:197
  32.9 1.3 %collective-permute-start.1 = (bf16[192,256]{1,0:T(8,128)(2,1)S(1)}, bf16[192,256]{1,0:T(8,128)(2,1)S(1)}, u32[]{:S(2)}, u32[]{:S(2)}) collective-permute-start(bf16[192,256]{1,0:T(8,128)(2,1)S(1)} %get-tuple-element.7), channel_id=1, source_target_pairs={{8,16},{16,8},{24,0},{9,17},{17,9},{25,1},{10,18},{18,10},{26,2},{... | collective-permute-start | bytes 294920 | tf_op jit(solution)/shard_map/ppermute | solution.py:201
  34.2 4.3 %collective-permute-start.2 = (bf16[192,256]{1,0:T(8,128)(2,1)S(1)}, bf16[192,256]{1,0:T(8,128)(2,1)S(1)}, u32[]{:S(2)}, u32[]{:S(2)}) collective-permute-start(bf16[192,256]{1,0:T(8,128)(2,1)S(1)} %get-tuple-element.8), channel_id=1, source_target_pairs={{0,16},{16,0},{24,8},{1,17},{17,1},{25,9},{2,18},{18,2},{26,10},{3... | collective-permute-start | bytes 294920 | tf_op jit(solution)/shard_map/ppermute | solution.py:201
  38.5 1.9 %collective-permute-start.3 = (bf16[192,256]{1,0:T(8,128)(2,1)S(1)}, bf16[192,256]{1,0:T(8,128)(2,1)S(1)}, u32[]{:S(2)}, u32[]{:S(2)}) collective-permute-start(bf16[192,256]{1,0:T(8,128)(2,1)S(1)} %get-tuple-element.9), channel_id=1, source_target_pairs={{0,8},{8,0},{24,16},{1,9},{9,1},{25,17},{2,10},{10,2},{26,18},{3,1... | collective-permute-start | bytes 294920 | tf_op jit(solution)/shard_map/ppermute | solution.py:201
  40.4 1.1 %all-to-all-done.1 = bf16[32,24,128]{2,1,0:T(8,128)(2,1)S(1)} async-done(((bf16[32,24,128]{2,1,0:T(8,128)(2,1)}), bf16[32,24,128]{2,1,0:T(8,128)(2,1)S(1)}, u32[]{:S(2)}, u32[]{:S(2)}) %all-to-all-start.1) | async-done | bytes 196640 | tf_op jit(solution)/shard_map/all_to_all | solution.py:197
  41.5 0.0 copy-done.2
  41.5 0.8 %update.1.refs_3_ = bf16[1,24,4096]{2,1,0:T(8,128)(2,1)} custom-call(bf16[768,128]{1,0:T(8,128)(2,1)S(1)} %bitcast.6, bf16[32,4096]{1,0:T(8,128)(2,1)S(1)} %collective-permute-done.after_ref.moved_ref, bf16[24,4096]{1,0:T(8,128)(2,1)S(1)} %copy-done.2), custom_call_target="tpu_custom_call" | custom-call | bytes 851968 | tf_op jit(solution)/shard_map/update/pallas_call | solution.py:150
  42.3 0.0 collective-permute-done.1.refs_0_
  42.3 0.9 %collective-permute-done.2.refs_1_ = bf16[192,256]{1,0:T(8,128)(2,1)S(1)} collective-permute-done((bf16[192,256]{1,0:T(8,128)(2,1)S(1)}, bf16[192,256]{1,0:T(8,128)(2,1)S(1)}, u32[]{:S(2)}, u32[]{:S(2)}) %collective-permute-start.2) | collective-permute-done | bytes 98336 | tf_op jit(solution)/shard_map/ppermute | solution.py:201
  43.2 0.0 collective-permute-done.3.refs_2_
  43.2 0.8 %cache.1 = bf16[1,2,192,512]{3,2,1,0:T(8,128)(2,1)} custom-call(bf16[768,384]{1,0:T(8,128)(2,1)S(1)} %bitcast.5, bf16[192,256]{1,0:T(8,128)(2,1)S(1)} %collective-permute-done.1.refs_0_, bf16[192,256]{1,0:T(8,128)(2,1)S(1)} %collective-permute-done.2.refs_1_, bf16[192,256]{1,0:T(8,128)(2,1)S(1)} %collective-permute-done.3.refs_2_, ...), custom_call_target="tpu_custom_call" | custom-call | bytes 1474560 | tf_op jit(solution)/shard_map/cache/pallas_call | solution.py:150
Async XLA Ops:
  0.6 10.1 %copy-start = (f32[50,4096]{1,0:T(8,128)S(1)}, f32[50,4096]{1,0:T(8,128)}, u32[]{:S(2)}) copy-start(f32[50,4096]{1,0:T(8,128)} %gate_ref.1) | copy-start | bytes 2457604
  2.7 8.0 %copy-start.1 = (bf16[1,24,4096]{2,1,0:T(8,128)(2,1)S(1)}, bf16[1,24,4096]{2,1,0:T(8,128)(2,1)}, u32[]{:S(2)}) copy-start(bf16[1,24,4096]{2,1,0:T(8,128)(2,1)} %h_ref.1) | copy-start | bytes 589828
  2.7 25.1 %all-to-all-start = ((bf16[32,24,384]{2,1,0:T(8,128)(2,1)}), bf16[32,24,384]{2,1,0:T(8,128)(2,1)S(1)}, u32[]{:S(2)}, u32[]{:S(2)}) async-start(bf16[32,24,384]{2,1,0:T(8,128)(2,1)} %bitcast), calls=%async_computation | async-start | bytes 1179648 | tf_op jit(solution)/shard_map/all_to_all | solution.py:178
  10.7 17.1 %copy-start.3 = (s32[4,4]{1,0:T(4,128)S(1)}, s32[4,4]{1,0:T(4,128)}, u32[]{:S(2)}) copy-start(s32[4,4]{1,0:T(4,128)} %pattern_ref.1) | copy-start | bytes 196
  10.8 3.4 %collective-permute-start = (bf16[32,4096]{1,0:T(8,128)(2,1)S(1)}, bf16[32,4096]{1,0:T(8,128)(2,1)S(1)}, u32[]{:S(2)}, u32[]{:S(2)}) collective-permute-start(bf16[32,4096]{1,0:T(8,128)(2,1)S(1)} %residual.1), channel_id=1, source_target_pairs={{8,0},{16,8},{24,16},{9,1},{17,9},{25,17},{10,2},{18,10},{26,18},{... | collective-permute-start | bytes 786440 | tf_op jit(solution)/shard_map/ppermute | solution.py:20
  30.2 11.3 %copy-start.2 = (bf16[24,4096]{1,0:T(8,128)(2,1)S(1)}, bf16[24,4096]{1,0:T(8,128)(2,1)}, u32[]{:S(2)}) copy-start(bf16[24,4096]{1,0:T(8,128)(2,1)} %fresh_ref.1) | copy-start | bytes 589828
  30.2 11.3 %all-to-all-start.1 = ((bf16[32,24,128]{2,1,0:T(8,128)(2,1)}), bf16[32,24,128]{2,1,0:T(8,128)(2,1)S(1)}, u32[]{:S(2)}, u32[]{:S(2)}) async-start(bf16[32,24,128]{2,1,0:T(8,128)(2,1)} %bitcast.2), calls=%async_computation.1 | async-start | bytes 393216 | tf_op jit(solution)/shard_map/all_to_all | solution.py:197
  32.9 9.3 %collective-permute-start.1 = (bf16[192,256]{1,0:T(8,128)(2,1)S(1)}, bf16[192,256]{1,0:T(8,128)(2,1)S(1)}, u32[]{:S(2)}, u32[]{:S(2)}) collective-permute-start(bf16[192,256]{1,0:T(8,128)(2,1)S(1)} %get-tuple-element.7), channel_id=1, source_target_pairs={{8,16},{16,8},{24,0},{9,17},{17,9},{25,1},{10,18},{18,10},{26,2},{... | collective-permute-start | bytes 294920 | tf_op jit(solution)/shard_map/ppermute | solution.py:201
  34.2 8.9 %collective-permute-start.2 = (bf16[192,256]{1,0:T(8,128)(2,1)S(1)}, bf16[192,256]{1,0:T(8,128)(2,1)S(1)}, u32[]{:S(2)}, u32[]{:S(2)}) collective-permute-start(bf16[192,256]{1,0:T(8,128)(2,1)S(1)} %get-tuple-element.8), channel_id=1, source_target_pairs={{0,16},{16,0},{24,8},{1,17},{17,1},{25,9},{2,18},{18,2},{26,10},{3... | collective-permute-start | bytes 294920 | tf_op jit(solution)/shard_map/ppermute | solution.py:201
  38.5 4.7 %collective-permute-start.3 = (bf16[192,256]{1,0:T(8,128)(2,1)S(1)}, bf16[192,256]{1,0:T(8,128)(2,1)S(1)}, u32[]{:S(2)}, u32[]{:S(2)}) collective-permute-start(bf16[192,256]{1,0:T(8,128)(2,1)S(1)} %get-tuple-element.9), channel_id=1, source_target_pairs={{0,8},{8,0},{24,16},{1,9},{9,1},{25,17},{2,10},{10,2},{26,18},{3,1... | collective-permute-start | bytes 294920 | tf_op jit(solution)/shard_map/ppermute | solution.py:201

commit v5 on v4

--- a/solution.py
+++ b/solution.py
@@ -12,6 +12,7 @@
 BOTH = ("tm", "seq")
 VMEM = pltpu.VMEM
 SMEM = pltpu.SMEM
+HBM = pltpu.HBM
 
 
 def shifted(block, axis, distance):
@@ -20,27 +21,19 @@
     return lax.ppermute(block, axis, route)
 
 
-def pack_kernel(seq_count, q_hbm, k_hbm, v_hbm, out_ref, *scratch):
-    held, sems = scratch
-    tok = held.shape[1]
-    wide = out_ref.shape[1] // 3
-    count = out_ref.shape[0] // tok
+def pack_kernel(seq_count, q_hbm, k_hbm, v_hbm, out_hbm, sem):
+    count, _, wide = out_hbm.shape
+    wide //= 3
     tm_count = count // seq_count
-    copies = [
-        pltpu.make_async_copy(ref.at[0], held.at[place], sems.at[place])
-        for place, ref in enumerate((q_hbm, k_hbm, v_hbm))
-    ]
-    for copy in copies:
-        copy.start()
-    for place, copy in enumerate(copies):
-        copy.wait()
-        for pair in range(count // 2):
-            rows = []
-            for dest in (2 * pair, 2 * pair + 1):
-                start = ((dest % seq_count) * tm_count + dest // seq_count) * wide
-                rows.append(held[place, :, start : start + wide].astype(jnp.float32))
-            both = jnp.concatenate(rows, axis=0).astype(jnp.bfloat16)
-            out_ref[2 * pair * tok : 2 * (pair + 1) * tok, place * wide : (place + 1) * wide] = both
+    for place, ref in enumerate((q_hbm, k_hbm, v_hbm)):
+        for dest in range(count):
+            start = ((dest % seq_count) * tm_count + dest // seq_count) * wide
+            pltpu.make_async_copy(
+                ref.at[0, :, start : start + wide],
+                out_hbm.at[dest, :, place * wide : (place + 1) * wide],
+                sem,
+            ).start()
+    pltpu.make_async_copy(out_hbm, out_hbm, sem).wait()
 
 
 def residual_kernel(noise_ref, h_ref, gate_ref, after_ref, out_ref):
@@ -60,15 +53,14 @@
     return range(groups - 1, 0, -1)
 
 
-def attend_kernel(groups, pattern_ref, x_ref, after_ref, out_ref, *hand_refs):
-    wide = out_ref.shape[1]
-    rows = x_ref.shape[0] // groups
+def attend_kernel(groups, pattern_ref, x_ref, after_ref, out_hbm, *refs):
+    *hand_refs, held, sems = refs
+    wide = held.shape[2]
+    rows = held.shape[1]
     factor = math.log2(math.e) / math.sqrt(HD)
     here = lax.axis_index("tm")
-    for distance, hand_ref in zip(distances(groups), hand_refs):
-        group = lax.rem(partner(here, distance, groups) + 1, groups)
-        hand_ref[...] = x_ref[pl.ds(pl.multiple_of(group * rows, rows), rows), wide:]
-    for group in range(1, groups):
+    copies = []
+    for group in range(groups - 1, 0, -1):
         span = (group + 1) * rows
         column = lax.broadcasted_iota(jnp.int32, (1, span), 1)
         kept = jnp.zeros((1, span), jnp.int32)
@@ -87,10 +79,19 @@
             raised = jnp.exp2((scores - highest) * factor)
             total = jnp.sum(raised, axis=-1, keepdims=True)
             numer = jnp.dot(raised.astype(jnp.bfloat16), value, preferred_element_type=jnp.float32)
-            out_ref[(group - 1) * rows : group * rows, head : head + HD] = (numer / total).astype(
-                jnp.bfloat16
+            held[group - 1, :, head : head + HD] = (numer / total).astype(jnp.bfloat16)
+        for place in (group - 1, groups - 1) if group == groups - 1 else (group - 1,):
+            copies.append(
+                pltpu.make_async_copy(
+                    held.at[group - 1], out_hbm.at[place * rows : (place + 1) * rows], sems.at[place]
+                )
             )
-    out_ref[(groups - 1) * rows :, :] = jnp.zeros((rows, wide), jnp.bfloat16)
+            copies[-1].start()
+    for distance, hand_ref in zip(distances(groups), hand_refs):
+        group = lax.rem(partner(here, distance, groups) + 1, groups)
+        hand_ref[...] = x_ref[pl.ds(pl.multiple_of(group * rows, rows), rows), wide:]
+    for copy in copies:
+        copy.wait()
 
 
 def cache_kernel(x_ref, *refs):
@@ -141,22 +142,22 @@
     return pl.BlockSpec(memory_space=space)
 
 
-def run(kernel, name, out_shape, specs, operands, flops=0, scratch=(), space=VMEM):
+def run(kernel, name, outs, specs, operands, flops=0, scratch=()):
     def size(a):
-        return math.prod(a.shape) * a.dtype.itemsize
-
-    outs = jax.tree.leaves(out_shape)
+        return math.prod(a.shape) * jnp.dtype(a.dtype).itemsize
+
     moved = sum(map(size, operands)) + sum(map(size, outs))
-    return pl.pallas_call(
+    results = pl.pallas_call(
         kernel,
-        out_shape=jax.tree.map(lambda a: space(a.shape, a.dtype), out_shape),
+        out_shape=outs,
         in_specs=specs,
-        out_specs=jax.tree.map(lambda a: whole(), out_shape),
+        out_specs=[whole(getattr(a, "memory_space", VMEM)) for a in outs],
         scratch_shapes=scratch,
         compiler_params=pltpu.CompilerParams(vmem_limit_bytes=4 * moved + (4 << 20)),
         cost_estimate=pl.CostEstimate(flops=flops, bytes_accessed=moved, transcendentals=0),
         name=name,
     )(*operands)
+    return results if len(outs) > 1 else results[0]
 
 
 def spread_body(queries, keys_proj, values, hidden, fresh_latent, gate_table, noise_step, pattern):
@@ -165,34 +166,37 @@
     _, tok, width = queries.shape
     wide = width // count
     group_tok = tok * seq_count
-    shape = functools.partial(jax.ShapeDtypeStruct, dtype=queries.dtype)
+    kind = queries.dtype
+    DMA = pltpu.SemaphoreType.DMA
 
     packed = run(
         functools.partial(pack_kernel, seq_count),
         "pack",
-        shape((count * tok, 3 * wide)),
-        [whole(pltpu.HBM)] * 3,
-        [pltpu.with_memory_space_constraint(a, pltpu.HBM) for a in (queries, keys_proj, values)],
-        scratch=[VMEM((3, tok, width), queries.dtype), pltpu.SemaphoreType.DMA((3,))],
+        [HBM((count, tok, 3 * wide), kind)],
+        [whole(HBM)] * 3,
+        [pltpu.with_memory_space_constraint(a, HBM) for a in (queries, keys_proj, values)],
+        scratch=[DMA],
     )
     exchanged = lax.all_to_all(packed, BOTH, split_axis=0, concat_axis=0, tiled=True)
+    exchanged = exchanged.reshape(count * tok, 3 * wide)
 
     residual = run(
         residual_kernel,
         "residual",
-        shape((tok + 8, width)),
-        [whole(SMEM), whole(), whole(), whole(pl.ANY)],
-        (noise_step, hidden, gate_table, packed),
+        [VMEM((tok + 8, width), kind)],
+        [whole(SMEM), whole(), whole(), whole(HBM)],
+        (noise_step, hidden, gate_table, pltpu.with_memory_space_constraint(packed, HBM)),
     )
     moved = shifted(residual, "tm", -1)
 
     attended, *hands = run(
         functools.partial(attend_kernel, tm_count),
         "attend",
-        [shape((count * tok, wide))] + [shape((group_tok, 2 * wide))] * (tm_count - 1),
+        [HBM((count * tok, wide), kind)] + [VMEM((group_tok, 2 * wide), kind)] * (tm_count - 1),
         [whole(SMEM), whole(), whole(pl.ANY)],
         (pattern, exchanged, moved),
         flops=2 * count * tok * count * tok * wide,
+        scratch=[VMEM((tm_count - 1, group_tok, wide), kind), DMA((tm_count,))],
     )
     returned = lax.all_to_all(attended, BOTH, split_axis=0, concat_axis=0, tiled=True)
     handed = []
@@ -203,18 +207,16 @@
     advanced = run(
         functools.partial(update_kernel, seq_count, tm_count),
         "update",
-        shape((1, tok, width)),
+        [jax.ShapeDtypeStruct((1, tok, width), kind)],
         [whole()] * 3,
         (returned, moved, fresh_latent),
-        space=pltpu.HBM,
     )
     next_cache = run(
         cache_kernel,
         "cache",
-        shape((1, 2, group_tok, tm_count * wide)),
-        [whole()] * tm_count + [whole(pltpu.HBM)],
-        (exchanged, *handed, pltpu.with_memory_space_constraint(advanced, pltpu.HBM)),
-        space=pltpu.HBM,
+        [jax.ShapeDtypeStruct((1, 2, group_tok, tm_count * wide), kind)],
+        [whole()] * tm_count + [whole(HBM)],
+        (exchanged, *handed, pltpu.with_memory_space_constraint(advanced, HBM)),
     )
     return (advanced, next_cache)
 

time: 44.4 us -> 61.3 us (1.38)
  Pallas kernels: 6.18 us -> 23.1 us
    pallas_call x5, Pallas kernels: 6.18 us -> 23.1 us  [run(): pl.pallas_call(kernel, out_shape=outs, in_specs=specs, out_specs=[whole(g...]
  transfers between devices with their start and end apart: 6 -> 6, of which waited for: 4 -> 4; matrix products, arithmetic and copies ran while one was open for 0% -> 0% of each run, Pallas kernels for 2% -> 1%
where the time goes in v5:
time: 61.3 us; the launch traced here: 60.9 us
  Pallas kernels  23.1 us (38%)
  starting transfers between devices  18.8 us (31%)
  waiting for transfers between devices  17.6 us (29%)
  between operations  1.4 us (2%)
    pallas_call x5, Pallas kernels, run(): pl.pallas_call(kernel, out_shape=outs, in_specs=specs, out_specs=[whole(g...  23.1 us
    all_to_all x1, waiting for transfers between devices, spread_body(): lax.all_to_all(packed, BOTH, split_axis=0, concat_axis=0, tiled=True)  13.6 us
    ppermute x3, starting transfers between devices, spread_body(): lax.ppermute(hand, 'tm', [(i, j) for i, j in route if j < tm_count - 1])  7.48 us
    all_to_all x1, starting transfers between devices, spread_body(): lax.all_to_all(packed, BOTH, split_axis=0, concat_axis=0, tiled=True)  7.3 us
    all_to_all x1, starting transfers between devices, spread_body(): lax.all_to_all(attended, BOTH, split_axis=0, concat_axis=0, tiled=True)  2.73 us
    ppermute x1, waiting for transfers between devices, shifted(): return lax.ppermute(block, axis, route)  2.13 us
    ppermute x1, starting transfers between devices, shifted(): return lax.ppermute(block, axis, route)  1.29 us
  transfers between devices with their start and end apart: 6, of which 4 were waited for; matrix products, arithmetic and copies ran while one was open for 0% of the time, Pallas kernels for 1%

profile of v5, /device:TPU:0, one launch (start us, length us, event | category | flops | bytes accessed | tf_op | source)
XLA Modules:
  0.0 60.9 jit_solution(123043086145004842)
XLA Ops:
  0.6 0.0 copy-start
  0.6 19.0 %pack.1.after_ref = bf16[32,24,384]{2,1,0:T(8,128)(2,1)} custom-call(bf16[1,24,4096]{2,1,0:T(8,128)(2,1)} %q_hbm.1, bf16[1,24,4096]{2,1,0:T(8,128)(2,1)} %k_hbm.1, bf16[1,24,4096]{2,1,0:T(8,128)(2,1)} %v_hbm.1), custom_call_target="tpu_custom_call" | custom-call | bytes 1179648 | tf_op jit(solution)/shard_map/pack/pallas_call | solution.py:150
  19.6 0.0 copy-start.1
  19.7 7.3 %all-to-all-start = ((bf16[32,24,384]{2,1,0:T(8,128)(2,1)}), bf16[32,24,384]{2,1,0:T(8,128)(2,1)S(1)}, u32[]{:S(2)}, u32[]{:S(2)}) async-start(bf16[32,24,384]{2,1,0:T(8,128)(2,1)} %pack.1.after_ref), calls=%async_computation | async-start | bytes 1179648 | tf_op jit(solution)/shard_map/all_to_all | solution.py:180
  27.6 0.0 copy-done
  27.6 0.0 copy-done.1
  27.6 0.0 copy-start.3
  27.6 0.1 residual.1
  27.7 1.3 %collective-permute-start = (bf16[32,4096]{1,0:T(8,128)(2,1)S(1)}, bf16[32,4096]{1,0:T(8,128)(2,1)S(1)}, u32[]{:S(2)}, u32[]{:S(2)}) collective-permute-start(bf16[32,4096]{1,0:T(8,128)(2,1)S(1)} %residual.1), channel_id=1, source_target_pairs={{8,0},{16,8},{24,16},{9,1},{17,9},{25,17},{10,2},{18,10},{26,18},{... | collective-permute-start | bytes 786440 | tf_op jit(solution)/shard_map/ppermute | solution.py:21
  29.0 2.1 %collective-permute-done.after_ref.moved_ref = bf16[32,4096]{1,0:T(8,128)(2,1)S(1)} collective-permute-done((bf16[32,4096]{1,0:T(8,128)(2,1)S(1)}, bf16[32,4096]{1,0:T(8,128)(2,1)S(1)}, u32[]{:S(2)}, u32[]{:S(2)}) %collective-permute-start) | collective-permute-done | bytes 262176 | tf_op jit(solution)/shard_map/ppermute | solution.py:21
  31.2 13.6 %all-to-all-done = bf16[32,24,384]{2,1,0:T(8,128)(2,1)S(1)} async-done(((bf16[32,24,384]{2,1,0:T(8,128)(2,1)}), bf16[32,24,384]{2,1,0:T(8,128)(2,1)S(1)}, u32[]{:S(2)}, u32[]{:S(2)}) %all-to-all-start) | async-done | bytes 589856 | tf_op jit(solution)/shard_map/all_to_all | solution.py:180
  44.7 0.0 copy-done.3
  44.7 2.4 %attend.1 = (bf16[768,128]{1,0:T(8,128)(2,1)}, bf16[192,256]{1,0:T(8,128)(2,1)S(1)}, bf16[192,256]{1,0:T(8,128)(2,1)S(1)}, bf16[192,256]{1,0:T(8,128)(2,1)S(1)}) custom-call(s32[4,4]{1,0:T(4,128)S(1)} %copy-done.3, bf16[768,384]{1,0:T(8,128)(2,1)S(1)} %bitcast.3, bf16[32,4096]{1,0:T(8,128)(2,1)S(1)} %collective-permute-done.after_ref.moved_ref), custom_call_target="tpu_custom_call" | custom-call | flops 150994944 | bytes 1343552 | tf_op jit(solution)/shard_map/attend/pallas_call | solution.py:150
  47.1 0.0 copy-start.2
  47.1 2.7 %all-to-all-start.1 = ((bf16[32,24,128]{2,1,0:T(8,128)(2,1)}), bf16[32,24,128]{2,1,0:T(8,128)(2,1)S(1)}, u32[]{:S(2)}, u32[]{:S(2)}) async-start(bf16[32,24,128]{2,1,0:T(8,128)(2,1)} %bitcast.6), calls=%async_computation.1 | async-start | bytes 393216 | tf_op jit(solution)/shard_map/all_to_all | solution.py:201
  49.9 1.3 %collective-permute-start.1 = (bf16[192,256]{1,0:T(8,128)(2,1)S(1)}, bf16[192,256]{1,0:T(8,128)(2,1)S(1)}, u32[]{:S(2)}, u32[]{:S(2)}) collective-permute-start(bf16[192,256]{1,0:T(8,128)(2,1)S(1)} %get-tuple-element.7), channel_id=1, source_target_pairs={{8,16},{16,8},{24,0},{9,17},{17,9},{25,1},{10,18},{18,10},{26,2},{... | collective-permute-start | bytes 294920 | tf_op jit(solution)/shard_map/ppermute | solution.py:205
  51.2 4.3 %collective-permute-start.2 = (bf16[192,256]{1,0:T(8,128)(2,1)S(1)}, bf16[192,256]{1,0:T(8,128)(2,1)S(1)}, u32[]{:S(2)}, u32[]{:S(2)}) collective-permute-start(bf16[192,256]{1,0:T(8,128)(2,1)S(1)} %get-tuple-element.8), channel_id=1, source_target_pairs={{0,16},{16,0},{24,8},{1,17},{17,1},{25,9},{2,18},{18,2},{26,10},{3... | collective-permute-start | bytes 294920 | tf_op jit(solution)/shard_map/ppermute | solution.py:205
  55.4 1.9 %collective-permute-start.3 = (bf16[192,256]{1,0:T(8,128)(2,1)S(1)}, bf16[192,256]{1,0:T(8,128)(2,1)S(1)}, u32[]{:S(2)}, u32[]{:S(2)}) collective-permute-start(bf16[192,256]{1,0:T(8,128)(2,1)S(1)} %get-tuple-element.9), channel_id=1, source_target_pairs={{0,8},{8,0},{24,16},{1,9},{9,1},{25,17},{2,10},{10,2},{26,18},{3,1... | collective-permute-start | bytes 294920 | tf_op jit(solution)/shard_map/ppermute | solution.py:205
  57.4 1.1 %all-to-all-done.1 = bf16[32,24,128]{2,1,0:T(8,128)(2,1)S(1)} async-done(((bf16[32,24,128]{2,1,0:T(8,128)(2,1)}), bf16[32,24,128]{2,1,0:T(8,128)(2,1)S(1)}, u32[]{:S(2)}, u32[]{:S(2)}) %all-to-all-start.1) | async-done | bytes 196640 | tf_op jit(solution)/shard_map/all_to_all | solution.py:201
  58.4 0.0 copy-done.2
  58.4 0.8 %update.1.refs_3_ = bf16[1,24,4096]{2,1,0:T(8,128)(2,1)} custom-call(bf16[768,128]{1,0:T(8,128)(2,1)S(1)} %bitcast.5, bf16[32,4096]{1,0:T(8,128)(2,1)S(1)} %collective-permute-done.after_ref.moved_ref, bf16[24,4096]{1,0:T(8,128)(2,1)S(1)} %copy-done.2), custom_call_target="tpu_custom_call" | custom-call | bytes 851968 | tf_op jit(solution)/shard_map/update/pallas_call | solution.py:150
  59.2 0.0 collective-permute-done.1.refs_0_
  59.2 0.9 %collective-permute-done.2.refs_1_ = bf16[192,256]{1,0:T(8,128)(2,1)S(1)} collective-permute-done((bf16[192,256]{1,0:T(8,128)(2,1)S(1)}, bf16[192,256]{1,0:T(8,128)(2,1)S(1)}, u32[]{:S(2)}, u32[]{:S(2)}) %collective-permute-start.2) | collective-permute-done | bytes 98336 | tf_op jit(solution)/shard_map/ppermute | solution.py:205
  60.1 0.0 collective-permute-done.3.refs_2_
  60.1 0.8 %cache.1 = bf16[1,2,192,512]{3,2,1,0:T(8,128)(2,1)} custom-call(bf16[768,384]{1,0:T(8,128)(2,1)S(1)} %bitcast.4, bf16[192,256]{1,0:T(8,128)(2,1)S(1)} %collective-permute-done.1.refs_0_, bf16[192,256]{1,0:T(8,128)(2,1)S(1)} %collective-permute-done.2.refs_1_, bf16[192,256]{1,0:T(8,128)(2,1)S(1)} %collective-permute-done.3.refs_2_, ...), custom_call_target="tpu_custom_call" | custom-call | bytes 1474560 | tf_op jit(solution)/shard_map/cache/pallas_call | solution.py:150
Async XLA Ops:
  0.6 27.0 %copy-start = (f32[50,4096]{1,0:T(8,128)S(1)}, f32[50,4096]{1,0:T(8,128)}, u32[]{:S(2)}) copy-start(f32[50,4096]{1,0:T(8,128)} %gate_ref.1) | copy-start | bytes 2457604
  19.6 8.0 %copy-start.1 = (bf16[1,24,4096]{2,1,0:T(8,128)(2,1)S(1)}, bf16[1,24,4096]{2,1,0:T(8,128)(2,1)}, u32[]{:S(2)}) copy-start(bf16[1,24,4096]{2,1,0:T(8,128)(2,1)} %h_ref.1) | copy-start | bytes 589828
  19.7 25.1 %all-to-all-start = ((bf16[32,24,384]{2,1,0:T(8,128)(2,1)}), bf16[32,24,384]{2,1,0:T(8,128)(2,1)S(1)}, u32[]{:S(2)}, u32[]{:S(2)}) async-start(bf16[32,24,384]{2,1,0:T(8,128)(2,1)} %pack.1.after_ref), calls=%async_computation | async-start | bytes 1179648 | tf_op jit(solution)/shard_map/all_to_all | solution.py:180
  27.6 17.1 %copy-start.3 = (s32[4,4]{1,0:T(4,128)S(1)}, s32[4,4]{1,0:T(4,128)}, u32[]{:S(2)}) copy-start(s32[4,4]{1,0:T(4,128)} %pattern_ref.1) | copy-start | bytes 196
  27.7 3.4 %collective-permute-start = (bf16[32,4096]{1,0:T(8,128)(2,1)S(1)}, bf16[32,4096]{1,0:T(8,128)(2,1)S(1)}, u32[]{:S(2)}, u32[]{:S(2)}) collective-permute-start(bf16[32,4096]{1,0:T(8,128)(2,1)S(1)} %residual.1), channel_id=1, source_target_pairs={{8,0},{16,8},{24,16},{9,1},{17,9},{25,17},{10,2},{18,10},{26,18},{... | collective-permute-start | bytes 786440 | tf_op jit(solution)/shard_map/ppermute | solution.py:21
  47.1 11.3 %copy-start.2 = (bf16[24,4096]{1,0:T(8,128)(2,1)S(1)}, bf16[24,4096]{1,0:T(8,128)(2,1)}, u32[]{:S(2)}) copy-start(bf16[24,4096]{1,0:T(8,128)(2,1)} %fresh_ref.1) | copy-start | bytes 589828
  47.1 11.3 %all-to-all-start.1 = ((bf16[32,24,128]{2,1,0:T(8,128)(2,1)}), bf16[32,24,128]{2,1,0:T(8,128)(2,1)S(1)}, u32[]{:S(2)}, u32[]{:S(2)}) async-start(bf16[32,24,128]{2,1,0:T(8,128)(2,1)} %bitcast.6), calls=%async_computation.1 | async-start | bytes 393216 | tf_op jit(solution)/shard_map/all_to_all | solution.py:201
  49.9 9.3 %collective-permute-start.1 = (bf16[192,256]{1,0:T(8,128)(2,1)S(1)}, bf16[192,256]{1,0:T(8,128)(2,1)S(1)}, u32[]{:S(2)}, u32[]{:S(2)}) collective-permute-start(bf16[192,256]{1,0:T(8,128)(2,1)S(1)} %get-tuple-element.7), channel_id=1, source_target_pairs={{8,16},{16,8},{24,0},{9,17},{17,9},{25,1},{10,18},{18,10},{26,2},{... | collective-permute-start | bytes 294920 | tf_op jit(solution)/shard_map/ppermute | solution.py:205
  51.2 8.9 %collective-permute-start.2 = (bf16[192,256]{1,0:T(8,128)(2,1)S(1)}, bf16[192,256]{1,0:T(8,128)(2,1)S(1)}, u32[]{:S(2)}, u32[]{:S(2)}) collective-permute-start(bf16[192,256]{1,0:T(8,128)(2,1)S(1)} %get-tuple-element.8), channel_id=1, source_target_pairs={{0,16},{16,0},{24,8},{1,17},{17,1},{25,9},{2,18},{18,2},{26,10},{3... | collective-permute-start | bytes 294920 | tf_op jit(solution)/shard_map/ppermute | solution.py:205
  55.4 4.7 %collective-permute-start.3 = (bf16[192,256]{1,0:T(8,128)(2,1)S(1)}, bf16[192,256]{1,0:T(8,128)(2,1)S(1)}, u32[]{:S(2)}, u32[]{:S(2)}) collective-permute-start(bf16[192,256]{1,0:T(8,128)(2,1)S(1)} %get-tuple-element.9), channel_id=1, source_target_pairs={{0,8},{8,0},{24,16},{1,9},{9,1},{25,17},{2,10},{10,2},{26,18},{3,1... | collective-permute-start | bytes 294920 | tf_op jit(solution)/shard_map/ppermute | solution.py:205

commit v6 on v5

--- a/solution.py
+++ b/solution.py
@@ -21,19 +21,45 @@
     return lax.ppermute(block, axis, route)
 
 
-def pack_kernel(seq_count, q_hbm, k_hbm, v_hbm, out_hbm, sem):
-    count, _, wide = out_hbm.shape
-    wide //= 3
+def pack_kernel(seq_count, halves, q_hbm, k_hbm, v_hbm, out_hbm, held, block, in_sems, out_sems):
+    tok, width = held.shape[1:]
+    wide = out_hbm.shape[1] // 3
+    count = out_hbm.shape[0] // tok
     tm_count = count // seq_count
-    for place, ref in enumerate((q_hbm, k_hbm, v_hbm)):
-        for dest in range(count):
-            start = ((dest % seq_count) * tm_count + dest // seq_count) * wide
-            pltpu.make_async_copy(
-                ref.at[0, :, start : start + wide],
-                out_hbm.at[dest, :, place * wide : (place + 1) * wide],
-                sem,
-            ).start()
-    pltpu.make_async_copy(out_hbm, out_hbm, sem).wait()
+    span, part = width // halves, seq_count // halves
+    copies = []
+    for half in range(halves):
+        columns = slice(half * span, (half + 1) * span)
+        for place, ref in enumerate((q_hbm, k_hbm, v_hbm)):
+            copies.append(
+                pltpu.make_async_copy(
+                    ref.at[0, :, columns], held.at[place, :, columns], in_sems.at[half, place]
+                )
+            )
+            copies[-1].start()
+    outs = []
+    for half in range(halves):
+        for place in range(3):
+            copies[3 * half + place].wait()
+            for tm in range(tm_count):
+                for seq in range(half * part, (half + 1) * part, 2):
+                    rows = []
+                    for member in (seq, seq + 1):
+                        start = (member * tm_count + tm) * wide
+                        rows.append(held[place, :, start : start + wide].astype(jnp.float32))
+                    first = (tm * seq_count + seq) * tok
+                    block[first : first + 2 * tok, place * wide : (place + 1) * wide] = jnp.concatenate(
+                        rows, axis=0
+                    ).astype(jnp.bfloat16)
+        for tm in range(tm_count):
+            first = (tm * seq_count + half * part) * tok
+            rows = slice(first, first + part * tok)
+            outs.append(
+                pltpu.make_async_copy(block.at[rows], out_hbm.at[rows], out_sems.at[half, tm])
+            )
+            outs[-1].start()
+    for out in outs:
+        out.wait()
 
 
 def residual_kernel(noise_ref, h_ref, gate_ref, after_ref, out_ref):
@@ -60,26 +86,32 @@
     factor = math.log2(math.e) / math.sqrt(HD)
     here = lax.axis_index("tm")
     copies = []
+    turned = [jnp.transpose(x_ref[:, 2 * wide + head : 2 * wide + head + HD]) for head in range(0, wide, HD)]
     for group in range(groups - 1, 0, -1):
-        span = (group + 1) * rows
-        column = lax.broadcasted_iota(jnp.int32, (1, span), 1)
-        kept = jnp.zeros((1, span), jnp.int32)
-        for source in range(group + 1):
-            inside = (column >= source * rows) & (column < (source + 1) * rows)
-            kept = jnp.where(inside, pattern_ref[group, source], kept)
         for head in range(0, wide, HD):
-            query = x_ref[group * rows : span, head : head + HD]
-            key = x_ref[:span, wide + head : wide + head + HD]
-            value = x_ref[:span, 2 * wide + head : 2 * wide + head + HD]
-            scores = lax.dot_general(
-                query, key, (((1,), (1,)), ((), ())), preferred_element_type=jnp.float32
+            query = x_ref[group * rows : (group + 1) * rows, head : head + HD]
+            scores, peaks = [], []
+            for source in range(group + 1):
+                key = x_ref[source * rows : (source + 1) * rows, wide + head : wide + head + HD]
+                block = lax.dot_general(
+                    key, query, (((1,), (1,)), ((), ())), preferred_element_type=jnp.float32
+                )
+                peak = jnp.max(block, axis=0, keepdims=True)
+                scores.append(block)
+                peaks.append(jnp.where(pattern_ref[group, source] > 0, peak, -1e30))
+            highest = functools.reduce(jnp.maximum, peaks) * factor
+            total, probs = 0.0, []
+            for source in range(group + 1):
+                offset = jnp.where(pattern_ref[group, source] > 0, -highest, -1e30)
+                raised = jnp.exp2(scores[source] * factor + offset)
+                total += jnp.sum(raised, axis=0, keepdims=True)
+                probs.append(raised.astype(jnp.bfloat16))
+            numer = jnp.dot(
+                turned[head // HD][:, : (group + 1) * rows],
+                jnp.concatenate(probs, axis=0),
+                preferred_element_type=jnp.float32,
             )
-            scores = jnp.where(kept > 0, scores, -1e30)
-            highest = jnp.max(scores, axis=-1, keepdims=True)
-            raised = jnp.exp2((scores - highest) * factor)
-            total = jnp.sum(raised, axis=-1, keepdims=True)
-            numer = jnp.dot(raised.astype(jnp.bfloat16), value, preferred_element_type=jnp.float32)
-            held[group - 1, :, head : head + HD] = (numer / total).astype(jnp.bfloat16)
+            held[group - 1, :, head : head + HD] = jnp.transpose(numer / total).astype(jnp.bfloat16)
         for place in (group - 1, groups - 1) if group == groups - 1 else (group - 1,):
             copies.append(
                 pltpu.make_async_copy(
@@ -168,17 +200,22 @@
     group_tok = tok * seq_count
     kind = queries.dtype
     DMA = pltpu.SemaphoreType.DMA
+    halves = 2 if seq_count % 4 == 0 else 1
 
     packed = run(
-        functools.partial(pack_kernel, seq_count),
+        functools.partial(pack_kernel, seq_count, halves),
         "pack",
-        [HBM((count, tok, 3 * wide), kind)],
+        [HBM((count * tok, 3 * wide), kind)],
         [whole(HBM)] * 3,
         [pltpu.with_memory_space_constraint(a, HBM) for a in (queries, keys_proj, values)],
-        scratch=[DMA],
+        scratch=[
+            VMEM((3, tok, width), kind),
+            VMEM((count * tok, 3 * wide), kind),
+            DMA((halves, 3)),
+            DMA((halves, tm_count)),
+        ],
     )
     exchanged = lax.all_to_all(packed, BOTH, split_axis=0, concat_axis=0, tiled=True)
-    exchanged = exchanged.reshape(count * tok, 3 * wide)
 
     residual = run(
         residual_kernel,

time: 61.3 us -> 44.2 us (0.72)
  Pallas kernels: 23.1 us -> 5.93 us
    pallas_call x5, Pallas kernels: 23.1 us -> 5.93 us  [run(): pl.pallas_call(kernel, out_shape=outs, in_specs=specs, out_specs=[whole(g...]
  transfers between devices with their start and end apart: 6 -> 6, of which waited for: 4 -> 4; matrix products, arithmetic and copies ran while one was open for 0% -> 0% of each run, Pallas kernels for 1% -> 2%
where the time goes in v6:
time: 44.2 us; the launch traced here: 43.8 us
  starting transfers between devices  18.8 us (43%)
  waiting for transfers between devices  17.6 us (40%)
  Pallas kernels  5.93 us (13%)
  between operations  1.4 us (3%)
    all_to_all x1, waiting for transfers between devices, spread_body(): lax.all_to_all(packed, BOTH, split_axis=0, concat_axis=0, tiled=True)  13.6 us
    ppermute x3, starting transfers between devices, spread_body(): lax.ppermute(hand, 'tm', [(i, j) for i, j in route if j < tm_count - 1])  7.48 us
    all_to_all x1, starting transfers between devices, spread_body(): lax.all_to_all(packed, BOTH, split_axis=0, concat_axis=0, tiled=True)  7.3 us
    pallas_call x5, Pallas kernels, run(): pl.pallas_call(kernel, out_shape=outs, in_specs=specs, out_specs=[whole(g...  5.93 us
    all_to_all x1, starting transfers between devices, spread_body(): lax.all_to_all(attended, BOTH, split_axis=0, concat_axis=0, tiled=True)  2.73 us
    ppermute x1, waiting for transfers between devices, shifted(): return lax.ppermute(block, axis, route)  2.13 us
    ppermute x1, starting transfers between devices, shifted(): return lax.ppermute(block, axis, route)  1.29 us
    all_to_all x1, waiting for transfers between devices, spread_body(): lax.all_to_all(attended, BOTH, split_axis=0, concat_axis=0, tiled=True)  1.06 us
  transfers between devices with their start and end apart: 6, of which 4 were waited for; matrix products, arithmetic and copies ran while one was open for 0% of the time, Pallas kernels for 2%

profile of v6, /device:TPU:0, one launch (start us, length us, event | category | flops | bytes accessed | tf_op | source)
XLA Modules:
  0.0 43.8 jit_solution(17906464141212557489)
XLA Ops:
  0.6 0.0 copy-start
  0.6 2.1 %pack.1.after_ref = bf16[768,384]{1,0:T(8,128)(2,1)} custom-call(bf16[1,24,4096]{2,1,0:T(8,128)(2,1)} %q_hbm.1, bf16[1,24,4096]{2,1,0:T(8,128)(2,1)} %k_hbm.1, bf16[1,24,4096]{2,1,0:T(8,128)(2,1)} %v_hbm.1), custom_call_target="tpu_custom_call" | custom-call | bytes 1179648 | tf_op jit(solution)/shard_map/pack/pallas_call | solution.py:182
  2.7 0.0 copy-start.1
  2.7 7.3 %all-to-all-start = ((bf16[32,24,384]{2,1,0:T(8,128)(2,1)}), bf16[32,24,384]{2,1,0:T(8,128)(2,1)S(1)}, u32[]{:S(2)}, u32[]{:S(2)}) async-start(bf16[32,24,384]{2,1,0:T(8,128)(2,1)} %bitcast.7), calls=%async_computation | async-start | bytes 1179648 | tf_op jit(solution)/shard_map/all_to_all | solution.py:218
  10.7 0.0 copy-done
  10.7 0.0 copy-done.1
  10.7 0.0 copy-start.3
  10.7 0.1 residual.1
  10.8 1.3 %collective-permute-start = (bf16[32,4096]{1,0:T(8,128)(2,1)S(1)}, bf16[32,4096]{1,0:T(8,128)(2,1)S(1)}, u32[]{:S(2)}, u32[]{:S(2)}) collective-permute-start(bf16[32,4096]{1,0:T(8,128)(2,1)S(1)} %residual.1), channel_id=1, source_target_pairs={{8,0},{16,8},{24,16},{9,1},{17,9},{25,17},{10,2},{18,10},{26,18},{... | collective-permute-start | bytes 786440 | tf_op jit(solution)/shard_map/ppermute | solution.py:21
  12.1 2.1 %collective-permute-done.after_ref.moved_ref = bf16[32,4096]{1,0:T(8,128)(2,1)S(1)} collective-permute-done((bf16[32,4096]{1,0:T(8,128)(2,1)S(1)}, bf16[32,4096]{1,0:T(8,128)(2,1)S(1)}, u32[]{:S(2)}, u32[]{:S(2)}) %collective-permute-start) | collective-permute-done | bytes 262176 | tf_op jit(solution)/shard_map/ppermute | solution.py:21
  14.2 13.6 %all-to-all-done = bf16[32,24,384]{2,1,0:T(8,128)(2,1)S(1)} async-done(((bf16[32,24,384]{2,1,0:T(8,128)(2,1)}), bf16[32,24,384]{2,1,0:T(8,128)(2,1)S(1)}, u32[]{:S(2)}, u32[]{:S(2)}) %all-to-all-start) | async-done | bytes 589856 | tf_op jit(solution)/shard_map/all_to_all | solution.py:218
  27.8 0.0 copy-done.3
  27.8 2.2 %attend.1 = (bf16[768,128]{1,0:T(8,128)(2,1)}, bf16[192,256]{1,0:T(8,128)(2,1)S(1)}, bf16[192,256]{1,0:T(8,128)(2,1)S(1)}, bf16[192,256]{1,0:T(8,128)(2,1)S(1)}) custom-call(s32[4,4]{1,0:T(4,128)S(1)} %copy-done.3, bf16[768,384]{1,0:T(8,128)(2,1)S(1)} %bitcast.4, bf16[32,4096]{1,0:T(8,128)(2,1)S(1)} %collective-permute-done.after_ref.moved_ref), custom_call_target="tpu_custom_call" | custom-call | flops 150994944 | bytes 1343552 | tf_op jit(solution)/shard_map/attend/pallas_call | solution.py:182
  30.0 0.0 copy-start.2
  30.0 2.7 %all-to-all-start.1 = ((bf16[32,24,128]{2,1,0:T(8,128)(2,1)}), bf16[32,24,128]{2,1,0:T(8,128)(2,1)S(1)}, u32[]{:S(2)}, u32[]{:S(2)}) async-start(bf16[32,24,128]{2,1,0:T(8,128)(2,1)} %bitcast.8), calls=%async_computation.1 | async-start | bytes 393216 | tf_op jit(solution)/shard_map/all_to_all | solution.py:238
  32.7 1.3 %collective-permute-start.1 = (bf16[192,256]{1,0:T(8,128)(2,1)S(1)}, bf16[192,256]{1,0:T(8,128)(2,1)S(1)}, u32[]{:S(2)}, u32[]{:S(2)}) collective-permute-start(bf16[192,256]{1,0:T(8,128)(2,1)S(1)} %get-tuple-element.7), channel_id=1, source_target_pairs={{8,16},{16,8},{24,0},{9,17},{17,9},{25,1},{10,18},{18,10},{26,2},{... | collective-permute-start | bytes 294920 | tf_op jit(solution)/shard_map/ppermute | solution.py:242
  34.0 4.3 %collective-permute-start.2 = (bf16[192,256]{1,0:T(8,128)(2,1)S(1)}, bf16[192,256]{1,0:T(8,128)(2,1)S(1)}, u32[]{:S(2)}, u32[]{:S(2)}) collective-permute-start(bf16[192,256]{1,0:T(8,128)(2,1)S(1)} %get-tuple-element.8), channel_id=1, source_target_pairs={{0,16},{16,0},{24,8},{1,17},{17,1},{25,9},{2,18},{18,2},{26,10},{3... | collective-permute-start | bytes 294920 | tf_op jit(solution)/shard_map/ppermute | solution.py:242
  38.3 1.9 %collective-permute-start.3 = (bf16[192,256]{1,0:T(8,128)(2,1)S(1)}, bf16[192,256]{1,0:T(8,128)(2,1)S(1)}, u32[]{:S(2)}, u32[]{:S(2)}) collective-permute-start(bf16[192,256]{1,0:T(8,128)(2,1)S(1)} %get-tuple-element.9), channel_id=1, source_target_pairs={{0,8},{8,0},{24,16},{1,9},{9,1},{25,17},{2,10},{10,2},{26,18},{3,1... | collective-permute-start | bytes 294920 | tf_op jit(solution)/shard_map/ppermute | solution.py:242
  40.2 1.1 %all-to-all-done.1 = bf16[32,24,128]{2,1,0:T(8,128)(2,1)S(1)} async-done(((bf16[32,24,128]{2,1,0:T(8,128)(2,1)}), bf16[32,24,128]{2,1,0:T(8,128)(2,1)S(1)}, u32[]{:S(2)}, u32[]{:S(2)}) %all-to-all-start.1) | async-done | bytes 196640 | tf_op jit(solution)/shard_map/all_to_all | solution.py:238
  41.3 0.0 copy-done.2
  41.3 0.8 %update.1.refs_3_ = bf16[1,24,4096]{2,1,0:T(8,128)(2,1)} custom-call(bf16[768,128]{1,0:T(8,128)(2,1)S(1)} %bitcast.6, bf16[32,4096]{1,0:T(8,128)(2,1)S(1)} %collective-permute-done.after_ref.moved_ref, bf16[24,4096]{1,0:T(8,128)(2,1)S(1)} %copy-done.2), custom_call_target="tpu_custom_call" | custom-call | bytes 851968 | tf_op jit(solution)/shard_map/update/pallas_call | solution.py:182
  42.1 0.0 collective-permute-done.1.refs_0_
  42.1 0.9 %collective-permute-done.2.refs_1_ = bf16[192,256]{1,0:T(8,128)(2,1)S(1)} collective-permute-done((bf16[192,256]{1,0:T(8,128)(2,1)S(1)}, bf16[192,256]{1,0:T(8,128)(2,1)S(1)}, u32[]{:S(2)}, u32[]{:S(2)}) %collective-permute-start.2) | collective-permute-done | bytes 98336 | tf_op jit(solution)/shard_map/ppermute | solution.py:242
  43.0 0.0 collective-permute-done.3.refs_2_
  43.0 0.8 %cache.1 = bf16[1,2,192,512]{3,2,1,0:T(8,128)(2,1)} custom-call(bf16[768,384]{1,0:T(8,128)(2,1)S(1)} %bitcast.5, bf16[192,256]{1,0:T(8,128)(2,1)S(1)} %collective-permute-done.1.refs_0_, bf16[192,256]{1,0:T(8,128)(2,1)S(1)} %collective-permute-done.2.refs_1_, bf16[192,256]{1,0:T(8,128)(2,1)S(1)} %collective-permute-done.3.refs_2_, ...), custom_call_target="tpu_custom_call" | custom-call | bytes 1474560 | tf_op jit(solution)/shard_map/cache/pallas_call | solution.py:182
Async XLA Ops:
  0.6 10.0 %copy-start = (f32[50,4096]{1,0:T(8,128)S(1)}, f32[50,4096]{1,0:T(8,128)}, u32[]{:S(2)}) copy-start(f32[50,4096]{1,0:T(8,128)} %gate_ref.1) | copy-start | bytes 2457604
  2.7 8.0 %copy-start.1 = (bf16[1,24,4096]{2,1,0:T(8,128)(2,1)S(1)}, bf16[1,24,4096]{2,1,0:T(8,128)(2,1)}, u32[]{:S(2)}) copy-start(bf16[1,24,4096]{2,1,0:T(8,128)(2,1)} %h_ref.1) | copy-start | bytes 589828
  2.7 25.1 %all-to-all-start = ((bf16[32,24,384]{2,1,0:T(8,128)(2,1)}), bf16[32,24,384]{2,1,0:T(8,128)(2,1)S(1)}, u32[]{:S(2)}, u32[]{:S(2)}) async-start(bf16[32,24,384]{2,1,0:T(8,128)(2,1)} %bitcast.7), calls=%async_computation | async-start | bytes 1179648 | tf_op jit(solution)/shard_map/all_to_all | solution.py:218
  10.7 17.1 %copy-start.3 = (s32[4,4]{1,0:T(4,128)S(1)}, s32[4,4]{1,0:T(4,128)}, u32[]{:S(2)}) copy-start(s32[4,4]{1,0:T(4,128)} %pattern_ref.1) | copy-start | bytes 196
  10.8 3.4 %collective-permute-start = (bf16[32,4096]{1,0:T(8,128)(2,1)S(1)}, bf16[32,4096]{1,0:T(8,128)(2,1)S(1)}, u32[]{:S(2)}, u32[]{:S(2)}) collective-permute-start(bf16[32,4096]{1,0:T(8,128)(2,1)S(1)} %residual.1), channel_id=1, source_target_pairs={{8,0},{16,8},{24,16},{9,1},{17,9},{25,17},{10,2},{18,10},{26,18},{... | collective-permute-start | bytes 786440 | tf_op jit(solution)/shard_map/ppermute | solution.py:21
  30.0 11.3 %copy-start.2 = (bf16[24,4096]{1,0:T(8,128)(2,1)S(1)}, bf16[24,4096]{1,0:T(8,128)(2,1)}, u32[]{:S(2)}) copy-start(bf16[24,4096]{1,0:T(8,128)(2,1)} %fresh_ref.1) | copy-start | bytes 589828
  30.0 11.3 %all-to-all-start.1 = ((bf16[32,24,128]{2,1,0:T(8,128)(2,1)}), bf16[32,24,128]{2,1,0:T(8,128)(2,1)S(1)}, u32[]{:S(2)}, u32[]{:S(2)}) async-start(bf16[32,24,128]{2,1,0:T(8,128)(2,1)} %bitcast.8), calls=%async_computation.1 | async-start | bytes 393216 | tf_op jit(solution)/shard_map/all_to_all | solution.py:238
  32.7 9.3 %collective-permute-start.1 = (bf16[192,256]{1,0:T(8,128)(2,1)S(1)}, bf16[192,256]{1,0:T(8,128)(2,1)S(1)}, u32[]{:S(2)}, u32[]{:S(2)}) collective-permute-start(bf16[192,256]{1,0:T(8,128)(2,1)S(1)} %get-tuple-element.7), channel_id=1, source_target_pairs={{8,16},{16,8},{24,0},{9,17},{17,9},{25,1},{10,18},{18,10},{26,2},{... | collective-permute-start | bytes 294920 | tf_op jit(solution)/shard_map/ppermute | solution.py:242
  34.0 8.9 %collective-permute-start.2 = (bf16[192,256]{1,0:T(8,128)(2,1)S(1)}, bf16[192,256]{1,0:T(8,128)(2,1)S(1)}, u32[]{:S(2)}, u32[]{:S(2)}) collective-permute-start(bf16[192,256]{1,0:T(8,128)(2,1)S(1)} %get-tuple-element.8), channel_id=1, source_target_pairs={{0,16},{16,0},{24,8},{1,17},{17,1},{25,9},{2,18},{18,2},{26,10},{3... | collective-permute-start | bytes 294920 | tf_op jit(solution)/shard_map/ppermute | solution.py:242
  38.3 4.7 %collective-permute-start.3 = (bf16[192,256]{1,0:T(8,128)(2,1)S(1)}, bf16[192,256]{1,0:T(8,128)(2,1)S(1)}, u32[]{:S(2)}, u32[]{:S(2)}) collective-permute-start(bf16[192,256]{1,0:T(8,128)(2,1)S(1)} %get-tuple-element.9), channel_id=1, source_target_pairs={{0,8},{8,0},{24,16},{1,9},{9,1},{25,17},{2,10},{10,2},{26,18},{3,1... | collective-permute-start | bytes 294920 | tf_op jit(solution)/shard_map/ppermute | solution.py:242

commit v7 on v6

--- a/solution.py
+++ b/solution.py
@@ -21,12 +21,18 @@
     return lax.ppermute(block, axis, route)
 
 
+def mixed(index, count):
+    if count & (count - 1):
+        return index
+    return sum(((index >> bit) & 1) * (count >> (bit + 1)) for bit in range(count.bit_length() - 1))
+
+
 def pack_kernel(seq_count, halves, q_hbm, k_hbm, v_hbm, out_hbm, held, block, in_sems, out_sems):
     tok, width = held.shape[1:]
     wide = out_hbm.shape[1] // 3
     count = out_hbm.shape[0] // tok
     tm_count = count // seq_count
-    span, part = width // halves, seq_count // halves
+    span = width // halves
     copies = []
     for half in range(halves):
         columns = slice(half * span, (half + 1) * span)
@@ -37,27 +43,22 @@
                 )
             )
             copies[-1].start()
+    for copy in copies:
+        copy.wait()
+    for place in range(3):
+        for pair in range(count // 2):
+            rows = []
+            for dest in (2 * pair, 2 * pair + 1):
+                start = (mixed(dest % seq_count, seq_count) * tm_count + dest // seq_count) * wide
+                rows.append(held[place, :, start : start + wide].astype(jnp.float32))
+            block[2 * pair * tok : 2 * (pair + 1) * tok, place * wide : (place + 1) * wide] = jnp.concatenate(
+                rows, axis=0
+            ).astype(jnp.bfloat16)
     outs = []
-    for half in range(halves):
-        for place in range(3):
-            copies[3 * half + place].wait()
-            for tm in range(tm_count):
-                for seq in range(half * part, (half + 1) * part, 2):
-                    rows = []
-                    for member in (seq, seq + 1):
-                        start = (member * tm_count + tm) * wide
-                        rows.append(held[place, :, start : start + wide].astype(jnp.float32))
-                    first = (tm * seq_count + seq) * tok
-                    block[first : first + 2 * tok, place * wide : (place + 1) * wide] = jnp.concatenate(
-                        rows, axis=0
-                    ).astype(jnp.bfloat16)
-        for tm in range(tm_count):
-            first = (tm * seq_count + half * part) * tok
-            rows = slice(first, first + part * tok)
-            outs.append(
-                pltpu.make_async_copy(block.at[rows], out_hbm.at[rows], out_sems.at[half, tm])
-            )
-            outs[-1].start()
+    for tm in range(tm_count):
+        rows = slice(tm * seq_count * tok, (tm + 1) * seq_count * tok)
+        outs.append(pltpu.make_async_copy(block.at[rows], out_hbm.at[rows], out_sems.at[tm]))
+        outs[-1].start()
     for out in outs:
         out.wait()
 
@@ -126,7 +127,7 @@
         copy.wait()
 
 
-def cache_kernel(x_ref, *refs):
+def cache_kernel(seq_count, x_ref, *refs):
     hand_refs, out_ref = refs[:-2], refs[-1]
     groups = len(hand_refs) + 1
     wide = x_ref.shape[1] // 3
@@ -140,11 +141,19 @@
     @pl.when(here < groups - 1)
     def place():
         own = x_ref[pl.ds(pl.multiple_of((here + 1) * rows, rows), rows), wide:]
+        tok = rows // seq_count
         for distance, block in zip((0, *distances(groups)), (own,) + hand_refs):
             source = partner(here, groups - distance if groups & (groups - 1) else distance, groups)
             lanes = pl.ds(pl.multiple_of(source * wide, wide), wide)
-            for kind in range(2):
-                out_ref[0, kind, :, lanes] = block[:, kind * wide : (kind + 1) * wide]
+            block = block[...].astype(jnp.float32)
+            for seq in range(0, seq_count, 2):
+                starts = [mixed(member, seq_count) * tok for member in (seq, seq + 1)]
+                pair = jnp.concatenate([block[start : start + tok] for start in starts], axis=0)
+                pair = pair.astype(jnp.bfloat16)
+                for kind in range(2):
+                    out_ref[0, kind, seq * tok : (seq + 2) * tok, lanes] = pair[
+                        :, kind * wide : (kind + 1) * wide
+                    ]
 
 
 def update_kernel(seq_count, tm_count, att_ref, moved_ref, fresh_ref, out_ref):
@@ -163,7 +172,7 @@
             rows = att_ref[2 * pair * tok : 2 * (pair + 1) * tok, :].astype(jnp.float32)
             for half in range(2):
                 source = 2 * pair + half
-                start = ((source % seq_count) * tm_count + source // seq_count) * wide
+                start = (mixed(source % seq_count, seq_count) * tm_count + source // seq_count) * wide
                 moved = moved_ref[:, start : start + wide].astype(jnp.float32)
                 gate = (moved[tok : tok + 1] + moved[tok + 1 : tok + 2]) + moved[tok + 2 : tok + 3]
                 result = moved[:tok] + gate * rows[half * tok : (half + 1) * tok]
@@ -212,10 +221,14 @@
             VMEM((3, tok, width), kind),
             VMEM((count * tok, 3 * wide), kind),
             DMA((halves, 3)),
-            DMA((halves, tm_count)),
+            DMA((tm_count,)),
         ],
     )
-    exchanged = lax.all_to_all(packed, BOTH, split_axis=0, concat_axis=0, tiled=True)
+    order = [tm * seq_count + mixed(s, seq_count) for tm in range(tm_count) for s in range(seq_count)]
+    exchange = functools.partial(
+        lax.all_to_all, axis_name=BOTH, split_axis=0, concat_axis=0, tiled=True, axis_index_groups=[order]
+    )
+    exchanged = exchange(packed)
 
     residual = run(
         residual_kernel,
@@ -235,7 +248,7 @@
         flops=2 * count * tok * count * tok * wide,
         scratch=[VMEM((tm_count - 1, group_tok, wide), kind), DMA((tm_count,))],
     )
-    returned = lax.all_to_all(attended, BOTH, split_axis=0, concat_axis=0, tiled=True)
+    returned = exchange(attended)
     handed = []
     for distance, hand in zip(distances(tm_count), hands):
         route = [(i, partner(i, distance, tm_count)) for i in range(tm_count)]
@@ -249,7 +262,7 @@
         (returned, moved, fresh_latent),
     )
     next_cache = run(
-        cache_kernel,
+        functools.partial(cache_kernel, seq_count),
         "cache",
         [jax.ShapeDtypeStruct((1, 2, group_tok, tm_count * wide), kind)],
         [whole()] * tm_count + [whole(HBM)],

time: 44.2 us -> 44.3 us (level)
  no operation moved by 1% of the time
where the time goes in v7:
time: 44.3 us; the launch traced here: 43.9 us
  starting transfers between devices  18.8 us (42%)
  waiting for transfers between devices  17.6 us (40%)
  Pallas kernels  6.08 us (14%)
  between operations  1.4 us (3%)
    all_to_all x1, waiting for transfers between devices, spread_body(): exchanged = exchange(packed)  13.6 us
    ppermute x3, starting transfers between devices, spread_body(): lax.ppermute(hand, 'tm', [(i, j) for i, j in route if j < tm_count - 1])  7.48 us
    all_to_all x1, starting transfers between devices, spread_body(): exchanged = exchange(packed)  7.3 us
    pallas_call x5, Pallas kernels, run(): pl.pallas_call(kernel, out_shape=outs, in_specs=specs, out_specs=[whole(g...  6.08 us
    all_to_all x1, starting transfers between devices, spread_body(): returned = exchange(attended)  2.73 us
    ppermute x1, waiting for transfers between devices, shifted(): return lax.ppermute(block, axis, route)  2.13 us
    ppermute x1, starting transfers between devices, shifted(): return lax.ppermute(block, axis, route)  1.29 us
    all_to_all x1, waiting for transfers between devices, spread_body(): returned = exchange(attended)  1.11 us
  transfers between devices with their start and end apart: 6, of which 4 were waited for; matrix products, arithmetic and copies ran while one was open for 0% of the time, Pallas kernels for 2%

profile of v7, /device:TPU:0, one launch (start us, length us, event | category | flops | bytes accessed | tf_op | source)
XLA Modules:
  0.0 43.9 jit_solution(6121576344394598157)
XLA Ops:
  0.6 0.0 copy-start
  0.6 2.2 %pack.1.after_ref = bf16[768,384]{1,0:T(8,128)(2,1)} custom-call(bf16[1,24,4096]{2,1,0:T(8,128)(2,1)} %q_hbm.1, bf16[1,24,4096]{2,1,0:T(8,128)(2,1)} %k_hbm.1, bf16[1,24,4096]{2,1,0:T(8,128)(2,1)} %v_hbm.1), custom_call_target="tpu_custom_call" | custom-call | bytes 1179648 | tf_op jit(solution)/shard_map/pack/pallas_call | solution.py:191
  2.9 0.0 copy-start.1
  2.9 7.3 %all-to-all-start = ((bf16[32,24,384]{2,1,0:T(8,128)(2,1)}), bf16[32,24,384]{2,1,0:T(8,128)(2,1)S(1)}, u32[]{:S(2)}, u32[]{:S(2)}) async-start(bf16[32,24,384]{2,1,0:T(8,128)(2,1)} %bitcast.7), calls=%async_computation | async-start | bytes 1179648 | tf_op jit(solution)/shard_map/all_to_all | solution.py:231
  10.8 0.0 copy-done
  10.8 0.0 copy-done.1
  10.9 0.0 copy-start.3
  10.9 0.1 residual.1
  11.0 1.3 %collective-permute-start = (bf16[32,4096]{1,0:T(8,128)(2,1)S(1)}, bf16[32,4096]{1,0:T(8,128)(2,1)S(1)}, u32[]{:S(2)}, u32[]{:S(2)}) collective-permute-start(bf16[32,4096]{1,0:T(8,128)(2,1)S(1)} %residual.1), channel_id=1, source_target_pairs={{8,0},{16,8},{24,16},{9,1},{17,9},{25,17},{10,2},{18,10},{26,18},{... | collective-permute-start | bytes 786440 | tf_op jit(solution)/shard_map/ppermute | solution.py:21
  12.3 2.1 %collective-permute-done.after_ref.moved_ref = bf16[32,4096]{1,0:T(8,128)(2,1)S(1)} collective-permute-done((bf16[32,4096]{1,0:T(8,128)(2,1)S(1)}, bf16[32,4096]{1,0:T(8,128)(2,1)S(1)}, u32[]{:S(2)}, u32[]{:S(2)}) %collective-permute-start) | collective-permute-done | bytes 262176 | tf_op jit(solution)/shard_map/ppermute | solution.py:21
  14.4 13.6 %all-to-all-done = bf16[32,24,384]{2,1,0:T(8,128)(2,1)S(1)} async-done(((bf16[32,24,384]{2,1,0:T(8,128)(2,1)}), bf16[32,24,384]{2,1,0:T(8,128)(2,1)S(1)}, u32[]{:S(2)}, u32[]{:S(2)}) %all-to-all-start) | async-done | bytes 589856 | tf_op jit(solution)/shard_map/all_to_all | solution.py:231
  27.9 0.0 copy-done.3
  27.9 2.2 %attend.1 = (bf16[768,128]{1,0:T(8,128)(2,1)}, bf16[192,256]{1,0:T(8,128)(2,1)S(1)}, bf16[192,256]{1,0:T(8,128)(2,1)S(1)}, bf16[192,256]{1,0:T(8,128)(2,1)S(1)}) custom-call(s32[4,4]{1,0:T(4,128)S(1)} %copy-done.3, bf16[768,384]{1,0:T(8,128)(2,1)S(1)} %bitcast.4, bf16[32,4096]{1,0:T(8,128)(2,1)S(1)} %collective-permute-done.after_ref.moved_ref), custom_call_target="tpu_custom_call" | custom-call | flops 150994944 | bytes 1343552 | tf_op jit(solution)/shard_map/attend/pallas_call | solution.py:191
  30.1 0.0 copy-start.2
  30.2 2.7 %all-to-all-start.1 = ((bf16[32,24,128]{2,1,0:T(8,128)(2,1)}), bf16[32,24,128]{2,1,0:T(8,128)(2,1)S(1)}, u32[]{:S(2)}, u32[]{:S(2)}) async-start(bf16[32,24,128]{2,1,0:T(8,128)(2,1)} %bitcast.8), calls=%async_computation.1 | async-start | bytes 393216 | tf_op jit(solution)/shard_map/all_to_all | solution.py:251
  32.9 1.3 %collective-permute-start.1 = (bf16[192,256]{1,0:T(8,128)(2,1)S(1)}, bf16[192,256]{1,0:T(8,128)(2,1)S(1)}, u32[]{:S(2)}, u32[]{:S(2)}) collective-permute-start(bf16[192,256]{1,0:T(8,128)(2,1)S(1)} %get-tuple-element.7), channel_id=1, source_target_pairs={{8,16},{16,8},{24,0},{9,17},{17,9},{25,1},{10,18},{18,10},{26,2},{... | collective-permute-start | bytes 294920 | tf_op jit(solution)/shard_map/ppermute | solution.py:255
  34.2 4.3 %collective-permute-start.2 = (bf16[192,256]{1,0:T(8,128)(2,1)S(1)}, bf16[192,256]{1,0:T(8,128)(2,1)S(1)}, u32[]{:S(2)}, u32[]{:S(2)}) collective-permute-start(bf16[192,256]{1,0:T(8,128)(2,1)S(1)} %get-tuple-element.8), channel_id=1, source_target_pairs={{0,16},{16,0},{24,8},{1,17},{17,1},{25,9},{2,18},{18,2},{26,10},{3... | collective-permute-start | bytes 294920 | tf_op jit(solution)/shard_map/ppermute | solution.py:255
  38.5 1.9 %collective-permute-start.3 = (bf16[192,256]{1,0:T(8,128)(2,1)S(1)}, bf16[192,256]{1,0:T(8,128)(2,1)S(1)}, u32[]{:S(2)}, u32[]{:S(2)}) collective-permute-start(bf16[192,256]{1,0:T(8,128)(2,1)S(1)} %get-tuple-element.9), channel_id=1, source_target_pairs={{0,8},{8,0},{24,16},{1,9},{9,1},{25,17},{2,10},{10,2},{26,18},{3,1... | collective-permute-start | bytes 294920 | tf_op jit(solution)/shard_map/ppermute | solution.py:255
  40.4 1.1 %all-to-all-done.1 = bf16[32,24,128]{2,1,0:T(8,128)(2,1)S(1)} async-done(((bf16[32,24,128]{2,1,0:T(8,128)(2,1)}), bf16[32,24,128]{2,1,0:T(8,128)(2,1)S(1)}, u32[]{:S(2)}, u32[]{:S(2)}) %all-to-all-start.1) | async-done | bytes 196640 | tf_op jit(solution)/shard_map/all_to_all | solution.py:251
  41.5 0.0 copy-done.2
  41.5 0.8 %update.1.refs_3_ = bf16[1,24,4096]{2,1,0:T(8,128)(2,1)} custom-call(bf16[768,128]{1,0:T(8,128)(2,1)S(1)} %bitcast.6, bf16[32,4096]{1,0:T(8,128)(2,1)S(1)} %collective-permute-done.after_ref.moved_ref, bf16[24,4096]{1,0:T(8,128)(2,1)S(1)} %copy-done.2), custom_call_target="tpu_custom_call" | custom-call | bytes 851968 | tf_op jit(solution)/shard_map/update/pallas_call | solution.py:191
  42.3 0.0 collective-permute-done.1.refs_0_
  42.3 0.8 %collective-permute-done.2.refs_1_ = bf16[192,256]{1,0:T(8,128)(2,1)S(1)} collective-permute-done((bf16[192,256]{1,0:T(8,128)(2,1)S(1)}, bf16[192,256]{1,0:T(8,128)(2,1)S(1)}, u32[]{:S(2)}, u32[]{:S(2)}) %collective-permute-start.2) | collective-permute-done | bytes 98336 | tf_op jit(solution)/shard_map/ppermute | solution.py:255
  43.1 0.0 collective-permute-done.3.refs_2_
  43.1 0.8 %cache.1 = bf16[1,2,192,512]{3,2,1,0:T(8,128)(2,1)} custom-call(bf16[768,384]{1,0:T(8,128)(2,1)S(1)} %bitcast.5, bf16[192,256]{1,0:T(8,128)(2,1)S(1)} %collective-permute-done.1.refs_0_, bf16[192,256]{1,0:T(8,128)(2,1)S(1)} %collective-permute-done.2.refs_1_, bf16[192,256]{1,0:T(8,128)(2,1)S(1)} %collective-permute-done.3.refs_2_, ...), custom_call_target="tpu_custom_call" | custom-call | bytes 1474560 | tf_op jit(solution)/shard_map/cache/pallas_call | solution.py:191
Async XLA Ops:
  0.6 10.2 %copy-start = (f32[50,4096]{1,0:T(8,128)S(1)}, f32[50,4096]{1,0:T(8,128)}, u32[]{:S(2)}) copy-start(f32[50,4096]{1,0:T(8,128)} %gate_ref.1) | copy-start | bytes 2457604
  2.9 8.0 %copy-start.1 = (bf16[1,24,4096]{2,1,0:T(8,128)(2,1)S(1)}, bf16[1,24,4096]{2,1,0:T(8,128)(2,1)}, u32[]{:S(2)}) copy-start(bf16[1,24,4096]{2,1,0:T(8,128)(2,1)} %h_ref.1) | copy-start | bytes 589828
  2.9 25.1 %all-to-all-start = ((bf16[32,24,384]{2,1,0:T(8,128)(2,1)}), bf16[32,24,384]{2,1,0:T(8,128)(2,1)S(1)}, u32[]{:S(2)}, u32[]{:S(2)}) async-start(bf16[32,24,384]{2,1,0:T(8,128)(2,1)} %bitcast.7), calls=%async_computation | async-start | bytes 1179648 | tf_op jit(solution)/shard_map/all_to_all | solution.py:231
  10.9 17.1 %copy-start.3 = (s32[4,4]{1,0:T(4,128)S(1)}, s32[4,4]{1,0:T(4,128)}, u32[]{:S(2)}) copy-start(s32[4,4]{1,0:T(4,128)} %pattern_ref.1) | copy-start | bytes 196
  11.0 3.4 %collective-permute-start = (bf16[32,4096]{1,0:T(8,128)(2,1)S(1)}, bf16[32,4096]{1,0:T(8,128)(2,1)S(1)}, u32[]{:S(2)}, u32[]{:S(2)}) collective-permute-start(bf16[32,4096]{1,0:T(8,128)(2,1)S(1)} %residual.1), channel_id=1, source_target_pairs={{8,0},{16,8},{24,16},{9,1},{17,9},{25,17},{10,2},{18,10},{26,18},{... | collective-permute-start | bytes 786440 | tf_op jit(solution)/shard_map/ppermute | solution.py:21
  30.1 11.4 %copy-start.2 = (bf16[24,4096]{1,0:T(8,128)(2,1)S(1)}, bf16[24,4096]{1,0:T(8,128)(2,1)}, u32[]{:S(2)}) copy-start(bf16[24,4096]{1,0:T(8,128)(2,1)} %fresh_ref.1) | copy-start | bytes 589828
  30.2 11.4 %all-to-all-start.1 = ((bf16[32,24,128]{2,1,0:T(8,128)(2,1)}), bf16[32,24,128]{2,1,0:T(8,128)(2,1)S(1)}, u32[]{:S(2)}, u32[]{:S(2)}) async-start(bf16[32,24,128]{2,1,0:T(8,128)(2,1)} %bitcast.8), calls=%async_computation.1 | async-start | bytes 393216 | tf_op jit(solution)/shard_map/all_to_all | solution.py:251
  32.9 9.4 %collective-permute-start.1 = (bf16[192,256]{1,0:T(8,128)(2,1)S(1)}, bf16[192,256]{1,0:T(8,128)(2,1)S(1)}, u32[]{:S(2)}, u32[]{:S(2)}) collective-permute-start(bf16[192,256]{1,0:T(8,128)(2,1)S(1)} %get-tuple-element.7), channel_id=1, source_target_pairs={{8,16},{16,8},{24,0},{9,17},{17,9},{25,1},{10,18},{18,10},{26,2},{... | collective-permute-start | bytes 294920 | tf_op jit(solution)/shard_map/ppermute | solution.py:255
  34.2 8.9 %collective-permute-start.2 = (bf16[192,256]{1,0:T(8,128)(2,1)S(1)}, bf16[192,256]{1,0:T(8,128)(2,1)S(1)}, u32[]{:S(2)}, u32[]{:S(2)}) collective-permute-start(bf16[192,256]{1,0:T(8,128)(2,1)S(1)} %get-tuple-element.8), channel_id=1, source_target_pairs={{0,16},{16,0},{24,8},{1,17},{17,1},{25,9},{2,18},{18,2},{26,10},{3... | collective-permute-start | bytes 294920 | tf_op jit(solution)/shard_map/ppermute | solution.py:255
  38.5 4.7 %collective-permute-start.3 = (bf16[192,256]{1,0:T(8,128)(2,1)S(1)}, bf16[192,256]{1,0:T(8,128)(2,1)S(1)}, u32[]{:S(2)}, u32[]{:S(2)}) collective-permute-start(bf16[192,256]{1,0:T(8,128)(2,1)S(1)} %get-tuple-element.9), channel_id=1, source_target_pairs={{0,8},{8,0},{24,16},{1,9},{9,1},{25,17},{2,10},{10,2},{26,18},{3,1... | collective-permute-start | bytes 294920 | tf_op jit(solution)/shard_map/ppermute | solution.py:255

commit v8 on v6

--- a/solution.py
+++ b/solution.py
@@ -19,6 +19,10 @@
     devices = range(lax.axis_size(axis))
     route = [(i - distance, i) for i in devices if i - distance in devices]
     return lax.ppermute(block, axis, route)
+
+
+def mixed(index, count):
+    return (index + count // 2) % count
 
 
 def pack_kernel(seq_count, halves, q_hbm, k_hbm, v_hbm, out_hbm, held, block, in_sems, out_sems):
@@ -47,12 +51,12 @@
                     for member in (seq, seq + 1):
                         start = (member * tm_count + tm) * wide
                         rows.append(held[place, :, start : start + wide].astype(jnp.float32))
-                    first = (tm * seq_count + seq) * tok
+                    first = (tm * seq_count + mixed(seq, seq_count)) * tok
                     block[first : first + 2 * tok, place * wide : (place + 1) * wide] = jnp.concatenate(
                         rows, axis=0
                     ).astype(jnp.bfloat16)
         for tm in range(tm_count):
-            first = (tm * seq_count + half * part) * tok
+            first = (tm * seq_count + mixed(half * part, seq_count)) * tok
             rows = slice(first, first + part * tok)
             outs.append(
                 pltpu.make_async_copy(block.at[rows], out_hbm.at[rows], out_sems.at[half, tm])
@@ -126,7 +130,7 @@
         copy.wait()
 
 
-def cache_kernel(x_ref, *refs):
+def cache_kernel(seq_count, x_ref, *refs):
     hand_refs, out_ref = refs[:-2], refs[-1]
     groups = len(hand_refs) + 1
     wide = x_ref.shape[1] // 3
@@ -140,11 +144,17 @@
     @pl.when(here < groups - 1)
     def place():
         own = x_ref[pl.ds(pl.multiple_of((here + 1) * rows, rows), rows), wide:]
+        tok = rows // seq_count
         for distance, block in zip((0, *distances(groups)), (own,) + hand_refs):
             source = partner(here, groups - distance if groups & (groups - 1) else distance, groups)
             lanes = pl.ds(pl.multiple_of(source * wide, wide), wide)
-            for kind in range(2):
-                out_ref[0, kind, :, lanes] = block[:, kind * wide : (kind + 1) * wide]
+            for half in range(2):
+                start = half * (rows // 2)
+                place = mixed(half * (seq_count // 2), seq_count) * tok
+                for kind in range(2):
+                    out_ref[0, kind, start : start + rows // 2, lanes] = block[
+                        place : place + rows // 2, kind * wide : (kind + 1) * wide
+                    ]
 
 
 def update_kernel(seq_count, tm_count, att_ref, moved_ref, fresh_ref, out_ref):
@@ -163,7 +173,7 @@
             rows = att_ref[2 * pair * tok : 2 * (pair + 1) * tok, :].astype(jnp.float32)
             for half in range(2):
                 source = 2 * pair + half
-                start = ((source % seq_count) * tm_count + source // seq_count) * wide
+                start = (mixed(source % seq_count, seq_count) * tm_count + source // seq_count) * wide
                 moved = moved_ref[:, start : start + wide].astype(jnp.float32)
                 gate = (moved[tok : tok + 1] + moved[tok + 1 : tok + 2]) + moved[tok + 2 : tok + 3]
                 result = moved[:tok] + gate * rows[half * tok : (half + 1) * tok]
@@ -200,7 +210,7 @@
     group_tok = tok * seq_count
     kind = queries.dtype
     DMA = pltpu.SemaphoreType.DMA
-    halves = 2 if seq_count % 4 == 0 else 1
+    halves = 2
 
     packed = run(
         functools.partial(pack_kernel, seq_count, halves),
@@ -215,7 +225,11 @@
             DMA((halves, tm_count)),
         ],
     )
-    exchanged = lax.all_to_all(packed, BOTH, split_axis=0, concat_axis=0, tiled=True)
+    order = [tm * seq_count + mixed(s, seq_count) for tm in range(tm_count) for s in range(seq_count)]
+    exchange = functools.partial(
+        lax.all_to_all, axis_name=BOTH, split_axis=0, concat_axis=0, tiled=True, axis_index_groups=[order]
+    )
+    exchanged = exchange(packed)
 
     residual = run(
         residual_kernel,
@@ -235,7 +249,7 @@
         flops=2 * count * tok * count * tok * wide,
         scratch=[VMEM((tm_count - 1, group_tok, wide), kind), DMA((tm_count,))],
     )
-    returned = lax.all_to_all(attended, BOTH, split_axis=0, concat_axis=0, tiled=True)
+    returned = exchange(attended)
     handed = []
     for distance, hand in zip(distances(tm_count), hands):
         route = [(i, partner(i, distance, tm_count)) for i in range(tm_count)]
@@ -249,7 +263,7 @@
         (returned, moved, fresh_latent),
     )
     next_cache = run(
-        cache_kernel,
+        functools.partial(cache_kernel, seq_count),
         "cache",
         [jax.ShapeDtypeStruct((1, 2, group_tok, tm_count * wide), kind)],
         [whole()] * tm_count + [whole(HBM)],
@@ -332,7 +346,7 @@
     tm_count, seq_count = lax.axis_size("tm"), lax.axis_size("seq")
     _, tok, width = queries.shape
     count = tm_count * seq_count
-    even = width % (count * HD) == 0 and tok % 8 == 0 and seq_count % 2 == 0
+    even = width % (count * HD) == 0 and tok % 8 == 0 and seq_count % 4 == 0
     return (spread_body if even else gather_body)(queries, *others)
 
 

time: 44.2 us -> 43.6 us (0.986)
  waiting for transfers between devices: 17.6 us -> 17 us
where the time goes in v8:
time: 43.6 us; the launch traced here: 43.3 us
  starting transfers between devices  18.9 us (43%)
  waiting for transfers between devices  17 us (39%)
  Pallas kernels  5.93 us (14%)
  between operations  1.4 us (3%)
    all_to_all x1, waiting for transfers between devices, spread_body(): exchanged = exchange(packed)  13.1 us
    ppermute x3, starting transfers between devices, spread_body(): lax.ppermute(hand, 'tm', [(i, j) for i, j in route if j < tm_count - 1])  7.57 us
    all_to_all x1, starting transfers between devices, spread_body(): exchanged = exchange(packed)  7.3 us
    pallas_call x5, Pallas kernels, run(): pl.pallas_call(kernel, out_shape=outs, in_specs=specs, out_specs=[whole(g...  5.93 us
    all_to_all x1, starting transfers between devices, spread_body(): returned = exchange(attended)  2.73 us
    ppermute x1, waiting for transfers between devices, shifted(): return lax.ppermute(block, axis, route)  2.13 us
    ppermute x1, starting transfers between devices, shifted(): return lax.ppermute(block, axis, route)  1.29 us
    all_to_all x1, waiting for transfers between devices, spread_body(): returned = exchange(attended)  1.29 us
  transfers between devices with their start and end apart: 6, of which 4 were waited for; matrix products, arithmetic and copies ran while one was open for 0% of the time, Pallas kernels for 2%

profile of v8, /device:TPU:0, one launch (start us, length us, event | category | flops | bytes accessed | tf_op | source)
XLA Modules:
  0.0 43.3 jit_solution(7882394639340837782)
XLA Ops:
  0.6 0.0 copy-start
  0.6 2.1 %pack.1.after_ref = bf16[768,384]{1,0:T(8,128)(2,1)} custom-call(bf16[1,24,4096]{2,1,0:T(8,128)(2,1)} %q_hbm.1, bf16[1,24,4096]{2,1,0:T(8,128)(2,1)} %k_hbm.1, bf16[1,24,4096]{2,1,0:T(8,128)(2,1)} %v_hbm.1), custom_call_target="tpu_custom_call" | custom-call | bytes 1179648 | tf_op jit(solution)/shard_map/pack/pallas_call | solution.py:192
  2.7 0.0 copy-start.1
  2.7 7.3 %all-to-all-start = ((bf16[32,24,384]{2,1,0:T(8,128)(2,1)}), bf16[32,24,384]{2,1,0:T(8,128)(2,1)S(1)}, u32[]{:S(2)}, u32[]{:S(2)}) async-start(bf16[32,24,384]{2,1,0:T(8,128)(2,1)} %bitcast.7), calls=%async_computation | async-start | bytes 1179648 | tf_op jit(solution)/shard_map/all_to_all | solution.py:232
  10.7 0.0 copy-done
  10.7 0.0 copy-done.1
  10.7 0.0 copy-start.3
  10.7 0.1 residual.1
  10.8 1.3 %collective-permute-start = (bf16[32,4096]{1,0:T(8,128)(2,1)S(1)}, bf16[32,4096]{1,0:T(8,128)(2,1)S(1)}, u32[]{:S(2)}, u32[]{:S(2)}) collective-permute-start(bf16[32,4096]{1,0:T(8,128)(2,1)S(1)} %residual.1), channel_id=1, source_target_pairs={{8,0},{16,8},{24,16},{9,1},{17,9},{25,17},{10,2},{18,10},{26,18},{... | collective-permute-start | bytes 786440 | tf_op jit(solution)/shard_map/ppermute | solution.py:21
  12.1 2.1 %collective-permute-done.after_ref.moved_ref = bf16[32,4096]{1,0:T(8,128)(2,1)S(1)} collective-permute-done((bf16[32,4096]{1,0:T(8,128)(2,1)S(1)}, bf16[32,4096]{1,0:T(8,128)(2,1)S(1)}, u32[]{:S(2)}, u32[]{:S(2)}) %collective-permute-start) | collective-permute-done | bytes 262176 | tf_op jit(solution)/shard_map/ppermute | solution.py:21
  14.2 13.1 %all-to-all-done = bf16[32,24,384]{2,1,0:T(8,128)(2,1)S(1)} async-done(((bf16[32,24,384]{2,1,0:T(8,128)(2,1)}), bf16[32,24,384]{2,1,0:T(8,128)(2,1)S(1)}, u32[]{:S(2)}, u32[]{:S(2)}) %all-to-all-start) | async-done | bytes 589856 | tf_op jit(solution)/shard_map/all_to_all | solution.py:232
  27.3 0.0 copy-done.3
  27.4 2.2 %attend.1 = (bf16[768,128]{1,0:T(8,128)(2,1)}, bf16[192,256]{1,0:T(8,128)(2,1)S(1)}, bf16[192,256]{1,0:T(8,128)(2,1)S(1)}, bf16[192,256]{1,0:T(8,128)(2,1)S(1)}) custom-call(s32[4,4]{1,0:T(4,128)S(1)} %copy-done.3, bf16[768,384]{1,0:T(8,128)(2,1)S(1)} %bitcast.4, bf16[32,4096]{1,0:T(8,128)(2,1)S(1)} %collective-permute-done.after_ref.moved_ref), custom_call_target="tpu_custom_call" | custom-call | flops 150994944 | bytes 1343552 | tf_op jit(solution)/shard_map/attend/pallas_call | solution.py:192
  29.5 0.0 copy-start.2
  29.6 2.7 %all-to-all-start.1 = ((bf16[32,24,128]{2,1,0:T(8,128)(2,1)}), bf16[32,24,128]{2,1,0:T(8,128)(2,1)S(1)}, u32[]{:S(2)}, u32[]{:S(2)}) async-start(bf16[32,24,128]{2,1,0:T(8,128)(2,1)} %bitcast.8), calls=%async_computation.1 | async-start | bytes 393216 | tf_op jit(solution)/shard_map/all_to_all | solution.py:252
  32.3 1.3 %collective-permute-start.1 = (bf16[192,256]{1,0:T(8,128)(2,1)S(1)}, bf16[192,256]{1,0:T(8,128)(2,1)S(1)}, u32[]{:S(2)}, u32[]{:S(2)}) collective-permute-start(bf16[192,256]{1,0:T(8,128)(2,1)S(1)} %get-tuple-element.7), channel_id=1, source_target_pairs={{8,16},{16,8},{24,0},{9,17},{17,9},{25,1},{10,18},{18,10},{26,2},{... | collective-permute-start | bytes 294920 | tf_op jit(solution)/shard_map/ppermute | solution.py:256
  33.6 4.4 %collective-permute-start.2 = (bf16[192,256]{1,0:T(8,128)(2,1)S(1)}, bf16[192,256]{1,0:T(8,128)(2,1)S(1)}, u32[]{:S(2)}, u32[]{:S(2)}) collective-permute-start(bf16[192,256]{1,0:T(8,128)(2,1)S(1)} %get-tuple-element.8), channel_id=1, source_target_pairs={{0,16},{16,0},{24,8},{1,17},{17,1},{25,9},{2,18},{18,2},{26,10},{3... | collective-permute-start | bytes 294920 | tf_op jit(solution)/shard_map/ppermute | solution.py:256
  38.0 1.9 %collective-permute-start.3 = (bf16[192,256]{1,0:T(8,128)(2,1)S(1)}, bf16[192,256]{1,0:T(8,128)(2,1)S(1)}, u32[]{:S(2)}, u32[]{:S(2)}) collective-permute-start(bf16[192,256]{1,0:T(8,128)(2,1)S(1)} %get-tuple-element.9), channel_id=1, source_target_pairs={{0,8},{8,0},{24,16},{1,9},{9,1},{25,17},{2,10},{10,2},{26,18},{3,1... | collective-permute-start | bytes 294920 | tf_op jit(solution)/shard_map/ppermute | solution.py:256
  39.9 1.3 %all-to-all-done.1 = bf16[32,24,128]{2,1,0:T(8,128)(2,1)S(1)} async-done(((bf16[32,24,128]{2,1,0:T(8,128)(2,1)}), bf16[32,24,128]{2,1,0:T(8,128)(2,1)S(1)}, u32[]{:S(2)}, u32[]{:S(2)}) %all-to-all-start.1) | async-done | bytes 196640 | tf_op jit(solution)/shard_map/all_to_all | solution.py:252
  41.2 0.0 copy-done.2
  41.2 0.8 %update.1.refs_3_ = bf16[1,24,4096]{2,1,0:T(8,128)(2,1)} custom-call(bf16[768,128]{1,0:T(8,128)(2,1)S(1)} %bitcast.6, bf16[32,4096]{1,0:T(8,128)(2,1)S(1)} %collective-permute-done.after_ref.moved_ref, bf16[24,4096]{1,0:T(8,128)(2,1)S(1)} %copy-done.2), custom_call_target="tpu_custom_call" | custom-call | bytes 851968 | tf_op jit(solution)/shard_map/update/pallas_call | solution.py:192
  41.9 0.0 collective-permute-done.1.refs_0_
  41.9 0.5 %collective-permute-done.2.refs_1_ = bf16[192,256]{1,0:T(8,128)(2,1)S(1)} collective-permute-done((bf16[192,256]{1,0:T(8,128)(2,1)S(1)}, bf16[192,256]{1,0:T(8,128)(2,1)S(1)}, u32[]{:S(2)}, u32[]{:S(2)}) %collective-permute-start.2) | collective-permute-done | bytes 98336 | tf_op jit(solution)/shard_map/ppermute | solution.py:256
  42.4 0.0 collective-permute-done.3.refs_2_
  42.5 0.8 %cache.1 = bf16[1,2,192,512]{3,2,1,0:T(8,128)(2,1)} custom-call(bf16[768,384]{1,0:T(8,128)(2,1)S(1)} %bitcast.5, bf16[192,256]{1,0:T(8,128)(2,1)S(1)} %collective-permute-done.1.refs_0_, bf16[192,256]{1,0:T(8,128)(2,1)S(1)} %collective-permute-done.2.refs_1_, bf16[192,256]{1,0:T(8,128)(2,1)S(1)} %collective-permute-done.3.refs_2_, ...), custom_call_target="tpu_custom_call" | custom-call | bytes 1474560 | tf_op jit(solution)/shard_map/cache/pallas_call | solution.py:192
Async XLA Ops:
  0.6 10.1 %copy-start = (f32[50,4096]{1,0:T(8,128)S(1)}, f32[50,4096]{1,0:T(8,128)}, u32[]{:S(2)}) copy-start(f32[50,4096]{1,0:T(8,128)} %gate_ref.1) | copy-start | bytes 2457604
  2.7 8.0 %copy-start.1 = (bf16[1,24,4096]{2,1,0:T(8,128)(2,1)S(1)}, bf16[1,24,4096]{2,1,0:T(8,128)(2,1)}, u32[]{:S(2)}) copy-start(bf16[1,24,4096]{2,1,0:T(8,128)(2,1)} %h_ref.1) | copy-start | bytes 589828
  2.7 24.6 %all-to-all-start = ((bf16[32,24,384]{2,1,0:T(8,128)(2,1)}), bf16[32,24,384]{2,1,0:T(8,128)(2,1)S(1)}, u32[]{:S(2)}, u32[]{:S(2)}) async-start(bf16[32,24,384]{2,1,0:T(8,128)(2,1)} %bitcast.7), calls=%async_computation | async-start | bytes 1179648 | tf_op jit(solution)/shard_map/all_to_all | solution.py:232
  10.7 16.6 %copy-start.3 = (s32[4,4]{1,0:T(4,128)S(1)}, s32[4,4]{1,0:T(4,128)}, u32[]{:S(2)}) copy-start(s32[4,4]{1,0:T(4,128)} %pattern_ref.1) | copy-start | bytes 196
  10.8 3.4 %collective-permute-start = (bf16[32,4096]{1,0:T(8,128)(2,1)S(1)}, bf16[32,4096]{1,0:T(8,128)(2,1)S(1)}, u32[]{:S(2)}, u32[]{:S(2)}) collective-permute-start(bf16[32,4096]{1,0:T(8,128)(2,1)S(1)} %residual.1), channel_id=1, source_target_pairs={{8,0},{16,8},{24,16},{9,1},{17,9},{25,17},{10,2},{18,10},{26,18},{... | collective-permute-start | bytes 786440 | tf_op jit(solution)/shard_map/ppermute | solution.py:21
  29.5 11.6 %copy-start.2 = (bf16[24,4096]{1,0:T(8,128)(2,1)S(1)}, bf16[24,4096]{1,0:T(8,128)(2,1)}, u32[]{:S(2)}) copy-start(bf16[24,4096]{1,0:T(8,128)(2,1)} %fresh_ref.1) | copy-start | bytes 589828
  29.6 11.6 %all-to-all-start.1 = ((bf16[32,24,128]{2,1,0:T(8,128)(2,1)}), bf16[32,24,128]{2,1,0:T(8,128)(2,1)S(1)}, u32[]{:S(2)}, u32[]{:S(2)}) async-start(bf16[32,24,128]{2,1,0:T(8,128)(2,1)} %bitcast.8), calls=%async_computation.1 | async-start | bytes 393216 | tf_op jit(solution)/shard_map/all_to_all | solution.py:252
  32.3 9.7 %collective-permute-start.1 = (bf16[192,256]{1,0:T(8,128)(2,1)S(1)}, bf16[192,256]{1,0:T(8,128)(2,1)S(1)}, u32[]{:S(2)}, u32[]{:S(2)}) collective-permute-start(bf16[192,256]{1,0:T(8,128)(2,1)S(1)} %get-tuple-element.7), channel_id=1, source_target_pairs={{8,16},{16,8},{24,0},{9,17},{17,9},{25,1},{10,18},{18,10},{26,2},{... | collective-permute-start | bytes 294920 | tf_op jit(solution)/shard_map/ppermute | solution.py:256
  33.6 8.9 %collective-permute-start.2 = (bf16[192,256]{1,0:T(8,128)(2,1)S(1)}, bf16[192,256]{1,0:T(8,128)(2,1)S(1)}, u32[]{:S(2)}, u32[]{:S(2)}) collective-permute-start(bf16[192,256]{1,0:T(8,128)(2,1)S(1)} %get-tuple-element.8), channel_id=1, source_target_pairs={{0,16},{16,0},{24,8},{1,17},{17,1},{25,9},{2,18},{18,2},{26,10},{3... | collective-permute-start | bytes 294920 | tf_op jit(solution)/shard_map/ppermute | solution.py:256
  38.0 4.5 %collective-permute-start.3 = (bf16[192,256]{1,0:T(8,128)(2,1)S(1)}, bf16[192,256]{1,0:T(8,128)(2,1)S(1)}, u32[]{:S(2)}, u32[]{:S(2)}) collective-permute-start(bf16[192,256]{1,0:T(8,128)(2,1)S(1)} %get-tuple-element.9), channel_id=1, source_target_pairs={{0,8},{8,0},{24,16},{1,9},{9,1},{25,17},{2,10},{10,2},{26,18},{3,1... | collective-permute-start | bytes 294920 | tf_op jit(solution)/shard_map/ppermute | solution.py:256

commit v9 on v8

--- a/solution.py
+++ b/solution.py
@@ -87,42 +87,71 @@
     *hand_refs, held, sems = refs
     wide = held.shape[2]
     rows = held.shape[1]
+    across = (groups - 1) * rows
     factor = math.log2(math.e) / math.sqrt(HD)
     here = lax.axis_index("tm")
-    copies = []
-    turned = [jnp.transpose(x_ref[:, 2 * wide + head : 2 * wide + head + HD]) for head in range(0, wide, HD)]
-    for group in range(groups - 1, 0, -1):
-        for head in range(0, wide, HD):
-            query = x_ref[group * rows : (group + 1) * rows, head : head + HD]
-            scores, peaks = [], []
-            for source in range(group + 1):
-                key = x_ref[source * rows : (source + 1) * rows, wide + head : wide + head + HD]
-                block = lax.dot_general(
-                    key, query, (((1,), (1,)), ((), ())), preferred_element_type=jnp.float32
+    lane = lax.broadcasted_iota(jnp.int32, (1, across), 1)
+    ends, kept = [], []
+    for source in range(groups):
+        first = max(source, 1)
+        ends.append(min(across, -(-(groups - first) * rows // 128) * 128))
+        chosen = jnp.zeros((1, across), jnp.int32)
+        for group in range(first, groups):
+            start = (groups - 1 - group) * rows
+            chosen = jnp.where((lane >= start) & (lane < start + rows), pattern_ref[group, source], chosen)
+        kept.append(chosen[:, : ends[-1]] > 0)
+
+    def spread(row, fill):
+        rest = across - row.shape[1]
+        return jnp.concatenate([row, jnp.full((1, rest), fill, row.dtype)], axis=1) if rest else row
+
+    for head in range(0, wide, HD):
+        query = jnp.concatenate(
+            [x_ref[group * rows : (group + 1) * rows, head : head + HD] for group in range(groups - 1, 0, -1)],
+            axis=0,
+        )
+        query = jnp.transpose(query)
+        value = jnp.transpose(x_ref[:, 2 * wide + head : 2 * wide + head + HD])
+        scores, highest = [], None
+        for source in range(groups):
+            key = x_ref[source * rows : (source + 1) * rows, wide + head : wide + head + HD]
+            scores.append(
+                jnp.dot(key, query[:, : ends[source]], preferred_element_type=jnp.float32)
+            )
+            peak = jnp.where(kept[source], jnp.max(scores[-1], axis=0, keepdims=True), -1e30)
+            peak = spread(peak, -1e30)
+            highest = peak if highest is None else jnp.maximum(highest, peak)
+        highest = highest * factor
+        total, probs = 0.0, []
+        for source in range(groups):
+            offset = jnp.where(kept[source], -highest[:, : ends[source]], -1e30)
+            raised = jnp.exp2(scores[source] * factor + offset)
+            total += spread(jnp.sum(raised, axis=0, keepdims=True), 0.0)
+            probs.append(raised.astype(jnp.bfloat16))
+        inverse = 1.0 / total
+        start, pieces = 0, []
+        for source in range(groups - 1, 0, -1):
+            stop = ends[source]
+            if stop > start:
+                numer = jnp.dot(
+                    value[:, : (source + 1) * rows],
+                    jnp.concatenate([p[:, start:stop] for p in probs[: source + 1]], axis=0),
+                    preferred_element_type=jnp.float32,
                 )
-                peak = jnp.max(block, axis=0, keepdims=True)
-                scores.append(block)
-                peaks.append(jnp.where(pattern_ref[group, source] > 0, peak, -1e30))
-            highest = functools.reduce(jnp.maximum, peaks) * factor
-            total, probs = 0.0, []
-            for source in range(group + 1):
-                offset = jnp.where(pattern_ref[group, source] > 0, -highest, -1e30)
-                raised = jnp.exp2(scores[source] * factor + offset)
-                total += jnp.sum(raised, axis=0, keepdims=True)
-                probs.append(raised.astype(jnp.bfloat16))
-            numer = jnp.dot(
-                turned[head // HD][:, : (group + 1) * rows],
-                jnp.concatenate(probs, axis=0),
-                preferred_element_type=jnp.float32,
-            )
-            held[group - 1, :, head : head + HD] = jnp.transpose(numer / total).astype(jnp.bfloat16)
-        for place in (group - 1, groups - 1) if group == groups - 1 else (group - 1,):
-            copies.append(
-                pltpu.make_async_copy(
-                    held.at[group - 1], out_hbm.at[place * rows : (place + 1) * rows], sems.at[place]
-                )
-            )
-            copies[-1].start()
+                pieces.append(numer * inverse[:, start:stop])
+                start = stop
+        result = jnp.transpose(jnp.concatenate(pieces, axis=1)).astype(jnp.bfloat16)
+        for group in range(1, groups):
+            start = (groups - 1 - group) * rows
+            held[group - 1, :, head : head + HD] = result[start : start + rows]
+    copies = [
+        pltpu.make_async_copy(
+            held.at[min(place, groups - 2)], out_hbm.at[place * rows : (place + 1) * rows], sems.at[place]
+        )
+        for place in range(groups)
+    ]
+    for copy in copies:
+        copy.start()
     for distance, hand_ref in zip(distances(groups), hand_refs):
         group = lax.rem(partner(here, distance, groups) + 1, groups)
         hand_ref[...] = x_ref[pl.ds(pl.multiple_of(group * rows, rows), rows), wide:]

time: 43.6 us -> 43.6 us (level)
  no operation moved by 1% of the time
where the time goes in v9:
time: 43.6 us; the launch traced here: 43.2 us
  starting transfers between devices  18.9 us (43%)
  waiting for transfers between devices  17 us (39%)
  Pallas kernels  5.9 us (14%)
  between operations  1.4 us (3%)
    all_to_all x1, waiting for transfers between devices, spread_body(): exchanged = exchange(packed)  13.1 us
    ppermute x3, starting transfers between devices, spread_body(): lax.ppermute(hand, 'tm', [(i, j) for i, j in route if j < tm_count - 1])  7.57 us
    all_to_all x1, starting transfers between devices, spread_body(): exchanged = exchange(packed)  7.3 us
    pallas_call x5, Pallas kernels, run(): pl.pallas_call(kernel, out_shape=outs, in_specs=specs, out_specs=[whole(g...  5.9 us
    all_to_all x1, starting transfers between devices, spread_body(): returned = exchange(attended)  2.73 us
    ppermute x1, waiting for transfers between devices, shifted(): return lax.ppermute(block, axis, route)  2.13 us
    ppermute x1, starting transfers between devices, shifted(): return lax.ppermute(block, axis, route)  1.29 us
    all_to_all x1, waiting for transfers between devices, spread_body(): returned = exchange(attended)  1.29 us
  transfers between devices with their start and end apart: 6, of which 4 were waited for; matrix products, arithmetic and copies ran while one was open for 0% of the time, Pallas kernels for 2%

profile of v9, /device:TPU:0, one launch (start us, length us, event | category | flops | bytes accessed | tf_op | source)
XLA Modules:
  0.0 43.2 jit_solution(8284920515574026950)
XLA Ops:
  0.6 0.0 copy-start
  0.6 2.1 %pack.1.after_ref = bf16[768,384]{1,0:T(8,128)(2,1)} custom-call(bf16[1,24,4096]{2,1,0:T(8,128)(2,1)} %q_hbm.1, bf16[1,24,4096]{2,1,0:T(8,128)(2,1)} %k_hbm.1, bf16[1,24,4096]{2,1,0:T(8,128)(2,1)} %v_hbm.1), custom_call_target="tpu_custom_call" | custom-call | bytes 1179648 | tf_op jit(solution)/shard_map/pack/pallas_call | solution.py:221
  2.7 0.0 copy-start.1
  2.7 7.3 %all-to-all-start = ((bf16[32,24,384]{2,1,0:T(8,128)(2,1)}), bf16[32,24,384]{2,1,0:T(8,128)(2,1)S(1)}, u32[]{:S(2)}, u32[]{:S(2)}) async-start(bf16[32,24,384]{2,1,0:T(8,128)(2,1)} %bitcast.7), calls=%async_computation | async-start | bytes 1179648 | tf_op jit(solution)/shard_map/all_to_all | solution.py:261
  10.7 0.0 copy-done
  10.7 0.0 copy-done.1
  10.7 0.0 copy-start.3
  10.7 0.1 residual.1
  10.8 1.3 %collective-permute-start = (bf16[32,4096]{1,0:T(8,128)(2,1)S(1)}, bf16[32,4096]{1,0:T(8,128)(2,1)S(1)}, u32[]{:S(2)}, u32[]{:S(2)}) collective-permute-start(bf16[32,4096]{1,0:T(8,128)(2,1)S(1)} %residual.1), channel_id=1, source_target_pairs={{8,0},{16,8},{24,16},{9,1},{17,9},{25,17},{10,2},{18,10},{26,18},{... | collective-permute-start | bytes 786440 | tf_op jit(solution)/shard_map/ppermute | solution.py:21
  12.1 2.1 %collective-permute-done.after_ref.moved_ref = bf16[32,4096]{1,0:T(8,128)(2,1)S(1)} collective-permute-done((bf16[32,4096]{1,0:T(8,128)(2,1)S(1)}, bf16[32,4096]{1,0:T(8,128)(2,1)S(1)}, u32[]{:S(2)}, u32[]{:S(2)}) %collective-permute-start) | collective-permute-done | bytes 262176 | tf_op jit(solution)/shard_map/ppermute | solution.py:21
  14.2 13.1 %all-to-all-done = bf16[32,24,384]{2,1,0:T(8,128)(2,1)S(1)} async-done(((bf16[32,24,384]{2,1,0:T(8,128)(2,1)}), bf16[32,24,384]{2,1,0:T(8,128)(2,1)S(1)}, u32[]{:S(2)}, u32[]{:S(2)}) %all-to-all-start) | async-done | bytes 589856 | tf_op jit(solution)/shard_map/all_to_all | solution.py:261
  27.3 0.0 copy-done.3
  27.4 2.1 %attend.1 = (bf16[768,128]{1,0:T(8,128)(2,1)}, bf16[192,256]{1,0:T(8,128)(2,1)S(1)}, bf16[192,256]{1,0:T(8,128)(2,1)S(1)}, bf16[192,256]{1,0:T(8,128)(2,1)S(1)}) custom-call(s32[4,4]{1,0:T(4,128)S(1)} %copy-done.3, bf16[768,384]{1,0:T(8,128)(2,1)S(1)} %bitcast.4, bf16[32,4096]{1,0:T(8,128)(2,1)S(1)} %collective-permute-done.after_ref.moved_ref), custom_call_target="tpu_custom_call" | custom-call | flops 150994944 | bytes 1343552 | tf_op jit(solution)/shard_map/attend/pallas_call | solution.py:221
  29.5 0.0 copy-start.2
  29.5 2.7 %all-to-all-start.1 = ((bf16[32,24,128]{2,1,0:T(8,128)(2,1)}), bf16[32,24,128]{2,1,0:T(8,128)(2,1)S(1)}, u32[]{:S(2)}, u32[]{:S(2)}) async-start(bf16[32,24,128]{2,1,0:T(8,128)(2,1)} %bitcast.8), calls=%async_computation.1 | async-start | bytes 393216 | tf_op jit(solution)/shard_map/all_to_all | solution.py:281
  32.3 1.3 %collective-permute-start.1 = (bf16[192,256]{1,0:T(8,128)(2,1)S(1)}, bf16[192,256]{1,0:T(8,128)(2,1)S(1)}, u32[]{:S(2)}, u32[]{:S(2)}) collective-permute-start(bf16[192,256]{1,0:T(8,128)(2,1)S(1)} %get-tuple-element.7), channel_id=1, source_target_pairs={{8,16},{16,8},{24,0},{9,17},{17,9},{25,1},{10,18},{18,10},{26,2},{... | collective-permute-start | bytes 294920 | tf_op jit(solution)/shard_map/ppermute | solution.py:285
  33.6 4.4 %collective-permute-start.2 = (bf16[192,256]{1,0:T(8,128)(2,1)S(1)}, bf16[192,256]{1,0:T(8,128)(2,1)S(1)}, u32[]{:S(2)}, u32[]{:S(2)}) collective-permute-start(bf16[192,256]{1,0:T(8,128)(2,1)S(1)} %get-tuple-element.8), channel_id=1, source_target_pairs={{0,16},{16,0},{24,8},{1,17},{17,1},{25,9},{2,18},{18,2},{26,10},{3... | collective-permute-start | bytes 294920 | tf_op jit(solution)/shard_map/ppermute | solution.py:285
  37.9 1.9 %collective-permute-start.3 = (bf16[192,256]{1,0:T(8,128)(2,1)S(1)}, bf16[192,256]{1,0:T(8,128)(2,1)S(1)}, u32[]{:S(2)}, u32[]{:S(2)}) collective-permute-start(bf16[192,256]{1,0:T(8,128)(2,1)S(1)} %get-tuple-element.9), channel_id=1, source_target_pairs={{0,8},{8,0},{24,16},{1,9},{9,1},{25,17},{2,10},{10,2},{26,18},{3,1... | collective-permute-start | bytes 294920 | tf_op jit(solution)/shard_map/ppermute | solution.py:285
  39.8 1.3 %all-to-all-done.1 = bf16[32,24,128]{2,1,0:T(8,128)(2,1)S(1)} async-done(((bf16[32,24,128]{2,1,0:T(8,128)(2,1)}), bf16[32,24,128]{2,1,0:T(8,128)(2,1)S(1)}, u32[]{:S(2)}, u32[]{:S(2)}) %all-to-all-start.1) | async-done | bytes 196640 | tf_op jit(solution)/shard_map/all_to_all | solution.py:281
  41.1 0.0 copy-done.2
  41.1 0.8 %update.1.refs_3_ = bf16[1,24,4096]{2,1,0:T(8,128)(2,1)} custom-call(bf16[768,128]{1,0:T(8,128)(2,1)S(1)} %bitcast.6, bf16[32,4096]{1,0:T(8,128)(2,1)S(1)} %collective-permute-done.after_ref.moved_ref, bf16[24,4096]{1,0:T(8,128)(2,1)S(1)} %copy-done.2), custom_call_target="tpu_custom_call" | custom-call | bytes 851968 | tf_op jit(solution)/shard_map/update/pallas_call | solution.py:221
  41.9 0.0 collective-permute-done.1.refs_0_
  41.9 0.5 %collective-permute-done.2.refs_1_ = bf16[192,256]{1,0:T(8,128)(2,1)S(1)} collective-permute-done((bf16[192,256]{1,0:T(8,128)(2,1)S(1)}, bf16[192,256]{1,0:T(8,128)(2,1)S(1)}, u32[]{:S(2)}, u32[]{:S(2)}) %collective-permute-start.2) | collective-permute-done | bytes 98336 | tf_op jit(solution)/shard_map/ppermute | solution.py:285
  42.4 0.0 collective-permute-done.3.refs_2_
  42.4 0.8 %cache.1 = bf16[1,2,192,512]{3,2,1,0:T(8,128)(2,1)} custom-call(bf16[768,384]{1,0:T(8,128)(2,1)S(1)} %bitcast.5, bf16[192,256]{1,0:T(8,128)(2,1)S(1)} %collective-permute-done.1.refs_0_, bf16[192,256]{1,0:T(8,128)(2,1)S(1)} %collective-permute-done.2.refs_1_, bf16[192,256]{1,0:T(8,128)(2,1)S(1)} %collective-permute-done.3.refs_2_, ...), custom_call_target="tpu_custom_call" | custom-call | bytes 1474560 | tf_op jit(solution)/shard_map/cache/pallas_call | solution.py:221
Async XLA Ops:
  0.6 10.1 %copy-start = (f32[50,4096]{1,0:T(8,128)S(1)}, f32[50,4096]{1,0:T(8,128)}, u32[]{:S(2)}) copy-start(f32[50,4096]{1,0:T(8,128)} %gate_ref.1) | copy-start | bytes 2457604
  2.7 8.0 %copy-start.1 = (bf16[1,24,4096]{2,1,0:T(8,128)(2,1)S(1)}, bf16[1,24,4096]{2,1,0:T(8,128)(2,1)}, u32[]{:S(2)}) copy-start(bf16[1,24,4096]{2,1,0:T(8,128)(2,1)} %h_ref.1) | copy-start | bytes 589828
  2.7 24.6 %all-to-all-start = ((bf16[32,24,384]{2,1,0:T(8,128)(2,1)}), bf16[32,24,384]{2,1,0:T(8,128)(2,1)S(1)}, u32[]{:S(2)}, u32[]{:S(2)}) async-start(bf16[32,24,384]{2,1,0:T(8,128)(2,1)} %bitcast.7), calls=%async_computation | async-start | bytes 1179648 | tf_op jit(solution)/shard_map/all_to_all | solution.py:261
  10.7 16.6 %copy-start.3 = (s32[4,4]{1,0:T(4,128)S(1)}, s32[4,4]{1,0:T(4,128)}, u32[]{:S(2)}) copy-start(s32[4,4]{1,0:T(4,128)} %pattern_ref.1) | copy-start | bytes 196
  10.8 3.4 %collective-permute-start = (bf16[32,4096]{1,0:T(8,128)(2,1)S(1)}, bf16[32,4096]{1,0:T(8,128)(2,1)S(1)}, u32[]{:S(2)}, u32[]{:S(2)}) collective-permute-start(bf16[32,4096]{1,0:T(8,128)(2,1)S(1)} %residual.1), channel_id=1, source_target_pairs={{8,0},{16,8},{24,16},{9,1},{17,9},{25,17},{10,2},{18,10},{26,18},{... | collective-permute-start | bytes 786440 | tf_op jit(solution)/shard_map/ppermute | solution.py:21
  29.5 11.6 %copy-start.2 = (bf16[24,4096]{1,0:T(8,128)(2,1)S(1)}, bf16[24,4096]{1,0:T(8,128)(2,1)}, u32[]{:S(2)}) copy-start(bf16[24,4096]{1,0:T(8,128)(2,1)} %fresh_ref.1) | copy-start | bytes 589828
  29.5 11.6 %all-to-all-start.1 = ((bf16[32,24,128]{2,1,0:T(8,128)(2,1)}), bf16[32,24,128]{2,1,0:T(8,128)(2,1)S(1)}, u32[]{:S(2)}, u32[]{:S(2)}) async-start(bf16[32,24,128]{2,1,0:T(8,128)(2,1)} %bitcast.8), calls=%async_computation.1 | async-start | bytes 393216 | tf_op jit(solution)/shard_map/all_to_all | solution.py:281
  32.3 9.7 %collective-permute-start.1 = (bf16[192,256]{1,0:T(8,128)(2,1)S(1)}, bf16[192,256]{1,0:T(8,128)(2,1)S(1)}, u32[]{:S(2)}, u32[]{:S(2)}) collective-permute-start(bf16[192,256]{1,0:T(8,128)(2,1)S(1)} %get-tuple-element.7), channel_id=1, source_target_pairs={{8,16},{16,8},{24,0},{9,17},{17,9},{25,1},{10,18},{18,10},{26,2},{... | collective-permute-start | bytes 294920 | tf_op jit(solution)/shard_map/ppermute | solution.py:285
  33.6 8.9 %collective-permute-start.2 = (bf16[192,256]{1,0:T(8,128)(2,1)S(1)}, bf16[192,256]{1,0:T(8,128)(2,1)S(1)}, u32[]{:S(2)}, u32[]{:S(2)}) collective-permute-start(bf16[192,256]{1,0:T(8,128)(2,1)S(1)} %get-tuple-element.8), channel_id=1, source_target_pairs={{0,16},{16,0},{24,8},{1,17},{17,1},{25,9},{2,18},{18,2},{26,10},{3... | collective-permute-start | bytes 294920 | tf_op jit(solution)/shard_map/ppermute | solution.py:285
  37.9 4.5 %collective-permute-start.3 = (bf16[192,256]{1,0:T(8,128)(2,1)S(1)}, bf16[192,256]{1,0:T(8,128)(2,1)S(1)}, u32[]{:S(2)}, u32[]{:S(2)}) collective-permute-start(bf16[192,256]{1,0:T(8,128)(2,1)S(1)} %get-tuple-element.9), channel_id=1, source_target_pairs={{0,8},{8,0},{24,16},{1,9},{9,1},{25,17},{2,10},{10,2},{26,18},{3,1... | collective-permute-start | bytes 294920 | tf_op jit(solution)/shard_map/ppermute | solution.py:285

commit v10 on v9

--- a/solution.py
+++ b/solution.py
@@ -98,7 +98,8 @@
         chosen = jnp.zeros((1, across), jnp.int32)
         for group in range(first, groups):
             start = (groups - 1 - group) * rows
-            chosen = jnp.where((lane >= start) & (lane < start + rows), pattern_ref[group, source], chosen)
+            flag = pattern_ref[group : group + 1, source : source + 1]
+            chosen = jnp.where((lane >= start) & (lane < start + rows), flag, chosen)
         kept.append(chosen[:, : ends[-1]] > 0)
 
     def spread(row, fill):
@@ -159,34 +160,56 @@
         copy.wait()
 
 
-def cache_kernel(seq_count, x_ref, *refs):
-    hand_refs, out_ref = refs[:-2], refs[-1]
-    groups = len(hand_refs) + 1
+def cache_places(seq_count, groups, rows, wide, distance, here):
+    source = partner(here, groups - distance if groups & (groups - 1) else distance, groups)
+    lanes = pl.ds(pl.multiple_of(source * wide, wide), wide)
+    tok = rows // seq_count
+    for half in range(2):
+        start = half * (rows // 2)
+        place = mixed(half * (seq_count // 2), seq_count) * tok
+        yield slice(start, start + rows // 2), lanes, slice(place, place + rows // 2)
+
+
+def cache_kernel(seq_count, groups, x_ref, hand_ref, out_ref):
     wide = x_ref.shape[1] // 3
     rows = out_ref.shape[2]
     here = lax.axis_index("tm")
-
-    @pl.when(here == groups - 1)
-    def clear():
-        out_ref[...] = jnp.zeros_like(out_ref)
+    out_ref[...] = jnp.zeros_like(out_ref)
 
     @pl.when(here < groups - 1)
     def place():
         own = x_ref[pl.ds(pl.multiple_of((here + 1) * rows, rows), rows), wide:]
-        tok = rows // seq_count
-        for distance, block in zip((0, *distances(groups)), (own,) + hand_refs):
-            source = partner(here, groups - distance if groups & (groups - 1) else distance, groups)
-            lanes = pl.ds(pl.multiple_of(source * wide, wide), wide)
-            for half in range(2):
-                start = half * (rows // 2)
-                place = mixed(half * (seq_count // 2), seq_count) * tok
+        for distance, block in ((0, own), (distances(groups)[0], hand_ref)):
+            for to, lanes, at in cache_places(seq_count, groups, rows, wide, distance, here):
                 for kind in range(2):
-                    out_ref[0, kind, start : start + rows // 2, lanes] = block[
-                        place : place + rows // 2, kind * wide : (kind + 1) * wide
-                    ]
-
-
-def update_kernel(seq_count, tm_count, att_ref, moved_ref, fresh_ref, out_ref):
+                    out_ref[0, kind, to, lanes] = block[at, kind * wide : (kind + 1) * wide]
+
+
+def cache_rest_kernel(seq_count, groups, begun_hbm, after_ref, *refs):
+    *hand_refs, out_hbm, sems = refs
+    wide = hand_refs[0].shape[1] // 2
+    rows = out_hbm.shape[2]
+    here = lax.axis_index("tm")
+
+    @pl.when(here < groups - 1)
+    def place():
+        copies = []
+        for distance, block in zip(distances(groups)[1:], hand_refs):
+            for to, lanes, at in cache_places(seq_count, groups, rows, wide, distance, here):
+                for kind in range(2):
+                    copies.append(
+                        pltpu.make_async_copy(
+                            block.at[at, kind * wide : (kind + 1) * wide],
+                            out_hbm.at[0, kind, to, lanes],
+                            sems.at[len(copies)],
+                        )
+                    )
+                    copies[-1].start()
+        for copy in copies:
+            copy.wait()
+
+
+def update_kernel(seq_count, tm_count, att_ref, moved_ref, fresh_ref, after_ref, out_ref):
     tok = out_ref.shape[1]
     wide = att_ref.shape[1]
     count = att_ref.shape[0] // tok
@@ -213,7 +236,7 @@
     return pl.BlockSpec(memory_space=space)
 
 
-def run(kernel, name, outs, specs, operands, flops=0, scratch=()):
+def run(kernel, name, outs, specs, operands, flops=0, scratch=(), aliases={}):
     def size(a):
         return math.prod(a.shape) * jnp.dtype(a.dtype).itemsize
 
@@ -224,6 +247,7 @@
         in_specs=specs,
         out_specs=[whole(getattr(a, "memory_space", VMEM)) for a in outs],
         scratch_shapes=scratch,
+        input_output_aliases=aliases,
         compiler_params=pltpu.CompilerParams(vmem_limit_bytes=4 * moved + (4 << 20)),
         cost_estimate=pl.CostEstimate(flops=flops, bytes_accessed=moved, transcendentals=0),
         name=name,
@@ -273,7 +297,7 @@
         functools.partial(attend_kernel, tm_count),
         "attend",
         [HBM((count * tok, wide), kind)] + [VMEM((group_tok, 2 * wide), kind)] * (tm_count - 1),
-        [whole(SMEM), whole(), whole(pl.ANY)],
+        [whole(), whole(), whole(pl.ANY)],
         (pattern, exchanged, moved),
         flops=2 * count * tok * count * tok * wide,
         scratch=[VMEM((tm_count - 1, group_tok, wide), kind), DMA((tm_count,))],
@@ -284,19 +308,30 @@
         route = [(i, partner(i, distance, tm_count)) for i in range(tm_count)]
         handed.append(lax.ppermute(hand, "tm", [(i, j) for i, j in route if j < tm_count - 1]))
 
+    first, *rest = handed
+    begun = run(
+        functools.partial(cache_kernel, seq_count, tm_count),
+        "cache",
+        [jax.ShapeDtypeStruct((1, 2, group_tok, tm_count * wide), kind)],
+        [whole()] * 2,
+        (exchanged, first),
+    )
+    begun = pltpu.with_memory_space_constraint(begun, HBM)
     advanced = run(
         functools.partial(update_kernel, seq_count, tm_count),
         "update",
         [jax.ShapeDtypeStruct((1, tok, width), kind)],
-        [whole()] * 3,
-        (returned, moved, fresh_latent),
+        [whole()] * 3 + [whole(HBM)],
+        (returned, moved, fresh_latent, begun),
     )
     next_cache = run(
-        functools.partial(cache_kernel, seq_count),
-        "cache",
-        [jax.ShapeDtypeStruct((1, 2, group_tok, tm_count * wide), kind)],
-        [whole()] * tm_count + [whole(HBM)],
-        (exchanged, *handed, pltpu.with_memory_space_constraint(advanced, HBM)),
+        functools.partial(cache_rest_kernel, seq_count, tm_count),
+        "cache_rest",
+        [HBM(begun.shape, kind)],
+        [whole(HBM)] * 2 + [whole()] * len(rest),
+        (begun, pltpu.with_memory_space_constraint(advanced, HBM), *rest),
+        scratch=[DMA((4 * len(rest),))],
+        aliases={0: 0},
     )
     return (advanced, next_cache)
 
@@ -375,7 +410,7 @@
     tm_count, seq_count = lax.axis_size("tm"), lax.axis_size("seq")
     _, tok, width = queries.shape
     count = tm_count * seq_count
-    even = width % (count * HD) == 0 and tok % 8 == 0 and seq_count % 4 == 0
+    even = width % (count * HD) == 0 and tok % 8 == 0 and seq_count % 4 == 0 and tm_count > 2
     return (spread_body if even else gather_body)(queries, *others)
 
 

time: 43.6 us -> 42.9 us (0.984)
  waiting for transfers between devices: 17 us -> 16 us
    all_to_all x1, waiting for transfers between devices: 1.29 us -> 0.26 us  [spread_body(): returned = exchange(attended)]
    pallas_call x5 -> x6, Pallas kernels: 5.9 us -> 6.05 us  [run(): pl.pallas_call(kernel, out_shape=outs, in_specs=specs, out_specs=[whole(g...]
  transfers between devices with their start and end apart: 6 -> 6, of which waited for: 4 -> 4; matrix products, arithmetic and copies ran while one was open for 0% -> 0% of each run, Pallas kernels for 2% -> 4%
where the time goes in v10:
time: 42.9 us; the launch traced here: 42.5 us
  starting transfers between devices  19 us (44%)
  waiting for transfers between devices  16 us (37%)
  Pallas kernels  6.05 us (14%)
  between operations  1.4 us (3%)
    all_to_all x1, waiting for transfers between devices, spread_body(): exchanged = exchange(packed)  13.1 us
    ppermute x3, starting transfers between devices, spread_body(): lax.ppermute(hand, 'tm', [(i, j) for i, j in route if j < tm_count - 1])  7.75 us
    all_to_all x1, starting transfers between devices, spread_body(): exchanged = exchange(packed)  7.3 us
    pallas_call x6, Pallas kernels, run(): pl.pallas_call(kernel, out_shape=outs, in_specs=specs, out_specs=[whole(g...  6.05 us
    all_to_all x1, starting transfers between devices, spread_body(): returned = exchange(attended)  2.68 us
    ppermute x1, waiting for transfers between devices, shifted(): return lax.ppermute(block, axis, route)  2.13 us
    ppermute x1, starting transfers between devices, shifted(): return lax.ppermute(block, axis, route)  1.29 us
  transfers between devices with their start and end apart: 6, of which 4 were waited for; matrix products, arithmetic and copies ran while one was open for 0% of the time, Pallas kernels for 4%

profile of v10, /device:TPU:0, one launch (start us, length us, event | category | flops | bytes accessed | tf_op | source)
XLA Modules:
  0.0 42.5 jit_solution(8957862868318564486)
XLA Ops:
  0.6 0.0 copy-start
  0.6 2.1 %pack.1.after_ref = bf16[768,384]{1,0:T(8,128)(2,1)} custom-call(bf16[1,24,4096]{2,1,0:T(8,128)(2,1)} %q_hbm.1, bf16[1,24,4096]{2,1,0:T(8,128)(2,1)} %k_hbm.1, bf16[1,24,4096]{2,1,0:T(8,128)(2,1)} %v_hbm.1), custom_call_target="tpu_custom_call" | custom-call | bytes 1179648 | tf_op jit(solution)/shard_map/pack/pallas_call | solution.py:244
  2.7 0.0 copy-start.1
  2.7 7.3 %all-to-all-start = ((bf16[32,24,384]{2,1,0:T(8,128)(2,1)}), bf16[32,24,384]{2,1,0:T(8,128)(2,1)S(1)}, u32[]{:S(2)}, u32[]{:S(2)}) async-start(bf16[32,24,384]{2,1,0:T(8,128)(2,1)} %bitcast.7), calls=%async_computation | async-start | bytes 1179648 | tf_op jit(solution)/shard_map/all_to_all | solution.py:285
  10.7 0.0 copy-done
  10.7 0.0 copy-done.1
  10.7 0.0 copy-start.3
  10.7 0.1 residual.1
  10.8 1.3 %collective-permute-start = (bf16[32,4096]{1,0:T(8,128)(2,1)S(1)}, bf16[32,4096]{1,0:T(8,128)(2,1)S(1)}, u32[]{:S(2)}, u32[]{:S(2)}) collective-permute-start(bf16[32,4096]{1,0:T(8,128)(2,1)S(1)} %residual.1), channel_id=1, source_target_pairs={{8,0},{16,8},{24,16},{9,1},{17,9},{25,17},{10,2},{18,10},{26,18},{... | collective-permute-start | bytes 786440 | tf_op jit(solution)/shard_map/ppermute | solution.py:21
  12.1 2.1 %collective-permute-done.after_ref.moved_ref = bf16[32,4096]{1,0:T(8,128)(2,1)S(1)} collective-permute-done((bf16[32,4096]{1,0:T(8,128)(2,1)S(1)}, bf16[32,4096]{1,0:T(8,128)(2,1)S(1)}, u32[]{:S(2)}, u32[]{:S(2)}) %collective-permute-start) | collective-permute-done | bytes 262176 | tf_op jit(solution)/shard_map/ppermute | solution.py:21
  14.2 13.1 %all-to-all-done = bf16[32,24,384]{2,1,0:T(8,128)(2,1)S(1)} async-done(((bf16[32,24,384]{2,1,0:T(8,128)(2,1)}), bf16[32,24,384]{2,1,0:T(8,128)(2,1)S(1)}, u32[]{:S(2)}, u32[]{:S(2)}) %all-to-all-start) | async-done | bytes 589856 | tf_op jit(solution)/shard_map/all_to_all | solution.py:285
  27.3 0.0 copy-done.3
  27.4 1.6 %attend.1 = (bf16[768,128]{1,0:T(8,128)(2,1)}, bf16[192,256]{1,0:T(8,128)(2,1)S(1)}, bf16[192,256]{1,0:T(8,128)(2,1)S(1)}, bf16[192,256]{1,0:T(8,128)(2,1)S(1)}) custom-call(s32[4,4]{1,0:T(4,128)S(1)} %copy-done.3, bf16[768,384]{1,0:T(8,128)(2,1)S(1)} %bitcast.4, bf16[32,4096]{1,0:T(8,128)(2,1)S(1)} %collective-permute-done.after_ref.moved_ref), custom_call_target="tpu_custom_call" | custom-call | flops 150994944 | bytes 1343552 | tf_op jit(solution)/shard_map/attend/pallas_call | solution.py:244
  28.9 2.7 %all-to-all-start.1 = ((bf16[32,24,128]{2,1,0:T(8,128)(2,1)}), bf16[32,24,128]{2,1,0:T(8,128)(2,1)S(1)}, u32[]{:S(2)}, u32[]{:S(2)}) async-start(bf16[32,24,128]{2,1,0:T(8,128)(2,1)} %bitcast.8), calls=%async_computation.1 | async-start | bytes 393216 | tf_op jit(solution)/shard_map/all_to_all | solution.py:305
  31.6 1.3 %collective-permute-start.1 = (bf16[192,256]{1,0:T(8,128)(2,1)S(1)}, bf16[192,256]{1,0:T(8,128)(2,1)S(1)}, u32[]{:S(2)}, u32[]{:S(2)}) collective-permute-start(bf16[192,256]{1,0:T(8,128)(2,1)S(1)} %get-tuple-element.7), channel_id=1, source_target_pairs={{8,16},{16,8},{24,0},{9,17},{17,9},{25,1},{10,18},{18,10},{26,2},{... | collective-permute-start | bytes 294920 | tf_op jit(solution)/shard_map/ppermute | solution.py:309
  32.9 4.4 %collective-permute-start.2 = (bf16[192,256]{1,0:T(8,128)(2,1)S(1)}, bf16[192,256]{1,0:T(8,128)(2,1)S(1)}, u32[]{:S(2)}, u32[]{:S(2)}) collective-permute-start(bf16[192,256]{1,0:T(8,128)(2,1)S(1)} %get-tuple-element.8), channel_id=1, source_target_pairs={{0,16},{16,0},{24,8},{1,17},{17,1},{25,9},{2,18},{18,2},{26,10},{3... | collective-permute-start | bytes 294920 | tf_op jit(solution)/shard_map/ppermute | solution.py:309
  37.3 0.0 copy-start.2
  37.4 2.1 %collective-permute-start.3 = (bf16[192,256]{1,0:T(8,128)(2,1)S(1)}, bf16[192,256]{1,0:T(8,128)(2,1)S(1)}, u32[]{:S(2)}, u32[]{:S(2)}) collective-permute-start(bf16[192,256]{1,0:T(8,128)(2,1)S(1)} %get-tuple-element.9), channel_id=1, source_target_pairs={{0,8},{8,0},{24,16},{1,9},{9,1},{25,17},{2,10},{10,2},{26,18},{3,1... | collective-permute-start | bytes 294920 | tf_op jit(solution)/shard_map/ppermute | solution.py:309
  39.4 0.0 collective-permute-done.1.hand_ref
  39.5 0.8 %cache.1.after_ref.begun_hbm = bf16[1,2,192,512]{3,2,1,0:T(8,128)(2,1)} custom-call(bf16[768,384]{1,0:T(8,128)(2,1)S(1)} %bitcast.5, bf16[192,256]{1,0:T(8,128)(2,1)S(1)} %collective-permute-done.1.hand_ref), custom_call_target="tpu_custom_call" | custom-call | bytes 1081344 | tf_op jit(solution)/shard_map/cache/pallas_call | solution.py:244
  40.3 0.3 all-to-all-done.1
  40.5 0.0 copy-done.2
  40.5 0.8 %update.1.after_ref = bf16[1,24,4096]{2,1,0:T(8,128)(2,1)} custom-call(bf16[768,128]{1,0:T(8,128)(2,1)S(1)} %bitcast.6, bf16[32,4096]{1,0:T(8,128)(2,1)S(1)} %collective-permute-done.after_ref.moved_ref, bf16[24,4096]{1,0:T(8,128)(2,1)S(1)} %copy-done.2, bf16[1,2,192,512]{3,2,1,0:T(8,128)(2,1)} %cache.1.after_ref.begun_hbm), custom_call_target="tpu_custom_call" | custom-call | bytes 1245184 | tf_op jit(solution)/shard_map/update/pallas_call | solution.py:244
  41.3 0.4 %collective-permute-done.2.refs_0_ = bf16[192,256]{1,0:T(8,128)(2,1)S(1)} collective-permute-done((bf16[192,256]{1,0:T(8,128)(2,1)S(1)}, bf16[192,256]{1,0:T(8,128)(2,1)S(1)}, u32[]{:S(2)}, u32[]{:S(2)}) %collective-permute-start.2) | collective-permute-done | bytes 98336 | tf_op jit(solution)/shard_map/ppermute | solution.py:309
  41.7 0.0 collective-permute-done.3.refs_1_
  41.7 0.7 %cache_rest.1 = bf16[1,2,192,512]{3,2,1,0:T(8,128)(2,1)} custom-call(bf16[1,2,192,512]{3,2,1,0:T(8,128)(2,1)} %cache.1.after_ref.begun_hbm, bf16[1,24,4096]{2,1,0:T(8,128)(2,1)} %update.1.after_ref, bf16[192,256]{1,0:T(8,128)(2,1)S(1)} %collective-permute-done.2.refs_0_, ...), custom_call_target="tpu_custom_call", output_to_operand_aliasing={{}: (0, {})} | custom-call | bytes 1179648 | tf_op jit(solution)/shard_map/cache_rest/pallas_call | solution.py:244
Async XLA Ops:
  0.6 10.1 %copy-start = (f32[50,4096]{1,0:T(8,128)S(1)}, f32[50,4096]{1,0:T(8,128)}, u32[]{:S(2)}) copy-start(f32[50,4096]{1,0:T(8,128)} %gate_ref.1) | copy-start | bytes 2457604
  2.7 8.0 %copy-start.1 = (bf16[1,24,4096]{2,1,0:T(8,128)(2,1)S(1)}, bf16[1,24,4096]{2,1,0:T(8,128)(2,1)}, u32[]{:S(2)}) copy-start(bf16[1,24,4096]{2,1,0:T(8,128)(2,1)} %h_ref.1) | copy-start | bytes 589828
  2.7 24.6 %all-to-all-start = ((bf16[32,24,384]{2,1,0:T(8,128)(2,1)}), bf16[32,24,384]{2,1,0:T(8,128)(2,1)S(1)}, u32[]{:S(2)}, u32[]{:S(2)}) async-start(bf16[32,24,384]{2,1,0:T(8,128)(2,1)} %bitcast.7), calls=%async_computation | async-start | bytes 1179648 | tf_op jit(solution)/shard_map/all_to_all | solution.py:285
  10.7 16.6 %copy-start.3 = (s32[4,4]{1,0:T(4,128)S(1)}, s32[4,4]{1,0:T(4,128)}, u32[]{:S(2)}) copy-start(s32[4,4]{1,0:T(4,128)} %pattern_ref.1) | copy-start | bytes 196
  10.8 3.4 %collective-permute-start = (bf16[32,4096]{1,0:T(8,128)(2,1)S(1)}, bf16[32,4096]{1,0:T(8,128)(2,1)S(1)}, u32[]{:S(2)}, u32[]{:S(2)}) collective-permute-start(bf16[32,4096]{1,0:T(8,128)(2,1)S(1)} %residual.1), channel_id=1, source_target_pairs={{8,0},{16,8},{24,16},{9,1},{17,9},{25,17},{10,2},{18,10},{26,18},{... | collective-permute-start | bytes 786440 | tf_op jit(solution)/shard_map/ppermute | solution.py:21
  28.9 11.6 %all-to-all-start.1 = ((bf16[32,24,128]{2,1,0:T(8,128)(2,1)}), bf16[32,24,128]{2,1,0:T(8,128)(2,1)S(1)}, u32[]{:S(2)}, u32[]{:S(2)}) async-start(bf16[32,24,128]{2,1,0:T(8,128)(2,1)} %bitcast.8), calls=%async_computation.1 | async-start | bytes 393216 | tf_op jit(solution)/shard_map/all_to_all | solution.py:305
  31.6 7.8 %collective-permute-start.1 = (bf16[192,256]{1,0:T(8,128)(2,1)S(1)}, bf16[192,256]{1,0:T(8,128)(2,1)S(1)}, u32[]{:S(2)}, u32[]{:S(2)}) collective-permute-start(bf16[192,256]{1,0:T(8,128)(2,1)S(1)} %get-tuple-element.7), channel_id=1, source_target_pairs={{8,16},{16,8},{24,0},{9,17},{17,9},{25,1},{10,18},{18,10},{26,2},{... | collective-permute-start | bytes 294920 | tf_op jit(solution)/shard_map/ppermute | solution.py:309
  32.9 8.8 %collective-permute-start.2 = (bf16[192,256]{1,0:T(8,128)(2,1)S(1)}, bf16[192,256]{1,0:T(8,128)(2,1)S(1)}, u32[]{:S(2)}, u32[]{:S(2)}) collective-permute-start(bf16[192,256]{1,0:T(8,128)(2,1)S(1)} %get-tuple-element.8), channel_id=1, source_target_pairs={{0,16},{16,0},{24,8},{1,17},{17,1},{25,9},{2,18},{18,2},{26,10},{3... | collective-permute-start | bytes 294920 | tf_op jit(solution)/shard_map/ppermute | solution.py:309
  37.3 3.2 %copy-start.2 = (bf16[24,4096]{1,0:T(8,128)(2,1)S(1)}, bf16[24,4096]{1,0:T(8,128)(2,1)}, u32[]{:S(2)}) copy-start(bf16[24,4096]{1,0:T(8,128)(2,1)} %fresh_ref.1) | copy-start | bytes 589828
  37.4 4.4 %collective-permute-start.3 = (bf16[192,256]{1,0:T(8,128)(2,1)S(1)}, bf16[192,256]{1,0:T(8,128)(2,1)S(1)}, u32[]{:S(2)}, u32[]{:S(2)}) collective-permute-start(bf16[192,256]{1,0:T(8,128)(2,1)S(1)} %get-tuple-element.9), channel_id=1, source_target_pairs={{0,8},{8,0},{24,16},{1,9},{9,1},{25,17},{2,10},{10,2},{26,18},{3,1... | collective-permute-start | bytes 294920 | tf_op jit(solution)/shard_map/ppermute | solution.py:309

commit v11 on v10

--- a/solution.py
+++ b/solution.py
@@ -25,41 +25,41 @@
     return (index + count // 2) % count
 
 
-def pack_kernel(seq_count, halves, q_hbm, k_hbm, v_hbm, out_hbm, held, block, in_sems, out_sems):
+def pack_kernel(seq_count, parts, q_hbm, k_hbm, v_hbm, out_hbm, held, block, in_sems, out_sems):
     tok, width = held.shape[1:]
     wide = out_hbm.shape[1] // 3
     count = out_hbm.shape[0] // tok
     tm_count = count // seq_count
-    span, part = width // halves, seq_count // halves
+    span, members = width // parts, seq_count // parts
     copies = []
-    for half in range(halves):
-        columns = slice(half * span, (half + 1) * span)
+    for part in range(parts):
+        columns = slice(part * span, (part + 1) * span)
         for place, ref in enumerate((q_hbm, k_hbm, v_hbm)):
             copies.append(
                 pltpu.make_async_copy(
-                    ref.at[0, :, columns], held.at[place, :, columns], in_sems.at[half, place]
+                    ref.at[0, :, columns], held.at[place, :, columns], in_sems.at[part, place]
                 )
             )
             copies[-1].start()
     outs = []
-    for half in range(halves):
+    for part in range(parts):
         for place in range(3):
-            copies[3 * half + place].wait()
-            for tm in range(tm_count):
-                for seq in range(half * part, (half + 1) * part, 2):
+            copies[3 * part + place].wait()
+        for tm in range(tm_count):
+            for seq in range(part * members, (part + 1) * members, 2):
+                first = (tm * seq_count + mixed(seq, seq_count)) * tok
+                for place in range(3):
                     rows = []
                     for member in (seq, seq + 1):
                         start = (member * tm_count + tm) * wide
                         rows.append(held[place, :, start : start + wide].astype(jnp.float32))
-                    first = (tm * seq_count + mixed(seq, seq_count)) * tok
                     block[first : first + 2 * tok, place * wide : (place + 1) * wide] = jnp.concatenate(
                         rows, axis=0
                     ).astype(jnp.bfloat16)
-        for tm in range(tm_count):
-            first = (tm * seq_count + mixed(half * part, seq_count)) * tok
-            rows = slice(first, first + part * tok)
+            first = (tm * seq_count + mixed(part * members, seq_count)) * tok
+            rows = slice(first, first + members * tok)
             outs.append(
-                pltpu.make_async_copy(block.at[rows], out_hbm.at[rows], out_sems.at[half, tm])
+                pltpu.make_async_copy(block.at[rows], out_hbm.at[rows], out_sems.at[part, tm])
             )
             outs[-1].start()
     for out in outs:
@@ -263,10 +263,10 @@
     group_tok = tok * seq_count
     kind = queries.dtype
     DMA = pltpu.SemaphoreType.DMA
-    halves = 2
+    parts = 4 if seq_count % 8 == 0 else 2
 
     packed = run(
-        functools.partial(pack_kernel, seq_count, halves),
+        functools.partial(pack_kernel, seq_count, parts),
         "pack",
         [HBM((count * tok, 3 * wide), kind)],
         [whole(HBM)] * 3,
@@ -274,8 +274,8 @@
         scratch=[
             VMEM((3, tok, width), kind),
             VMEM((count * tok, 3 * wide), kind),
-            DMA((halves, 3)),
-            DMA((halves, tm_count)),
+            DMA((parts, 3)),
+            DMA((parts, tm_count)),
         ],
     )
     order = [tm * seq_count + mixed(s, seq_count) for tm in range(tm_count) for s in range(seq_count)]

time: 42.9 us -> 42.9 us (level)
  no operation moved by 1% of the time
where the time goes in v11:
time: 42.9 us; the launch traced here: 42.5 us
  starting transfers between devices  19 us (44%)
  waiting for transfers between devices  16 us (37%)
  Pallas kernels  6.07 us (14%)
  between operations  1.4 us (3%)
    all_to_all x1, waiting for transfers between devices, spread_body(): exchanged = exchange(packed)  13.1 us
    ppermute x3, starting transfers between devices, spread_body(): lax.ppermute(hand, 'tm', [(i, j) for i, j in route if j < tm_count - 1])  7.75 us
    all_to_all x1, starting transfers between devices, spread_body(): exchanged = exchange(packed)  7.3 us
    pallas_call x6, Pallas kernels, run(): pl.pallas_call(kernel, out_shape=outs, in_specs=specs, out_specs=[whole(g...  6.07 us
    all_to_all x1, starting transfers between devices, spread_body(): returned = exchange(attended)  2.68 us
    ppermute x1, waiting for transfers between devices, shifted(): return lax.ppermute(block, axis, route)  2.13 us
    ppermute x1, starting transfers between devices, shifted(): return lax.ppermute(block, axis, route)  1.29 us
  transfers between devices with their start and end apart: 6, of which 4 were waited for; matrix products, arithmetic and copies ran while one was open for 0% of the time, Pallas kernels for 4%

profile of v11, /device:TPU:0, one launch (start us, length us, event | category | flops | bytes accessed | tf_op | source)
XLA Modules:
  0.0 42.5 jit_solution(8204541959582530943)
XLA Ops:
  0.6 0.0 copy-start
  0.6 2.1 %pack.1.after_ref = bf16[768,384]{1,0:T(8,128)(2,1)} custom-call(bf16[1,24,4096]{2,1,0:T(8,128)(2,1)} %q_hbm.1, bf16[1,24,4096]{2,1,0:T(8,128)(2,1)} %k_hbm.1, bf16[1,24,4096]{2,1,0:T(8,128)(2,1)} %v_hbm.1), custom_call_target="tpu_custom_call" | custom-call | bytes 1179648 | tf_op jit(solution)/shard_map/pack/pallas_call | solution.py:244
  2.7 0.0 copy-start.1
  2.7 7.3 %all-to-all-start = ((bf16[32,24,384]{2,1,0:T(8,128)(2,1)}), bf16[32,24,384]{2,1,0:T(8,128)(2,1)S(1)}, u32[]{:S(2)}, u32[]{:S(2)}) async-start(bf16[32,24,384]{2,1,0:T(8,128)(2,1)} %bitcast.7), calls=%async_computation | async-start | bytes 1179648 | tf_op jit(solution)/shard_map/all_to_all | solution.py:285
  10.7 0.0 copy-done
  10.7 0.0 copy-done.1
  10.7 0.0 copy-start.3
  10.7 0.1 residual.1
  10.8 1.3 %collective-permute-start = (bf16[32,4096]{1,0:T(8,128)(2,1)S(1)}, bf16[32,4096]{1,0:T(8,128)(2,1)S(1)}, u32[]{:S(2)}, u32[]{:S(2)}) collective-permute-start(bf16[32,4096]{1,0:T(8,128)(2,1)S(1)} %residual.1), channel_id=1, source_target_pairs={{8,0},{16,8},{24,16},{9,1},{17,9},{25,17},{10,2},{18,10},{26,18},{... | collective-permute-start | bytes 786440 | tf_op jit(solution)/shard_map/ppermute | solution.py:21
  12.1 2.1 %collective-permute-done.after_ref.moved_ref = bf16[32,4096]{1,0:T(8,128)(2,1)S(1)} collective-permute-done((bf16[32,4096]{1,0:T(8,128)(2,1)S(1)}, bf16[32,4096]{1,0:T(8,128)(2,1)S(1)}, u32[]{:S(2)}, u32[]{:S(2)}) %collective-permute-start) | collective-permute-done | bytes 262176 | tf_op jit(solution)/shard_map/ppermute | solution.py:21
  14.3 13.1 %all-to-all-done = bf16[32,24,384]{2,1,0:T(8,128)(2,1)S(1)} async-done(((bf16[32,24,384]{2,1,0:T(8,128)(2,1)}), bf16[32,24,384]{2,1,0:T(8,128)(2,1)S(1)}, u32[]{:S(2)}, u32[]{:S(2)}) %all-to-all-start) | async-done | bytes 589856 | tf_op jit(solution)/shard_map/all_to_all | solution.py:285
  27.4 0.0 copy-done.3
  27.4 1.6 %attend.1 = (bf16[768,128]{1,0:T(8,128)(2,1)}, bf16[192,256]{1,0:T(8,128)(2,1)S(1)}, bf16[192,256]{1,0:T(8,128)(2,1)S(1)}, bf16[192,256]{1,0:T(8,128)(2,1)S(1)}) custom-call(s32[4,4]{1,0:T(4,128)S(1)} %copy-done.3, bf16[768,384]{1,0:T(8,128)(2,1)S(1)} %bitcast.4, bf16[32,4096]{1,0:T(8,128)(2,1)S(1)} %collective-permute-done.after_ref.moved_ref), custom_call_target="tpu_custom_call" | custom-call | flops 150994944 | bytes 1343552 | tf_op jit(solution)/shard_map/attend/pallas_call | solution.py:244
  29.0 2.7 %all-to-all-start.1 = ((bf16[32,24,128]{2,1,0:T(8,128)(2,1)}), bf16[32,24,128]{2,1,0:T(8,128)(2,1)S(1)}, u32[]{:S(2)}, u32[]{:S(2)}) async-start(bf16[32,24,128]{2,1,0:T(8,128)(2,1)} %bitcast.8), calls=%async_computation.1 | async-start | bytes 393216 | tf_op jit(solution)/shard_map/all_to_all | solution.py:305
  31.6 1.3 %collective-permute-start.1 = (bf16[192,256]{1,0:T(8,128)(2,1)S(1)}, bf16[192,256]{1,0:T(8,128)(2,1)S(1)}, u32[]{:S(2)}, u32[]{:S(2)}) collective-permute-start(bf16[192,256]{1,0:T(8,128)(2,1)S(1)} %get-tuple-element.7), channel_id=1, source_target_pairs={{8,16},{16,8},{24,0},{9,17},{17,9},{25,1},{10,18},{18,10},{26,2},{... | collective-permute-start | bytes 294920 | tf_op jit(solution)/shard_map/ppermute | solution.py:309
  32.9 4.4 %collective-permute-start.2 = (bf16[192,256]{1,0:T(8,128)(2,1)S(1)}, bf16[192,256]{1,0:T(8,128)(2,1)S(1)}, u32[]{:S(2)}, u32[]{:S(2)}) collective-permute-start(bf16[192,256]{1,0:T(8,128)(2,1)S(1)} %get-tuple-element.8), channel_id=1, source_target_pairs={{0,16},{16,0},{24,8},{1,17},{17,1},{25,9},{2,18},{18,2},{26,10},{3... | collective-permute-start | bytes 294920 | tf_op jit(solution)/shard_map/ppermute | solution.py:309
  37.4 0.0 copy-start.2
  37.4 2.1 %collective-permute-start.3 = (bf16[192,256]{1,0:T(8,128)(2,1)S(1)}, bf16[192,256]{1,0:T(8,128)(2,1)S(1)}, u32[]{:S(2)}, u32[]{:S(2)}) collective-permute-start(bf16[192,256]{1,0:T(8,128)(2,1)S(1)} %get-tuple-element.9), channel_id=1, source_target_pairs={{0,8},{8,0},{24,16},{1,9},{9,1},{25,17},{2,10},{10,2},{26,18},{3,1... | collective-permute-start | bytes 294920 | tf_op jit(solution)/shard_map/ppermute | solution.py:309
  39.4 0.0 collective-permute-done.1.hand_ref
  39.5 0.8 %cache.1.after_ref.begun_hbm = bf16[1,2,192,512]{3,2,1,0:T(8,128)(2,1)} custom-call(bf16[768,384]{1,0:T(8,128)(2,1)S(1)} %bitcast.5, bf16[192,256]{1,0:T(8,128)(2,1)S(1)} %collective-permute-done.1.hand_ref), custom_call_target="tpu_custom_call" | custom-call | bytes 1081344 | tf_op jit(solution)/shard_map/cache/pallas_call | solution.py:244
  40.3 0.3 all-to-all-done.1
  40.5 0.0 copy-done.2
  40.5 0.8 %update.1.after_ref = bf16[1,24,4096]{2,1,0:T(8,128)(2,1)} custom-call(bf16[768,128]{1,0:T(8,128)(2,1)S(1)} %bitcast.6, bf16[32,4096]{1,0:T(8,128)(2,1)S(1)} %collective-permute-done.after_ref.moved_ref, bf16[24,4096]{1,0:T(8,128)(2,1)S(1)} %copy-done.2, bf16[1,2,192,512]{3,2,1,0:T(8,128)(2,1)} %cache.1.after_ref.begun_hbm), custom_call_target="tpu_custom_call" | custom-call | bytes 1245184 | tf_op jit(solution)/shard_map/update/pallas_call | solution.py:244
  41.3 0.4 %collective-permute-done.2.refs_0_ = bf16[192,256]{1,0:T(8,128)(2,1)S(1)} collective-permute-done((bf16[192,256]{1,0:T(8,128)(2,1)S(1)}, bf16[192,256]{1,0:T(8,128)(2,1)S(1)}, u32[]{:S(2)}, u32[]{:S(2)}) %collective-permute-start.2) | collective-permute-done | bytes 98336 | tf_op jit(solution)/shard_map/ppermute | solution.py:309
  41.7 0.0 collective-permute-done.3.refs_1_
  41.8 0.7 %cache_rest.1 = bf16[1,2,192,512]{3,2,1,0:T(8,128)(2,1)} custom-call(bf16[1,2,192,512]{3,2,1,0:T(8,128)(2,1)} %cache.1.after_ref.begun_hbm, bf16[1,24,4096]{2,1,0:T(8,128)(2,1)} %update.1.after_ref, bf16[192,256]{1,0:T(8,128)(2,1)S(1)} %collective-permute-done.2.refs_0_, ...), custom_call_target="tpu_custom_call", output_to_operand_aliasing={{}: (0, {})} | custom-call | bytes 1179648 | tf_op jit(solution)/shard_map/cache_rest/pallas_call | solution.py:244
Async XLA Ops:
  0.6 10.1 %copy-start = (f32[50,4096]{1,0:T(8,128)S(1)}, f32[50,4096]{1,0:T(8,128)}, u32[]{:S(2)}) copy-start(f32[50,4096]{1,0:T(8,128)} %gate_ref.1) | copy-start | bytes 2457604
  2.7 8.0 %copy-start.1 = (bf16[1,24,4096]{2,1,0:T(8,128)(2,1)S(1)}, bf16[1,24,4096]{2,1,0:T(8,128)(2,1)}, u32[]{:S(2)}) copy-start(bf16[1,24,4096]{2,1,0:T(8,128)(2,1)} %h_ref.1) | copy-start | bytes 589828
  2.7 24.6 %all-to-all-start = ((bf16[32,24,384]{2,1,0:T(8,128)(2,1)}), bf16[32,24,384]{2,1,0:T(8,128)(2,1)S(1)}, u32[]{:S(2)}, u32[]{:S(2)}) async-start(bf16[32,24,384]{2,1,0:T(8,128)(2,1)} %bitcast.7), calls=%async_computation | async-start | bytes 1179648 | tf_op jit(solution)/shard_map/all_to_all | solution.py:285
  10.7 16.6 %copy-start.3 = (s32[4,4]{1,0:T(4,128)S(1)}, s32[4,4]{1,0:T(4,128)}, u32[]{:S(2)}) copy-start(s32[4,4]{1,0:T(4,128)} %pattern_ref.1) | copy-start | bytes 196
  10.8 3.4 %collective-permute-start = (bf16[32,4096]{1,0:T(8,128)(2,1)S(1)}, bf16[32,4096]{1,0:T(8,128)(2,1)S(1)}, u32[]{:S(2)}, u32[]{:S(2)}) collective-permute-start(bf16[32,4096]{1,0:T(8,128)(2,1)S(1)} %residual.1), channel_id=1, source_target_pairs={{8,0},{16,8},{24,16},{9,1},{17,9},{25,17},{10,2},{18,10},{26,18},{... | collective-permute-start | bytes 786440 | tf_op jit(solution)/shard_map/ppermute | solution.py:21
  29.0 11.6 %all-to-all-start.1 = ((bf16[32,24,128]{2,1,0:T(8,128)(2,1)}), bf16[32,24,128]{2,1,0:T(8,128)(2,1)S(1)}, u32[]{:S(2)}, u32[]{:S(2)}) async-start(bf16[32,24,128]{2,1,0:T(8,128)(2,1)} %bitcast.8), calls=%async_computation.1 | async-start | bytes 393216 | tf_op jit(solution)/shard_map/all_to_all | solution.py:305
  31.6 7.8 %collective-permute-start.1 = (bf16[192,256]{1,0:T(8,128)(2,1)S(1)}, bf16[192,256]{1,0:T(8,128)(2,1)S(1)}, u32[]{:S(2)}, u32[]{:S(2)}) collective-permute-start(bf16[192,256]{1,0:T(8,128)(2,1)S(1)} %get-tuple-element.7), channel_id=1, source_target_pairs={{8,16},{16,8},{24,0},{9,17},{17,9},{25,1},{10,18},{18,10},{26,2},{... | collective-permute-start | bytes 294920 | tf_op jit(solution)/shard_map/ppermute | solution.py:309
  32.9 8.8 %collective-permute-start.2 = (bf16[192,256]{1,0:T(8,128)(2,1)S(1)}, bf16[192,256]{1,0:T(8,128)(2,1)S(1)}, u32[]{:S(2)}, u32[]{:S(2)}) collective-permute-start(bf16[192,256]{1,0:T(8,128)(2,1)S(1)} %get-tuple-element.8), channel_id=1, source_target_pairs={{0,16},{16,0},{24,8},{1,17},{17,1},{25,9},{2,18},{18,2},{26,10},{3... | collective-permute-start | bytes 294920 | tf_op jit(solution)/shard_map/ppermute | solution.py:309
  37.4 3.2 %copy-start.2 = (bf16[24,4096]{1,0:T(8,128)(2,1)S(1)}, bf16[24,4096]{1,0:T(8,128)(2,1)}, u32[]{:S(2)}) copy-start(bf16[24,4096]{1,0:T(8,128)(2,1)} %fresh_ref.1) | copy-start | bytes 589828
  37.4 4.4 %collective-permute-start.3 = (bf16[192,256]{1,0:T(8,128)(2,1)S(1)}, bf16[192,256]{1,0:T(8,128)(2,1)S(1)}, u32[]{:S(2)}, u32[]{:S(2)}) collective-permute-start(bf16[192,256]{1,0:T(8,128)(2,1)S(1)} %get-tuple-element.9), channel_id=1, source_target_pairs={{0,8},{8,0},{24,16},{1,9},{9,1},{25,17},{2,10},{10,2},{26,18},{3,1... | collective-permute-start | bytes 294920 | tf_op jit(solution)/shard_map/ppermute | solution.py:309

commit v12 on v11

--- a/solution.py
+++ b/solution.py
@@ -66,8 +66,30 @@
         out.wait()
 
 
-def residual_kernel(noise_ref, h_ref, gate_ref, after_ref, out_ref):
-    gate = gate_ref[pl.ds(noise_ref[0], 1), :]
+def residual_kernel(noise_ref, h_ref, gate_hbm, after_ref, out_ref, held, sem):
+    step = noise_ref[0]
+    steps = gate_hbm.shape[0]
+    whole_tiles = steps // 8 * 8
+    first = step // 8 * 8
+
+    @pl.when(step < whole_tiles)
+    def take_tile():
+        rows = pl.ds(pl.multiple_of(first, 8), 8)
+        copy = pltpu.make_async_copy(gate_hbm.at[rows], held, sem)
+        copy.start()
+        copy.wait()
+
+    if steps > whole_tiles:
+
+        @pl.when(step >= whole_tiles)
+        def take_rest():
+            copy = pltpu.make_async_copy(
+                gate_hbm.at[whole_tiles:steps], held.at[0 : steps - whole_tiles], sem
+            )
+            copy.start()
+            copy.wait()
+
+    gate = held[pl.ds(step - first, 1), :]
     high = gate.astype(jnp.bfloat16).astype(jnp.float32)
     middle = (gate - high).astype(jnp.bfloat16).astype(jnp.float32)
     low = gate - high - middle
@@ -288,8 +310,14 @@
         residual_kernel,
         "residual",
         [VMEM((tok + 8, width), kind)],
-        [whole(SMEM), whole(), whole(), whole(HBM)],
-        (noise_step, hidden, gate_table, pltpu.with_memory_space_constraint(packed, HBM)),
+        [whole(SMEM), whole(), whole(HBM), whole(HBM)],
+        (
+            noise_step,
+            hidden,
+            pltpu.with_memory_space_constraint(gate_table, HBM),
+            pltpu.with_memory_space_constraint(packed, HBM),
+        ),
+        scratch=[VMEM((8, width), jnp.float32), DMA],
     )
     moved = shifted(residual, "tm", -1)
 

time: 42.9 us -> 42.8 us (level)
  waiting for transfers between devices: 16 us -> 15.1 us
  Pallas kernels: 6.07 us -> 6.88 us
    all_to_all x1, waiting for transfers between devices: 13.1 us -> 12.2 us  [spread_body(): exchanged = exchange(packed)]
    pallas_call x6, Pallas kernels: 6.07 us -> 6.88 us  [run(): pl.pallas_call(kernel, out_shape=outs, in_specs=specs, out_specs=[whole(g...]
  transfers between devices with their start and end apart: 6 -> 6, of which waited for: 4 -> 4; matrix products, arithmetic and copies ran while one was open for 0% -> 0% of each run, Pallas kernels for 4% -> 6%
where the time goes in v12:
time: 42.8 us; the launch traced here: 42.4 us
  starting transfers between devices  19 us (44%)
  waiting for transfers between devices  15.1 us (35%)
  Pallas kernels  6.88 us (16%)
  between operations  1.38 us (3%)
    all_to_all x1, waiting for transfers between devices, spread_body(): exchanged = exchange(packed)  12.2 us
    ppermute x3, starting transfers between devices, spread_body(): lax.ppermute(hand, 'tm', [(i, j) for i, j in route if j < tm_count - 1])  7.75 us
    all_to_all x1, starting transfers between devices, spread_body(): exchanged = exchange(packed)  7.3 us
    pallas_call x6, Pallas kernels, run(): pl.pallas_call(kernel, out_shape=outs, in_specs=specs, out_specs=[whole(g...  6.88 us
    all_to_all x1, starting transfers between devices, spread_body(): returned = exchange(attended)  2.68 us
    ppermute x1, waiting for transfers between devices, shifted(): return lax.ppermute(block, axis, route)  2.13 us
    ppermute x1, starting transfers between devices, shifted(): return lax.ppermute(block, axis, route)  1.29 us
  transfers between devices with their start and end apart: 6, of which 4 were waited for; matrix products, arithmetic and copies ran while one was open for 0% of the time, Pallas kernels for 6%

profile of v12, /device:TPU:0, one launch (start us, length us, event | category | flops | bytes accessed | tf_op | source)
XLA Modules:
  0.0 42.4 jit_solution(8320285962449190299)
XLA Ops:
  0.6 2.0 %pack.1.after_ref = bf16[768,384]{1,0:T(8,128)(2,1)} custom-call(bf16[1,24,4096]{2,1,0:T(8,128)(2,1)} %q_hbm.1, bf16[1,24,4096]{2,1,0:T(8,128)(2,1)} %k_hbm.1, bf16[1,24,4096]{2,1,0:T(8,128)(2,1)} %v_hbm.1), custom_call_target="tpu_custom_call" | custom-call | bytes 1179648 | tf_op jit(solution)/shard_map/pack/pallas_call | solution.py:266
  2.6 0.0 copy-start
  2.6 7.3 %all-to-all-start = ((bf16[32,24,384]{2,1,0:T(8,128)(2,1)}), bf16[32,24,384]{2,1,0:T(8,128)(2,1)S(1)}, u32[]{:S(2)}, u32[]{:S(2)}) async-start(bf16[32,24,384]{2,1,0:T(8,128)(2,1)} %bitcast.7), calls=%async_computation | async-start | bytes 1179648 | tf_op jit(solution)/shard_map/all_to_all | solution.py:307
  10.6 0.0 copy-done
  10.6 0.0 copy-start.2
  10.6 1.0 %residual.1 = bf16[32,4096]{1,0:T(8,128)(2,1)S(1)} custom-call(s32[1]{0:T(128)S(6)} %copy.12.noise_ref, bf16[1,24,4096]{2,1,0:T(8,128)(2,1)S(1)} %copy-done, f32[50,4096]{1,0:T(8,128)} %gate_hbm.1, bf16[768,384]{1,0:T(8,128)(2,1)} %pack.1.after_ref), custom_call_target="tpu_custom_call" | custom-call | bytes 1867780 | tf_op jit(solution)/shard_map/residual/pallas_call | solution.py:266
  11.6 1.3 %collective-permute-start = (bf16[32,4096]{1,0:T(8,128)(2,1)S(1)}, bf16[32,4096]{1,0:T(8,128)(2,1)S(1)}, u32[]{:S(2)}, u32[]{:S(2)}) collective-permute-start(bf16[32,4096]{1,0:T(8,128)(2,1)S(1)} %residual.1), channel_id=1, source_target_pairs={{8,0},{16,8},{24,16},{9,1},{17,9},{25,17},{10,2},{18,10},{26,18},{... | collective-permute-start | bytes 786440 | tf_op jit(solution)/shard_map/ppermute | solution.py:21
  12.9 2.1 %collective-permute-done.after_ref.moved_ref = bf16[32,4096]{1,0:T(8,128)(2,1)S(1)} collective-permute-done((bf16[32,4096]{1,0:T(8,128)(2,1)S(1)}, bf16[32,4096]{1,0:T(8,128)(2,1)S(1)}, u32[]{:S(2)}, u32[]{:S(2)}) %collective-permute-start) | collective-permute-done | bytes 262176 | tf_op jit(solution)/shard_map/ppermute | solution.py:21
  15.1 12.2 %all-to-all-done = bf16[32,24,384]{2,1,0:T(8,128)(2,1)S(1)} async-done(((bf16[32,24,384]{2,1,0:T(8,128)(2,1)}), bf16[32,24,384]{2,1,0:T(8,128)(2,1)S(1)}, u32[]{:S(2)}, u32[]{:S(2)}) %all-to-all-start) | async-done | bytes 589856 | tf_op jit(solution)/shard_map/all_to_all | solution.py:307
  27.2 0.0 copy-done.2
  27.3 1.6 %attend.1 = (bf16[768,128]{1,0:T(8,128)(2,1)}, bf16[192,256]{1,0:T(8,128)(2,1)S(1)}, bf16[192,256]{1,0:T(8,128)(2,1)S(1)}, bf16[192,256]{1,0:T(8,128)(2,1)S(1)}) custom-call(s32[4,4]{1,0:T(4,128)S(1)} %copy-done.2, bf16[768,384]{1,0:T(8,128)(2,1)S(1)} %bitcast.4, bf16[32,4096]{1,0:T(8,128)(2,1)S(1)} %collective-permute-done.after_ref.moved_ref), custom_call_target="tpu_custom_call" | custom-call | flops 150994944 | bytes 1343552 | tf_op jit(solution)/shard_map/attend/pallas_call | solution.py:266
  28.8 2.7 %all-to-all-start.1 = ((bf16[32,24,128]{2,1,0:T(8,128)(2,1)}), bf16[32,24,128]{2,1,0:T(8,128)(2,1)S(1)}, u32[]{:S(2)}, u32[]{:S(2)}) async-start(bf16[32,24,128]{2,1,0:T(8,128)(2,1)} %bitcast.8), calls=%async_computation.1 | async-start | bytes 393216 | tf_op jit(solution)/shard_map/all_to_all | solution.py:333
  31.5 1.3 %collective-permute-start.1 = (bf16[192,256]{1,0:T(8,128)(2,1)S(1)}, bf16[192,256]{1,0:T(8,128)(2,1)S(1)}, u32[]{:S(2)}, u32[]{:S(2)}) collective-permute-start(bf16[192,256]{1,0:T(8,128)(2,1)S(1)} %get-tuple-element.7), channel_id=1, source_target_pairs={{8,16},{16,8},{24,0},{9,17},{17,9},{25,1},{10,18},{18,10},{26,2},{... | collective-permute-start | bytes 294920 | tf_op jit(solution)/shard_map/ppermute | solution.py:337
  32.8 4.4 %collective-permute-start.2 = (bf16[192,256]{1,0:T(8,128)(2,1)S(1)}, bf16[192,256]{1,0:T(8,128)(2,1)S(1)}, u32[]{:S(2)}, u32[]{:S(2)}) collective-permute-start(bf16[192,256]{1,0:T(8,128)(2,1)S(1)} %get-tuple-element.8), channel_id=1, source_target_pairs={{0,16},{16,0},{24,8},{1,17},{17,1},{25,9},{2,18},{18,2},{26,10},{3... | collective-permute-start | bytes 294920 | tf_op jit(solution)/shard_map/ppermute | solution.py:337
  37.2 0.0 copy-start.1
  37.3 2.1 %collective-permute-start.3 = (bf16[192,256]{1,0:T(8,128)(2,1)S(1)}, bf16[192,256]{1,0:T(8,128)(2,1)S(1)}, u32[]{:S(2)}, u32[]{:S(2)}) collective-permute-start(bf16[192,256]{1,0:T(8,128)(2,1)S(1)} %get-tuple-element.9), channel_id=1, source_target_pairs={{0,8},{8,0},{24,16},{1,9},{9,1},{25,17},{2,10},{10,2},{26,18},{3,1... | collective-permute-start | bytes 294920 | tf_op jit(solution)/shard_map/ppermute | solution.py:337
  39.3 0.0 collective-permute-done.1.hand_ref
  39.4 0.8 %cache.1.after_ref.begun_hbm = bf16[1,2,192,512]{3,2,1,0:T(8,128)(2,1)} custom-call(bf16[768,384]{1,0:T(8,128)(2,1)S(1)} %bitcast.5, bf16[192,256]{1,0:T(8,128)(2,1)S(1)} %collective-permute-done.1.hand_ref), custom_call_target="tpu_custom_call" | custom-call | bytes 1081344 | tf_op jit(solution)/shard_map/cache/pallas_call | solution.py:266
  40.2 0.3 all-to-all-done.1
  40.4 0.0 copy-done.1
  40.4 0.8 %update.1.after_ref = bf16[1,24,4096]{2,1,0:T(8,128)(2,1)} custom-call(bf16[768,128]{1,0:T(8,128)(2,1)S(1)} %bitcast.6, bf16[32,4096]{1,0:T(8,128)(2,1)S(1)} %collective-permute-done.after_ref.moved_ref, bf16[24,4096]{1,0:T(8,128)(2,1)S(1)} %copy-done.1, bf16[1,2,192,512]{3,2,1,0:T(8,128)(2,1)} %cache.1.after_ref.begun_hbm), custom_call_target="tpu_custom_call" | custom-call | bytes 1245184 | tf_op jit(solution)/shard_map/update/pallas_call | solution.py:266
  41.2 0.4 %collective-permute-done.2.refs_0_ = bf16[192,256]{1,0:T(8,128)(2,1)S(1)} collective-permute-done((bf16[192,256]{1,0:T(8,128)(2,1)S(1)}, bf16[192,256]{1,0:T(8,128)(2,1)S(1)}, u32[]{:S(2)}, u32[]{:S(2)}) %collective-permute-start.2) | collective-permute-done | bytes 98336 | tf_op jit(solution)/shard_map/ppermute | solution.py:337
  41.6 0.0 collective-permute-done.3.refs_1_
  41.6 0.7 %cache_rest.1 = bf16[1,2,192,512]{3,2,1,0:T(8,128)(2,1)} custom-call(bf16[1,2,192,512]{3,2,1,0:T(8,128)(2,1)} %cache.1.after_ref.begun_hbm, bf16[1,24,4096]{2,1,0:T(8,128)(2,1)} %update.1.after_ref, bf16[192,256]{1,0:T(8,128)(2,1)S(1)} %collective-permute-done.2.refs_0_, ...), custom_call_target="tpu_custom_call", output_to_operand_aliasing={{}: (0, {})} | custom-call | bytes 1179648 | tf_op jit(solution)/shard_map/cache_rest/pallas_call | solution.py:266
Async XLA Ops:
  2.6 8.0 %copy-start = (bf16[1,24,4096]{2,1,0:T(8,128)(2,1)S(1)}, bf16[1,24,4096]{2,1,0:T(8,128)(2,1)}, u32[]{:S(2)}) copy-start(bf16[1,24,4096]{2,1,0:T(8,128)(2,1)} %h_ref.1) | copy-start | bytes 589828
  2.6 24.6 %all-to-all-start = ((bf16[32,24,384]{2,1,0:T(8,128)(2,1)}), bf16[32,24,384]{2,1,0:T(8,128)(2,1)S(1)}, u32[]{:S(2)}, u32[]{:S(2)}) async-start(bf16[32,24,384]{2,1,0:T(8,128)(2,1)} %bitcast.7), calls=%async_computation | async-start | bytes 1179648 | tf_op jit(solution)/shard_map/all_to_all | solution.py:307
  10.6 16.7 %copy-start.2 = (s32[4,4]{1,0:T(4,128)S(1)}, s32[4,4]{1,0:T(4,128)}, u32[]{:S(2)}) copy-start(s32[4,4]{1,0:T(4,128)} %pattern_ref.1) | copy-start | bytes 196
  11.6 3.4 %collective-permute-start = (bf16[32,4096]{1,0:T(8,128)(2,1)S(1)}, bf16[32,4096]{1,0:T(8,128)(2,1)S(1)}, u32[]{:S(2)}, u32[]{:S(2)}) collective-permute-start(bf16[32,4096]{1,0:T(8,128)(2,1)S(1)} %residual.1), channel_id=1, source_target_pairs={{8,0},{16,8},{24,16},{9,1},{17,9},{25,17},{10,2},{18,10},{26,18},{... | collective-permute-start | bytes 786440 | tf_op jit(solution)/shard_map/ppermute | solution.py:21
  28.8 11.6 %all-to-all-start.1 = ((bf16[32,24,128]{2,1,0:T(8,128)(2,1)}), bf16[32,24,128]{2,1,0:T(8,128)(2,1)S(1)}, u32[]{:S(2)}, u32[]{:S(2)}) async-start(bf16[32,24,128]{2,1,0:T(8,128)(2,1)} %bitcast.8), calls=%async_computation.1 | async-start | bytes 393216 | tf_op jit(solution)/shard_map/all_to_all | solution.py:333
  31.5 7.8 %collective-permute-start.1 = (bf16[192,256]{1,0:T(8,128)(2,1)S(1)}, bf16[192,256]{1,0:T(8,128)(2,1)S(1)}, u32[]{:S(2)}, u32[]{:S(2)}) collective-permute-start(bf16[192,256]{1,0:T(8,128)(2,1)S(1)} %get-tuple-element.7), channel_id=1, source_target_pairs={{8,16},{16,8},{24,0},{9,17},{17,9},{25,1},{10,18},{18,10},{26,2},{... | collective-permute-start | bytes 294920 | tf_op jit(solution)/shard_map/ppermute | solution.py:337
  32.8 8.8 %collective-permute-start.2 = (bf16[192,256]{1,0:T(8,128)(2,1)S(1)}, bf16[192,256]{1,0:T(8,128)(2,1)S(1)}, u32[]{:S(2)}, u32[]{:S(2)}) collective-permute-start(bf16[192,256]{1,0:T(8,128)(2,1)S(1)} %get-tuple-element.8), channel_id=1, source_target_pairs={{0,16},{16,0},{24,8},{1,17},{17,1},{25,9},{2,18},{18,2},{26,10},{3... | collective-permute-start | bytes 294920 | tf_op jit(solution)/shard_map/ppermute | solution.py:337
  37.2 3.2 %copy-start.1 = (bf16[24,4096]{1,0:T(8,128)(2,1)S(1)}, bf16[24,4096]{1,0:T(8,128)(2,1)}, u32[]{:S(2)}) copy-start(bf16[24,4096]{1,0:T(8,128)(2,1)} %fresh_ref.1) | copy-start | bytes 589828
  37.3 4.4 %collective-permute-start.3 = (bf16[192,256]{1,0:T(8,128)(2,1)S(1)}, bf16[192,256]{1,0:T(8,128)(2,1)S(1)}, u32[]{:S(2)}, u32[]{:S(2)}) collective-permute-start(bf16[192,256]{1,0:T(8,128)(2,1)S(1)} %get-tuple-element.9), channel_id=1, source_target_pairs={{0,8},{8,0},{24,16},{1,9},{9,1},{25,17},{2,10},{10,2},{26,18},{3,1... | collective-permute-start | bytes 294920 | tf_op jit(solution)/shard_map/ppermute | solution.py:337

commit v13 on v12

--- a/solution.py
+++ b/solution.py
@@ -167,14 +167,20 @@
         for group in range(1, groups):
             start = (groups - 1 - group) * rows
             held[group - 1, :, head : head + HD] = result[start : start + rows]
-    copies = [
-        pltpu.make_async_copy(
-            held.at[min(place, groups - 2)], out_hbm.at[place * rows : (place + 1) * rows], sems.at[place]
-        )
-        for place in range(groups)
-    ]
-    for copy in copies:
-        copy.start()
+    copies = []
+    half = rows // 2
+    for place in range(groups):
+        for part in range(2):
+            at = mixed(part, 2) * half
+            to = place * rows + part * half
+            copies.append(
+                pltpu.make_async_copy(
+                    held.at[min(place, groups - 2), at : at + half],
+                    out_hbm.at[to : to + half],
+                    sems.at[place, part],
+                )
+            )
+            copies[-1].start()
     for distance, hand_ref in zip(distances(groups), hand_refs):
         group = lax.rem(partner(here, distance, groups) + 1, groups)
         hand_ref[...] = x_ref[pl.ds(pl.multiple_of(group * rows, rows), rows), wide:]
@@ -247,7 +253,7 @@
             rows = att_ref[2 * pair * tok : 2 * (pair + 1) * tok, :].astype(jnp.float32)
             for half in range(2):
                 source = 2 * pair + half
-                start = (mixed(source % seq_count, seq_count) * tm_count + source // seq_count) * wide
+                start = ((source % seq_count) * tm_count + source // seq_count) * wide
                 moved = moved_ref[:, start : start + wide].astype(jnp.float32)
                 gate = (moved[tok : tok + 1] + moved[tok + 1 : tok + 2]) + moved[tok + 2 : tok + 3]
                 result = moved[:tok] + gate * rows[half * tok : (half + 1) * tok]
@@ -302,9 +308,9 @@
     )
     order = [tm * seq_count + mixed(s, seq_count) for tm in range(tm_count) for s in range(seq_count)]
     exchange = functools.partial(
-        lax.all_to_all, axis_name=BOTH, split_axis=0, concat_axis=0, tiled=True, axis_index_groups=[order]
-    )
-    exchanged = exchange(packed)
+        lax.all_to_all, axis_name=BOTH, split_axis=0, concat_axis=0, tiled=True
+    )
+    exchanged = exchange(packed, axis_index_groups=[order])
 
     residual = run(
         residual_kernel,
@@ -328,7 +334,7 @@
         [whole(), whole(), whole(pl.ANY)],
         (pattern, exchanged, moved),
         flops=2 * count * tok * count * tok * wide,
-        scratch=[VMEM((tm_count - 1, group_tok, wide), kind), DMA((tm_count,))],
+        scratch=[VMEM((tm_count - 1, group_tok, wide), kind), DMA((tm_count, 2))],
     )
     returned = exchange(attended)
     handed = []

time: 42.8 us -> 42.9 us (level)
  transfers between devices with their start and end apart: 6 -> 6, of which waited for: 4 -> 3; matrix products, arithmetic and copies ran while one was open for 0% -> 0% of each run, Pallas kernels for 6% -> 6%
where the time goes in v13:
time: 42.9 us; the launch traced here: 42.5 us
  starting transfers between devices  19 us (44%)
  waiting for transfers between devices  15.1 us (35%)
  Pallas kernels  6.91 us (16%)
  between operations  1.38 us (3%)
    all_to_all x1, waiting for transfers between devices, spread_body(): exchanged = exchange(packed, axis_index_groups=[order])  12.2 us
    ppermute x3, starting transfers between devices, spread_body(): lax.ppermute(hand, 'tm', [(i, j) for i, j in route if j < tm_count - 1])  7.75 us
    all_to_all x1, starting transfers between devices, spread_body(): exchanged = exchange(packed, axis_index_groups=[order])  7.3 us
    pallas_call x6, Pallas kernels, run(): pl.pallas_call(kernel, out_shape=outs, in_specs=specs, out_specs=[whole(g...  6.91 us
    all_to_all x1, starting transfers between devices, spread_body(): returned = exchange(attended)  2.68 us
    ppermute x1, waiting for transfers between devices, shifted(): return lax.ppermute(block, axis, route)  2.13 us
    ppermute x1, starting transfers between devices, shifted(): return lax.ppermute(block, axis, route)  1.29 us
  transfers between devices with their start and end apart: 6, of which 3 were waited for; matrix products, arithmetic and copies ran while one was open for 0% of the time, Pallas kernels for 6%

profile of v13, /device:TPU:0, one launch (start us, length us, event | category | flops | bytes accessed | tf_op | source)
XLA Modules:
  0.0 42.5 jit_solution(17092995858287430904)
XLA Ops:
  0.6 2.0 %pack.1.after_ref = bf16[768,384]{1,0:T(8,128)(2,1)} custom-call(bf16[1,24,4096]{2,1,0:T(8,128)(2,1)} %q_hbm.1, bf16[1,24,4096]{2,1,0:T(8,128)(2,1)} %k_hbm.1, bf16[1,24,4096]{2,1,0:T(8,128)(2,1)} %v_hbm.1), custom_call_target="tpu_custom_call" | custom-call | bytes 1179648 | tf_op jit(solution)/shard_map/pack/pallas_call | solution.py:272
  2.6 0.0 copy-start
  2.6 7.3 %all-to-all-start = ((bf16[32,24,384]{2,1,0:T(8,128)(2,1)}), bf16[32,24,384]{2,1,0:T(8,128)(2,1)S(1)}, u32[]{:S(2)}, u32[]{:S(2)}) async-start(bf16[32,24,384]{2,1,0:T(8,128)(2,1)} %bitcast.7), calls=%async_computation | async-start | bytes 1179648 | tf_op jit(solution)/shard_map/all_to_all | solution.py:313
  10.6 0.0 copy-done
  10.6 0.0 copy-start.2
  10.6 1.0 %residual.1 = bf16[32,4096]{1,0:T(8,128)(2,1)S(1)} custom-call(s32[1]{0:T(128)S(6)} %copy.12.noise_ref, bf16[1,24,4096]{2,1,0:T(8,128)(2,1)S(1)} %copy-done, f32[50,4096]{1,0:T(8,128)} %gate_hbm.1, bf16[768,384]{1,0:T(8,128)(2,1)} %pack.1.after_ref), custom_call_target="tpu_custom_call" | custom-call | bytes 1867780 | tf_op jit(solution)/shard_map/residual/pallas_call | solution.py:272
  11.6 1.3 %collective-permute-start = (bf16[32,4096]{1,0:T(8,128)(2,1)S(1)}, bf16[32,4096]{1,0:T(8,128)(2,1)S(1)}, u32[]{:S(2)}, u32[]{:S(2)}) collective-permute-start(bf16[32,4096]{1,0:T(8,128)(2,1)S(1)} %residual.1), channel_id=1, source_target_pairs={{8,0},{16,8},{24,16},{9,1},{17,9},{25,17},{10,2},{18,10},{26,18},{... | collective-permute-start | bytes 786440 | tf_op jit(solution)/shard_map/ppermute | solution.py:21
  12.9 2.1 %collective-permute-done.after_ref.moved_ref = bf16[32,4096]{1,0:T(8,128)(2,1)S(1)} collective-permute-done((bf16[32,4096]{1,0:T(8,128)(2,1)S(1)}, bf16[32,4096]{1,0:T(8,128)(2,1)S(1)}, u32[]{:S(2)}, u32[]{:S(2)}) %collective-permute-start) | collective-permute-done | bytes 262176 | tf_op jit(solution)/shard_map/ppermute | solution.py:21
  15.1 12.2 %all-to-all-done = bf16[32,24,384]{2,1,0:T(8,128)(2,1)S(1)} async-done(((bf16[32,24,384]{2,1,0:T(8,128)(2,1)}), bf16[32,24,384]{2,1,0:T(8,128)(2,1)S(1)}, u32[]{:S(2)}, u32[]{:S(2)}) %all-to-all-start) | async-done | bytes 589856 | tf_op jit(solution)/shard_map/all_to_all | solution.py:313
  27.2 0.0 copy-done.2
  27.3 1.6 %attend.1 = (bf16[768,128]{1,0:T(8,128)(2,1)}, bf16[192,256]{1,0:T(8,128)(2,1)S(1)}, bf16[192,256]{1,0:T(8,128)(2,1)S(1)}, bf16[192,256]{1,0:T(8,128)(2,1)S(1)}) custom-call(s32[4,4]{1,0:T(4,128)S(1)} %copy-done.2, bf16[768,384]{1,0:T(8,128)(2,1)S(1)} %bitcast.4, bf16[32,4096]{1,0:T(8,128)(2,1)S(1)} %collective-permute-done.after_ref.moved_ref), custom_call_target="tpu_custom_call" | custom-call | flops 150994944 | bytes 1343552 | tf_op jit(solution)/shard_map/attend/pallas_call | solution.py:272
  28.9 2.7 %all-to-all-start.1 = ((bf16[32,24,128]{2,1,0:T(8,128)(2,1)}), bf16[32,24,128]{2,1,0:T(8,128)(2,1)S(1)}, u32[]{:S(2)}, u32[]{:S(2)}) async-start(bf16[32,24,128]{2,1,0:T(8,128)(2,1)} %bitcast.8), calls=%async_computation.1 | async-start | bytes 393216 | tf_op jit(solution)/shard_map/all_to_all | solution.py:339
  31.6 1.3 %collective-permute-start.1 = (bf16[192,256]{1,0:T(8,128)(2,1)S(1)}, bf16[192,256]{1,0:T(8,128)(2,1)S(1)}, u32[]{:S(2)}, u32[]{:S(2)}) collective-permute-start(bf16[192,256]{1,0:T(8,128)(2,1)S(1)} %get-tuple-element.7), channel_id=1, source_target_pairs={{8,16},{16,8},{24,0},{9,17},{17,9},{25,1},{10,18},{18,10},{26,2},{... | collective-permute-start | bytes 294920 | tf_op jit(solution)/shard_map/ppermute | solution.py:343
  32.9 4.4 %collective-permute-start.2 = (bf16[192,256]{1,0:T(8,128)(2,1)S(1)}, bf16[192,256]{1,0:T(8,128)(2,1)S(1)}, u32[]{:S(2)}, u32[]{:S(2)}) collective-permute-start(bf16[192,256]{1,0:T(8,128)(2,1)S(1)} %get-tuple-element.8), channel_id=1, source_target_pairs={{0,16},{16,0},{24,8},{1,17},{17,1},{25,9},{2,18},{18,2},{26,10},{3... | collective-permute-start | bytes 294920 | tf_op jit(solution)/shard_map/ppermute | solution.py:343
  37.3 0.0 copy-start.1
  37.3 2.1 %collective-permute-start.3 = (bf16[192,256]{1,0:T(8,128)(2,1)S(1)}, bf16[192,256]{1,0:T(8,128)(2,1)S(1)}, u32[]{:S(2)}, u32[]{:S(2)}) collective-permute-start(bf16[192,256]{1,0:T(8,128)(2,1)S(1)} %get-tuple-element.9), channel_id=1, source_target_pairs={{0,8},{8,0},{24,16},{1,9},{9,1},{25,17},{2,10},{10,2},{26,18},{3,1... | collective-permute-start | bytes 294920 | tf_op jit(solution)/shard_map/ppermute | solution.py:343
  39.4 0.0 collective-permute-done.1.hand_ref
  39.4 0.8 %cache.1.after_ref.begun_hbm = bf16[1,2,192,512]{3,2,1,0:T(8,128)(2,1)} custom-call(bf16[768,384]{1,0:T(8,128)(2,1)S(1)} %bitcast.5, bf16[192,256]{1,0:T(8,128)(2,1)S(1)} %collective-permute-done.1.hand_ref), custom_call_target="tpu_custom_call" | custom-call | bytes 1081344 | tf_op jit(solution)/shard_map/cache/pallas_call | solution.py:272
  40.2 0.0 all-to-all-done.1
  40.2 0.0 copy-done.1
  40.2 0.8 %update.1.after_ref = bf16[1,24,4096]{2,1,0:T(8,128)(2,1)} custom-call(bf16[768,128]{1,0:T(8,128)(2,1)S(1)} %bitcast.6, bf16[32,4096]{1,0:T(8,128)(2,1)S(1)} %collective-permute-done.after_ref.moved_ref, bf16[24,4096]{1,0:T(8,128)(2,1)S(1)} %copy-done.1, bf16[1,2,192,512]{3,2,1,0:T(8,128)(2,1)} %cache.1.after_ref.begun_hbm), custom_call_target="tpu_custom_call" | custom-call | bytes 1245184 | tf_op jit(solution)/shard_map/update/pallas_call | solution.py:272
  40.9 0.8 %collective-permute-done.2.refs_0_ = bf16[192,256]{1,0:T(8,128)(2,1)S(1)} collective-permute-done((bf16[192,256]{1,0:T(8,128)(2,1)S(1)}, bf16[192,256]{1,0:T(8,128)(2,1)S(1)}, u32[]{:S(2)}, u32[]{:S(2)}) %collective-permute-start.2) | collective-permute-done | bytes 98336 | tf_op jit(solution)/shard_map/ppermute | solution.py:343
  41.8 0.0 collective-permute-done.3.refs_1_
  41.8 0.7 %cache_rest.1 = bf16[1,2,192,512]{3,2,1,0:T(8,128)(2,1)} custom-call(bf16[1,2,192,512]{3,2,1,0:T(8,128)(2,1)} %cache.1.after_ref.begun_hbm, bf16[1,24,4096]{2,1,0:T(8,128)(2,1)} %update.1.after_ref, bf16[192,256]{1,0:T(8,128)(2,1)S(1)} %collective-permute-done.2.refs_0_, ...), custom_call_target="tpu_custom_call", output_to_operand_aliasing={{}: (0, {})} | custom-call | bytes 1179648 | tf_op jit(solution)/shard_map/cache_rest/pallas_call | solution.py:272
Async XLA Ops:
  2.6 8.0 %copy-start = (bf16[1,24,4096]{2,1,0:T(8,128)(2,1)S(1)}, bf16[1,24,4096]{2,1,0:T(8,128)(2,1)}, u32[]{:S(2)}) copy-start(bf16[1,24,4096]{2,1,0:T(8,128)(2,1)} %h_ref.1) | copy-start | bytes 589828
  2.6 24.6 %all-to-all-start = ((bf16[32,24,384]{2,1,0:T(8,128)(2,1)}), bf16[32,24,384]{2,1,0:T(8,128)(2,1)S(1)}, u32[]{:S(2)}, u32[]{:S(2)}) async-start(bf16[32,24,384]{2,1,0:T(8,128)(2,1)} %bitcast.7), calls=%async_computation | async-start | bytes 1179648 | tf_op jit(solution)/shard_map/all_to_all | solution.py:313
  10.6 16.7 %copy-start.2 = (s32[4,4]{1,0:T(4,128)S(1)}, s32[4,4]{1,0:T(4,128)}, u32[]{:S(2)}) copy-start(s32[4,4]{1,0:T(4,128)} %pattern_ref.1) | copy-start | bytes 196
  11.6 3.4 %collective-permute-start = (bf16[32,4096]{1,0:T(8,128)(2,1)S(1)}, bf16[32,4096]{1,0:T(8,128)(2,1)S(1)}, u32[]{:S(2)}, u32[]{:S(2)}) collective-permute-start(bf16[32,4096]{1,0:T(8,128)(2,1)S(1)} %residual.1), channel_id=1, source_target_pairs={{8,0},{16,8},{24,16},{9,1},{17,9},{25,17},{10,2},{18,10},{26,18},{... | collective-permute-start | bytes 786440 | tf_op jit(solution)/shard_map/ppermute | solution.py:21
  28.9 11.3 %all-to-all-start.1 = ((bf16[32,24,128]{2,1,0:T(8,128)(2,1)}), bf16[32,24,128]{2,1,0:T(8,128)(2,1)S(1)}, u32[]{:S(2)}, u32[]{:S(2)}) async-start(bf16[32,24,128]{2,1,0:T(8,128)(2,1)} %bitcast.8), calls=%async_computation.1 | async-start | bytes 393216 | tf_op jit(solution)/shard_map/all_to_all | solution.py:339
  31.6 7.8 %collective-permute-start.1 = (bf16[192,256]{1,0:T(8,128)(2,1)S(1)}, bf16[192,256]{1,0:T(8,128)(2,1)S(1)}, u32[]{:S(2)}, u32[]{:S(2)}) collective-permute-start(bf16[192,256]{1,0:T(8,128)(2,1)S(1)} %get-tuple-element.7), channel_id=1, source_target_pairs={{8,16},{16,8},{24,0},{9,17},{17,9},{25,1},{10,18},{18,10},{26,2},{... | collective-permute-start | bytes 294920 | tf_op jit(solution)/shard_map/ppermute | solution.py:343
  32.9 8.9 %collective-permute-start.2 = (bf16[192,256]{1,0:T(8,128)(2,1)S(1)}, bf16[192,256]{1,0:T(8,128)(2,1)S(1)}, u32[]{:S(2)}, u32[]{:S(2)}) collective-permute-start(bf16[192,256]{1,0:T(8,128)(2,1)S(1)} %get-tuple-element.8), channel_id=1, source_target_pairs={{0,16},{16,0},{24,8},{1,17},{17,1},{25,9},{2,18},{18,2},{26,10},{3... | collective-permute-start | bytes 294920 | tf_op jit(solution)/shard_map/ppermute | solution.py:343
  37.3 2.9 %copy-start.1 = (bf16[24,4096]{1,0:T(8,128)(2,1)S(1)}, bf16[24,4096]{1,0:T(8,128)(2,1)}, u32[]{:S(2)}) copy-start(bf16[24,4096]{1,0:T(8,128)(2,1)} %fresh_ref.1) | copy-start | bytes 589828
  37.3 4.5 %collective-permute-start.3 = (bf16[192,256]{1,0:T(8,128)(2,1)S(1)}, bf16[192,256]{1,0:T(8,128)(2,1)S(1)}, u32[]{:S(2)}, u32[]{:S(2)}) collective-permute-start(bf16[192,256]{1,0:T(8,128)(2,1)S(1)} %get-tuple-element.9), channel_id=1, source_target_pairs={{0,8},{8,0},{24,16},{1,9},{9,1},{25,17},{2,10},{10,2},{26,18},{3,1... | collective-permute-start | bytes 294920 | tf_op jit(solution)/shard_map/ppermute | solution.py:343

commit v14 on v12

--- a/solution.py
+++ b/solution.py
@@ -22,7 +22,17 @@
 
 
 def mixed(index, count):
-    return (index + count // 2) % count
+    return (index + 2) % count
+
+
+def runs(count):
+    found = []
+    for index in range(count):
+        if found and found[-1][1] + found[-1][2] == mixed(index, count):
+            found[-1][2] += 1
+        else:
+            found.append([index, mixed(index, count), 1])
+    return found
 
 
 def pack_kernel(seq_count, parts, q_hbm, k_hbm, v_hbm, out_hbm, held, block, in_sems, out_sems):
@@ -186,10 +196,12 @@
     source = partner(here, groups - distance if groups & (groups - 1) else distance, groups)
     lanes = pl.ds(pl.multiple_of(source * wide, wide), wide)
     tok = rows // seq_count
-    for half in range(2):
-        start = half * (rows // 2)
-        place = mixed(half * (seq_count // 2), seq_count) * tok
-        yield slice(start, start + rows // 2), lanes, slice(place, place + rows // 2)
+    for index, place, length in runs(seq_count):
+        yield (
+            slice(index * tok, (index + length) * tok),
+            lanes,
+            slice(place * tok, (place + length) * tok),
+        )
 
 
 def cache_kernel(seq_count, groups, x_ref, hand_ref, out_ref):
@@ -235,6 +247,7 @@
     tok = out_ref.shape[1]
     wide = att_ref.shape[1]
     count = att_ref.shape[0] // tok
+    ordered = sorted(range(seq_count), key=lambda index: mixed(index, seq_count))
     last = lax.axis_index("tm") == tm_count - 1
 
     @pl.when(last)
@@ -247,7 +260,7 @@
             rows = att_ref[2 * pair * tok : 2 * (pair + 1) * tok, :].astype(jnp.float32)
             for half in range(2):
                 source = 2 * pair + half
-                start = (mixed(source % seq_count, seq_count) * tm_count + source // seq_count) * wide
+                start = (ordered[source % seq_count] * tm_count + source // seq_count) * wide
                 moved = moved_ref[:, start : start + wide].astype(jnp.float32)
                 gate = (moved[tok : tok + 1] + moved[tok + 1 : tok + 2]) + moved[tok + 2 : tok + 3]
                 result = moved[:tok] + gate * rows[half * tok : (half + 1) * tok]
@@ -285,7 +298,7 @@
     group_tok = tok * seq_count
     kind = queries.dtype
     DMA = pltpu.SemaphoreType.DMA
-    parts = 4 if seq_count % 8 == 0 else 2
+    parts = seq_count // 2
 
     packed = run(
         functools.partial(pack_kernel, seq_count, parts),
@@ -300,7 +313,8 @@
             DMA((parts, tm_count)),
         ],
     )
-    order = [tm * seq_count + mixed(s, seq_count) for tm in range(tm_count) for s in range(seq_count)]
+    ordered = sorted(range(seq_count), key=lambda index: mixed(index, seq_count))
+    order = [tm * seq_count + index for tm in range(tm_count) for index in ordered]
     exchange = functools.partial(
         lax.all_to_all, axis_name=BOTH, split_axis=0, concat_axis=0, tiled=True, axis_index_groups=[order]
     )
@@ -358,7 +372,7 @@
         [HBM(begun.shape, kind)],
         [whole(HBM)] * 2 + [whole()] * len(rest),
         (begun, pltpu.with_memory_space_constraint(advanced, HBM), *rest),
-        scratch=[DMA((4 * len(rest),))],
+        scratch=[DMA((2 * len(runs(seq_count)) * len(rest),))],
         aliases={0: 0},
     )
     return (advanced, next_cache)
@@ -438,7 +452,7 @@
     tm_count, seq_count = lax.axis_size("tm"), lax.axis_size("seq")
     _, tok, width = queries.shape
     count = tm_count * seq_count
-    even = width % (count * HD) == 0 and tok % 8 == 0 and seq_count % 4 == 0 and tm_count > 2
+    even = width % (count * HD) == 0 and tok % 8 == 0 and seq_count % 2 == 0 and tm_count > 2
     return (spread_body if even else gather_body)(queries, *others)
 
 

time: 42.8 us -> 43.3 us (1.012)
  waiting for transfers between devices: 15.1 us -> 15.7 us
    ppermute x3, waiting for transfers between devices: 0.49 us -> 0.94 us  [spread_body(): lax.ppermute(hand, 'tm', [(i, j) for i, j in route if j < tm_count - 1])]
    all_to_all x1, waiting for transfers between devices: 12.2 us -> 12.6 us  [spread_body(): exchanged = exchange(packed)]
where the time goes in v14:
time: 43.3 us; the launch traced here: 42.8 us
  starting transfers between devices  18.8 us (43%)
  waiting for transfers between devices  15.7 us (36%)
  Pallas kernels  6.91 us (16%)
  between operations  1.38 us (3%)
    all_to_all x1, waiting for transfers between devices, spread_body(): exchanged = exchange(packed)  12.6 us
    ppermute x3, starting transfers between devices, spread_body(): lax.ppermute(hand, 'tm', [(i, j) for i, j in route if j < tm_count - 1])  7.61 us
    all_to_all x1, starting transfers between devices, spread_body(): exchanged = exchange(packed)  7.3 us
    pallas_call x6, Pallas kernels, run(): pl.pallas_call(kernel, out_shape=outs, in_specs=specs, out_specs=[whole(g...  6.91 us
    all_to_all x1, starting transfers between devices, spread_body(): returned = exchange(attended)  2.6 us
    ppermute x1, waiting for transfers between devices, shifted(): return lax.ppermute(block, axis, route)  2.13 us
    ppermute x1, starting transfers between devices, shifted(): return lax.ppermute(block, axis, route)  1.29 us
    ppermute x3, waiting for transfers between devices, spread_body(): lax.ppermute(hand, 'tm', [(i, j) for i, j in route if j < tm_count - 1])  0.94 us
  transfers between devices with their start and end apart: 6, of which 4 were waited for; matrix products, arithmetic and copies ran while one was open for 0% of the time, Pallas kernels for 6%

profile of v14, /device:TPU:0, one launch (start us, length us, event | category | flops | bytes accessed | tf_op | source)
XLA Modules:
  0.0 42.8 jit_solution(8021978697807923083)
XLA Ops:
  0.6 2.0 %pack.1.after_ref = bf16[768,384]{1,0:T(8,128)(2,1)} custom-call(bf16[1,24,4096]{2,1,0:T(8,128)(2,1)} %q_hbm.1, bf16[1,24,4096]{2,1,0:T(8,128)(2,1)} %k_hbm.1, bf16[1,24,4096]{2,1,0:T(8,128)(2,1)} %v_hbm.1), custom_call_target="tpu_custom_call" | custom-call | bytes 1179648 | tf_op jit(solution)/shard_map/pack/pallas_call | solution.py:279
  2.6 0.0 copy-start
  2.7 7.3 %all-to-all-start = ((bf16[32,24,384]{2,1,0:T(8,128)(2,1)}), bf16[32,24,384]{2,1,0:T(8,128)(2,1)S(1)}, u32[]{:S(2)}, u32[]{:S(2)}) async-start(bf16[32,24,384]{2,1,0:T(8,128)(2,1)} %bitcast.7), calls=%async_computation | async-start | bytes 1179648 | tf_op jit(solution)/shard_map/all_to_all | solution.py:321
  10.6 0.0 copy-done
  10.6 0.0 copy-start.2
  10.6 1.0 %residual.1 = bf16[32,4096]{1,0:T(8,128)(2,1)S(1)} custom-call(s32[1]{0:T(128)S(6)} %copy.12.noise_ref, bf16[1,24,4096]{2,1,0:T(8,128)(2,1)S(1)} %copy-done, f32[50,4096]{1,0:T(8,128)} %gate_hbm.1, bf16[768,384]{1,0:T(8,128)(2,1)} %pack.1.after_ref), custom_call_target="tpu_custom_call" | custom-call | bytes 1867780 | tf_op jit(solution)/shard_map/residual/pallas_call | solution.py:279
  11.7 1.3 %collective-permute-start = (bf16[32,4096]{1,0:T(8,128)(2,1)S(1)}, bf16[32,4096]{1,0:T(8,128)(2,1)S(1)}, u32[]{:S(2)}, u32[]{:S(2)}) collective-permute-start(bf16[32,4096]{1,0:T(8,128)(2,1)S(1)} %residual.1), channel_id=1, source_target_pairs={{8,0},{16,8},{24,16},{9,1},{17,9},{25,17},{10,2},{18,10},{26,18},{... | collective-permute-start | bytes 786440 | tf_op jit(solution)/shard_map/ppermute | solution.py:21
  13.0 2.1 %collective-permute-done.after_ref.moved_ref = bf16[32,4096]{1,0:T(8,128)(2,1)S(1)} collective-permute-done((bf16[32,4096]{1,0:T(8,128)(2,1)S(1)}, bf16[32,4096]{1,0:T(8,128)(2,1)S(1)}, u32[]{:S(2)}, u32[]{:S(2)}) %collective-permute-start) | collective-permute-done | bytes 262176 | tf_op jit(solution)/shard_map/ppermute | solution.py:21
  15.1 12.6 %all-to-all-done = bf16[32,24,384]{2,1,0:T(8,128)(2,1)S(1)} async-done(((bf16[32,24,384]{2,1,0:T(8,128)(2,1)}), bf16[32,24,384]{2,1,0:T(8,128)(2,1)S(1)}, u32[]{:S(2)}, u32[]{:S(2)}) %all-to-all-start) | async-done | bytes 589856 | tf_op jit(solution)/shard_map/all_to_all | solution.py:321
  27.7 0.0 copy-done.2
  27.7 1.6 %attend.1 = (bf16[768,128]{1,0:T(8,128)(2,1)}, bf16[192,256]{1,0:T(8,128)(2,1)S(1)}, bf16[192,256]{1,0:T(8,128)(2,1)S(1)}, bf16[192,256]{1,0:T(8,128)(2,1)S(1)}) custom-call(s32[4,4]{1,0:T(4,128)S(1)} %copy-done.2, bf16[768,384]{1,0:T(8,128)(2,1)S(1)} %bitcast.4, bf16[32,4096]{1,0:T(8,128)(2,1)S(1)} %collective-permute-done.after_ref.moved_ref), custom_call_target="tpu_custom_call" | custom-call | flops 150994944 | bytes 1343552 | tf_op jit(solution)/shard_map/attend/pallas_call | solution.py:279
  29.3 2.6 %all-to-all-start.1 = ((bf16[32,24,128]{2,1,0:T(8,128)(2,1)}), bf16[32,24,128]{2,1,0:T(8,128)(2,1)S(1)}, u32[]{:S(2)}, u32[]{:S(2)}) async-start(bf16[32,24,128]{2,1,0:T(8,128)(2,1)} %bitcast.8), calls=%async_computation.1 | async-start | bytes 393216 | tf_op jit(solution)/shard_map/all_to_all | solution.py:347
  31.9 1.3 %collective-permute-start.1 = (bf16[192,256]{1,0:T(8,128)(2,1)S(1)}, bf16[192,256]{1,0:T(8,128)(2,1)S(1)}, u32[]{:S(2)}, u32[]{:S(2)}) collective-permute-start(bf16[192,256]{1,0:T(8,128)(2,1)S(1)} %get-tuple-element.7), channel_id=1, source_target_pairs={{8,16},{16,8},{24,0},{9,17},{17,9},{25,1},{10,18},{18,10},{26,2},{... | collective-permute-start | bytes 294920 | tf_op jit(solution)/shard_map/ppermute | solution.py:351
  33.2 4.3 %collective-permute-start.2 = (bf16[192,256]{1,0:T(8,128)(2,1)S(1)}, bf16[192,256]{1,0:T(8,128)(2,1)S(1)}, u32[]{:S(2)}, u32[]{:S(2)}) collective-permute-start(bf16[192,256]{1,0:T(8,128)(2,1)S(1)} %get-tuple-element.8), channel_id=1, source_target_pairs={{0,16},{16,0},{24,8},{1,17},{17,1},{25,9},{2,18},{18,2},{26,10},{3... | collective-permute-start | bytes 294920 | tf_op jit(solution)/shard_map/ppermute | solution.py:351
  37.5 0.0 copy-start.1
  37.5 2.1 %collective-permute-start.3 = (bf16[192,256]{1,0:T(8,128)(2,1)S(1)}, bf16[192,256]{1,0:T(8,128)(2,1)S(1)}, u32[]{:S(2)}, u32[]{:S(2)}) collective-permute-start(bf16[192,256]{1,0:T(8,128)(2,1)S(1)} %get-tuple-element.9), channel_id=1, source_target_pairs={{0,8},{8,0},{24,16},{1,9},{9,1},{25,17},{2,10},{10,2},{26,18},{3,1... | collective-permute-start | bytes 294920 | tf_op jit(solution)/shard_map/ppermute | solution.py:351
  39.6 0.2 collective-permute-done.1.hand_ref
  39.8 0.8 %cache.1.after_ref.begun_hbm = bf16[1,2,192,512]{3,2,1,0:T(8,128)(2,1)} custom-call(bf16[768,384]{1,0:T(8,128)(2,1)S(1)} %bitcast.5, bf16[192,256]{1,0:T(8,128)(2,1)S(1)} %collective-permute-done.1.hand_ref), custom_call_target="tpu_custom_call" | custom-call | bytes 1081344 | tf_op jit(solution)/shard_map/cache/pallas_call | solution.py:279
  40.5 0.0 all-to-all-done.1
  40.6 0.0 copy-done.1
  40.6 0.8 %update.1.after_ref = bf16[1,24,4096]{2,1,0:T(8,128)(2,1)} custom-call(bf16[768,128]{1,0:T(8,128)(2,1)S(1)} %bitcast.6, bf16[32,4096]{1,0:T(8,128)(2,1)S(1)} %collective-permute-done.after_ref.moved_ref, bf16[24,4096]{1,0:T(8,128)(2,1)S(1)} %copy-done.1, bf16[1,2,192,512]{3,2,1,0:T(8,128)(2,1)} %cache.1.after_ref.begun_hbm), custom_call_target="tpu_custom_call" | custom-call | bytes 1245184 | tf_op jit(solution)/shard_map/update/pallas_call | solution.py:279
  41.3 0.8 %collective-permute-done.2.refs_0_ = bf16[192,256]{1,0:T(8,128)(2,1)S(1)} collective-permute-done((bf16[192,256]{1,0:T(8,128)(2,1)S(1)}, bf16[192,256]{1,0:T(8,128)(2,1)S(1)}, u32[]{:S(2)}, u32[]{:S(2)}) %collective-permute-start.2) | collective-permute-done | bytes 98336 | tf_op jit(solution)/shard_map/ppermute | solution.py:351
  42.1 0.0 collective-permute-done.3.refs_1_
  42.1 0.7 %cache_rest.1 = bf16[1,2,192,512]{3,2,1,0:T(8,128)(2,1)} custom-call(bf16[1,2,192,512]{3,2,1,0:T(8,128)(2,1)} %cache.1.after_ref.begun_hbm, bf16[1,24,4096]{2,1,0:T(8,128)(2,1)} %update.1.after_ref, bf16[192,256]{1,0:T(8,128)(2,1)S(1)} %collective-permute-done.2.refs_0_, ...), custom_call_target="tpu_custom_call", output_to_operand_aliasing={{}: (0, {})} | custom-call | bytes 1179648 | tf_op jit(solution)/shard_map/cache_rest/pallas_call | solution.py:279
Async XLA Ops:
  2.6 8.0 %copy-start = (bf16[1,24,4096]{2,1,0:T(8,128)(2,1)S(1)}, bf16[1,24,4096]{2,1,0:T(8,128)(2,1)}, u32[]{:S(2)}) copy-start(bf16[1,24,4096]{2,1,0:T(8,128)(2,1)} %h_ref.1) | copy-start | bytes 589828
  2.7 25.1 %all-to-all-start = ((bf16[32,24,384]{2,1,0:T(8,128)(2,1)}), bf16[32,24,384]{2,1,0:T(8,128)(2,1)S(1)}, u32[]{:S(2)}, u32[]{:S(2)}) async-start(bf16[32,24,384]{2,1,0:T(8,128)(2,1)} %bitcast.7), calls=%async_computation | async-start | bytes 1179648 | tf_op jit(solution)/shard_map/all_to_all | solution.py:321
  10.6 17.1 %copy-start.2 = (s32[4,4]{1,0:T(4,128)S(1)}, s32[4,4]{1,0:T(4,128)}, u32[]{:S(2)}) copy-start(s32[4,4]{1,0:T(4,128)} %pattern_ref.1) | copy-start | bytes 196
  11.7 3.4 %collective-permute-start = (bf16[32,4096]{1,0:T(8,128)(2,1)S(1)}, bf16[32,4096]{1,0:T(8,128)(2,1)S(1)}, u32[]{:S(2)}, u32[]{:S(2)}) collective-permute-start(bf16[32,4096]{1,0:T(8,128)(2,1)S(1)} %residual.1), channel_id=1, source_target_pairs={{8,0},{16,8},{24,16},{9,1},{17,9},{25,17},{10,2},{18,10},{26,18},{... | collective-permute-start | bytes 786440 | tf_op jit(solution)/shard_map/ppermute | solution.py:21
  29.3 11.2 %all-to-all-start.1 = ((bf16[32,24,128]{2,1,0:T(8,128)(2,1)}), bf16[32,24,128]{2,1,0:T(8,128)(2,1)S(1)}, u32[]{:S(2)}, u32[]{:S(2)}) async-start(bf16[32,24,128]{2,1,0:T(8,128)(2,1)} %bitcast.8), calls=%async_computation.1 | async-start | bytes 393216 | tf_op jit(solution)/shard_map/all_to_all | solution.py:347
  31.9 7.8 %collective-permute-start.1 = (bf16[192,256]{1,0:T(8,128)(2,1)S(1)}, bf16[192,256]{1,0:T(8,128)(2,1)S(1)}, u32[]{:S(2)}, u32[]{:S(2)}) collective-permute-start(bf16[192,256]{1,0:T(8,128)(2,1)S(1)} %get-tuple-element.7), channel_id=1, source_target_pairs={{8,16},{16,8},{24,0},{9,17},{17,9},{25,1},{10,18},{18,10},{26,2},{... | collective-permute-start | bytes 294920 | tf_op jit(solution)/shard_map/ppermute | solution.py:351
  33.2 8.9 %collective-permute-start.2 = (bf16[192,256]{1,0:T(8,128)(2,1)S(1)}, bf16[192,256]{1,0:T(8,128)(2,1)S(1)}, u32[]{:S(2)}, u32[]{:S(2)}) collective-permute-start(bf16[192,256]{1,0:T(8,128)(2,1)S(1)} %get-tuple-element.8), channel_id=1, source_target_pairs={{0,16},{16,0},{24,8},{1,17},{17,1},{25,9},{2,18},{18,2},{26,10},{3... | collective-permute-start | bytes 294920 | tf_op jit(solution)/shard_map/ppermute | solution.py:351
  37.5 3.0 %copy-start.1 = (bf16[24,4096]{1,0:T(8,128)(2,1)S(1)}, bf16[24,4096]{1,0:T(8,128)(2,1)}, u32[]{:S(2)}) copy-start(bf16[24,4096]{1,0:T(8,128)(2,1)} %fresh_ref.1) | copy-start | bytes 589828
  37.5 4.6 %collective-permute-start.3 = (bf16[192,256]{1,0:T(8,128)(2,1)S(1)}, bf16[192,256]{1,0:T(8,128)(2,1)S(1)}, u32[]{:S(2)}, u32[]{:S(2)}) collective-permute-start(bf16[192,256]{1,0:T(8,128)(2,1)S(1)} %get-tuple-element.9), channel_id=1, source_target_pairs={{0,8},{8,0},{24,16},{1,9},{9,1},{25,17},{2,10},{10,2},{26,18},{3,1... | collective-permute-start | bytes 294920 | tf_op jit(solution)/shard_map/ppermute | solution.py:351

commit v15 on v12

--- a/solution.py
+++ b/solution.py
@@ -105,6 +105,18 @@
     return range(groups - 1, 0, -1)
 
 
+def hand_over(group, x_ref, out_ref, lanes=slice(None)):
+    wide = x_ref.shape[1] // 3
+    rows = out_ref.shape[1]
+    half = rows // 2
+    for part in range(2):
+        first = pl.multiple_of(group * rows + mixed(part, 2) * half, half)
+        for kind in range(2):
+            out_ref[kind, part * half : (part + 1) * half, lanes] = x_ref[
+                pl.ds(first, half), (kind + 1) * wide : (kind + 2) * wide
+            ]
+
+
 def attend_kernel(groups, pattern_ref, x_ref, after_ref, out_hbm, *refs):
     *hand_refs, held, sems = refs
     wide = held.shape[2]
@@ -124,6 +136,17 @@
             chosen = jnp.where((lane >= start) & (lane < start + rows), flag, chosen)
         kept.append(chosen[:, : ends[-1]] > 0)
 
+    copies = []
+
+    def send(group):
+        for place in (group - 1, groups - 1) if group == groups - 1 else (group - 1,):
+            copies.append(
+                pltpu.make_async_copy(
+                    held.at[group - 1], out_hbm.at[place * rows : (place + 1) * rows], sems.at[place]
+                )
+            )
+            copies[-1].start()
+
     def spread(row, fill):
         rest = across - row.shape[1]
         return jnp.concatenate([row, jnp.full((1, rest), fill, row.dtype)], axis=1) if rest else row
@@ -152,7 +175,8 @@
             total += spread(jnp.sum(raised, axis=0, keepdims=True), 0.0)
             probs.append(raised.astype(jnp.bfloat16))
         inverse = 1.0 / total
-        start, pieces = 0, []
+        last = head + HD == wide
+        start, left, waiting = 0, None, groups - 1
         for source in range(groups - 1, 0, -1):
             stop = ends[source]
             if stop > start:
@@ -161,72 +185,51 @@
                     jnp.concatenate([p[:, start:stop] for p in probs[: source + 1]], axis=0),
                     preferred_element_type=jnp.float32,
                 )
-                pieces.append(numer * inverse[:, start:stop])
+                result = jnp.transpose(numer * inverse[:, start:stop])
+                left = result if left is None else jnp.concatenate([left, result], axis=0)
                 start = stop
-        result = jnp.transpose(jnp.concatenate(pieces, axis=1)).astype(jnp.bfloat16)
-        for group in range(1, groups):
-            start = (groups - 1 - group) * rows
-            held[group - 1, :, head : head + HD] = result[start : start + rows]
-    copies = [
-        pltpu.make_async_copy(
-            held.at[min(place, groups - 2)], out_hbm.at[place * rows : (place + 1) * rows], sems.at[place]
-        )
-        for place in range(groups)
-    ]
-    for copy in copies:
-        copy.start()
+            while left is not None and left.shape[0] >= rows:
+                held[waiting - 1, :, head : head + HD] = left[:rows].astype(jnp.bfloat16)
+                left = left[rows:] if left.shape[0] > rows else None
+                if last:
+                    send(waiting)
+                waiting -= 1
     for distance, hand_ref in zip(distances(groups), hand_refs):
-        group = lax.rem(partner(here, distance, groups) + 1, groups)
-        hand_ref[...] = x_ref[pl.ds(pl.multiple_of(group * rows, rows), rows), wide:]
+        hand_over(lax.rem(partner(here, distance, groups) + 1, groups), x_ref, hand_ref)
     for copy in copies:
         copy.wait()
 
 
-def cache_places(seq_count, groups, rows, wide, distance, here):
+def lanes_of(distance, groups, here, wide):
     source = partner(here, groups - distance if groups & (groups - 1) else distance, groups)
-    lanes = pl.ds(pl.multiple_of(source * wide, wide), wide)
-    tok = rows // seq_count
-    for half in range(2):
-        start = half * (rows // 2)
-        place = mixed(half * (seq_count // 2), seq_count) * tok
-        yield slice(start, start + rows // 2), lanes, slice(place, place + rows // 2)
-
-
-def cache_kernel(seq_count, groups, x_ref, hand_ref, out_ref):
+    return pl.ds(pl.multiple_of(source * wide, wide), wide)
+
+
+def cache_kernel(groups, x_ref, hand_ref, out_ref):
     wide = x_ref.shape[1] // 3
-    rows = out_ref.shape[2]
     here = lax.axis_index("tm")
     out_ref[...] = jnp.zeros_like(out_ref)
 
     @pl.when(here < groups - 1)
     def place():
-        own = x_ref[pl.ds(pl.multiple_of((here + 1) * rows, rows), rows), wide:]
-        for distance, block in ((0, own), (distances(groups)[0], hand_ref)):
-            for to, lanes, at in cache_places(seq_count, groups, rows, wide, distance, here):
-                for kind in range(2):
-                    out_ref[0, kind, to, lanes] = block[at, kind * wide : (kind + 1) * wide]
-
-
-def cache_rest_kernel(seq_count, groups, begun_hbm, after_ref, *refs):
+        hand_over(here + 1, x_ref, out_ref.at[0], lanes_of(0, groups, here, wide))
+        out_ref[0, :, :, lanes_of(distances(groups)[0], groups, here, wide)] = hand_ref[...]
+
+
+def cache_rest_kernel(groups, begun_hbm, after_ref, *refs):
     *hand_refs, out_hbm, sems = refs
-    wide = hand_refs[0].shape[1] // 2
-    rows = out_hbm.shape[2]
     here = lax.axis_index("tm")
 
     @pl.when(here < groups - 1)
     def place():
-        copies = []
-        for distance, block in zip(distances(groups)[1:], hand_refs):
-            for to, lanes, at in cache_places(seq_count, groups, rows, wide, distance, here):
-                for kind in range(2):
-                    copies.append(
-                        pltpu.make_async_copy(
-                            block.at[at, kind * wide : (kind + 1) * wide],
-                            out_hbm.at[0, kind, to, lanes],
-                            sems.at[len(copies)],
-                        )
-                    )
-                    copies[-1].start()
+        copies = [
+            pltpu.make_async_copy(
+                block, out_hbm.at[0, :, :, lanes_of(distance, groups, here, block.shape[2])], sems.at[index]
+            )
+            for index, (distance, block) in enumerate(zip(distances(groups)[1:], hand_refs))
+        ]
+        for copy in copies:
+            copy.start()
         for copy in copies:
             copy.wait()
 
@@ -324,7 +327,7 @@
     attended, *hands = run(
         functools.partial(attend_kernel, tm_count),
         "attend",
-        [HBM((count * tok, wide), kind)] + [VMEM((group_tok, 2 * wide), kind)] * (tm_count - 1),
+        [HBM((count * tok, wide), kind)] + [VMEM((2, group_tok, wide), kind)] * (tm_count - 1),
         [whole(), whole(), whole(pl.ANY)],
         (pattern, exchanged, moved),
         flops=2 * count * tok * count * tok * wide,
@@ -338,7 +341,7 @@
 
     first, *rest = handed
     begun = run(
-        functools.partial(cache_kernel, seq_count, tm_count),
+        functools.partial(cache_kernel, tm_count),
         "cache",
         [jax.ShapeDtypeStruct((1, 2, group_tok, tm_count * wide), kind)],
         [whole()] * 2,
@@ -353,12 +356,12 @@
         (returned, moved, fresh_latent, begun),
     )
     next_cache = run(
-        functools.partial(cache_rest_kernel, seq_count, tm_count),
+        functools.partial(cache_rest_kernel, tm_count),
         "cache_rest",
         [HBM(begun.shape, kind)],
         [whole(HBM)] * 2 + [whole()] * len(rest),
         (begun, pltpu.with_memory_space_constraint(advanced, HBM), *rest),
-        scratch=[DMA((4 * len(rest),))],
+        scratch=[DMA((len(rest),))],
         aliases={0: 0},
     )
     return (advanced, next_cache)

time: 42.8 us -> 42.7 us (level)
  no operation moved by 1% of the time
where the time goes in v15:
time: 42.7 us; the launch traced here: 42.3 us
  starting transfers between devices  19 us (44%)
  waiting for transfers between devices  15.1 us (35%)
  Pallas kernels  6.81 us (16%)
  between operations  1.38 us (3%)
    all_to_all x1, waiting for transfers between devices, spread_body(): exchanged = exchange(packed)  12.2 us
    ppermute x3, starting transfers between devices, spread_body(): lax.ppermute(hand, 'tm', [(i, j) for i, j in route if j < tm_count - 1])  7.75 us
    all_to_all x1, starting transfers between devices, spread_body(): exchanged = exchange(packed)  7.3 us
    pallas_call x6, Pallas kernels, run(): pl.pallas_call(kernel, out_shape=outs, in_specs=specs, out_specs=[whole(g...  6.81 us
    all_to_all x1, starting transfers between devices, spread_body(): returned = exchange(attended)  2.68 us
    ppermute x1, waiting for transfers between devices, shifted(): return lax.ppermute(block, axis, route)  2.13 us
    ppermute x1, starting transfers between devices, shifted(): return lax.ppermute(block, axis, route)  1.29 us
  transfers between devices with their start and end apart: 6, of which 4 were waited for; matrix products, arithmetic and copies ran while one was open for 0% of the time, Pallas kernels for 6%

profile of v15, /device:TPU:0, one launch (start us, length us, event | category | flops | bytes accessed | tf_op | source)
XLA Modules:
  0.0 42.3 jit_solution(15848139652274408436)
XLA Ops:
  0.6 2.0 %pack.1.after_ref = bf16[768,384]{1,0:T(8,128)(2,1)} custom-call(bf16[1,24,4096]{2,1,0:T(8,128)(2,1)} %q_hbm.1, bf16[1,24,4096]{2,1,0:T(8,128)(2,1)} %k_hbm.1, bf16[1,24,4096]{2,1,0:T(8,128)(2,1)} %v_hbm.1), custom_call_target="tpu_custom_call" | custom-call | bytes 1179648 | tf_op jit(solution)/shard_map/pack/pallas_call | solution.py:269
  2.6 0.0 copy-start
  2.6 7.3 %all-to-all-start = ((bf16[32,24,384]{2,1,0:T(8,128)(2,1)}), bf16[32,24,384]{2,1,0:T(8,128)(2,1)S(1)}, u32[]{:S(2)}, u32[]{:S(2)}) async-start(bf16[32,24,384]{2,1,0:T(8,128)(2,1)} %bitcast.7), calls=%async_computation | async-start | bytes 1179648 | tf_op jit(solution)/shard_map/all_to_all | solution.py:310
  10.6 0.0 copy-done
  10.6 0.0 copy-start.2
  10.6 1.0 %residual.1 = bf16[32,4096]{1,0:T(8,128)(2,1)S(1)} custom-call(s32[1]{0:T(128)S(6)} %copy.12.noise_ref, bf16[1,24,4096]{2,1,0:T(8,128)(2,1)S(1)} %copy-done, f32[50,4096]{1,0:T(8,128)} %gate_hbm.1, bf16[768,384]{1,0:T(8,128)(2,1)} %pack.1.after_ref), custom_call_target="tpu_custom_call" | custom-call | bytes 1867780 | tf_op jit(solution)/shard_map/residual/pallas_call | solution.py:269
  11.6 1.3 %collective-permute-start = (bf16[32,4096]{1,0:T(8,128)(2,1)S(1)}, bf16[32,4096]{1,0:T(8,128)(2,1)S(1)}, u32[]{:S(2)}, u32[]{:S(2)}) collective-permute-start(bf16[32,4096]{1,0:T(8,128)(2,1)S(1)} %residual.1), channel_id=1, source_target_pairs={{8,0},{16,8},{24,16},{9,1},{17,9},{25,17},{10,2},{18,10},{26,18},{... | collective-permute-start | bytes 786440 | tf_op jit(solution)/shard_map/ppermute | solution.py:21
  12.9 2.1 %collective-permute-done.after_ref.moved_ref = bf16[32,4096]{1,0:T(8,128)(2,1)S(1)} collective-permute-done((bf16[32,4096]{1,0:T(8,128)(2,1)S(1)}, bf16[32,4096]{1,0:T(8,128)(2,1)S(1)}, u32[]{:S(2)}, u32[]{:S(2)}) %collective-permute-start) | collective-permute-done | bytes 262176 | tf_op jit(solution)/shard_map/ppermute | solution.py:21
  15.1 12.2 %all-to-all-done = bf16[32,24,384]{2,1,0:T(8,128)(2,1)S(1)} async-done(((bf16[32,24,384]{2,1,0:T(8,128)(2,1)}), bf16[32,24,384]{2,1,0:T(8,128)(2,1)S(1)}, u32[]{:S(2)}, u32[]{:S(2)}) %all-to-all-start) | async-done | bytes 589856 | tf_op jit(solution)/shard_map/all_to_all | solution.py:310
  27.2 0.0 copy-done.2
  27.3 1.6 %attend.1 = (bf16[768,128]{1,0:T(8,128)(2,1)}, bf16[2,192,128]{2,1,0:T(8,128)(2,1)S(1)}, bf16[2,192,128]{2,1,0:T(8,128)(2,1)S(1)}, bf16[2,192,128]{2,1,0:T(8,128)(2,1)S(1)}) custom-call(s32[4,4]{1,0:T(4,128)S(1)} %copy-done.2, bf16[768,384]{1,0:T(8,128)(2,1)S(1)} %bitcast.4, bf16[32,4096]{1,0:T(8,128)(2,1)S(1)} %collective-permute-done.after_ref.moved_ref), custom_call_target="tpu_custom_call" | custom-call | flops 150994944 | bytes 1343552 | tf_op jit(solution)/shard_map/attend/pallas_call | solution.py:269
  28.8 2.7 %all-to-all-start.1 = ((bf16[32,24,128]{2,1,0:T(8,128)(2,1)}), bf16[32,24,128]{2,1,0:T(8,128)(2,1)S(1)}, u32[]{:S(2)}, u32[]{:S(2)}) async-start(bf16[32,24,128]{2,1,0:T(8,128)(2,1)} %bitcast.8), calls=%async_computation.1 | async-start | bytes 393216 | tf_op jit(solution)/shard_map/all_to_all | solution.py:336
  31.5 1.3 %collective-permute-start.1 = (bf16[2,192,128]{2,1,0:T(8,128)(2,1)S(1)}, bf16[2,192,128]{2,1,0:T(8,128)(2,1)S(1)}, u32[]{:S(2)}, u32[]{:S(2)}) collective-permute-start(bf16[2,192,128]{2,1,0:T(8,128)(2,1)S(1)} %get-tuple-element.7), channel_id=1, source_target_pairs={{8,16},{16,8},{24,0},{9,17},{17,9},{25,1},{10,18},{18,10},{26,2},{... | collective-permute-start | bytes 294920 | tf_op jit(solution)/shard_map/ppermute | solution.py:340
  32.8 4.4 %collective-permute-start.2 = (bf16[2,192,128]{2,1,0:T(8,128)(2,1)S(1)}, bf16[2,192,128]{2,1,0:T(8,128)(2,1)S(1)}, u32[]{:S(2)}, u32[]{:S(2)}) collective-permute-start(bf16[2,192,128]{2,1,0:T(8,128)(2,1)S(1)} %get-tuple-element.8), channel_id=1, source_target_pairs={{0,16},{16,0},{24,8},{1,17},{17,1},{25,9},{2,18},{18,2},{26,10},{3... | collective-permute-start | bytes 294920 | tf_op jit(solution)/shard_map/ppermute | solution.py:340
  37.2 0.0 copy-start.1
  37.2 2.1 %collective-permute-start.3 = (bf16[2,192,128]{2,1,0:T(8,128)(2,1)S(1)}, bf16[2,192,128]{2,1,0:T(8,128)(2,1)S(1)}, u32[]{:S(2)}, u32[]{:S(2)}) collective-permute-start(bf16[2,192,128]{2,1,0:T(8,128)(2,1)S(1)} %get-tuple-element.9), channel_id=1, source_target_pairs={{0,8},{8,0},{24,16},{1,9},{9,1},{25,17},{2,10},{10,2},{26,18},{3,1... | collective-permute-start | bytes 294920 | tf_op jit(solution)/shard_map/ppermute | solution.py:340
  39.3 0.0 collective-permute-done.1.hand_ref
  39.3 0.8 %cache.1.after_ref.begun_hbm = bf16[1,2,192,512]{3,2,1,0:T(8,128)(2,1)} custom-call(bf16[768,384]{1,0:T(8,128)(2,1)S(1)} %bitcast.5, bf16[2,192,128]{2,1,0:T(8,128)(2,1)S(1)} %collective-permute-done.1.hand_ref), custom_call_target="tpu_custom_call" | custom-call | bytes 1081344 | tf_op jit(solution)/shard_map/cache/pallas_call | solution.py:269
  40.1 0.3 all-to-all-done.1
  40.4 0.0 copy-done.1
  40.4 0.8 %update.1.after_ref = bf16[1,24,4096]{2,1,0:T(8,128)(2,1)} custom-call(bf16[768,128]{1,0:T(8,128)(2,1)S(1)} %bitcast.6, bf16[32,4096]{1,0:T(8,128)(2,1)S(1)} %collective-permute-done.after_ref.moved_ref, bf16[24,4096]{1,0:T(8,128)(2,1)S(1)} %copy-done.1, bf16[1,2,192,512]{3,2,1,0:T(8,128)(2,1)} %cache.1.after_ref.begun_hbm), custom_call_target="tpu_custom_call" | custom-call | bytes 1245184 | tf_op jit(solution)/shard_map/update/pallas_call | solution.py:269
  41.2 0.4 %collective-permute-done.2.refs_0_ = bf16[2,192,128]{2,1,0:T(8,128)(2,1)S(1)} collective-permute-done((bf16[2,192,128]{2,1,0:T(8,128)(2,1)S(1)}, bf16[2,192,128]{2,1,0:T(8,128)(2,1)S(1)}, u32[]{:S(2)}, u32[]{:S(2)}) %collective-permute-start.2) | collective-permute-done | bytes 98336 | tf_op jit(solution)/shard_map/ppermute | solution.py:340
  41.6 0.0 collective-permute-done.3.refs_1_
  41.6 0.7 %cache_rest.1 = bf16[1,2,192,512]{3,2,1,0:T(8,128)(2,1)} custom-call(bf16[1,2,192,512]{3,2,1,0:T(8,128)(2,1)} %cache.1.after_ref.begun_hbm, bf16[1,24,4096]{2,1,0:T(8,128)(2,1)} %update.1.after_ref, bf16[2,192,128]{2,1,0:T(8,128)(2,1)S(1)} %collective-permute-done.2.refs_0_, ...), custom_call_target="tpu_custom_call", output_to_operand_aliasing={{}: (0, {})} | custom-call | bytes 1179648 | tf_op jit(solution)/shard_map/cache_rest/pallas_call | solution.py:269
Async XLA Ops:
  2.6 8.0 %copy-start = (bf16[1,24,4096]{2,1,0:T(8,128)(2,1)S(1)}, bf16[1,24,4096]{2,1,0:T(8,128)(2,1)}, u32[]{:S(2)}) copy-start(bf16[1,24,4096]{2,1,0:T(8,128)(2,1)} %h_ref.1) | copy-start | bytes 589828
  2.6 24.6 %all-to-all-start = ((bf16[32,24,384]{2,1,0:T(8,128)(2,1)}), bf16[32,24,384]{2,1,0:T(8,128)(2,1)S(1)}, u32[]{:S(2)}, u32[]{:S(2)}) async-start(bf16[32,24,384]{2,1,0:T(8,128)(2,1)} %bitcast.7), calls=%async_computation | async-start | bytes 1179648 | tf_op jit(solution)/shard_map/all_to_all | solution.py:310
  10.6 16.7 %copy-start.2 = (s32[4,4]{1,0:T(4,128)S(1)}, s32[4,4]{1,0:T(4,128)}, u32[]{:S(2)}) copy-start(s32[4,4]{1,0:T(4,128)} %pattern_ref.1) | copy-start | bytes 196
  11.6 3.4 %collective-permute-start = (bf16[32,4096]{1,0:T(8,128)(2,1)S(1)}, bf16[32,4096]{1,0:T(8,128)(2,1)S(1)}, u32[]{:S(2)}, u32[]{:S(2)}) collective-permute-start(bf16[32,4096]{1,0:T(8,128)(2,1)S(1)} %residual.1), channel_id=1, source_target_pairs={{8,0},{16,8},{24,16},{9,1},{17,9},{25,17},{10,2},{18,10},{26,18},{... | collective-permute-start | bytes 786440 | tf_op jit(solution)/shard_map/ppermute | solution.py:21
  28.8 11.6 %all-to-all-start.1 = ((bf16[32,24,128]{2,1,0:T(8,128)(2,1)}), bf16[32,24,128]{2,1,0:T(8,128)(2,1)S(1)}, u32[]{:S(2)}, u32[]{:S(2)}) async-start(bf16[32,24,128]{2,1,0:T(8,128)(2,1)} %bitcast.8), calls=%async_computation.1 | async-start | bytes 393216 | tf_op jit(solution)/shard_map/all_to_all | solution.py:336
  31.5 7.8 %collective-permute-start.1 = (bf16[2,192,128]{2,1,0:T(8,128)(2,1)S(1)}, bf16[2,192,128]{2,1,0:T(8,128)(2,1)S(1)}, u32[]{:S(2)}, u32[]{:S(2)}) collective-permute-start(bf16[2,192,128]{2,1,0:T(8,128)(2,1)S(1)} %get-tuple-element.7), channel_id=1, source_target_pairs={{8,16},{16,8},{24,0},{9,17},{17,9},{25,1},{10,18},{18,10},{26,2},{... | collective-permute-start | bytes 294920 | tf_op jit(solution)/shard_map/ppermute | solution.py:340
  32.8 8.8 %collective-permute-start.2 = (bf16[2,192,128]{2,1,0:T(8,128)(2,1)S(1)}, bf16[2,192,128]{2,1,0:T(8,128)(2,1)S(1)}, u32[]{:S(2)}, u32[]{:S(2)}) collective-permute-start(bf16[2,192,128]{2,1,0:T(8,128)(2,1)S(1)} %get-tuple-element.8), channel_id=1, source_target_pairs={{0,16},{16,0},{24,8},{1,17},{17,1},{25,9},{2,18},{18,2},{26,10},{3... | collective-permute-start | bytes 294920 | tf_op jit(solution)/shard_map/ppermute | solution.py:340
  37.2 3.2 %copy-start.1 = (bf16[24,4096]{1,0:T(8,128)(2,1)S(1)}, bf16[24,4096]{1,0:T(8,128)(2,1)}, u32[]{:S(2)}) copy-start(bf16[24,4096]{1,0:T(8,128)(2,1)} %fresh_ref.1) | copy-start | bytes 589828
  37.2 4.4 %collective-permute-start.3 = (bf16[2,192,128]{2,1,0:T(8,128)(2,1)S(1)}, bf16[2,192,128]{2,1,0:T(8,128)(2,1)S(1)}, u32[]{:S(2)}, u32[]{:S(2)}) collective-permute-start(bf16[2,192,128]{2,1,0:T(8,128)(2,1)S(1)} %get-tuple-element.9), channel_id=1, source_target_pairs={{0,8},{8,0},{24,16},{1,9},{9,1},{25,17},{2,10},{10,2},{26,18},{3,1... | collective-permute-start | bytes 294920 | tf_op jit(solution)/shard_map/ppermute | solution.py:340

commit v16 on v15

--- a/solution.py
+++ b/solution.py
@@ -23,6 +23,18 @@
 
 def mixed(index, count):
     return (index + count // 2) % count
+
+
+def back_order(tm_count, seq_count):
+    ordered = sorted(range(seq_count), key=lambda index: mixed(index, seq_count))
+    half = tm_count // 2
+    return [
+        (high * half + low, ordered[pair + member])
+        for low in range(half)
+        for pair in range(0, seq_count, 2)
+        for high in range(tm_count // half)
+        for member in range(2)
+    ]
 
 
 def pack_kernel(seq_count, parts, q_hbm, k_hbm, v_hbm, out_hbm, held, block, in_sems, out_sems):
@@ -117,10 +129,10 @@
             ]
 
 
-def attend_kernel(groups, pattern_ref, x_ref, after_ref, out_hbm, *refs):
+def attend_kernel(groups, seq_count, pattern_ref, x_ref, after_ref, out_hbm, *refs):
     *hand_refs, held, sems = refs
-    wide = held.shape[2]
-    rows = held.shape[1]
+    wide = held.shape[1]
+    rows = held.shape[0] // groups
     across = (groups - 1) * rows
     factor = math.log2(math.e) / math.sqrt(HD)
     here = lax.axis_index("tm")
@@ -136,16 +148,16 @@
             chosen = jnp.where((lane >= start) & (lane < start + rows), flag, chosen)
         kept.append(chosen[:, : ends[-1]] > 0)
 
-    copies = []
-
-    def send(group):
+    halves = groups // (groups // 2)
+    pairs = seq_count // 2
+    step = rows // pairs
+
+    def keep(group, head, result):
         for place in (group - 1, groups - 1) if group == groups - 1 else (group - 1,):
-            copies.append(
-                pltpu.make_async_copy(
-                    held.at[group - 1], out_hbm.at[place * rows : (place + 1) * rows], sems.at[place]
-                )
-            )
-            copies[-1].start()
+            low, high = place % (groups // 2), place // (groups // 2)
+            for pair in range(pairs):
+                to = ((low * pairs + pair) * halves + high) * step
+                held[to : to + step, head : head + HD] = result[pair * step : (pair + 1) * step]
 
     def spread(row, fill):
         rest = across - row.shape[1]
@@ -175,7 +187,6 @@
             total += spread(jnp.sum(raised, axis=0, keepdims=True), 0.0)
             probs.append(raised.astype(jnp.bfloat16))
         inverse = 1.0 / total
-        last = head + HD == wide
         start, left, waiting = 0, None, groups - 1
         for source in range(groups - 1, 0, -1):
             stop = ends[source]
@@ -189,11 +200,17 @@
                 left = result if left is None else jnp.concatenate([left, result], axis=0)
                 start = stop
             while left is not None and left.shape[0] >= rows:
-                held[waiting - 1, :, head : head + HD] = left[:rows].astype(jnp.bfloat16)
+                keep(waiting, head, left[:rows].astype(jnp.bfloat16))
                 left = left[rows:] if left.shape[0] > rows else None
-                if last:
-                    send(waiting)
                 waiting -= 1
+    copies = [
+        pltpu.make_async_copy(
+            held.at[place * rows : (place + 1) * rows], out_hbm.at[place * rows : (place + 1) * rows], sems.at[place]
+        )
+        for place in range(groups)
+    ]
+    for copy in copies:
+        copy.start()
     for distance, hand_ref in zip(distances(groups), hand_refs):
         hand_over(lax.rem(partner(here, distance, groups) + 1, groups), x_ref, hand_ref)
     for copy in copies:
@@ -238,6 +255,7 @@
     tok = out_ref.shape[1]
     wide = att_ref.shape[1]
     count = att_ref.shape[0] // tok
+    order = back_order(tm_count, seq_count)
     last = lax.axis_index("tm") == tm_count - 1
 
     @pl.when(last)
@@ -250,7 +268,7 @@
             rows = att_ref[2 * pair * tok : 2 * (pair + 1) * tok, :].astype(jnp.float32)
             for half in range(2):
                 source = 2 * pair + half
-                start = (mixed(source % seq_count, seq_count) * tm_count + source // seq_count) * wide
+                start = (order[source][1] * tm_count + order[source][0]) * wide
                 moved = moved_ref[:, start : start + wide].astype(jnp.float32)
                 gate = (moved[tok : tok + 1] + moved[tok + 1 : tok + 2]) + moved[tok + 2 : tok + 3]
                 result = moved[:tok] + gate * rows[half * tok : (half + 1) * tok]
@@ -304,10 +322,11 @@
         ],
     )
     order = [tm * seq_count + mixed(s, seq_count) for tm in range(tm_count) for s in range(seq_count)]
+    back = [tm * seq_count + index for tm, index in back_order(tm_count, seq_count)]
     exchange = functools.partial(
-        lax.all_to_all, axis_name=BOTH, split_axis=0, concat_axis=0, tiled=True, axis_index_groups=[order]
-    )
-    exchanged = exchange(packed)
+        lax.all_to_all, axis_name=BOTH, split_axis=0, concat_axis=0, tiled=True
+    )
+    exchanged = exchange(packed, axis_index_groups=[order])
 
     residual = run(
         residual_kernel,
@@ -325,15 +344,15 @@
     moved = shifted(residual, "tm", -1)
 
     attended, *hands = run(
-        functools.partial(attend_kernel, tm_count),
+        functools.partial(attend_kernel, tm_count, seq_count),
         "attend",
         [HBM((count * tok, wide), kind)] + [VMEM((2, group_tok, wide), kind)] * (tm_count - 1),
         [whole(), whole(), whole(pl.ANY)],
         (pattern, exchanged, moved),
         flops=2 * count * tok * count * tok * wide,
-        scratch=[VMEM((tm_count - 1, group_tok, wide), kind), DMA((tm_count,))],
-    )
-    returned = exchange(attended)
+        scratch=[VMEM((count * tok, wide), kind), DMA((tm_count,))],
+    )
+    returned = exchange(attended, axis_index_groups=[back])
     handed = []
     for distance, hand in zip(distances(tm_count), hands):
         route = [(i, partner(i, distance, tm_count)) for i in range(tm_count)]
@@ -441,7 +460,7 @@
     tm_count, seq_count = lax.axis_size("tm"), lax.axis_size("seq")
     _, tok, width = queries.shape
     count = tm_count * seq_count
-    even = width % (count * HD) == 0 and tok % 8 == 0 and seq_count % 4 == 0 and tm_count > 2
+    even = width % (count * HD) == 0 and tok % 8 == 0 and seq_count % 4 == 0 and tm_count > 2 and tm_count % 2 == 0
     return (spread_body if even else gather_body)(queries, *others)
 
 

time: 42.7 us -> 42.7 us (level)
  no operation moved by 1% of the time
where the time goes in v16:
time: 42.7 us; the launch traced here: 42.2 us
  starting transfers between devices  19 us (44%)
  waiting for transfers between devices  15 us (35%)
  Pallas kernels  6.84 us (16%)
  between operations  1.39 us (3%)
    all_to_all x1, waiting for transfers between devices, spread_body(): exchanged = exchange(packed, axis_index_groups=[order])  12.2 us
    ppermute x3, starting transfers between devices, spread_body(): lax.ppermute(hand, 'tm', [(i, j) for i, j in route if j < tm_count - 1])  7.75 us
    all_to_all x1, starting transfers between devices, spread_body(): exchanged = exchange(packed, axis_index_groups=[order])  7.3 us
    pallas_call x6, Pallas kernels, run(): pl.pallas_call(kernel, out_shape=outs, in_specs=specs, out_specs=[whole(g...  6.84 us
    all_to_all x1, starting transfers between devices, spread_body(): returned = exchange(attended, axis_index_groups=[back])  2.68 us
    ppermute x1, waiting for transfers between devices, shifted(): return lax.ppermute(block, axis, route)  2.13 us
    ppermute x1, starting transfers between devices, shifted(): return lax.ppermute(block, axis, route)  1.29 us
  transfers between devices with their start and end apart: 6, of which 4 were waited for; matrix products, arithmetic and copies ran while one was open for 0% of the time, Pallas kernels for 6%

profile of v16, /device:TPU:0, one launch (start us, length us, event | category | flops | bytes accessed | tf_op | source)
XLA Modules:
  0.0 42.2 jit_solution(1218266062236560315)
XLA Ops:
  0.6 2.0 %pack.1.after_ref = bf16[768,384]{1,0:T(8,128)(2,1)} custom-call(bf16[1,24,4096]{2,1,0:T(8,128)(2,1)} %q_hbm.1, bf16[1,24,4096]{2,1,0:T(8,128)(2,1)} %k_hbm.1, bf16[1,24,4096]{2,1,0:T(8,128)(2,1)} %v_hbm.1), custom_call_target="tpu_custom_call" | custom-call | bytes 1179648 | tf_op jit(solution)/shard_map/pack/pallas_call | solution.py:287
  2.6 0.0 copy-start
  2.6 7.3 %all-to-all-start = ((bf16[32,24,384]{2,1,0:T(8,128)(2,1)}), bf16[32,24,384]{2,1,0:T(8,128)(2,1)S(1)}, u32[]{:S(2)}, u32[]{:S(2)}) async-start(bf16[32,24,384]{2,1,0:T(8,128)(2,1)} %bitcast.7), calls=%async_computation | async-start | bytes 1179648 | tf_op jit(solution)/shard_map/all_to_all | solution.py:329
  10.6 0.0 copy-done
  10.6 0.0 copy-start.2
  10.6 1.0 %residual.1 = bf16[32,4096]{1,0:T(8,128)(2,1)S(1)} custom-call(s32[1]{0:T(128)S(6)} %copy.12.noise_ref, bf16[1,24,4096]{2,1,0:T(8,128)(2,1)S(1)} %copy-done, f32[50,4096]{1,0:T(8,128)} %gate_hbm.1, bf16[768,384]{1,0:T(8,128)(2,1)} %pack.1.after_ref), custom_call_target="tpu_custom_call" | custom-call | bytes 1867780 | tf_op jit(solution)/shard_map/residual/pallas_call | solution.py:287
  11.6 1.3 %collective-permute-start = (bf16[32,4096]{1,0:T(8,128)(2,1)S(1)}, bf16[32,4096]{1,0:T(8,128)(2,1)S(1)}, u32[]{:S(2)}, u32[]{:S(2)}) collective-permute-start(bf16[32,4096]{1,0:T(8,128)(2,1)S(1)} %residual.1), channel_id=1, source_target_pairs={{8,0},{16,8},{24,16},{9,1},{17,9},{25,17},{10,2},{18,10},{26,18},{... | collective-permute-start | bytes 786440 | tf_op jit(solution)/shard_map/ppermute | solution.py:21
  12.9 2.1 %collective-permute-done.after_ref.moved_ref = bf16[32,4096]{1,0:T(8,128)(2,1)S(1)} collective-permute-done((bf16[32,4096]{1,0:T(8,128)(2,1)S(1)}, bf16[32,4096]{1,0:T(8,128)(2,1)S(1)}, u32[]{:S(2)}, u32[]{:S(2)}) %collective-permute-start) | collective-permute-done | bytes 262176 | tf_op jit(solution)/shard_map/ppermute | solution.py:21
  15.1 12.2 %all-to-all-done = bf16[32,24,384]{2,1,0:T(8,128)(2,1)S(1)} async-done(((bf16[32,24,384]{2,1,0:T(8,128)(2,1)}), bf16[32,24,384]{2,1,0:T(8,128)(2,1)S(1)}, u32[]{:S(2)}, u32[]{:S(2)}) %all-to-all-start) | async-done | bytes 589856 | tf_op jit(solution)/shard_map/all_to_all | solution.py:329
  27.2 0.0 copy-done.2
  27.3 1.6 %attend.1 = (bf16[768,128]{1,0:T(8,128)(2,1)}, bf16[2,192,128]{2,1,0:T(8,128)(2,1)S(1)}, bf16[2,192,128]{2,1,0:T(8,128)(2,1)S(1)}, bf16[2,192,128]{2,1,0:T(8,128)(2,1)S(1)}) custom-call(s32[4,4]{1,0:T(4,128)S(1)} %copy-done.2, bf16[768,384]{1,0:T(8,128)(2,1)S(1)} %bitcast.4, bf16[32,4096]{1,0:T(8,128)(2,1)S(1)} %collective-permute-done.after_ref.moved_ref), custom_call_target="tpu_custom_call" | custom-call | flops 150994944 | bytes 1343552 | tf_op jit(solution)/shard_map/attend/pallas_call | solution.py:287
  28.8 2.7 %all-to-all-start.1 = ((bf16[32,24,128]{2,1,0:T(8,128)(2,1)}), bf16[32,24,128]{2,1,0:T(8,128)(2,1)S(1)}, u32[]{:S(2)}, u32[]{:S(2)}) async-start(bf16[32,24,128]{2,1,0:T(8,128)(2,1)} %bitcast.8), calls=%async_computation.1 | async-start | bytes 393216 | tf_op jit(solution)/shard_map/all_to_all | solution.py:355
  31.5 1.3 %collective-permute-start.1 = (bf16[2,192,128]{2,1,0:T(8,128)(2,1)S(1)}, bf16[2,192,128]{2,1,0:T(8,128)(2,1)S(1)}, u32[]{:S(2)}, u32[]{:S(2)}) collective-permute-start(bf16[2,192,128]{2,1,0:T(8,128)(2,1)S(1)} %get-tuple-element.7), channel_id=1, source_target_pairs={{8,16},{16,8},{24,0},{9,17},{17,9},{25,1},{10,18},{18,10},{26,2},{... | collective-permute-start | bytes 294920 | tf_op jit(solution)/shard_map/ppermute | solution.py:359
  32.8 4.4 %collective-permute-start.2 = (bf16[2,192,128]{2,1,0:T(8,128)(2,1)S(1)}, bf16[2,192,128]{2,1,0:T(8,128)(2,1)S(1)}, u32[]{:S(2)}, u32[]{:S(2)}) collective-permute-start(bf16[2,192,128]{2,1,0:T(8,128)(2,1)S(1)} %get-tuple-element.8), channel_id=1, source_target_pairs={{0,16},{16,0},{24,8},{1,17},{17,1},{25,9},{2,18},{18,2},{26,10},{3... | collective-permute-start | bytes 294920 | tf_op jit(solution)/shard_map/ppermute | solution.py:359
  37.2 0.0 copy-start.1
  37.3 2.1 %collective-permute-start.3 = (bf16[2,192,128]{2,1,0:T(8,128)(2,1)S(1)}, bf16[2,192,128]{2,1,0:T(8,128)(2,1)S(1)}, u32[]{:S(2)}, u32[]{:S(2)}) collective-permute-start(bf16[2,192,128]{2,1,0:T(8,128)(2,1)S(1)} %get-tuple-element.9), channel_id=1, source_target_pairs={{0,8},{8,0},{24,16},{1,9},{9,1},{25,17},{2,10},{10,2},{26,18},{3,1... | collective-permute-start | bytes 294920 | tf_op jit(solution)/shard_map/ppermute | solution.py:359
  39.3 0.0 collective-permute-done.1.hand_ref
  39.3 0.8 %cache.1.after_ref.begun_hbm = bf16[1,2,192,512]{3,2,1,0:T(8,128)(2,1)} custom-call(bf16[768,384]{1,0:T(8,128)(2,1)S(1)} %bitcast.5, bf16[2,192,128]{2,1,0:T(8,128)(2,1)S(1)} %collective-permute-done.1.hand_ref), custom_call_target="tpu_custom_call" | custom-call | bytes 1081344 | tf_op jit(solution)/shard_map/cache/pallas_call | solution.py:287
  40.1 0.6 %all-to-all-done.1 = bf16[32,24,128]{2,1,0:T(8,128)(2,1)S(1)} async-done(((bf16[32,24,128]{2,1,0:T(8,128)(2,1)}), bf16[32,24,128]{2,1,0:T(8,128)(2,1)S(1)}, u32[]{:S(2)}, u32[]{:S(2)}) %all-to-all-start.1) | async-done | bytes 196640 | tf_op jit(solution)/shard_map/all_to_all | solution.py:355
  40.7 0.0 copy-done.1
  40.7 0.8 %update.1.after_ref = bf16[1,24,4096]{2,1,0:T(8,128)(2,1)} custom-call(bf16[768,128]{1,0:T(8,128)(2,1)S(1)} %bitcast.6, bf16[32,4096]{1,0:T(8,128)(2,1)S(1)} %collective-permute-done.after_ref.moved_ref, bf16[24,4096]{1,0:T(8,128)(2,1)S(1)} %copy-done.1, bf16[1,2,192,512]{3,2,1,0:T(8,128)(2,1)} %cache.1.after_ref.begun_hbm), custom_call_target="tpu_custom_call" | custom-call | bytes 1245184 | tf_op jit(solution)/shard_map/update/pallas_call | solution.py:287
  41.5 0.1 collective-permute-done.2.refs_0_
  41.5 0.0 collective-permute-done.3.refs_1_
  41.6 0.7 %cache_rest.1 = bf16[1,2,192,512]{3,2,1,0:T(8,128)(2,1)} custom-call(bf16[1,2,192,512]{3,2,1,0:T(8,128)(2,1)} %cache.1.after_ref.begun_hbm, bf16[1,24,4096]{2,1,0:T(8,128)(2,1)} %update.1.after_ref, bf16[2,192,128]{2,1,0:T(8,128)(2,1)S(1)} %collective-permute-done.2.refs_0_, ...), custom_call_target="tpu_custom_call", output_to_operand_aliasing={{}: (0, {})} | custom-call | bytes 1179648 | tf_op jit(solution)/shard_map/cache_rest/pallas_call | solution.py:287
Async XLA Ops:
  2.6 8.0 %copy-start = (bf16[1,24,4096]{2,1,0:T(8,128)(2,1)S(1)}, bf16[1,24,4096]{2,1,0:T(8,128)(2,1)}, u32[]{:S(2)}) copy-start(bf16[1,24,4096]{2,1,0:T(8,128)(2,1)} %h_ref.1) | copy-start | bytes 589828
  2.6 24.6 %all-to-all-start = ((bf16[32,24,384]{2,1,0:T(8,128)(2,1)}), bf16[32,24,384]{2,1,0:T(8,128)(2,1)S(1)}, u32[]{:S(2)}, u32[]{:S(2)}) async-start(bf16[32,24,384]{2,1,0:T(8,128)(2,1)} %bitcast.7), calls=%async_computation | async-start | bytes 1179648 | tf_op jit(solution)/shard_map/all_to_all | solution.py:329
  10.6 16.7 %copy-start.2 = (s32[4,4]{1,0:T(4,128)S(1)}, s32[4,4]{1,0:T(4,128)}, u32[]{:S(2)}) copy-start(s32[4,4]{1,0:T(4,128)} %pattern_ref.1) | copy-start | bytes 196
  11.6 3.4 %collective-permute-start = (bf16[32,4096]{1,0:T(8,128)(2,1)S(1)}, bf16[32,4096]{1,0:T(8,128)(2,1)S(1)}, u32[]{:S(2)}, u32[]{:S(2)}) collective-permute-start(bf16[32,4096]{1,0:T(8,128)(2,1)S(1)} %residual.1), channel_id=1, source_target_pairs={{8,0},{16,8},{24,16},{9,1},{17,9},{25,17},{10,2},{18,10},{26,18},{... | collective-permute-start | bytes 786440 | tf_op jit(solution)/shard_map/ppermute | solution.py:21
  28.8 11.9 %all-to-all-start.1 = ((bf16[32,24,128]{2,1,0:T(8,128)(2,1)}), bf16[32,24,128]{2,1,0:T(8,128)(2,1)S(1)}, u32[]{:S(2)}, u32[]{:S(2)}) async-start(bf16[32,24,128]{2,1,0:T(8,128)(2,1)} %bitcast.8), calls=%async_computation.1 | async-start | bytes 393216 | tf_op jit(solution)/shard_map/all_to_all | solution.py:355
  31.5 7.8 %collective-permute-start.1 = (bf16[2,192,128]{2,1,0:T(8,128)(2,1)S(1)}, bf16[2,192,128]{2,1,0:T(8,128)(2,1)S(1)}, u32[]{:S(2)}, u32[]{:S(2)}) collective-permute-start(bf16[2,192,128]{2,1,0:T(8,128)(2,1)S(1)} %get-tuple-element.7), channel_id=1, source_target_pairs={{8,16},{16,8},{24,0},{9,17},{17,9},{25,1},{10,18},{18,10},{26,2},{... | collective-permute-start | bytes 294920 | tf_op jit(solution)/shard_map/ppermute | solution.py:359
  32.8 8.7 %collective-permute-start.2 = (bf16[2,192,128]{2,1,0:T(8,128)(2,1)S(1)}, bf16[2,192,128]{2,1,0:T(8,128)(2,1)S(1)}, u32[]{:S(2)}, u32[]{:S(2)}) collective-permute-start(bf16[2,192,128]{2,1,0:T(8,128)(2,1)S(1)} %get-tuple-element.8), channel_id=1, source_target_pairs={{0,16},{16,0},{24,8},{1,17},{17,1},{25,9},{2,18},{18,2},{26,10},{3... | collective-permute-start | bytes 294920 | tf_op jit(solution)/shard_map/ppermute | solution.py:359
  37.2 3.5 %copy-start.1 = (bf16[24,4096]{1,0:T(8,128)(2,1)S(1)}, bf16[24,4096]{1,0:T(8,128)(2,1)}, u32[]{:S(2)}) copy-start(bf16[24,4096]{1,0:T(8,128)(2,1)} %fresh_ref.1) | copy-start | bytes 589828
  37.3 4.3 %collective-permute-start.3 = (bf16[2,192,128]{2,1,0:T(8,128)(2,1)S(1)}, bf16[2,192,128]{2,1,0:T(8,128)(2,1)S(1)}, u32[]{:S(2)}, u32[]{:S(2)}) collective-permute-start(bf16[2,192,128]{2,1,0:T(8,128)(2,1)S(1)} %get-tuple-element.9), channel_id=1, source_target_pairs={{0,8},{8,0},{24,16},{1,9},{9,1},{25,17},{2,10},{10,2},{26,18},{3,1... | collective-permute-start | bytes 294920 | tf_op jit(solution)/shard_map/ppermute | solution.py:359

commit v17 on v16

--- a/solution.py
+++ b/solution.py
@@ -25,7 +25,7 @@
     return (index + count // 2) % count
 
 
-def back_order(tm_count, seq_count):
+def out_order(tm_count, seq_count):
     ordered = sorted(range(seq_count), key=lambda index: mixed(index, seq_count))
     half = tm_count // 2
     return [
@@ -37,12 +37,23 @@
     ]
 
 
+def back_order(tm_count, seq_count):
+    ordered = sorted(range(seq_count), key=lambda index: mixed(index, seq_count))
+    return [(tm, index) for tm in range(tm_count) for index in ordered]
+
+
+def piece(group, pair, groups, pairs, step):
+    half = groups // 2
+    return ((group % half * pairs + pair) * (groups // half) + group // half) * step
+
+
 def pack_kernel(seq_count, parts, q_hbm, k_hbm, v_hbm, out_hbm, held, block, in_sems, out_sems):
     tok, width = held.shape[1:]
     wide = out_hbm.shape[1] // 3
     count = out_hbm.shape[0] // tok
     tm_count = count // seq_count
     span, members = width // parts, seq_count // parts
+    order = out_order(tm_count, seq_count)
     copies = []
     for part in range(parts):
         columns = slice(part * span, (part + 1) * span)
@@ -59,7 +70,7 @@
             copies[3 * part + place].wait()
         for tm in range(tm_count):
             for seq in range(part * members, (part + 1) * members, 2):
-                first = (tm * seq_count + mixed(seq, seq_count)) * tok
+                first = order.index((tm, seq)) * tok
                 for place in range(3):
                     rows = []
                     for member in (seq, seq + 1):
@@ -68,7 +79,7 @@
                     block[first : first + 2 * tok, place * wide : (place + 1) * wide] = jnp.concatenate(
                         rows, axis=0
                     ).astype(jnp.bfloat16)
-            first = (tm * seq_count + mixed(part * members, seq_count)) * tok
+            first = order.index((tm, part * members)) * tok
             rows = slice(first, first + members * tok)
             outs.append(
                 pltpu.make_async_copy(block.at[rows], out_hbm.at[rows], out_sems.at[part, tm])
@@ -117,15 +128,15 @@
     return range(groups - 1, 0, -1)
 
 
-def hand_over(group, x_ref, out_ref, lanes=slice(None)):
+def hand_over(group, groups, seq_count, x_ref, out_ref, lanes=slice(None)):
     wide = x_ref.shape[1] // 3
-    rows = out_ref.shape[1]
-    half = rows // 2
-    for part in range(2):
-        first = pl.multiple_of(group * rows + mixed(part, 2) * half, half)
+    pairs = seq_count // 2
+    step = out_ref.shape[1] // pairs
+    for pair in range(pairs):
+        first = pl.multiple_of(piece(group, mixed(2 * pair, seq_count) // 2, groups, pairs, step), step)
         for kind in range(2):
-            out_ref[kind, part * half : (part + 1) * half, lanes] = x_ref[
-                pl.ds(first, half), (kind + 1) * wide : (kind + 2) * wide
+            out_ref[kind, pair * step : (pair + 1) * step, lanes] = x_ref[
+                pl.ds(first, step), (kind + 1) * wide : (kind + 2) * wide
             ]
 
 
@@ -148,16 +159,16 @@
             chosen = jnp.where((lane >= start) & (lane < start + rows), flag, chosen)
         kept.append(chosen[:, : ends[-1]] > 0)
 
-    halves = groups // (groups // 2)
     pairs = seq_count // 2
     step = rows // pairs
 
+    def take(group, first):
+        starts = [piece(group, pair, groups, pairs, step) for pair in range(pairs)]
+        return jnp.concatenate([x_ref[at : at + step, first : first + HD] for at in starts], axis=0)
+
     def keep(group, head, result):
         for place in (group - 1, groups - 1) if group == groups - 1 else (group - 1,):
-            low, high = place % (groups // 2), place // (groups // 2)
-            for pair in range(pairs):
-                to = ((low * pairs + pair) * halves + high) * step
-                held[to : to + step, head : head + HD] = result[pair * step : (pair + 1) * step]
+            held[place * rows : (place + 1) * rows, head : head + HD] = result
 
     def spread(row, fill):
         rest = across - row.shape[1]
@@ -165,14 +176,15 @@
 
     for head in range(0, wide, HD):
         query = jnp.concatenate(
-            [x_ref[group * rows : (group + 1) * rows, head : head + HD] for group in range(groups - 1, 0, -1)],
-            axis=0,
+            [take(group, head) for group in range(groups - 1, 0, -1)], axis=0
         )
         query = jnp.transpose(query)
-        value = jnp.transpose(x_ref[:, 2 * wide + head : 2 * wide + head + HD])
+        value = jnp.transpose(
+            jnp.concatenate([take(group, 2 * wide + head) for group in range(groups)], axis=0)
+        )
         scores, highest = [], None
         for source in range(groups):
-            key = x_ref[source * rows : (source + 1) * rows, wide + head : wide + head + HD]
+            key = take(source, wide + head)
             scores.append(
                 jnp.dot(key, query[:, : ends[source]], preferred_element_type=jnp.float32)
             )
@@ -212,7 +224,8 @@
     for copy in copies:
         copy.start()
     for distance, hand_ref in zip(distances(groups), hand_refs):
-        hand_over(lax.rem(partner(here, distance, groups) + 1, groups), x_ref, hand_ref)
+        group = lax.rem(partner(here, distance, groups) + 1, groups)
+        hand_over(group, groups, seq_count, x_ref, hand_ref)
     for copy in copies:
         copy.wait()
 
@@ -222,14 +235,14 @@
     return pl.ds(pl.multiple_of(source * wide, wide), wide)
 
 
-def cache_kernel(groups, x_ref, hand_ref, out_ref):
+def cache_kernel(groups, seq_count, x_ref, hand_ref, out_ref):
     wide = x_ref.shape[1] // 3
     here = lax.axis_index("tm")
     out_ref[...] = jnp.zeros_like(out_ref)
 
     @pl.when(here < groups - 1)
     def place():
-        hand_over(here + 1, x_ref, out_ref.at[0], lanes_of(0, groups, here, wide))
+        hand_over(here + 1, groups, seq_count, x_ref, out_ref.at[0], lanes_of(0, groups, here, wide))
         out_ref[0, :, :, lanes_of(distances(groups)[0], groups, here, wide)] = hand_ref[...]
 
 
@@ -306,7 +319,7 @@
     group_tok = tok * seq_count
     kind = queries.dtype
     DMA = pltpu.SemaphoreType.DMA
-    parts = 4 if seq_count % 8 == 0 else 2
+    parts = seq_count // 2
 
     packed = run(
         functools.partial(pack_kernel, seq_count, parts),
@@ -321,12 +334,14 @@
             DMA((parts, tm_count)),
         ],
     )
-    order = [tm * seq_count + mixed(s, seq_count) for tm in range(tm_count) for s in range(seq_count)]
-    back = [tm * seq_count + index for tm, index in back_order(tm_count, seq_count)]
+    out, back = (
+        [tm * seq_count + index for tm, index in order(tm_count, seq_count)]
+        for order in (out_order, back_order)
+    )
     exchange = functools.partial(
         lax.all_to_all, axis_name=BOTH, split_axis=0, concat_axis=0, tiled=True
     )
-    exchanged = exchange(packed, axis_index_groups=[order])
+    exchanged = exchange(packed, axis_index_groups=[out])
 
     residual = run(
         residual_kernel,
@@ -360,7 +375,7 @@
 
     first, *rest = handed
     begun = run(
-        functools.partial(cache_kernel, tm_count),
+        functools.partial(cache_kernel, tm_count, seq_count),
         "cache",
         [jax.ShapeDtypeStruct((1, 2, group_tok, tm_count * wide), kind)],
         [whole()] * 2,

time: 42.7 us -> 43.3 us (1.014)
  waiting for transfers between devices: 15 us -> 15.8 us
    ppermute x3, waiting for transfers between devices: 0.07 us -> 0.79 us  [spread_body(): lax.ppermute(hand, 'tm', [(i, j) for i, j in route if j < tm_count - 1])]
    all_to_all x1, waiting for transfers between devices: 12.2 us -> 12.6 us  [spread_body(): exchanged = exchange(packed, axis_index_groups=[out])]
  transfers between devices with their start and end apart: 6 -> 6, of which waited for: 4 -> 5; matrix products, arithmetic and copies ran while one was open for 0% -> 0% of each run, Pallas kernels for 6% -> 6%
where the time goes in v17:
time: 43.3 us; the launch traced here: 42.8 us
  starting transfers between devices  18.8 us (43%)
  waiting for transfers between devices  15.8 us (36%)
  Pallas kernels  6.85 us (16%)
  between operations  1.38 us (3%)
    all_to_all x1, waiting for transfers between devices, spread_body(): exchanged = exchange(packed, axis_index_groups=[out])  12.6 us
    ppermute x3, starting transfers between devices, spread_body(): lax.ppermute(hand, 'tm', [(i, j) for i, j in route if j < tm_count - 1])  7.61 us
    all_to_all x1, starting transfers between devices, spread_body(): exchanged = exchange(packed, axis_index_groups=[out])  7.3 us
    pallas_call x6, Pallas kernels, run(): pl.pallas_call(kernel, out_shape=outs, in_specs=specs, out_specs=[whole(g...  6.85 us
    all_to_all x1, starting transfers between devices, spread_body(): returned = exchange(attended, axis_index_groups=[back])  2.6 us
    ppermute x1, waiting for transfers between devices, shifted(): return lax.ppermute(block, axis, route)  2.13 us
    ppermute x1, starting transfers between devices, shifted(): return lax.ppermute(block, axis, route)  1.29 us
  transfers between devices with their start and end apart: 6, of which 5 were waited for; matrix products, arithmetic and copies ran while one was open for 0% of the time, Pallas kernels for 6%

profile of v17, /device:TPU:0, one launch (start us, length us, event | category | flops | bytes accessed | tf_op | source)
XLA Modules:
  0.0 42.8 jit_solution(424261219115897092)
XLA Ops:
  0.6 2.0 %pack.1.after_ref = bf16[768,384]{1,0:T(8,128)(2,1)} custom-call(bf16[1,24,4096]{2,1,0:T(8,128)(2,1)} %q_hbm.1, bf16[1,24,4096]{2,1,0:T(8,128)(2,1)} %k_hbm.1, bf16[1,24,4096]{2,1,0:T(8,128)(2,1)} %v_hbm.1), custom_call_target="tpu_custom_call" | custom-call | bytes 1179648 | tf_op jit(solution)/shard_map/pack/pallas_call | solution.py:300
  2.6 0.0 copy-start
  2.6 7.3 %all-to-all-start = ((bf16[32,24,384]{2,1,0:T(8,128)(2,1)}), bf16[32,24,384]{2,1,0:T(8,128)(2,1)S(1)}, u32[]{:S(2)}, u32[]{:S(2)}) async-start(bf16[32,24,384]{2,1,0:T(8,128)(2,1)} %bitcast.7), calls=%async_computation | async-start | bytes 1179648 | tf_op jit(solution)/shard_map/all_to_all | solution.py:344
  10.6 0.0 copy-done
  10.6 0.0 copy-start.2
  10.6 1.0 %residual.1 = bf16[32,4096]{1,0:T(8,128)(2,1)S(1)} custom-call(s32[1]{0:T(128)S(6)} %copy.12.noise_ref, bf16[1,24,4096]{2,1,0:T(8,128)(2,1)S(1)} %copy-done, f32[50,4096]{1,0:T(8,128)} %gate_hbm.1, bf16[768,384]{1,0:T(8,128)(2,1)} %pack.1.after_ref), custom_call_target="tpu_custom_call" | custom-call | bytes 1867780 | tf_op jit(solution)/shard_map/residual/pallas_call | solution.py:300
  11.6 1.3 %collective-permute-start = (bf16[32,4096]{1,0:T(8,128)(2,1)S(1)}, bf16[32,4096]{1,0:T(8,128)(2,1)S(1)}, u32[]{:S(2)}, u32[]{:S(2)}) collective-permute-start(bf16[32,4096]{1,0:T(8,128)(2,1)S(1)} %residual.1), channel_id=1, source_target_pairs={{8,0},{16,8},{24,16},{9,1},{17,9},{25,17},{10,2},{18,10},{26,18},{... | collective-permute-start | bytes 786440 | tf_op jit(solution)/shard_map/ppermute | solution.py:21
  12.9 2.1 %collective-permute-done.after_ref.moved_ref = bf16[32,4096]{1,0:T(8,128)(2,1)S(1)} collective-permute-done((bf16[32,4096]{1,0:T(8,128)(2,1)S(1)}, bf16[32,4096]{1,0:T(8,128)(2,1)S(1)}, u32[]{:S(2)}, u32[]{:S(2)}) %collective-permute-start) | collective-permute-done | bytes 262176 | tf_op jit(solution)/shard_map/ppermute | solution.py:21
  15.1 12.6 %all-to-all-done = bf16[32,24,384]{2,1,0:T(8,128)(2,1)S(1)} async-done(((bf16[32,24,384]{2,1,0:T(8,128)(2,1)}), bf16[32,24,384]{2,1,0:T(8,128)(2,1)S(1)}, u32[]{:S(2)}, u32[]{:S(2)}) %all-to-all-start) | async-done | bytes 589856 | tf_op jit(solution)/shard_map/all_to_all | solution.py:344
  27.7 0.0 copy-done.2
  27.7 1.6 %attend.1 = (bf16[768,128]{1,0:T(8,128)(2,1)}, bf16[2,192,128]{2,1,0:T(8,128)(2,1)S(1)}, bf16[2,192,128]{2,1,0:T(8,128)(2,1)S(1)}, bf16[2,192,128]{2,1,0:T(8,128)(2,1)S(1)}) custom-call(s32[4,4]{1,0:T(4,128)S(1)} %copy-done.2, bf16[768,384]{1,0:T(8,128)(2,1)S(1)} %bitcast.4, bf16[32,4096]{1,0:T(8,128)(2,1)S(1)} %collective-permute-done.after_ref.moved_ref), custom_call_target="tpu_custom_call" | custom-call | flops 150994944 | bytes 1343552 | tf_op jit(solution)/shard_map/attend/pallas_call | solution.py:300
  29.3 2.6 %all-to-all-start.1 = ((bf16[32,24,128]{2,1,0:T(8,128)(2,1)}), bf16[32,24,128]{2,1,0:T(8,128)(2,1)S(1)}, u32[]{:S(2)}, u32[]{:S(2)}) async-start(bf16[32,24,128]{2,1,0:T(8,128)(2,1)} %bitcast.8), calls=%async_computation.1 | async-start | bytes 393216 | tf_op jit(solution)/shard_map/all_to_all | solution.py:370
  31.9 1.3 %collective-permute-start.1 = (bf16[2,192,128]{2,1,0:T(8,128)(2,1)S(1)}, bf16[2,192,128]{2,1,0:T(8,128)(2,1)S(1)}, u32[]{:S(2)}, u32[]{:S(2)}) collective-permute-start(bf16[2,192,128]{2,1,0:T(8,128)(2,1)S(1)} %get-tuple-element.7), channel_id=1, source_target_pairs={{8,16},{16,8},{24,0},{9,17},{17,9},{25,1},{10,18},{18,10},{26,2},{... | collective-permute-start | bytes 294920 | tf_op jit(solution)/shard_map/ppermute | solution.py:374
  33.2 4.3 %collective-permute-start.2 = (bf16[2,192,128]{2,1,0:T(8,128)(2,1)S(1)}, bf16[2,192,128]{2,1,0:T(8,128)(2,1)S(1)}, u32[]{:S(2)}, u32[]{:S(2)}) collective-permute-start(bf16[2,192,128]{2,1,0:T(8,128)(2,1)S(1)} %get-tuple-element.8), channel_id=1, source_target_pairs={{0,16},{16,0},{24,8},{1,17},{17,1},{25,9},{2,18},{18,2},{26,10},{3... | collective-permute-start | bytes 294920 | tf_op jit(solution)/shard_map/ppermute | solution.py:374
  37.5 0.0 copy-start.1
  37.5 2.1 %collective-permute-start.3 = (bf16[2,192,128]{2,1,0:T(8,128)(2,1)S(1)}, bf16[2,192,128]{2,1,0:T(8,128)(2,1)S(1)}, u32[]{:S(2)}, u32[]{:S(2)}) collective-permute-start(bf16[2,192,128]{2,1,0:T(8,128)(2,1)S(1)} %get-tuple-element.9), channel_id=1, source_target_pairs={{0,8},{8,0},{24,16},{1,9},{9,1},{25,17},{2,10},{10,2},{26,18},{3,1... | collective-permute-start | bytes 294920 | tf_op jit(solution)/shard_map/ppermute | solution.py:374
  39.6 0.2 collective-permute-done.1.hand_ref
  39.8 0.8 %cache.1.after_ref.begun_hbm = bf16[1,2,192,512]{3,2,1,0:T(8,128)(2,1)} custom-call(bf16[768,384]{1,0:T(8,128)(2,1)S(1)} %bitcast.5, bf16[2,192,128]{2,1,0:T(8,128)(2,1)S(1)} %collective-permute-done.1.hand_ref), custom_call_target="tpu_custom_call" | custom-call | bytes 1081344 | tf_op jit(solution)/shard_map/cache/pallas_call | solution.py:300
  40.6 0.2 all-to-all-done.1
  40.8 0.0 copy-done.1
  40.8 0.8 %update.1.after_ref = bf16[1,24,4096]{2,1,0:T(8,128)(2,1)} custom-call(bf16[768,128]{1,0:T(8,128)(2,1)S(1)} %bitcast.6, bf16[32,4096]{1,0:T(8,128)(2,1)S(1)} %collective-permute-done.after_ref.moved_ref, bf16[24,4096]{1,0:T(8,128)(2,1)S(1)} %copy-done.1, bf16[1,2,192,512]{3,2,1,0:T(8,128)(2,1)} %cache.1.after_ref.begun_hbm), custom_call_target="tpu_custom_call" | custom-call | bytes 1245184 | tf_op jit(solution)/shard_map/update/pallas_call | solution.py:300
  41.6 0.6 %collective-permute-done.2.refs_0_ = bf16[2,192,128]{2,1,0:T(8,128)(2,1)S(1)} collective-permute-done((bf16[2,192,128]{2,1,0:T(8,128)(2,1)S(1)}, bf16[2,192,128]{2,1,0:T(8,128)(2,1)S(1)}, u32[]{:S(2)}, u32[]{:S(2)}) %collective-permute-start.2) | collective-permute-done | bytes 98336 | tf_op jit(solution)/shard_map/ppermute | solution.py:374
  42.1 0.0 collective-permute-done.3.refs_1_
  42.1 0.7 %cache_rest.1 = bf16[1,2,192,512]{3,2,1,0:T(8,128)(2,1)} custom-call(bf16[1,2,192,512]{3,2,1,0:T(8,128)(2,1)} %cache.1.after_ref.begun_hbm, bf16[1,24,4096]{2,1,0:T(8,128)(2,1)} %update.1.after_ref, bf16[2,192,128]{2,1,0:T(8,128)(2,1)S(1)} %collective-permute-done.2.refs_0_, ...), custom_call_target="tpu_custom_call", output_to_operand_aliasing={{}: (0, {})} | custom-call | bytes 1179648 | tf_op jit(solution)/shard_map/cache_rest/pallas_call | solution.py:300
Async XLA Ops:
  2.6 8.0 %copy-start = (bf16[1,24,4096]{2,1,0:T(8,128)(2,1)S(1)}, bf16[1,24,4096]{2,1,0:T(8,128)(2,1)}, u32[]{:S(2)}) copy-start(bf16[1,24,4096]{2,1,0:T(8,128)(2,1)} %h_ref.1) | copy-start | bytes 589828
  2.6 25.1 %all-to-all-start = ((bf16[32,24,384]{2,1,0:T(8,128)(2,1)}), bf16[32,24,384]{2,1,0:T(8,128)(2,1)S(1)}, u32[]{:S(2)}, u32[]{:S(2)}) async-start(bf16[32,24,384]{2,1,0:T(8,128)(2,1)} %bitcast.7), calls=%async_computation | async-start | bytes 1179648 | tf_op jit(solution)/shard_map/all_to_all | solution.py:344
  10.6 17.1 %copy-start.2 = (s32[4,4]{1,0:T(4,128)S(1)}, s32[4,4]{1,0:T(4,128)}, u32[]{:S(2)}) copy-start(s32[4,4]{1,0:T(4,128)} %pattern_ref.1) | copy-start | bytes 196
  11.6 3.4 %collective-permute-start = (bf16[32,4096]{1,0:T(8,128)(2,1)S(1)}, bf16[32,4096]{1,0:T(8,128)(2,1)S(1)}, u32[]{:S(2)}, u32[]{:S(2)}) collective-permute-start(bf16[32,4096]{1,0:T(8,128)(2,1)S(1)} %residual.1), channel_id=1, source_target_pairs={{8,0},{16,8},{24,16},{9,1},{17,9},{25,17},{10,2},{18,10},{26,18},{... | collective-permute-start | bytes 786440 | tf_op jit(solution)/shard_map/ppermute | solution.py:21
  29.3 11.5 %all-to-all-start.1 = ((bf16[32,24,128]{2,1,0:T(8,128)(2,1)}), bf16[32,24,128]{2,1,0:T(8,128)(2,1)S(1)}, u32[]{:S(2)}, u32[]{:S(2)}) async-start(bf16[32,24,128]{2,1,0:T(8,128)(2,1)} %bitcast.8), calls=%async_computation.1 | async-start | bytes 393216 | tf_op jit(solution)/shard_map/all_to_all | solution.py:370
  31.9 7.9 %collective-permute-start.1 = (bf16[2,192,128]{2,1,0:T(8,128)(2,1)S(1)}, bf16[2,192,128]{2,1,0:T(8,128)(2,1)S(1)}, u32[]{:S(2)}, u32[]{:S(2)}) collective-permute-start(bf16[2,192,128]{2,1,0:T(8,128)(2,1)S(1)} %get-tuple-element.7), channel_id=1, source_target_pairs={{8,16},{16,8},{24,0},{9,17},{17,9},{25,1},{10,18},{18,10},{26,2},{... | collective-permute-start | bytes 294920 | tf_op jit(solution)/shard_map/ppermute | solution.py:374
  33.2 8.9 %collective-permute-start.2 = (bf16[2,192,128]{2,1,0:T(8,128)(2,1)S(1)}, bf16[2,192,128]{2,1,0:T(8,128)(2,1)S(1)}, u32[]{:S(2)}, u32[]{:S(2)}) collective-permute-start(bf16[2,192,128]{2,1,0:T(8,128)(2,1)S(1)} %get-tuple-element.8), channel_id=1, source_target_pairs={{0,16},{16,0},{24,8},{1,17},{17,1},{25,9},{2,18},{18,2},{26,10},{3... | collective-permute-start | bytes 294920 | tf_op jit(solution)/shard_map/ppermute | solution.py:374
  37.5 3.3 %copy-start.1 = (bf16[24,4096]{1,0:T(8,128)(2,1)S(1)}, bf16[24,4096]{1,0:T(8,128)(2,1)}, u32[]{:S(2)}) copy-start(bf16[24,4096]{1,0:T(8,128)(2,1)} %fresh_ref.1) | copy-start | bytes 589828
  37.5 4.6 %collective-permute-start.3 = (bf16[2,192,128]{2,1,0:T(8,128)(2,1)S(1)}, bf16[2,192,128]{2,1,0:T(8,128)(2,1)S(1)}, u32[]{:S(2)}, u32[]{:S(2)}) collective-permute-start(bf16[2,192,128]{2,1,0:T(8,128)(2,1)S(1)} %get-tuple-element.9), channel_id=1, source_target_pairs={{0,8},{8,0},{24,16},{1,9},{9,1},{25,17},{2,10},{10,2},{26,18},{3,1... | collective-permute-start | bytes 294920 | tf_op jit(solution)/shard_map/ppermute | solution.py:374

commit v18 on v15

--- a/solution.py
+++ b/solution.py
@@ -102,7 +102,7 @@
 
 
 def distances(groups):
-    return range(groups - 1, 0, -1)
+    return sorted(range(1, groups), key=lambda distance: (distance < groups // 2, distance))
 
 
 def hand_over(group, x_ref, out_ref, lanes=slice(None)):

time: 42.7 us -> 42.9 us (level)
  transfers between devices with their start and end apart: 6 -> 6, of which waited for: 4 -> 3; matrix products, arithmetic and copies ran while one was open for 0% -> 0% of each run, Pallas kernels for 6% -> 6%
where the time goes in v18:
time: 42.9 us; the launch traced here: 42.5 us
  starting transfers between devices  19.3 us (45%)
  waiting for transfers between devices  15 us (35%)
  Pallas kernels  6.81 us (16%)
  between operations  1.39 us (3%)
    all_to_all x1, waiting for transfers between devices, spread_body(): exchanged = exchange(packed)  12.2 us
    ppermute x3, starting transfers between devices, spread_body(): lax.ppermute(hand, 'tm', [(i, j) for i, j in route if j < tm_count - 1])  8 us
    all_to_all x1, starting transfers between devices, spread_body(): exchanged = exchange(packed)  7.3 us
    pallas_call x6, Pallas kernels, run(): pl.pallas_call(kernel, out_shape=outs, in_specs=specs, out_specs=[whole(g...  6.81 us
    all_to_all x1, starting transfers between devices, spread_body(): returned = exchange(attended)  2.68 us
    ppermute x1, waiting for transfers between devices, shifted(): return lax.ppermute(block, axis, route)  2.13 us
    ppermute x1, starting transfers between devices, shifted(): return lax.ppermute(block, axis, route)  1.29 us
  transfers between devices with their start and end apart: 6, of which 3 were waited for; matrix products, arithmetic and copies ran while one was open for 0% of the time, Pallas kernels for 6%

profile of v18, /device:TPU:0, one launch (start us, length us, event | category | flops | bytes accessed | tf_op | source)
XLA Modules:
  0.0 42.5 jit_solution(9558061107341616499)
XLA Ops:
  0.6 2.0 %pack.1.after_ref = bf16[768,384]{1,0:T(8,128)(2,1)} custom-call(bf16[1,24,4096]{2,1,0:T(8,128)(2,1)} %q_hbm.1, bf16[1,24,4096]{2,1,0:T(8,128)(2,1)} %k_hbm.1, bf16[1,24,4096]{2,1,0:T(8,128)(2,1)} %v_hbm.1), custom_call_target="tpu_custom_call" | custom-call | bytes 1179648 | tf_op jit(solution)/shard_map/pack/pallas_call | solution.py:269
  2.6 0.0 copy-start
  2.6 7.3 %all-to-all-start = ((bf16[32,24,384]{2,1,0:T(8,128)(2,1)}), bf16[32,24,384]{2,1,0:T(8,128)(2,1)S(1)}, u32[]{:S(2)}, u32[]{:S(2)}) async-start(bf16[32,24,384]{2,1,0:T(8,128)(2,1)} %bitcast.7), calls=%async_computation | async-start | bytes 1179648 | tf_op jit(solution)/shard_map/all_to_all | solution.py:310
  10.6 0.0 copy-done
  10.6 0.0 copy-start.2
  10.6 1.0 %residual.1 = bf16[32,4096]{1,0:T(8,128)(2,1)S(1)} custom-call(s32[1]{0:T(128)S(6)} %copy.12.noise_ref, bf16[1,24,4096]{2,1,0:T(8,128)(2,1)S(1)} %copy-done, f32[50,4096]{1,0:T(8,128)} %gate_hbm.1, bf16[768,384]{1,0:T(8,128)(2,1)} %pack.1.after_ref), custom_call_target="tpu_custom_call" | custom-call | bytes 1867780 | tf_op jit(solution)/shard_map/residual/pallas_call | solution.py:269
  11.6 1.3 %collective-permute-start = (bf16[32,4096]{1,0:T(8,128)(2,1)S(1)}, bf16[32,4096]{1,0:T(8,128)(2,1)S(1)}, u32[]{:S(2)}, u32[]{:S(2)}) collective-permute-start(bf16[32,4096]{1,0:T(8,128)(2,1)S(1)} %residual.1), channel_id=1, source_target_pairs={{8,0},{16,8},{24,16},{9,1},{17,9},{25,17},{10,2},{18,10},{26,18},{... | collective-permute-start | bytes 786440 | tf_op jit(solution)/shard_map/ppermute | solution.py:21
  12.9 2.1 %collective-permute-done.after_ref.moved_ref = bf16[32,4096]{1,0:T(8,128)(2,1)S(1)} collective-permute-done((bf16[32,4096]{1,0:T(8,128)(2,1)S(1)}, bf16[32,4096]{1,0:T(8,128)(2,1)S(1)}, u32[]{:S(2)}, u32[]{:S(2)}) %collective-permute-start) | collective-permute-done | bytes 262176 | tf_op jit(solution)/shard_map/ppermute | solution.py:21
  15.1 12.2 %all-to-all-done = bf16[32,24,384]{2,1,0:T(8,128)(2,1)S(1)} async-done(((bf16[32,24,384]{2,1,0:T(8,128)(2,1)}), bf16[32,24,384]{2,1,0:T(8,128)(2,1)S(1)}, u32[]{:S(2)}, u32[]{:S(2)}) %all-to-all-start) | async-done | bytes 589856 | tf_op jit(solution)/shard_map/all_to_all | solution.py:310
  27.2 0.0 copy-done.2
  27.3 1.6 %attend.1 = (bf16[768,128]{1,0:T(8,128)(2,1)}, bf16[2,192,128]{2,1,0:T(8,128)(2,1)S(1)}, bf16[2,192,128]{2,1,0:T(8,128)(2,1)S(1)}, bf16[2,192,128]{2,1,0:T(8,128)(2,1)S(1)}) custom-call(s32[4,4]{1,0:T(4,128)S(1)} %copy-done.2, bf16[768,384]{1,0:T(8,128)(2,1)S(1)} %bitcast.4, bf16[32,4096]{1,0:T(8,128)(2,1)S(1)} %collective-permute-done.after_ref.moved_ref), custom_call_target="tpu_custom_call" | custom-call | flops 150994944 | bytes 1343552 | tf_op jit(solution)/shard_map/attend/pallas_call | solution.py:269
  28.8 2.7 %all-to-all-start.1 = ((bf16[32,24,128]{2,1,0:T(8,128)(2,1)}), bf16[32,24,128]{2,1,0:T(8,128)(2,1)S(1)}, u32[]{:S(2)}, u32[]{:S(2)}) async-start(bf16[32,24,128]{2,1,0:T(8,128)(2,1)} %bitcast.8), calls=%async_computation.1 | async-start | bytes 393216 | tf_op jit(solution)/shard_map/all_to_all | solution.py:336
  31.5 3.7 %collective-permute-start.1 = (bf16[2,192,128]{2,1,0:T(8,128)(2,1)S(1)}, bf16[2,192,128]{2,1,0:T(8,128)(2,1)S(1)}, u32[]{:S(2)}, u32[]{:S(2)}) collective-permute-start(bf16[2,192,128]{2,1,0:T(8,128)(2,1)S(1)} %get-tuple-element.7), channel_id=1, source_target_pairs={{0,16},{16,0},{24,8},{1,17},{17,1},{25,9},{2,18},{18,2},{26,10},{3... | collective-permute-start | bytes 294920 | tf_op jit(solution)/shard_map/ppermute | solution.py:340
  35.2 1.3 %collective-permute-start.2 = (bf16[2,192,128]{2,1,0:T(8,128)(2,1)S(1)}, bf16[2,192,128]{2,1,0:T(8,128)(2,1)S(1)}, u32[]{:S(2)}, u32[]{:S(2)}) collective-permute-start(bf16[2,192,128]{2,1,0:T(8,128)(2,1)S(1)} %get-tuple-element.8), channel_id=1, source_target_pairs={{8,16},{16,8},{24,0},{9,17},{17,9},{25,1},{10,18},{18,10},{26,2},{... | collective-permute-start | bytes 294920 | tf_op jit(solution)/shard_map/ppermute | solution.py:340
  36.5 0.0 copy-start.1
  36.5 3.0 %collective-permute-start.3 = (bf16[2,192,128]{2,1,0:T(8,128)(2,1)S(1)}, bf16[2,192,128]{2,1,0:T(8,128)(2,1)S(1)}, u32[]{:S(2)}, u32[]{:S(2)}) collective-permute-start(bf16[2,192,128]{2,1,0:T(8,128)(2,1)S(1)} %get-tuple-element.9), channel_id=1, source_target_pairs={{0,8},{8,0},{24,16},{1,9},{9,1},{25,17},{2,10},{10,2},{26,18},{3,1... | collective-permute-start | bytes 294920 | tf_op jit(solution)/shard_map/ppermute | solution.py:340
  39.5 0.0 collective-permute-done.1.hand_ref
  39.5 0.8 %cache.1.after_ref.begun_hbm = bf16[1,2,192,512]{3,2,1,0:T(8,128)(2,1)} custom-call(bf16[768,384]{1,0:T(8,128)(2,1)S(1)} %bitcast.5, bf16[2,192,128]{2,1,0:T(8,128)(2,1)S(1)} %collective-permute-done.1.hand_ref), custom_call_target="tpu_custom_call" | custom-call | bytes 1081344 | tf_op jit(solution)/shard_map/cache/pallas_call | solution.py:269
  40.3 0.0 all-to-all-done.1
  40.4 0.0 copy-done.1
  40.4 0.8 %update.1.after_ref = bf16[1,24,4096]{2,1,0:T(8,128)(2,1)} custom-call(bf16[768,128]{1,0:T(8,128)(2,1)S(1)} %bitcast.6, bf16[32,4096]{1,0:T(8,128)(2,1)S(1)} %collective-permute-done.after_ref.moved_ref, bf16[24,4096]{1,0:T(8,128)(2,1)S(1)} %copy-done.1, bf16[1,2,192,512]{3,2,1,0:T(8,128)(2,1)} %cache.1.after_ref.begun_hbm), custom_call_target="tpu_custom_call" | custom-call | bytes 1245184 | tf_op jit(solution)/shard_map/update/pallas_call | solution.py:269
  41.2 0.6 %collective-permute-done.2.refs_0_ = bf16[2,192,128]{2,1,0:T(8,128)(2,1)S(1)} collective-permute-done((bf16[2,192,128]{2,1,0:T(8,128)(2,1)S(1)}, bf16[2,192,128]{2,1,0:T(8,128)(2,1)S(1)}, u32[]{:S(2)}, u32[]{:S(2)}) %collective-permute-start.2) | collective-permute-done | bytes 98336 | tf_op jit(solution)/shard_map/ppermute | solution.py:340
  41.8 0.0 collective-permute-done.3.refs_1_
  41.8 0.7 %cache_rest.1 = bf16[1,2,192,512]{3,2,1,0:T(8,128)(2,1)} custom-call(bf16[1,2,192,512]{3,2,1,0:T(8,128)(2,1)} %cache.1.after_ref.begun_hbm, bf16[1,24,4096]{2,1,0:T(8,128)(2,1)} %update.1.after_ref, bf16[2,192,128]{2,1,0:T(8,128)(2,1)S(1)} %collective-permute-done.2.refs_0_, ...), custom_call_target="tpu_custom_call", output_to_operand_aliasing={{}: (0, {})} | custom-call | bytes 1179648 | tf_op jit(solution)/shard_map/cache_rest/pallas_call | solution.py:269
Async XLA Ops:
  2.6 8.0 %copy-start = (bf16[1,24,4096]{2,1,0:T(8,128)(2,1)S(1)}, bf16[1,24,4096]{2,1,0:T(8,128)(2,1)}, u32[]{:S(2)}) copy-start(bf16[1,24,4096]{2,1,0:T(8,128)(2,1)} %h_ref.1) | copy-start | bytes 589828
  2.6 24.6 %all-to-all-start = ((bf16[32,24,384]{2,1,0:T(8,128)(2,1)}), bf16[32,24,384]{2,1,0:T(8,128)(2,1)S(1)}, u32[]{:S(2)}, u32[]{:S(2)}) async-start(bf16[32,24,384]{2,1,0:T(8,128)(2,1)} %bitcast.7), calls=%async_computation | async-start | bytes 1179648 | tf_op jit(solution)/shard_map/all_to_all | solution.py:310
  10.6 16.7 %copy-start.2 = (s32[4,4]{1,0:T(4,128)S(1)}, s32[4,4]{1,0:T(4,128)}, u32[]{:S(2)}) copy-start(s32[4,4]{1,0:T(4,128)} %pattern_ref.1) | copy-start | bytes 196
  11.6 3.4 %collective-permute-start = (bf16[32,4096]{1,0:T(8,128)(2,1)S(1)}, bf16[32,4096]{1,0:T(8,128)(2,1)S(1)}, u32[]{:S(2)}, u32[]{:S(2)}) collective-permute-start(bf16[32,4096]{1,0:T(8,128)(2,1)S(1)} %residual.1), channel_id=1, source_target_pairs={{8,0},{16,8},{24,16},{9,1},{17,9},{25,17},{10,2},{18,10},{26,18},{... | collective-permute-start | bytes 786440 | tf_op jit(solution)/shard_map/ppermute | solution.py:21
  28.8 11.6 %all-to-all-start.1 = ((bf16[32,24,128]{2,1,0:T(8,128)(2,1)}), bf16[32,24,128]{2,1,0:T(8,128)(2,1)S(1)}, u32[]{:S(2)}, u32[]{:S(2)}) async-start(bf16[32,24,128]{2,1,0:T(8,128)(2,1)} %bitcast.8), calls=%async_computation.1 | async-start | bytes 393216 | tf_op jit(solution)/shard_map/all_to_all | solution.py:336
  31.5 8.0 %collective-permute-start.1 = (bf16[2,192,128]{2,1,0:T(8,128)(2,1)S(1)}, bf16[2,192,128]{2,1,0:T(8,128)(2,1)S(1)}, u32[]{:S(2)}, u32[]{:S(2)}) collective-permute-start(bf16[2,192,128]{2,1,0:T(8,128)(2,1)S(1)} %get-tuple-element.7), channel_id=1, source_target_pairs={{0,16},{16,0},{24,8},{1,17},{17,1},{25,9},{2,18},{18,2},{26,10},{3... | collective-permute-start | bytes 294920 | tf_op jit(solution)/shard_map/ppermute | solution.py:340
  35.2 6.6 %collective-permute-start.2 = (bf16[2,192,128]{2,1,0:T(8,128)(2,1)S(1)}, bf16[2,192,128]{2,1,0:T(8,128)(2,1)S(1)}, u32[]{:S(2)}, u32[]{:S(2)}) collective-permute-start(bf16[2,192,128]{2,1,0:T(8,128)(2,1)S(1)} %get-tuple-element.8), channel_id=1, source_target_pairs={{8,16},{16,8},{24,0},{9,17},{17,9},{25,1},{10,18},{18,10},{26,2},{... | collective-permute-start | bytes 294920 | tf_op jit(solution)/shard_map/ppermute | solution.py:340
  36.5 3.9 %copy-start.1 = (bf16[24,4096]{1,0:T(8,128)(2,1)S(1)}, bf16[24,4096]{1,0:T(8,128)(2,1)}, u32[]{:S(2)}) copy-start(bf16[24,4096]{1,0:T(8,128)(2,1)} %fresh_ref.1) | copy-start | bytes 589828
  36.5 5.3 %collective-permute-start.3 = (bf16[2,192,128]{2,1,0:T(8,128)(2,1)S(1)}, bf16[2,192,128]{2,1,0:T(8,128)(2,1)S(1)}, u32[]{:S(2)}, u32[]{:S(2)}) collective-permute-start(bf16[2,192,128]{2,1,0:T(8,128)(2,1)S(1)} %get-tuple-element.9), channel_id=1, source_target_pairs={{0,8},{8,0},{24,16},{1,9},{9,1},{25,17},{2,10},{10,2},{26,18},{3,1... | collective-permute-start | bytes 294920 | tf_op jit(solution)/shard_map/ppermute | solution.py:340

commit v19 on v18

--- a/solution.py
+++ b/solution.py
@@ -97,12 +97,12 @@
     out_ref[...] = jnp.concatenate([h_ref[0].astype(jnp.float32), parts], axis=0).astype(jnp.bfloat16)
 
 
-def partner(here, distance, groups):
-    return here ^ distance if groups & (groups - 1) == 0 else (here + groups - distance) % groups
-
-
-def distances(groups):
-    return sorted(range(1, groups), key=lambda distance: (distance < groups // 2, distance))
+def rounds(groups):
+    half = groups // 2
+    far, near = range(half, groups), range(1, half)
+    upper, lower, every = range(half, groups), range(half), range(groups)
+    plan = [(d, upper) for d in far] + [(d, every) for d in near] + [(d, lower) for d in far]
+    return [(d, [(t, t ^ d) for t in senders if t ^ d < groups - 1]) for d, senders in plan]
 
 
 def hand_over(group, x_ref, out_ref, lanes=slice(None)):
@@ -194,44 +194,51 @@
                 if last:
                     send(waiting)
                 waiting -= 1
-    for distance, hand_ref in zip(distances(groups), hand_refs):
-        hand_over(lax.rem(partner(here, distance, groups) + 1, groups), x_ref, hand_ref)
+    for distance, hand_ref in enumerate(hand_refs, 1):
+        hand_over(lax.rem((here ^ distance) + 1, groups), x_ref, hand_ref)
     for copy in copies:
         copy.wait()
 
 
-def lanes_of(distance, groups, here, wide):
-    source = partner(here, groups - distance if groups & (groups - 1) else distance, groups)
+def lanes_of(source, wide):
     return pl.ds(pl.multiple_of(source * wide, wide), wide)
+
+
+def taking(here, sends):
+    return functools.reduce(jnp.logical_or, [here == target for _, target in sends])
 
 
 def cache_kernel(groups, x_ref, hand_ref, out_ref):
     wide = x_ref.shape[1] // 3
     here = lax.axis_index("tm")
+    distance, sends = rounds(groups)[0]
     out_ref[...] = jnp.zeros_like(out_ref)
 
     @pl.when(here < groups - 1)
-    def place():
-        hand_over(here + 1, x_ref, out_ref.at[0], lanes_of(0, groups, here, wide))
-        out_ref[0, :, :, lanes_of(distances(groups)[0], groups, here, wide)] = hand_ref[...]
+    def place_own():
+        hand_over(here + 1, x_ref, out_ref.at[0], lanes_of(here, wide))
+
+    @pl.when(taking(here, sends))
+    def place_first():
+        out_ref[0, :, :, lanes_of(here ^ distance, wide)] = hand_ref[...]
 
 
 def cache_rest_kernel(groups, begun_hbm, after_ref, *refs):
     *hand_refs, out_hbm, sems = refs
     here = lax.axis_index("tm")
-
-    @pl.when(here < groups - 1)
-    def place():
-        copies = [
+    copies = [
+        (
+            taking(here, sends),
             pltpu.make_async_copy(
-                block, out_hbm.at[0, :, :, lanes_of(distance, groups, here, block.shape[2])], sems.at[index]
-            )
-            for index, (distance, block) in enumerate(zip(distances(groups)[1:], hand_refs))
-        ]
-        for copy in copies:
-            copy.start()
-        for copy in copies:
-            copy.wait()
+                block, out_hbm.at[0, :, :, lanes_of(here ^ distance, block.shape[2])], sems.at[index]
+            ),
+        )
+        for index, ((distance, sends), block) in enumerate(zip(rounds(groups)[1:], hand_refs))
+    ]
+    for taken, copy in copies:
+        pl.when(taken)(copy.start)
+    for taken, copy in copies:
+        pl.when(taken)(copy.wait)
 
 
 def update_kernel(seq_count, tm_count, att_ref, moved_ref, fresh_ref, after_ref, out_ref):
@@ -334,10 +341,7 @@
         scratch=[VMEM((tm_count - 1, group_tok, wide), kind), DMA((tm_count,))],
     )
     returned = exchange(attended)
-    handed = []
-    for distance, hand in zip(distances(tm_count), hands):
-        route = [(i, partner(i, distance, tm_count)) for i in range(tm_count)]
-        handed.append(lax.ppermute(hand, "tm", [(i, j) for i, j in route if j < tm_count - 1]))
+    handed = [lax.ppermute(hands[distance - 1], "tm", sends) for distance, sends in rounds(tm_count)]
 
     first, *rest = handed
     begun = run(
@@ -441,7 +445,7 @@
     tm_count, seq_count = lax.axis_size("tm"), lax.axis_size("seq")
     _, tok, width = queries.shape
     count = tm_count * seq_count
-    even = width % (count * HD) == 0 and tok % 8 == 0 and seq_count % 4 == 0 and tm_count > 2
+    even = width % (count * HD) == 0 and tok % 8 == 0 and seq_count % 4 == 0 and tm_count > 2 and tm_count & (tm_count - 1) == 0
     return (spread_body if even else gather_body)(queries, *others)
 
 

time: 42.9 us -> 47.9 us (1.12)
  the two profiles are of different devices: /device:TPU:0 before, /device:TPU:1 now
where the time goes in v19:
time: 47.9 us; the launch traced here: 47.4 us
  starting transfers between devices  23.6 us (49%)
  waiting for transfers between devices  15.6 us (33%)
  Pallas kernels  6.83 us (14%)
  between operations  1.41 us (3%)
    ppermute x5, starting transfers between devices, spread_body(): lax.ppermute(hands[distance - 1], 'tm', sends)  10.7 us
    ppermute x1, waiting for transfers between devices, shifted(): return lax.ppermute(block, axis, route)  8.06 us
    all_to_all x1, starting transfers between devices, spread_body(): exchanged = exchange(packed)  7.1 us
    pallas_call x6, Pallas kernels, run(): pl.pallas_call(kernel, out_shape=outs, in_specs=specs, out_specs=[whole(g...  6.83 us
    all_to_all x1, waiting for transfers between devices, spread_body(): exchanged = exchange(packed)  4.48 us
    all_to_all x1, starting transfers between devices, spread_body(): returned = exchange(attended)  3.58 us
    ppermute x5, waiting for transfers between devices, spread_body(): lax.ppermute(hands[distance - 1], 'tm', sends)  3.04 us
    ppermute x1, starting transfers between devices, shifted(): return lax.ppermute(block, axis, route)  2.17 us
  transfers between devices with their start and end apart: 8, of which 3 were waited for; matrix products, arithmetic and copies ran while one was open for 0% of the time, Pallas kernels for 5%

profile of v19, /device:TPU:1, one launch (start us, length us, event | category | flops | bytes accessed | tf_op | source)
XLA Modules:
  0.0 47.4 jit_solution(10362078217701005919)
XLA Ops:
  0.6 2.0 %pack.1.after_ref = bf16[768,384]{1,0:T(8,128)(2,1)} custom-call(bf16[1,24,4096]{2,1,0:T(8,128)(2,1)} %q_hbm.1, bf16[1,24,4096]{2,1,0:T(8,128)(2,1)} %k_hbm.1, bf16[1,24,4096]{2,1,0:T(8,128)(2,1)} %v_hbm.1), custom_call_target="tpu_custom_call" | custom-call | bytes 1179648 | tf_op jit(solution)/shard_map/pack/pallas_call | solution.py:276
  2.6 0.0 copy-start
  2.6 7.1 %all-to-all-start = ((bf16[32,24,384]{2,1,0:T(8,128)(2,1)}), bf16[32,24,384]{2,1,0:T(8,128)(2,1)S(1)}, u32[]{:S(2)}, u32[]{:S(2)}) async-start(bf16[32,24,384]{2,1,0:T(8,128)(2,1)} %bitcast.7), calls=%async_computation | async-start | bytes 1179648 | tf_op jit(solution)/shard_map/all_to_all | solution.py:317
  10.4 0.0 copy-done
  10.4 0.0 copy-start.2
  10.4 1.0 %residual.1 = bf16[32,4096]{1,0:T(8,128)(2,1)S(1)} custom-call(s32[1]{0:T(128)S(6)} %copy.12.noise_ref, bf16[1,24,4096]{2,1,0:T(8,128)(2,1)S(1)} %copy-done, f32[50,4096]{1,0:T(8,128)} %gate_hbm.1, bf16[768,384]{1,0:T(8,128)(2,1)} %pack.1.after_ref), custom_call_target="tpu_custom_call" | custom-call | bytes 1867780 | tf_op jit(solution)/shard_map/residual/pallas_call | solution.py:276
  11.4 2.2 %collective-permute-start = (bf16[32,4096]{1,0:T(8,128)(2,1)S(1)}, bf16[32,4096]{1,0:T(8,128)(2,1)S(1)}, u32[]{:S(2)}, u32[]{:S(2)}) collective-permute-start(bf16[32,4096]{1,0:T(8,128)(2,1)S(1)} %residual.1), channel_id=1, source_target_pairs={{8,0},{16,8},{24,16},{9,1},{17,9},{25,17},{10,2},{18,10},{26,18},{... | collective-permute-start | bytes 786440 | tf_op jit(solution)/shard_map/ppermute | solution.py:21
  13.6 8.1 %collective-permute-done.after_ref.moved_ref = bf16[32,4096]{1,0:T(8,128)(2,1)S(1)} collective-permute-done((bf16[32,4096]{1,0:T(8,128)(2,1)S(1)}, bf16[32,4096]{1,0:T(8,128)(2,1)S(1)}, u32[]{:S(2)}, u32[]{:S(2)}) %collective-permute-start) | collective-permute-done | bytes 262176 | tf_op jit(solution)/shard_map/ppermute | solution.py:21
  21.7 4.5 %all-to-all-done = bf16[32,24,384]{2,1,0:T(8,128)(2,1)S(1)} async-done(((bf16[32,24,384]{2,1,0:T(8,128)(2,1)}), bf16[32,24,384]{2,1,0:T(8,128)(2,1)S(1)}, u32[]{:S(2)}, u32[]{:S(2)}) %all-to-all-start) | async-done | bytes 589856 | tf_op jit(solution)/shard_map/all_to_all | solution.py:317
  26.1 0.0 copy-done.2
  26.1 1.6 %attend.1 = (bf16[768,128]{1,0:T(8,128)(2,1)}, bf16[2,192,128]{2,1,0:T(8,128)(2,1)S(1)}, bf16[2,192,128]{2,1,0:T(8,128)(2,1)S(1)}, bf16[2,192,128]{2,1,0:T(8,128)(2,1)S(1)}) custom-call(s32[4,4]{1,0:T(4,128)S(1)} %copy-done.2, bf16[768,384]{1,0:T(8,128)(2,1)S(1)} %bitcast.4, bf16[32,4096]{1,0:T(8,128)(2,1)S(1)} %collective-permute-done.after_ref.moved_ref), custom_call_target="tpu_custom_call" | custom-call | flops 150994944 | bytes 1343552 | tf_op jit(solution)/shard_map/attend/pallas_call | solution.py:276
  27.7 3.6 %all-to-all-start.1 = ((bf16[32,24,128]{2,1,0:T(8,128)(2,1)}), bf16[32,24,128]{2,1,0:T(8,128)(2,1)S(1)}, u32[]{:S(2)}, u32[]{:S(2)}) async-start(bf16[32,24,128]{2,1,0:T(8,128)(2,1)} %bitcast.8), calls=%async_computation.1 | async-start | bytes 393216 | tf_op jit(solution)/shard_map/all_to_all | solution.py:343
  31.3 1.3 %collective-permute-start.1 = (bf16[2,192,128]{2,1,0:T(8,128)(2,1)S(1)}, bf16[2,192,128]{2,1,0:T(8,128)(2,1)S(1)}, u32[]{:S(2)}, u32[]{:S(2)}) collective-permute-start(bf16[2,192,128]{2,1,0:T(8,128)(2,1)S(1)} %get-tuple-element.7), channel_id=1, source_target_pairs={{16,0},{24,8},{17,1},{25,9},{18,2},{26,10},{19,3},{27,11},{20,4},{... | collective-permute-start | bytes 294920 | tf_op jit(solution)/shard_map/ppermute | solution.py:344
  32.6 0.7 %collective-permute-start.4 = (bf16[2,192,128]{2,1,0:T(8,128)(2,1)S(1)}, bf16[2,192,128]{2,1,0:T(8,128)(2,1)S(1)}, u32[]{:S(2)}, u32[]{:S(2)}) collective-permute-start(bf16[2,192,128]{2,1,0:T(8,128)(2,1)S(1)} %get-tuple-element.7), channel_id=1, source_target_pairs={{0,16},{1,17},{2,18},{3,19},{4,20},{5,21},{6,22},{7,23}} | collective-permute-start | bytes 294920 | tf_op jit(solution)/shard_map/ppermute | solution.py:344
  33.3 6.1 %collective-permute-start.3 = (bf16[2,192,128]{2,1,0:T(8,128)(2,1)S(1)}, bf16[2,192,128]{2,1,0:T(8,128)(2,1)S(1)}, u32[]{:S(2)}, u32[]{:S(2)}) collective-permute-start(bf16[2,192,128]{2,1,0:T(8,128)(2,1)S(1)} %get-tuple-element.9), channel_id=1, source_target_pairs={{0,8},{8,0},{24,16},{1,9},{9,1},{25,17},{2,10},{10,2},{26,18},{3,1... | collective-permute-start | bytes 294920 | tf_op jit(solution)/shard_map/ppermute | solution.py:344
  39.3 0.0 copy-start.1
  39.3 1.4 %collective-permute-start.5 = (bf16[2,192,128]{2,1,0:T(8,128)(2,1)S(1)}, bf16[2,192,128]{2,1,0:T(8,128)(2,1)S(1)}, u32[]{:S(2)}, u32[]{:S(2)}) collective-permute-start(bf16[2,192,128]{2,1,0:T(8,128)(2,1)S(1)} %get-tuple-element.8), channel_id=1, source_target_pairs={{8,16},{9,17},{10,18},{11,19},{12,20},{13,21},{14,22},{15,23}} | collective-permute-start | bytes 294920 | tf_op jit(solution)/shard_map/ppermute | solution.py:344
  40.8 1.3 %collective-permute-start.2 = (bf16[2,192,128]{2,1,0:T(8,128)(2,1)S(1)}, bf16[2,192,128]{2,1,0:T(8,128)(2,1)S(1)}, u32[]{:S(2)}, u32[]{:S(2)}) collective-permute-start(bf16[2,192,128]{2,1,0:T(8,128)(2,1)S(1)} %get-tuple-element.8), channel_id=1, source_target_pairs={{16,8},{24,0},{17,9},{25,1},{18,10},{26,2},{19,11},{27,3},{20,12},... | collective-permute-start | bytes 294920 | tf_op jit(solution)/shard_map/ppermute | solution.py:344
  42.1 0.0 collective-permute-done.1.hand_ref
  42.1 0.8 %cache.1.after_ref.begun_hbm = bf16[1,2,192,512]{3,2,1,0:T(8,128)(2,1)} custom-call(bf16[768,384]{1,0:T(8,128)(2,1)S(1)} %bitcast.5, bf16[2,192,128]{2,1,0:T(8,128)(2,1)S(1)} %collective-permute-done.1.hand_ref), custom_call_target="tpu_custom_call" | custom-call | bytes 1081344 | tf_op jit(solution)/shard_map/cache/pallas_call | solution.py:276
  42.9 0.0 all-to-all-done.1
  42.9 0.0 copy-done.1
  42.9 0.8 %update.1.after_ref = bf16[1,24,4096]{2,1,0:T(8,128)(2,1)} custom-call(bf16[768,128]{1,0:T(8,128)(2,1)S(1)} %bitcast.6, bf16[32,4096]{1,0:T(8,128)(2,1)S(1)} %collective-permute-done.after_ref.moved_ref, bf16[24,4096]{1,0:T(8,128)(2,1)S(1)} %copy-done.1, bf16[1,2,192,512]{3,2,1,0:T(8,128)(2,1)} %cache.1.after_ref.begun_hbm), custom_call_target="tpu_custom_call" | custom-call | bytes 1245184 | tf_op jit(solution)/shard_map/update/pallas_call | solution.py:276
  43.7 0.0 collective-permute-done.3.refs_1_
  43.7 0.0 collective-permute-done.4.refs_2_
  43.7 0.0 collective-permute-done.5.refs_3_
  43.7 3.0 %collective-permute-done.2.refs_0_ = bf16[2,192,128]{2,1,0:T(8,128)(2,1)S(1)} collective-permute-done((bf16[2,192,128]{2,1,0:T(8,128)(2,1)S(1)}, bf16[2,192,128]{2,1,0:T(8,128)(2,1)S(1)}, u32[]{:S(2)}, u32[]{:S(2)}) %collective-permute-start.2) | collective-permute-done | bytes 98336 | tf_op jit(solution)/shard_map/ppermute | solution.py:344
  46.7 0.7 %cache_rest.1 = bf16[1,2,192,512]{3,2,1,0:T(8,128)(2,1)} custom-call(bf16[1,2,192,512]{3,2,1,0:T(8,128)(2,1)} %cache.1.after_ref.begun_hbm, bf16[1,24,4096]{2,1,0:T(8,128)(2,1)} %update.1.after_ref, bf16[2,192,128]{2,1,0:T(8,128)(2,1)S(1)} %collective-permute-done.2.refs_0_, ...), custom_call_target="tpu_custom_call", output_to_operand_aliasing={{}: (0, {})} | custom-call | bytes 1376256 | tf_op jit(solution)/shard_map/cache_rest/pallas_call | solution.py:276
Async XLA Ops:
  2.6 7.8 %copy-start = (bf16[1,24,4096]{2,1,0:T(8,128)(2,1)S(1)}, bf16[1,24,4096]{2,1,0:T(8,128)(2,1)}, u32[]{:S(2)}) copy-start(bf16[1,24,4096]{2,1,0:T(8,128)(2,1)} %h_ref.1) | copy-start | bytes 589828
  2.6 23.5 %all-to-all-start = ((bf16[32,24,384]{2,1,0:T(8,128)(2,1)}), bf16[32,24,384]{2,1,0:T(8,128)(2,1)S(1)}, u32[]{:S(2)}, u32[]{:S(2)}) async-start(bf16[32,24,384]{2,1,0:T(8,128)(2,1)} %bitcast.7), calls=%async_computation | async-start | bytes 1179648 | tf_op jit(solution)/shard_map/all_to_all | solution.py:317
  10.4 15.7 %copy-start.2 = (s32[4,4]{1,0:T(4,128)S(1)}, s32[4,4]{1,0:T(4,128)}, u32[]{:S(2)}) copy-start(s32[4,4]{1,0:T(4,128)} %pattern_ref.1) | copy-start | bytes 196
  11.4 10.2 %collective-permute-start = (bf16[32,4096]{1,0:T(8,128)(2,1)S(1)}, bf16[32,4096]{1,0:T(8,128)(2,1)S(1)}, u32[]{:S(2)}, u32[]{:S(2)}) collective-permute-start(bf16[32,4096]{1,0:T(8,128)(2,1)S(1)} %residual.1), channel_id=1, source_target_pairs={{8,0},{16,8},{24,16},{9,1},{17,9},{25,17},{10,2},{18,10},{26,18},{... | collective-permute-start | bytes 786440 | tf_op jit(solution)/shard_map/ppermute | solution.py:21
  27.7 15.2 %all-to-all-start.1 = ((bf16[32,24,128]{2,1,0:T(8,128)(2,1)}), bf16[32,24,128]{2,1,0:T(8,128)(2,1)S(1)}, u32[]{:S(2)}, u32[]{:S(2)}) async-start(bf16[32,24,128]{2,1,0:T(8,128)(2,1)} %bitcast.8), calls=%async_computation.1 | async-start | bytes 393216 | tf_op jit(solution)/shard_map/all_to_all | solution.py:343
  31.3 10.8 %collective-permute-start.1 = (bf16[2,192,128]{2,1,0:T(8,128)(2,1)S(1)}, bf16[2,192,128]{2,1,0:T(8,128)(2,1)S(1)}, u32[]{:S(2)}, u32[]{:S(2)}) collective-permute-start(bf16[2,192,128]{2,1,0:T(8,128)(2,1)S(1)} %get-tuple-element.7), channel_id=1, source_target_pairs={{16,0},{24,8},{17,1},{25,9},{18,2},{26,10},{19,3},{27,11},{20,4},{... | collective-permute-start | bytes 294920 | tf_op jit(solution)/shard_map/ppermute | solution.py:344
  32.6 11.1 %collective-permute-start.4 = (bf16[2,192,128]{2,1,0:T(8,128)(2,1)S(1)}, bf16[2,192,128]{2,1,0:T(8,128)(2,1)S(1)}, u32[]{:S(2)}, u32[]{:S(2)}) collective-permute-start(bf16[2,192,128]{2,1,0:T(8,128)(2,1)S(1)} %get-tuple-element.7), channel_id=1, source_target_pairs={{0,16},{1,17},{2,18},{3,19},{4,20},{5,21},{6,22},{7,23}} | collective-permute-start | bytes 294920 | tf_op jit(solution)/shard_map/ppermute | solution.py:344
  33.3 10.4 %collective-permute-start.3 = (bf16[2,192,128]{2,1,0:T(8,128)(2,1)S(1)}, bf16[2,192,128]{2,1,0:T(8,128)(2,1)S(1)}, u32[]{:S(2)}, u32[]{:S(2)}) collective-permute-start(bf16[2,192,128]{2,1,0:T(8,128)(2,1)S(1)} %get-tuple-element.9), channel_id=1, source_target_pairs={{0,8},{8,0},{24,16},{1,9},{9,1},{25,17},{2,10},{10,2},{26,18},{3,1... | collective-permute-start | bytes 294920 | tf_op jit(solution)/shard_map/ppermute | solution.py:344
  39.3 3.6 %copy-start.1 = (bf16[24,4096]{1,0:T(8,128)(2,1)S(1)}, bf16[24,4096]{1,0:T(8,128)(2,1)}, u32[]{:S(2)}) copy-start(bf16[24,4096]{1,0:T(8,128)(2,1)} %fresh_ref.1) | copy-start | bytes 589828
  39.3 4.3 %collective-permute-start.5 = (bf16[2,192,128]{2,1,0:T(8,128)(2,1)S(1)}, bf16[2,192,128]{2,1,0:T(8,128)(2,1)S(1)}, u32[]{:S(2)}, u32[]{:S(2)}) collective-permute-start(bf16[2,192,128]{2,1,0:T(8,128)(2,1)S(1)} %get-tuple-element.8), channel_id=1, source_target_pairs={{8,16},{9,17},{10,18},{11,19},{12,20},{13,21},{14,22},{15,23}} | collective-permute-start | bytes 294920 | tf_op jit(solution)/shard_map/ppermute | solution.py:344
  40.8 5.9 %collective-permute-start.2 = (bf16[2,192,128]{2,1,0:T(8,128)(2,1)S(1)}, bf16[2,192,128]{2,1,0:T(8,128)(2,1)S(1)}, u32[]{:S(2)}, u32[]{:S(2)}) collective-permute-start(bf16[2,192,128]{2,1,0:T(8,128)(2,1)S(1)} %get-tuple-element.8), channel_id=1, source_target_pairs={{16,8},{24,0},{17,9},{25,1},{18,10},{26,2},{19,11},{27,3},{20,12},... | collective-permute-start | bytes 294920 | tf_op jit(solution)/shard_map/ppermute | solution.py:344

commit v20 on v15

--- a/solution.py
+++ b/solution.py
@@ -40,7 +40,7 @@
                     ref.at[0, :, columns], held.at[place, :, columns], in_sems.at[part, place]
                 )
             )
-            copies[-1].start()
+            copies[-1].start(priority=(len(copies) - 1) % 2)
     outs = []
     for part in range(parts):
         for place in range(3):
@@ -61,7 +61,7 @@
             outs.append(
                 pltpu.make_async_copy(block.at[rows], out_hbm.at[rows], out_sems.at[part, tm])
             )
-            outs[-1].start()
+            outs[-1].start(priority=(len(outs) - 1) % 2)
     for out in outs:
         out.wait()
 
@@ -145,7 +145,7 @@
                     held.at[group - 1], out_hbm.at[place * rows : (place + 1) * rows], sems.at[place]
                 )
             )
-            copies[-1].start()
+            copies[-1].start(priority=place % 2)
 
     def spread(row, fill):
         rest = across - row.shape[1]
@@ -228,8 +228,8 @@
             )
             for index, (distance, block) in enumerate(zip(distances(groups)[1:], hand_refs))
         ]
-        for copy in copies:
-            copy.start()
+        for index, copy in enumerate(copies):
+            copy.start(priority=index % 2)
         for copy in copies:
             copy.wait()
 

time: 42.7 us -> 42.8 us (level)
  no operation moved by 1% of the time
where the time goes in v20:
time: 42.8 us; the launch traced here: 42.3 us
  starting transfers between devices  19 us (44%)
  waiting for transfers between devices  15.1 us (35%)
  Pallas kernels  6.86 us (16%)
  between operations  1.38 us (3%)
    all_to_all x1, waiting for transfers between devices, spread_body(): exchanged = exchange(packed)  12.2 us
    ppermute x3, starting transfers between devices, spread_body(): lax.ppermute(hand, 'tm', [(i, j) for i, j in route if j < tm_count - 1])  7.75 us
    all_to_all x1, starting transfers between devices, spread_body(): exchanged = exchange(packed)  7.3 us
    pallas_call x6, Pallas kernels, run(): pl.pallas_call(kernel, out_shape=outs, in_specs=specs, out_specs=[whole(g...  6.86 us
    all_to_all x1, starting transfers between devices, spread_body(): returned = exchange(attended)  2.68 us
    ppermute x1, waiting for transfers between devices, shifted(): return lax.ppermute(block, axis, route)  2.13 us
    ppermute x1, starting transfers between devices, shifted(): return lax.ppermute(block, axis, route)  1.29 us
  transfers between devices with their start and end apart: 6, of which 4 were waited for; matrix products, arithmetic and copies ran while one was open for 0% of the time, Pallas kernels for 6%

profile of v20, /device:TPU:0, one launch (start us, length us, event | category | flops | bytes accessed | tf_op | source)
XLA Modules:
  0.0 42.3 jit_solution(11332935511558440420)
XLA Ops:
  0.6 2.0 %pack.1.after_ref = bf16[768,384]{1,0:T(8,128)(2,1)} custom-call(bf16[1,24,4096]{2,1,0:T(8,128)(2,1)} %q_hbm.1, bf16[1,24,4096]{2,1,0:T(8,128)(2,1)} %k_hbm.1, bf16[1,24,4096]{2,1,0:T(8,128)(2,1)} %v_hbm.1), custom_call_target="tpu_custom_call" | custom-call | bytes 1179648 | tf_op jit(solution)/shard_map/pack/pallas_call | solution.py:269
  2.7 0.0 copy-start
  2.7 7.3 %all-to-all-start = ((bf16[32,24,384]{2,1,0:T(8,128)(2,1)}), bf16[32,24,384]{2,1,0:T(8,128)(2,1)S(1)}, u32[]{:S(2)}, u32[]{:S(2)}) async-start(bf16[32,24,384]{2,1,0:T(8,128)(2,1)} %bitcast.7), calls=%async_computation | async-start | bytes 1179648 | tf_op jit(solution)/shard_map/all_to_all | solution.py:310
  10.6 0.0 copy-done
  10.6 0.0 copy-start.2
  10.7 1.0 %residual.1 = bf16[32,4096]{1,0:T(8,128)(2,1)S(1)} custom-call(s32[1]{0:T(128)S(6)} %copy.12.noise_ref, bf16[1,24,4096]{2,1,0:T(8,128)(2,1)S(1)} %copy-done, f32[50,4096]{1,0:T(8,128)} %gate_hbm.1, bf16[768,384]{1,0:T(8,128)(2,1)} %pack.1.after_ref), custom_call_target="tpu_custom_call" | custom-call | bytes 1867780 | tf_op jit(solution)/shard_map/residual/pallas_call | solution.py:269
  11.7 1.3 %collective-permute-start = (bf16[32,4096]{1,0:T(8,128)(2,1)S(1)}, bf16[32,4096]{1,0:T(8,128)(2,1)S(1)}, u32[]{:S(2)}, u32[]{:S(2)}) collective-permute-start(bf16[32,4096]{1,0:T(8,128)(2,1)S(1)} %residual.1), channel_id=1, source_target_pairs={{8,0},{16,8},{24,16},{9,1},{17,9},{25,17},{10,2},{18,10},{26,18},{... | collective-permute-start | bytes 786440 | tf_op jit(solution)/shard_map/ppermute | solution.py:21
  13.0 2.1 %collective-permute-done.after_ref.moved_ref = bf16[32,4096]{1,0:T(8,128)(2,1)S(1)} collective-permute-done((bf16[32,4096]{1,0:T(8,128)(2,1)S(1)}, bf16[32,4096]{1,0:T(8,128)(2,1)S(1)}, u32[]{:S(2)}, u32[]{:S(2)}) %collective-permute-start) | collective-permute-done | bytes 262176 | tf_op jit(solution)/shard_map/ppermute | solution.py:21
  15.1 12.2 %all-to-all-done = bf16[32,24,384]{2,1,0:T(8,128)(2,1)S(1)} async-done(((bf16[32,24,384]{2,1,0:T(8,128)(2,1)}), bf16[32,24,384]{2,1,0:T(8,128)(2,1)S(1)}, u32[]{:S(2)}, u32[]{:S(2)}) %all-to-all-start) | async-done | bytes 589856 | tf_op jit(solution)/shard_map/all_to_all | solution.py:310
  27.3 0.0 copy-done.2
  27.3 1.6 %attend.1 = (bf16[768,128]{1,0:T(8,128)(2,1)}, bf16[2,192,128]{2,1,0:T(8,128)(2,1)S(1)}, bf16[2,192,128]{2,1,0:T(8,128)(2,1)S(1)}, bf16[2,192,128]{2,1,0:T(8,128)(2,1)S(1)}) custom-call(s32[4,4]{1,0:T(4,128)S(1)} %copy-done.2, bf16[768,384]{1,0:T(8,128)(2,1)S(1)} %bitcast.4, bf16[32,4096]{1,0:T(8,128)(2,1)S(1)} %collective-permute-done.after_ref.moved_ref), custom_call_target="tpu_custom_call" | custom-call | flops 150994944 | bytes 1343552 | tf_op jit(solution)/shard_map/attend/pallas_call | solution.py:269
  28.9 2.7 %all-to-all-start.1 = ((bf16[32,24,128]{2,1,0:T(8,128)(2,1)}), bf16[32,24,128]{2,1,0:T(8,128)(2,1)S(1)}, u32[]{:S(2)}, u32[]{:S(2)}) async-start(bf16[32,24,128]{2,1,0:T(8,128)(2,1)} %bitcast.8), calls=%async_computation.1 | async-start | bytes 393216 | tf_op jit(solution)/shard_map/all_to_all | solution.py:336
  31.5 1.3 %collective-permute-start.1 = (bf16[2,192,128]{2,1,0:T(8,128)(2,1)S(1)}, bf16[2,192,128]{2,1,0:T(8,128)(2,1)S(1)}, u32[]{:S(2)}, u32[]{:S(2)}) collective-permute-start(bf16[2,192,128]{2,1,0:T(8,128)(2,1)S(1)} %get-tuple-element.7), channel_id=1, source_target_pairs={{8,16},{16,8},{24,0},{9,17},{17,9},{25,1},{10,18},{18,10},{26,2},{... | collective-permute-start | bytes 294920 | tf_op jit(solution)/shard_map/ppermute | solution.py:340
  32.8 4.4 %collective-permute-start.2 = (bf16[2,192,128]{2,1,0:T(8,128)(2,1)S(1)}, bf16[2,192,128]{2,1,0:T(8,128)(2,1)S(1)}, u32[]{:S(2)}, u32[]{:S(2)}) collective-permute-start(bf16[2,192,128]{2,1,0:T(8,128)(2,1)S(1)} %get-tuple-element.8), channel_id=1, source_target_pairs={{0,16},{16,0},{24,8},{1,17},{17,1},{25,9},{2,18},{18,2},{26,10},{3... | collective-permute-start | bytes 294920 | tf_op jit(solution)/shard_map/ppermute | solution.py:340
  37.3 0.0 copy-start.1
  37.3 2.1 %collective-permute-start.3 = (bf16[2,192,128]{2,1,0:T(8,128)(2,1)S(1)}, bf16[2,192,128]{2,1,0:T(8,128)(2,1)S(1)}, u32[]{:S(2)}, u32[]{:S(2)}) collective-permute-start(bf16[2,192,128]{2,1,0:T(8,128)(2,1)S(1)} %get-tuple-element.9), channel_id=1, source_target_pairs={{0,8},{8,0},{24,16},{1,9},{9,1},{25,17},{2,10},{10,2},{26,18},{3,1... | collective-permute-start | bytes 294920 | tf_op jit(solution)/shard_map/ppermute | solution.py:340
  39.3 0.0 collective-permute-done.1.hand_ref
  39.4 0.8 %cache.1.after_ref.begun_hbm = bf16[1,2,192,512]{3,2,1,0:T(8,128)(2,1)} custom-call(bf16[768,384]{1,0:T(8,128)(2,1)S(1)} %bitcast.5, bf16[2,192,128]{2,1,0:T(8,128)(2,1)S(1)} %collective-permute-done.1.hand_ref), custom_call_target="tpu_custom_call" | custom-call | bytes 1081344 | tf_op jit(solution)/shard_map/cache/pallas_call | solution.py:269
  40.2 0.3 all-to-all-done.1
  40.4 0.0 copy-done.1
  40.4 0.8 %update.1.after_ref = bf16[1,24,4096]{2,1,0:T(8,128)(2,1)} custom-call(bf16[768,128]{1,0:T(8,128)(2,1)S(1)} %bitcast.6, bf16[32,4096]{1,0:T(8,128)(2,1)S(1)} %collective-permute-done.after_ref.moved_ref, bf16[24,4096]{1,0:T(8,128)(2,1)S(1)} %copy-done.1, bf16[1,2,192,512]{3,2,1,0:T(8,128)(2,1)} %cache.1.after_ref.begun_hbm), custom_call_target="tpu_custom_call" | custom-call | bytes 1245184 | tf_op jit(solution)/shard_map/update/pallas_call | solution.py:269
  41.2 0.4 %collective-permute-done.2.refs_0_ = bf16[2,192,128]{2,1,0:T(8,128)(2,1)S(1)} collective-permute-done((bf16[2,192,128]{2,1,0:T(8,128)(2,1)S(1)}, bf16[2,192,128]{2,1,0:T(8,128)(2,1)S(1)}, u32[]{:S(2)}, u32[]{:S(2)}) %collective-permute-start.2) | collective-permute-done | bytes 98336 | tf_op jit(solution)/shard_map/ppermute | solution.py:340
  41.6 0.0 collective-permute-done.3.refs_1_
  41.7 0.7 %cache_rest.1 = bf16[1,2,192,512]{3,2,1,0:T(8,128)(2,1)} custom-call(bf16[1,2,192,512]{3,2,1,0:T(8,128)(2,1)} %cache.1.after_ref.begun_hbm, bf16[1,24,4096]{2,1,0:T(8,128)(2,1)} %update.1.after_ref, bf16[2,192,128]{2,1,0:T(8,128)(2,1)S(1)} %collective-permute-done.2.refs_0_, ...), custom_call_target="tpu_custom_call", output_to_operand_aliasing={{}: (0, {})} | custom-call | bytes 1179648 | tf_op jit(solution)/shard_map/cache_rest/pallas_call | solution.py:269
Async XLA Ops:
  2.7 8.0 %copy-start = (bf16[1,24,4096]{2,1,0:T(8,128)(2,1)S(1)}, bf16[1,24,4096]{2,1,0:T(8,128)(2,1)}, u32[]{:S(2)}) copy-start(bf16[1,24,4096]{2,1,0:T(8,128)(2,1)} %h_ref.1) | copy-start | bytes 589828
  2.7 24.6 %all-to-all-start = ((bf16[32,24,384]{2,1,0:T(8,128)(2,1)}), bf16[32,24,384]{2,1,0:T(8,128)(2,1)S(1)}, u32[]{:S(2)}, u32[]{:S(2)}) async-start(bf16[32,24,384]{2,1,0:T(8,128)(2,1)} %bitcast.7), calls=%async_computation | async-start | bytes 1179648 | tf_op jit(solution)/shard_map/all_to_all | solution.py:310
  10.6 16.7 %copy-start.2 = (s32[4,4]{1,0:T(4,128)S(1)}, s32[4,4]{1,0:T(4,128)}, u32[]{:S(2)}) copy-start(s32[4,4]{1,0:T(4,128)} %pattern_ref.1) | copy-start | bytes 196
  11.7 3.4 %collective-permute-start = (bf16[32,4096]{1,0:T(8,128)(2,1)S(1)}, bf16[32,4096]{1,0:T(8,128)(2,1)S(1)}, u32[]{:S(2)}, u32[]{:S(2)}) collective-permute-start(bf16[32,4096]{1,0:T(8,128)(2,1)S(1)} %residual.1), channel_id=1, source_target_pairs={{8,0},{16,8},{24,16},{9,1},{17,9},{25,17},{10,2},{18,10},{26,18},{... | collective-permute-start | bytes 786440 | tf_op jit(solution)/shard_map/ppermute | solution.py:21
  28.9 11.6 %all-to-all-start.1 = ((bf16[32,24,128]{2,1,0:T(8,128)(2,1)}), bf16[32,24,128]{2,1,0:T(8,128)(2,1)S(1)}, u32[]{:S(2)}, u32[]{:S(2)}) async-start(bf16[32,24,128]{2,1,0:T(8,128)(2,1)} %bitcast.8), calls=%async_computation.1 | async-start | bytes 393216 | tf_op jit(solution)/shard_map/all_to_all | solution.py:336
  31.5 7.8 %collective-permute-start.1 = (bf16[2,192,128]{2,1,0:T(8,128)(2,1)S(1)}, bf16[2,192,128]{2,1,0:T(8,128)(2,1)S(1)}, u32[]{:S(2)}, u32[]{:S(2)}) collective-permute-start(bf16[2,192,128]{2,1,0:T(8,128)(2,1)S(1)} %get-tuple-element.7), channel_id=1, source_target_pairs={{8,16},{16,8},{24,0},{9,17},{17,9},{25,1},{10,18},{18,10},{26,2},{... | collective-permute-start | bytes 294920 | tf_op jit(solution)/shard_map/ppermute | solution.py:340
  32.8 8.8 %collective-permute-start.2 = (bf16[2,192,128]{2,1,0:T(8,128)(2,1)S(1)}, bf16[2,192,128]{2,1,0:T(8,128)(2,1)S(1)}, u32[]{:S(2)}, u32[]{:S(2)}) collective-permute-start(bf16[2,192,128]{2,1,0:T(8,128)(2,1)S(1)} %get-tuple-element.8), channel_id=1, source_target_pairs={{0,16},{16,0},{24,8},{1,17},{17,1},{25,9},{2,18},{18,2},{26,10},{3... | collective-permute-start | bytes 294920 | tf_op jit(solution)/shard_map/ppermute | solution.py:340
  37.3 3.2 %copy-start.1 = (bf16[24,4096]{1,0:T(8,128)(2,1)S(1)}, bf16[24,4096]{1,0:T(8,128)(2,1)}, u32[]{:S(2)}) copy-start(bf16[24,4096]{1,0:T(8,128)(2,1)} %fresh_ref.1) | copy-start | bytes 589828
  37.3 4.4 %collective-permute-start.3 = (bf16[2,192,128]{2,1,0:T(8,128)(2,1)S(1)}, bf16[2,192,128]{2,1,0:T(8,128)(2,1)S(1)}, u32[]{:S(2)}, u32[]{:S(2)}) collective-permute-start(bf16[2,192,128]{2,1,0:T(8,128)(2,1)S(1)} %get-tuple-element.9), channel_id=1, source_target_pairs={{0,8},{8,0},{24,16},{1,9},{9,1},{25,17},{2,10},{10,2},{26,18},{3,1... | collective-permute-start | bytes 294920 | tf_op jit(solution)/shard_map/ppermute | solution.py:340

commit v21 on v15

--- a/solution.py
+++ b/solution.py
@@ -25,16 +25,16 @@
     return (index + count // 2) % count
 
 
-def pack_kernel(seq_count, parts, q_hbm, k_hbm, v_hbm, out_hbm, held, block, in_sems, out_sems):
+def pack_kernel(seq_count, parts, k_hbm, v_hbm, q_hbm, kv_hbm, out_hbm, held, kv_block, q_block, in_sems, out_sems):
     tok, width = held.shape[1:]
-    wide = out_hbm.shape[1] // 3
+    wide = out_hbm.shape[1]
     count = out_hbm.shape[0] // tok
     tm_count = count // seq_count
     span, members = width // parts, seq_count // parts
     copies = []
     for part in range(parts):
         columns = slice(part * span, (part + 1) * span)
-        for place, ref in enumerate((q_hbm, k_hbm, v_hbm)):
+        for place, ref in enumerate((k_hbm, v_hbm, q_hbm)):
             copies.append(
                 pltpu.make_async_copy(
                     ref.at[0, :, columns], held.at[place, :, columns], in_sems.at[part, place]
@@ -48,20 +48,21 @@
         for tm in range(tm_count):
             for seq in range(part * members, (part + 1) * members, 2):
                 first = (tm * seq_count + mixed(seq, seq_count)) * tok
-                for place in range(3):
+                for place, (block, lane) in enumerate(((kv_block, 0), (kv_block, wide), (q_block, 0))):
                     rows = []
                     for member in (seq, seq + 1):
                         start = (member * tm_count + tm) * wide
                         rows.append(held[place, :, start : start + wide].astype(jnp.float32))
-                    block[first : first + 2 * tok, place * wide : (place + 1) * wide] = jnp.concatenate(
+                    block[first : first + 2 * tok, lane : lane + wide] = jnp.concatenate(
                         rows, axis=0
                     ).astype(jnp.bfloat16)
             first = (tm * seq_count + mixed(part * members, seq_count)) * tok
             rows = slice(first, first + members * tok)
-            outs.append(
-                pltpu.make_async_copy(block.at[rows], out_hbm.at[rows], out_sems.at[part, tm])
-            )
-            outs[-1].start()
+            for index, (block, to) in enumerate(((kv_block, kv_hbm), (q_block, out_hbm))):
+                outs.append(
+                    pltpu.make_async_copy(block.at[rows], to.at[rows], out_sems.at[part, tm, index])
+                )
+                outs[-1].start()
     for out in outs:
         out.wait()
 
@@ -106,24 +107,28 @@
 
 
 def hand_over(group, x_ref, out_ref, lanes=slice(None)):
-    wide = x_ref.shape[1] // 3
+    wide = x_ref.shape[1] // 2
     rows = out_ref.shape[1]
     half = rows // 2
     for part in range(2):
         first = pl.multiple_of(group * rows + mixed(part, 2) * half, half)
         for kind in range(2):
             out_ref[kind, part * half : (part + 1) * half, lanes] = x_ref[
-                pl.ds(first, half), (kind + 1) * wide : (kind + 2) * wide
+                pl.ds(first, half), kind * wide : (kind + 1) * wide
             ]
 
 
-def attend_kernel(groups, pattern_ref, x_ref, after_ref, out_hbm, *refs):
-    *hand_refs, held, sems = refs
+def hand_kernel(groups, x_ref, *hand_refs):
+    here = lax.axis_index("tm")
+    for distance, hand_ref in zip(distances(groups), hand_refs):
+        hand_over(lax.rem(partner(here, distance, groups) + 1, groups), x_ref, hand_ref)
+
+
+def attend_kernel(groups, pattern_ref, x_ref, q_ref, after_ref, out_hbm, held, sems):
     wide = held.shape[2]
     rows = held.shape[1]
     across = (groups - 1) * rows
     factor = math.log2(math.e) / math.sqrt(HD)
-    here = lax.axis_index("tm")
     lane = lax.broadcasted_iota(jnp.int32, (1, across), 1)
     ends, kept = [], []
     for source in range(groups):
@@ -153,14 +158,14 @@
 
     for head in range(0, wide, HD):
         query = jnp.concatenate(
-            [x_ref[group * rows : (group + 1) * rows, head : head + HD] for group in range(groups - 1, 0, -1)],
+            [q_ref[group * rows : (group + 1) * rows, head : head + HD] for group in range(groups - 1, 0, -1)],
             axis=0,
         )
         query = jnp.transpose(query)
-        value = jnp.transpose(x_ref[:, 2 * wide + head : 2 * wide + head + HD])
+        value = jnp.transpose(x_ref[:, wide + head : wide + head + HD])
         scores, highest = [], None
         for source in range(groups):
-            key = x_ref[source * rows : (source + 1) * rows, wide + head : wide + head + HD]
+            key = x_ref[source * rows : (source + 1) * rows, head : head + HD]
             scores.append(
                 jnp.dot(key, query[:, : ends[source]], preferred_element_type=jnp.float32)
             )
@@ -194,8 +199,6 @@
                 if last:
                     send(waiting)
                 waiting -= 1
-    for distance, hand_ref in zip(distances(groups), hand_refs):
-        hand_over(lax.rem(partner(here, distance, groups) + 1, groups), x_ref, hand_ref)
     for copy in copies:
         copy.wait()
 
@@ -206,7 +209,7 @@
 
 
 def cache_kernel(groups, x_ref, hand_ref, out_ref):
-    wide = x_ref.shape[1] // 3
+    wide = x_ref.shape[1] // 2
     here = lax.axis_index("tm")
     out_ref[...] = jnp.zeros_like(out_ref)
 
@@ -290,24 +293,26 @@
     DMA = pltpu.SemaphoreType.DMA
     parts = 4 if seq_count % 8 == 0 else 2
 
-    packed = run(
+    packed_kv, packed = run(
         functools.partial(pack_kernel, seq_count, parts),
         "pack",
-        [HBM((count * tok, 3 * wide), kind)],
+        [HBM((count * tok, 2 * wide), kind), HBM((count * tok, wide), kind)],
         [whole(HBM)] * 3,
-        [pltpu.with_memory_space_constraint(a, HBM) for a in (queries, keys_proj, values)],
+        [pltpu.with_memory_space_constraint(a, HBM) for a in (keys_proj, values, queries)],
         scratch=[
             VMEM((3, tok, width), kind),
-            VMEM((count * tok, 3 * wide), kind),
+            VMEM((count * tok, 2 * wide), kind),
+            VMEM((count * tok, wide), kind),
             DMA((parts, 3)),
-            DMA((parts, tm_count)),
+            DMA((parts, tm_count, 2)),
         ],
     )
     order = [tm * seq_count + mixed(s, seq_count) for tm in range(tm_count) for s in range(seq_count)]
     exchange = functools.partial(
         lax.all_to_all, axis_name=BOTH, split_axis=0, concat_axis=0, tiled=True, axis_index_groups=[order]
     )
-    exchanged = exchange(packed)
+    exchanged = exchange(packed_kv)
+    asked = exchange(packed)
 
     residual = run(
         residual_kernel,
@@ -324,12 +329,19 @@
     )
     moved = shifted(residual, "tm", -1)
 
-    attended, *hands = run(
+    hands = run(
+        functools.partial(hand_kernel, tm_count),
+        "hand",
+        [VMEM((2, group_tok, wide), kind)] * (tm_count - 1),
+        [whole()],
+        (exchanged,),
+    )
+    attended = run(
         functools.partial(attend_kernel, tm_count),
         "attend",
-        [HBM((count * tok, wide), kind)] + [VMEM((2, group_tok, wide), kind)] * (tm_count - 1),
-        [whole(), whole(), whole(pl.ANY)],
-        (pattern, exchanged, moved),
+        [HBM((count * tok, wide), kind)],
+        [whole(), whole(), whole(), whole(pl.ANY)],
+        (pattern, exchanged, asked, moved),
         flops=2 * count * tok * count * tok * wide,
         scratch=[VMEM((tm_count - 1, group_tok, wide), kind), DMA((tm_count,))],
     )

time: 42.7 us -> 50.3 us (1.18)
  blocking collectives: 0 us -> 16.2 us
  starting transfers between devices: 19 us -> 14.3 us
  waiting for transfers between devices: 15.1 us -> 10.9 us
    all_to_all x0 -> x1, blocking collectives: none -> 16.2 us  [spread_body(): asked = exchange(packed)]
    all_to_all x1, starting transfers between devices: 7.3 us -> 2.73 us  [spread_body(): exchanged = exchange(packed_kv)]
    all_to_all x1, waiting for transfers between devices: 12.2 us -> 7.97 us  [spread_body(): exchanged = exchange(packed_kv)]
    pallas_call x6 -> x7, Pallas kernels: 6.81 us -> 7 us  [run(): pl.pallas_call(kernel, out_shape=outs, in_specs=specs, out_specs=[whole(g...]
  transfers between devices with their start and end apart: 6 -> 6, of which waited for: 4 -> 5; matrix products, arithmetic and copies ran while one was open for 0% -> 0% of each run, Pallas kernels for 6% -> 5%
where the time goes in v21:
time: 50.3 us; the launch traced here: 49.8 us
  blocking collectives  16.2 us (32%)
  starting transfers between devices  14.3 us (28%)
  waiting for transfers between devices  10.9 us (22%)
  Pallas kernels  7 us (14%)
  between operations  1.39 us (3%)
    all_to_all x1, blocking collectives, spread_body(): asked = exchange(packed)  16.2 us
    all_to_all x1, waiting for transfers between devices, spread_body(): exchanged = exchange(packed_kv)  7.97 us
    ppermute x3, starting transfers between devices, spread_body(): lax.ppermute(hand, 'tm', [(i, j) for i, j in route if j < tm_count - 1])  7.73 us
    pallas_call x7, Pallas kernels, run(): pl.pallas_call(kernel, out_shape=outs, in_specs=specs, out_specs=[whole(g...  7 us
    all_to_all x1, starting transfers between devices, spread_body(): exchanged = exchange(packed_kv)  2.73 us
    all_to_all x1, starting transfers between devices, spread_body(): returned = exchange(attended)  2.6 us
    ppermute x1, waiting for transfers between devices, shifted(): return lax.ppermute(block, axis, route)  2.13 us
    ppermute x1, starting transfers between devices, shifted(): return lax.ppermute(block, axis, route)  1.29 us
  transfers between devices with their start and end apart: 6, of which 5 were waited for; matrix products, arithmetic and copies ran while one was open for 0% of the time, Pallas kernels for 5%

profile of v21, /device:TPU:0, one launch (start us, length us, event | category | flops | bytes accessed | tf_op | source)
XLA Modules:
  0.0 49.8 jit_solution(4521177329803015357)
XLA Ops:
  0.6 2.1 %pack.1 = (bf16[768,256]{1,0:T(8,128)(2,1)}, bf16[768,128]{1,0:T(8,128)(2,1)}) custom-call(bf16[1,24,4096]{2,1,0:T(8,128)(2,1)} %k_hbm.1, bf16[1,24,4096]{2,1,0:T(8,128)(2,1)} %v_hbm.1, bf16[1,24,4096]{2,1,0:T(8,128)(2,1)} %q_hbm.1), custom_call_target="tpu_custom_call" | custom-call | bytes 1179648 | tf_op jit(solution)/shard_map/pack/pallas_call | solution.py:272
  2.7 16.2 %all_to_all.33 = bf16[32,24,128]{2,1,0:T(8,128)(2,1)S(1)} all-to-all(bf16[32,24,128]{2,1,0:T(8,128)(2,1)} %bitcast.12), channel_id=1, replica_groups={{4,5,6,7,0,1,2,3,12,13,14,15,8,9,10,11,20,21,22,23,16,17,18,19,28,29,30..., dimensions={0} | all-to-all | bytes 393216 | tf_op jit(solution)/shard_map/all_to_all | solution.py:315
  18.9 0.0 copy-start.1
  18.9 2.7 %all-to-all-start = ((bf16[32,24,256]{2,1,0:T(8,128)(2,1)}), bf16[32,24,256]{2,1,0:T(8,128)(2,1)S(1)}, u32[]{:S(2)}, u32[]{:S(2)}) async-start(bf16[32,24,256]{2,1,0:T(8,128)(2,1)} %bitcast), calls=%async_computation | async-start | bytes 786432 | tf_op jit(solution)/shard_map/all_to_all | solution.py:314
  22.3 0.0 copy-done.1
  22.3 1.0 %residual.1 = bf16[32,4096]{1,0:T(8,128)(2,1)S(1)} custom-call(s32[1]{0:T(128)S(6)} %copy.12.noise_ref, bf16[1,24,4096]{2,1,0:T(8,128)(2,1)S(1)} %copy-done.1, f32[50,4096]{1,0:T(8,128)} %gate_hbm.1, bf16[768,128]{1,0:T(8,128)(2,1)} %get-tuple-element.8.after_ref), custom_call_target="tpu_custom_call" | custom-call | bytes 1474564 | tf_op jit(solution)/shard_map/residual/pallas_call | solution.py:272
  23.4 0.0 copy-start.2
  23.4 1.3 %collective-permute-start = (bf16[32,4096]{1,0:T(8,128)(2,1)S(1)}, bf16[32,4096]{1,0:T(8,128)(2,1)S(1)}, u32[]{:S(2)}, u32[]{:S(2)}) collective-permute-start(bf16[32,4096]{1,0:T(8,128)(2,1)S(1)} %residual.1), channel_id=1, source_target_pairs={{8,0},{16,8},{24,16},{9,1},{17,9},{25,17},{10,2},{18,10},{26,18},{... | collective-permute-start | bytes 786440 | tf_op jit(solution)/shard_map/ppermute | solution.py:21
  24.7 2.1 %collective-permute-done.after_ref.moved_ref = bf16[32,4096]{1,0:T(8,128)(2,1)S(1)} collective-permute-done((bf16[32,4096]{1,0:T(8,128)(2,1)S(1)}, bf16[32,4096]{1,0:T(8,128)(2,1)S(1)}, u32[]{:S(2)}, u32[]{:S(2)}) %collective-permute-start) | collective-permute-done | bytes 262176 | tf_op jit(solution)/shard_map/ppermute | solution.py:21
  26.8 8.0 %all-to-all-done = bf16[32,24,256]{2,1,0:T(8,128)(2,1)S(1)} async-done(((bf16[32,24,256]{2,1,0:T(8,128)(2,1)}), bf16[32,24,256]{2,1,0:T(8,128)(2,1)S(1)}, u32[]{:S(2)}, u32[]{:S(2)}) %all-to-all-start) | async-done | bytes 393248 | tf_op jit(solution)/shard_map/all_to_all | solution.py:314
  34.8 0.0 copy-done.2
  34.8 1.6 %attend.1 = bf16[768,128]{1,0:T(8,128)(2,1)} custom-call(s32[4,4]{1,0:T(4,128)S(1)} %copy-done.2, bf16[768,256]{1,0:T(8,128)(2,1)S(1)} %bitcast.6, bf16[768,128]{1,0:T(8,128)(2,1)S(1)} %bitcast.10, bf16[32,4096]{1,0:T(8,128)(2,1)S(1)} %collective-permute-done.after_ref.moved_ref), custom_call_target="tpu_custom_call" | custom-call | flops 150994944 | bytes 1048640 | tf_op jit(solution)/shard_map/attend/pallas_call | solution.py:272
  36.3 2.6 %all-to-all-start.2 = ((bf16[32,24,128]{2,1,0:T(8,128)(2,1)}), bf16[32,24,128]{2,1,0:T(8,128)(2,1)S(1)}, u32[]{:S(2)}, u32[]{:S(2)}) async-start(bf16[32,24,128]{2,1,0:T(8,128)(2,1)} %bitcast.11), calls=%async_computation.2 | async-start | bytes 393216 | tf_op jit(solution)/shard_map/all_to_all | solution.py:348
  38.9 0.1 hand.1
  39.0 1.3 %collective-permute-start.1 = (bf16[2,192,128]{2,1,0:T(8,128)(2,1)S(1)}, bf16[2,192,128]{2,1,0:T(8,128)(2,1)S(1)}, u32[]{:S(2)}, u32[]{:S(2)}) collective-permute-start(bf16[2,192,128]{2,1,0:T(8,128)(2,1)S(1)} %get-tuple-element.9), channel_id=1, source_target_pairs={{8,16},{16,8},{24,0},{9,17},{17,9},{25,1},{10,18},{18,10},{26,2},{... | collective-permute-start | bytes 294920 | tf_op jit(solution)/shard_map/ppermute | solution.py:352
  40.3 4.4 %collective-permute-start.2 = (bf16[2,192,128]{2,1,0:T(8,128)(2,1)S(1)}, bf16[2,192,128]{2,1,0:T(8,128)(2,1)S(1)}, u32[]{:S(2)}, u32[]{:S(2)}) collective-permute-start(bf16[2,192,128]{2,1,0:T(8,128)(2,1)S(1)} %get-tuple-element.10), channel_id=1, source_target_pairs={{0,16},{16,0},{24,8},{1,17},{17,1},{25,9},{2,18},{18,2},{26,10},{3... | collective-permute-start | bytes 294920 | tf_op jit(solution)/shard_map/ppermute | solution.py:352
  44.7 0.0 copy-start
  44.7 2.1 %collective-permute-start.3 = (bf16[2,192,128]{2,1,0:T(8,128)(2,1)S(1)}, bf16[2,192,128]{2,1,0:T(8,128)(2,1)S(1)}, u32[]{:S(2)}, u32[]{:S(2)}) collective-permute-start(bf16[2,192,128]{2,1,0:T(8,128)(2,1)S(1)} %get-tuple-element.11), channel_id=1, source_target_pairs={{0,8},{8,0},{24,16},{1,9},{9,1},{25,17},{2,10},{10,2},{26,18},{3,1... | collective-permute-start | bytes 294920 | tf_op jit(solution)/shard_map/ppermute | solution.py:352
  46.8 0.1 collective-permute-done.1.hand_ref
  46.9 0.8 %cache.1.after_ref.begun_hbm = bf16[1,2,192,512]{3,2,1,0:T(8,128)(2,1)} custom-call(bf16[768,256]{1,0:T(8,128)(2,1)S(1)} %bitcast.8, bf16[2,192,128]{2,1,0:T(8,128)(2,1)S(1)} %collective-permute-done.1.hand_ref), custom_call_target="tpu_custom_call" | custom-call | bytes 884736 | tf_op jit(solution)/shard_map/cache/pallas_call | solution.py:272
  47.7 0.1 all-to-all-done.2
  47.8 0.0 copy-done
  47.8 0.8 %update.1.after_ref = bf16[1,24,4096]{2,1,0:T(8,128)(2,1)} custom-call(bf16[768,128]{1,0:T(8,128)(2,1)S(1)} %bitcast.9, bf16[32,4096]{1,0:T(8,128)(2,1)S(1)} %collective-permute-done.after_ref.moved_ref, bf16[24,4096]{1,0:T(8,128)(2,1)S(1)} %copy-done, bf16[1,2,192,512]{3,2,1,0:T(8,128)(2,1)} %cache.1.after_ref.begun_hbm), custom_call_target="tpu_custom_call" | custom-call | bytes 1245184 | tf_op jit(solution)/shard_map/update/pallas_call | solution.py:272
  48.6 0.6 %collective-permute-done.2.refs_0_ = bf16[2,192,128]{2,1,0:T(8,128)(2,1)S(1)} collective-permute-done((bf16[2,192,128]{2,1,0:T(8,128)(2,1)S(1)}, bf16[2,192,128]{2,1,0:T(8,128)(2,1)S(1)}, u32[]{:S(2)}, u32[]{:S(2)}) %collective-permute-start.2) | collective-permute-done | bytes 98336 | tf_op jit(solution)/shard_map/ppermute | solution.py:352
  49.1 0.0 collective-permute-done.3.refs_1_
  49.1 0.7 %cache_rest.1 = bf16[1,2,192,512]{3,2,1,0:T(8,128)(2,1)} custom-call(bf16[1,2,192,512]{3,2,1,0:T(8,128)(2,1)} %cache.1.after_ref.begun_hbm, bf16[1,24,4096]{2,1,0:T(8,128)(2,1)} %update.1.after_ref, bf16[2,192,128]{2,1,0:T(8,128)(2,1)S(1)} %collective-permute-done.2.refs_0_, ...), custom_call_target="tpu_custom_call", output_to_operand_aliasing={{}: (0, {})} | custom-call | bytes 1179648 | tf_op jit(solution)/shard_map/cache_rest/pallas_call | solution.py:272
Async XLA Ops:
  18.9 3.4 %copy-start.1 = (bf16[1,24,4096]{2,1,0:T(8,128)(2,1)S(1)}, bf16[1,24,4096]{2,1,0:T(8,128)(2,1)}, u32[]{:S(2)}) copy-start(bf16[1,24,4096]{2,1,0:T(8,128)(2,1)} %h_ref.1) | copy-start | bytes 589828
  18.9 15.8 %all-to-all-start = ((bf16[32,24,256]{2,1,0:T(8,128)(2,1)}), bf16[32,24,256]{2,1,0:T(8,128)(2,1)S(1)}, u32[]{:S(2)}, u32[]{:S(2)}) async-start(bf16[32,24,256]{2,1,0:T(8,128)(2,1)} %bitcast), calls=%async_computation | async-start | bytes 786432 | tf_op jit(solution)/shard_map/all_to_all | solution.py:314
  23.4 11.4 %copy-start.2 = (s32[4,4]{1,0:T(4,128)S(1)}, s32[4,4]{1,0:T(4,128)}, u32[]{:S(2)}) copy-start(s32[4,4]{1,0:T(4,128)} %pattern_ref.1) | copy-start | bytes 196
  23.4 3.4 %collective-permute-start = (bf16[32,4096]{1,0:T(8,128)(2,1)S(1)}, bf16[32,4096]{1,0:T(8,128)(2,1)S(1)}, u32[]{:S(2)}, u32[]{:S(2)}) collective-permute-start(bf16[32,4096]{1,0:T(8,128)(2,1)S(1)} %residual.1), channel_id=1, source_target_pairs={{8,0},{16,8},{24,16},{9,1},{17,9},{25,17},{10,2},{18,10},{26,18},{... | collective-permute-start | bytes 786440 | tf_op jit(solution)/shard_map/ppermute | solution.py:21
  36.3 11.5 %all-to-all-start.2 = ((bf16[32,24,128]{2,1,0:T(8,128)(2,1)}), bf16[32,24,128]{2,1,0:T(8,128)(2,1)S(1)}, u32[]{:S(2)}, u32[]{:S(2)}) async-start(bf16[32,24,128]{2,1,0:T(8,128)(2,1)} %bitcast.11), calls=%async_computation.2 | async-start | bytes 393216 | tf_op jit(solution)/shard_map/all_to_all | solution.py:348
  39.0 7.9 %collective-permute-start.1 = (bf16[2,192,128]{2,1,0:T(8,128)(2,1)S(1)}, bf16[2,192,128]{2,1,0:T(8,128)(2,1)S(1)}, u32[]{:S(2)}, u32[]{:S(2)}) collective-permute-start(bf16[2,192,128]{2,1,0:T(8,128)(2,1)S(1)} %get-tuple-element.9), channel_id=1, source_target_pairs={{8,16},{16,8},{24,0},{9,17},{17,9},{25,1},{10,18},{18,10},{26,2},{... | collective-permute-start | bytes 294920 | tf_op jit(solution)/shard_map/ppermute | solution.py:352
  40.3 8.8 %collective-permute-start.2 = (bf16[2,192,128]{2,1,0:T(8,128)(2,1)S(1)}, bf16[2,192,128]{2,1,0:T(8,128)(2,1)S(1)}, u32[]{:S(2)}, u32[]{:S(2)}) collective-permute-start(bf16[2,192,128]{2,1,0:T(8,128)(2,1)S(1)} %get-tuple-element.10), channel_id=1, source_target_pairs={{0,16},{16,0},{24,8},{1,17},{17,1},{25,9},{2,18},{18,2},{26,10},{3... | collective-permute-start | bytes 294920 | tf_op jit(solution)/shard_map/ppermute | solution.py:352
  44.7 3.1 %copy-start = (bf16[24,4096]{1,0:T(8,128)(2,1)S(1)}, bf16[24,4096]{1,0:T(8,128)(2,1)}, u32[]{:S(2)}) copy-start(bf16[24,4096]{1,0:T(8,128)(2,1)} %fresh_ref.1) | copy-start | bytes 589828
  44.7 4.4 %collective-permute-start.3 = (bf16[2,192,128]{2,1,0:T(8,128)(2,1)S(1)}, bf16[2,192,128]{2,1,0:T(8,128)(2,1)S(1)}, u32[]{:S(2)}, u32[]{:S(2)}) collective-permute-start(bf16[2,192,128]{2,1,0:T(8,128)(2,1)S(1)} %get-tuple-element.11), channel_id=1, source_target_pairs={{0,8},{8,0},{24,16},{1,9},{9,1},{25,17},{2,10},{10,2},{26,18},{3,1... | collective-permute-start | bytes 294920 | tf_op jit(solution)/shard_map/ppermute | solution.py:352

commit v22 on v15

--- a/solution.py
+++ b/solution.py
@@ -156,13 +156,17 @@
             [x_ref[group * rows : (group + 1) * rows, head : head + HD] for group in range(groups - 1, 0, -1)],
             axis=0,
         )
-        query = jnp.transpose(query)
         value = jnp.transpose(x_ref[:, 2 * wide + head : 2 * wide + head + HD])
         scores, highest = [], None
         for source in range(groups):
             key = x_ref[source * rows : (source + 1) * rows, wide + head : wide + head + HD]
             scores.append(
-                jnp.dot(key, query[:, : ends[source]], preferred_element_type=jnp.float32)
+                lax.dot_general(
+                    key,
+                    query[: ends[source]],
+                    (((1,), (1,)), ((), ())),
+                    preferred_element_type=jnp.float32,
+                )
             )
             peak = jnp.where(kept[source], jnp.max(scores[-1], axis=0, keepdims=True), -1e30)
             peak = spread(peak, -1e30)

time: 42.7 us -> 42.7 us (level)
  no operation moved by 1% of the time
where the time goes in v22:
time: 42.7 us; the launch traced here: 42.3 us
  starting transfers between devices  19 us (44%)
  waiting for transfers between devices  15.1 us (35%)
  Pallas kernels  6.81 us (16%)
  between operations  1.38 us (3%)
    all_to_all x1, waiting for transfers between devices, spread_body(): exchanged = exchange(packed)  12.2 us
    ppermute x3, starting transfers between devices, spread_body(): lax.ppermute(hand, 'tm', [(i, j) for i, j in route if j < tm_count - 1])  7.75 us
    all_to_all x1, starting transfers between devices, spread_body(): exchanged = exchange(packed)  7.3 us
    pallas_call x6, Pallas kernels, run(): pl.pallas_call(kernel, out_shape=outs, in_specs=specs, out_specs=[whole(g...  6.81 us
    all_to_all x1, starting transfers between devices, spread_body(): returned = exchange(attended)  2.68 us
    ppermute x1, waiting for transfers between devices, shifted(): return lax.ppermute(block, axis, route)  2.13 us
    ppermute x1, starting transfers between devices, shifted(): return lax.ppermute(block, axis, route)  1.29 us
  transfers between devices with their start and end apart: 6, of which 4 were waited for; matrix products, arithmetic and copies ran while one was open for 0% of the time, Pallas kernels for 6%

profile of v22, /device:TPU:0, one launch (start us, length us, event | category | flops | bytes accessed | tf_op | source)
XLA Modules:
  0.0 42.3 jit_solution(15848139652274408436)
XLA Ops:
  0.6 2.0 %pack.1.after_ref = bf16[768,384]{1,0:T(8,128)(2,1)} custom-call(bf16[1,24,4096]{2,1,0:T(8,128)(2,1)} %q_hbm.1, bf16[1,24,4096]{2,1,0:T(8,128)(2,1)} %k_hbm.1, bf16[1,24,4096]{2,1,0:T(8,128)(2,1)} %v_hbm.1), custom_call_target="tpu_custom_call" | custom-call | bytes 1179648 | tf_op jit(solution)/shard_map/pack/pallas_call | solution.py:273
  2.6 0.0 copy-start
  2.6 7.3 %all-to-all-start = ((bf16[32,24,384]{2,1,0:T(8,128)(2,1)}), bf16[32,24,384]{2,1,0:T(8,128)(2,1)S(1)}, u32[]{:S(2)}, u32[]{:S(2)}) async-start(bf16[32,24,384]{2,1,0:T(8,128)(2,1)} %bitcast.7), calls=%async_computation | async-start | bytes 1179648 | tf_op jit(solution)/shard_map/all_to_all | solution.py:314
  10.6 0.0 copy-done
  10.6 0.0 copy-start.2
  10.6 1.0 %residual.1 = bf16[32,4096]{1,0:T(8,128)(2,1)S(1)} custom-call(s32[1]{0:T(128)S(6)} %copy.12.noise_ref, bf16[1,24,4096]{2,1,0:T(8,128)(2,1)S(1)} %copy-done, f32[50,4096]{1,0:T(8,128)} %gate_hbm.1, bf16[768,384]{1,0:T(8,128)(2,1)} %pack.1.after_ref), custom_call_target="tpu_custom_call" | custom-call | bytes 1867780 | tf_op jit(solution)/shard_map/residual/pallas_call | solution.py:273
  11.6 1.3 %collective-permute-start = (bf16[32,4096]{1,0:T(8,128)(2,1)S(1)}, bf16[32,4096]{1,0:T(8,128)(2,1)S(1)}, u32[]{:S(2)}, u32[]{:S(2)}) collective-permute-start(bf16[32,4096]{1,0:T(8,128)(2,1)S(1)} %residual.1), channel_id=1, source_target_pairs={{8,0},{16,8},{24,16},{9,1},{17,9},{25,17},{10,2},{18,10},{26,18},{... | collective-permute-start | bytes 786440 | tf_op jit(solution)/shard_map/ppermute | solution.py:21
  12.9 2.1 %collective-permute-done.after_ref.moved_ref = bf16[32,4096]{1,0:T(8,128)(2,1)S(1)} collective-permute-done((bf16[32,4096]{1,0:T(8,128)(2,1)S(1)}, bf16[32,4096]{1,0:T(8,128)(2,1)S(1)}, u32[]{:S(2)}, u32[]{:S(2)}) %collective-permute-start) | collective-permute-done | bytes 262176 | tf_op jit(solution)/shard_map/ppermute | solution.py:21
  15.1 12.2 %all-to-all-done = bf16[32,24,384]{2,1,0:T(8,128)(2,1)S(1)} async-done(((bf16[32,24,384]{2,1,0:T(8,128)(2,1)}), bf16[32,24,384]{2,1,0:T(8,128)(2,1)S(1)}, u32[]{:S(2)}, u32[]{:S(2)}) %all-to-all-start) | async-done | bytes 589856 | tf_op jit(solution)/shard_map/all_to_all | solution.py:314
  27.2 0.0 copy-done.2
  27.3 1.6 %attend.1 = (bf16[768,128]{1,0:T(8,128)(2,1)}, bf16[2,192,128]{2,1,0:T(8,128)(2,1)S(1)}, bf16[2,192,128]{2,1,0:T(8,128)(2,1)S(1)}, bf16[2,192,128]{2,1,0:T(8,128)(2,1)S(1)}) custom-call(s32[4,4]{1,0:T(4,128)S(1)} %copy-done.2, bf16[768,384]{1,0:T(8,128)(2,1)S(1)} %bitcast.4, bf16[32,4096]{1,0:T(8,128)(2,1)S(1)} %collective-permute-done.after_ref.moved_ref), custom_call_target="tpu_custom_call" | custom-call | flops 150994944 | bytes 1343552 | tf_op jit(solution)/shard_map/attend/pallas_call | solution.py:273
  28.8 2.7 %all-to-all-start.1 = ((bf16[32,24,128]{2,1,0:T(8,128)(2,1)}), bf16[32,24,128]{2,1,0:T(8,128)(2,1)S(1)}, u32[]{:S(2)}, u32[]{:S(2)}) async-start(bf16[32,24,128]{2,1,0:T(8,128)(2,1)} %bitcast.8), calls=%async_computation.1 | async-start | bytes 393216 | tf_op jit(solution)/shard_map/all_to_all | solution.py:340
  31.5 1.3 %collective-permute-start.1 = (bf16[2,192,128]{2,1,0:T(8,128)(2,1)S(1)}, bf16[2,192,128]{2,1,0:T(8,128)(2,1)S(1)}, u32[]{:S(2)}, u32[]{:S(2)}) collective-permute-start(bf16[2,192,128]{2,1,0:T(8,128)(2,1)S(1)} %get-tuple-element.7), channel_id=1, source_target_pairs={{8,16},{16,8},{24,0},{9,17},{17,9},{25,1},{10,18},{18,10},{26,2},{... | collective-permute-start | bytes 294920 | tf_op jit(solution)/shard_map/ppermute | solution.py:344
  32.8 4.4 %collective-permute-start.2 = (bf16[2,192,128]{2,1,0:T(8,128)(2,1)S(1)}, bf16[2,192,128]{2,1,0:T(8,128)(2,1)S(1)}, u32[]{:S(2)}, u32[]{:S(2)}) collective-permute-start(bf16[2,192,128]{2,1,0:T(8,128)(2,1)S(1)} %get-tuple-element.8), channel_id=1, source_target_pairs={{0,16},{16,0},{24,8},{1,17},{17,1},{25,9},{2,18},{18,2},{26,10},{3... | collective-permute-start | bytes 294920 | tf_op jit(solution)/shard_map/ppermute | solution.py:344
  37.2 0.0 copy-start.1
  37.2 2.1 %collective-permute-start.3 = (bf16[2,192,128]{2,1,0:T(8,128)(2,1)S(1)}, bf16[2,192,128]{2,1,0:T(8,128)(2,1)S(1)}, u32[]{:S(2)}, u32[]{:S(2)}) collective-permute-start(bf16[2,192,128]{2,1,0:T(8,128)(2,1)S(1)} %get-tuple-element.9), channel_id=1, source_target_pairs={{0,8},{8,0},{24,16},{1,9},{9,1},{25,17},{2,10},{10,2},{26,18},{3,1... | collective-permute-start | bytes 294920 | tf_op jit(solution)/shard_map/ppermute | solution.py:344
  39.3 0.0 collective-permute-done.1.hand_ref
  39.3 0.8 %cache.1.after_ref.begun_hbm = bf16[1,2,192,512]{3,2,1,0:T(8,128)(2,1)} custom-call(bf16[768,384]{1,0:T(8,128)(2,1)S(1)} %bitcast.5, bf16[2,192,128]{2,1,0:T(8,128)(2,1)S(1)} %collective-permute-done.1.hand_ref), custom_call_target="tpu_custom_call" | custom-call | bytes 1081344 | tf_op jit(solution)/shard_map/cache/pallas_call | solution.py:273
  40.1 0.3 all-to-all-done.1
  40.4 0.0 copy-done.1
  40.4 0.8 %update.1.after_ref = bf16[1,24,4096]{2,1,0:T(8,128)(2,1)} custom-call(bf16[768,128]{1,0:T(8,128)(2,1)S(1)} %bitcast.6, bf16[32,4096]{1,0:T(8,128)(2,1)S(1)} %collective-permute-done.after_ref.moved_ref, bf16[24,4096]{1,0:T(8,128)(2,1)S(1)} %copy-done.1, bf16[1,2,192,512]{3,2,1,0:T(8,128)(2,1)} %cache.1.after_ref.begun_hbm), custom_call_target="tpu_custom_call" | custom-call | bytes 1245184 | tf_op jit(solution)/shard_map/update/pallas_call | solution.py:273
  41.2 0.4 %collective-permute-done.2.refs_0_ = bf16[2,192,128]{2,1,0:T(8,128)(2,1)S(1)} collective-permute-done((bf16[2,192,128]{2,1,0:T(8,128)(2,1)S(1)}, bf16[2,192,128]{2,1,0:T(8,128)(2,1)S(1)}, u32[]{:S(2)}, u32[]{:S(2)}) %collective-permute-start.2) | collective-permute-done | bytes 98336 | tf_op jit(solution)/shard_map/ppermute | solution.py:344
  41.6 0.0 collective-permute-done.3.refs_1_
  41.6 0.7 %cache_rest.1 = bf16[1,2,192,512]{3,2,1,0:T(8,128)(2,1)} custom-call(bf16[1,2,192,512]{3,2,1,0:T(8,128)(2,1)} %cache.1.after_ref.begun_hbm, bf16[1,24,4096]{2,1,0:T(8,128)(2,1)} %update.1.after_ref, bf16[2,192,128]{2,1,0:T(8,128)(2,1)S(1)} %collective-permute-done.2.refs_0_, ...), custom_call_target="tpu_custom_call", output_to_operand_aliasing={{}: (0, {})} | custom-call | bytes 1179648 | tf_op jit(solution)/shard_map/cache_rest/pallas_call | solution.py:273
Async XLA Ops:
  2.6 8.0 %copy-start = (bf16[1,24,4096]{2,1,0:T(8,128)(2,1)S(1)}, bf16[1,24,4096]{2,1,0:T(8,128)(2,1)}, u32[]{:S(2)}) copy-start(bf16[1,24,4096]{2,1,0:T(8,128)(2,1)} %h_ref.1) | copy-start | bytes 589828
  2.6 24.6 %all-to-all-start = ((bf16[32,24,384]{2,1,0:T(8,128)(2,1)}), bf16[32,24,384]{2,1,0:T(8,128)(2,1)S(1)}, u32[]{:S(2)}, u32[]{:S(2)}) async-start(bf16[32,24,384]{2,1,0:T(8,128)(2,1)} %bitcast.7), calls=%async_computation | async-start | bytes 1179648 | tf_op jit(solution)/shard_map/all_to_all | solution.py:314
  10.6 16.7 %copy-start.2 = (s32[4,4]{1,0:T(4,128)S(1)}, s32[4,4]{1,0:T(4,128)}, u32[]{:S(2)}) copy-start(s32[4,4]{1,0:T(4,128)} %pattern_ref.1) | copy-start | bytes 196
  11.6 3.4 %collective-permute-start = (bf16[32,4096]{1,0:T(8,128)(2,1)S(1)}, bf16[32,4096]{1,0:T(8,128)(2,1)S(1)}, u32[]{:S(2)}, u32[]{:S(2)}) collective-permute-start(bf16[32,4096]{1,0:T(8,128)(2,1)S(1)} %residual.1), channel_id=1, source_target_pairs={{8,0},{16,8},{24,16},{9,1},{17,9},{25,17},{10,2},{18,10},{26,18},{... | collective-permute-start | bytes 786440 | tf_op jit(solution)/shard_map/ppermute | solution.py:21
  28.8 11.6 %all-to-all-start.1 = ((bf16[32,24,128]{2,1,0:T(8,128)(2,1)}), bf16[32,24,128]{2,1,0:T(8,128)(2,1)S(1)}, u32[]{:S(2)}, u32[]{:S(2)}) async-start(bf16[32,24,128]{2,1,0:T(8,128)(2,1)} %bitcast.8), calls=%async_computation.1 | async-start | bytes 393216 | tf_op jit(solution)/shard_map/all_to_all | solution.py:340
  31.5 7.8 %collective-permute-start.1 = (bf16[2,192,128]{2,1,0:T(8,128)(2,1)S(1)}, bf16[2,192,128]{2,1,0:T(8,128)(2,1)S(1)}, u32[]{:S(2)}, u32[]{:S(2)}) collective-permute-start(bf16[2,192,128]{2,1,0:T(8,128)(2,1)S(1)} %get-tuple-element.7), channel_id=1, source_target_pairs={{8,16},{16,8},{24,0},{9,17},{17,9},{25,1},{10,18},{18,10},{26,2},{... | collective-permute-start | bytes 294920 | tf_op jit(solution)/shard_map/ppermute | solution.py:344
  32.8 8.8 %collective-permute-start.2 = (bf16[2,192,128]{2,1,0:T(8,128)(2,1)S(1)}, bf16[2,192,128]{2,1,0:T(8,128)(2,1)S(1)}, u32[]{:S(2)}, u32[]{:S(2)}) collective-permute-start(bf16[2,192,128]{2,1,0:T(8,128)(2,1)S(1)} %get-tuple-element.8), channel_id=1, source_target_pairs={{0,16},{16,0},{24,8},{1,17},{17,1},{25,9},{2,18},{18,2},{26,10},{3... | collective-permute-start | bytes 294920 | tf_op jit(solution)/shard_map/ppermute | solution.py:344
  37.2 3.2 %copy-start.1 = (bf16[24,4096]{1,0:T(8,128)(2,1)S(1)}, bf16[24,4096]{1,0:T(8,128)(2,1)}, u32[]{:S(2)}) copy-start(bf16[24,4096]{1,0:T(8,128)(2,1)} %fresh_ref.1) | copy-start | bytes 589828
  37.2 4.4 %collective-permute-start.3 = (bf16[2,192,128]{2,1,0:T(8,128)(2,1)S(1)}, bf16[2,192,128]{2,1,0:T(8,128)(2,1)S(1)}, u32[]{:S(2)}, u32[]{:S(2)}) collective-permute-start(bf16[2,192,128]{2,1,0:T(8,128)(2,1)S(1)} %get-tuple-element.9), channel_id=1, source_target_pairs={{0,8},{8,0},{24,16},{1,9},{9,1},{25,17},{2,10},{10,2},{26,18},{3,1... | collective-permute-start | bytes 294920 | tf_op jit(solution)/shard_map/ppermute | solution.py:344

commit v23 on v14

--- a/solution.py
+++ b/solution.py
@@ -22,7 +22,7 @@
 
 
 def mixed(index, count):
-    return (index + 2) % count
+    return count - 2 - index + 2 * (index % 2)
 
 
 def runs(count):

time: 43.3 us -> 43.3 us (level)
    all_to_all x1, waiting for transfers between devices: 0.01 us -> 1.19 us  [spread_body(): returned = exchange(attended)]
    ppermute x3, waiting for transfers between devices: 0.94 us -> 0.01 us  [spread_body(): lax.ppermute(hand, 'tm', [(i, j) for i, j in route if j < tm_count - 1])]
    all_to_all x1, waiting for transfers between devices: 12.6 us -> 12.2 us  [spread_body(): exchanged = exchange(packed)]
  transfers between devices with their start and end apart: 6 -> 6, of which waited for: 4 -> 3; matrix products, arithmetic and copies ran while one was open for 0% -> 0% of each run, Pallas kernels for 6% -> 6%
where the time goes in v23:
time: 43.3 us; the launch traced here: 42.8 us
  starting transfers between devices  18.9 us (44%)
  waiting for transfers between devices  15.5 us (36%)
  Pallas kernels  6.98 us (16%)
  between operations  1.39 us (3%)
    all_to_all x1, waiting for transfers between devices, spread_body(): exchanged = exchange(packed)  12.2 us
    ppermute x3, starting transfers between devices, spread_body(): lax.ppermute(hand, 'tm', [(i, j) for i, j in route if j < tm_count - 1])  7.73 us
    all_to_all x1, starting transfers between devices, spread_body(): exchanged = exchange(packed)  7.3 us
    pallas_call x6, Pallas kernels, run(): pl.pallas_call(kernel, out_shape=outs, in_specs=specs, out_specs=[whole(g...  6.98 us
    all_to_all x1, starting transfers between devices, spread_body(): returned = exchange(attended)  2.6 us
    ppermute x1, waiting for transfers between devices, shifted(): return lax.ppermute(block, axis, route)  2.13 us
    ppermute x1, starting transfers between devices, shifted(): return lax.ppermute(block, axis, route)  1.29 us
    all_to_all x1, waiting for transfers between devices, spread_body(): returned = exchange(attended)  1.19 us
  transfers between devices with their start and end apart: 6, of which 3 were waited for; matrix products, arithmetic and copies ran while one was open for 0% of the time, Pallas kernels for 6%

profile of v23, /device:TPU:0, one launch (start us, length us, event | category | flops | bytes accessed | tf_op | source)
XLA Modules:
  0.0 42.8 jit_solution(2107068084133970221)
XLA Ops:
  0.6 2.0 %pack.1.after_ref = bf16[768,384]{1,0:T(8,128)(2,1)} custom-call(bf16[1,24,4096]{2,1,0:T(8,128)(2,1)} %q_hbm.1, bf16[1,24,4096]{2,1,0:T(8,128)(2,1)} %k_hbm.1, bf16[1,24,4096]{2,1,0:T(8,128)(2,1)} %v_hbm.1), custom_call_target="tpu_custom_call" | custom-call | bytes 1179648 | tf_op jit(solution)/shard_map/pack/pallas_call | solution.py:279
  2.6 0.0 copy-start
  2.7 7.3 %all-to-all-start = ((bf16[32,24,384]{2,1,0:T(8,128)(2,1)}), bf16[32,24,384]{2,1,0:T(8,128)(2,1)S(1)}, u32[]{:S(2)}, u32[]{:S(2)}) async-start(bf16[32,24,384]{2,1,0:T(8,128)(2,1)} %bitcast.7), calls=%async_computation | async-start | bytes 1179648 | tf_op jit(solution)/shard_map/all_to_all | solution.py:321
  10.6 0.0 copy-done
  10.6 0.0 copy-start.2
  10.6 1.0 %residual.1 = bf16[32,4096]{1,0:T(8,128)(2,1)S(1)} custom-call(s32[1]{0:T(128)S(6)} %copy.12.noise_ref, bf16[1,24,4096]{2,1,0:T(8,128)(2,1)S(1)} %copy-done, f32[50,4096]{1,0:T(8,128)} %gate_hbm.1, bf16[768,384]{1,0:T(8,128)(2,1)} %pack.1.after_ref), custom_call_target="tpu_custom_call" | custom-call | bytes 1867780 | tf_op jit(solution)/shard_map/residual/pallas_call | solution.py:279
  11.7 1.3 %collective-permute-start = (bf16[32,4096]{1,0:T(8,128)(2,1)S(1)}, bf16[32,4096]{1,0:T(8,128)(2,1)S(1)}, u32[]{:S(2)}, u32[]{:S(2)}) collective-permute-start(bf16[32,4096]{1,0:T(8,128)(2,1)S(1)} %residual.1), channel_id=1, source_target_pairs={{8,0},{16,8},{24,16},{9,1},{17,9},{25,17},{10,2},{18,10},{26,18},{... | collective-permute-start | bytes 786440 | tf_op jit(solution)/shard_map/ppermute | solution.py:21
  13.0 2.1 %collective-permute-done.after_ref.moved_ref = bf16[32,4096]{1,0:T(8,128)(2,1)S(1)} collective-permute-done((bf16[32,4096]{1,0:T(8,128)(2,1)S(1)}, bf16[32,4096]{1,0:T(8,128)(2,1)S(1)}, u32[]{:S(2)}, u32[]{:S(2)}) %collective-permute-start) | collective-permute-done | bytes 262176 | tf_op jit(solution)/shard_map/ppermute | solution.py:21
  15.1 12.2 %all-to-all-done = bf16[32,24,384]{2,1,0:T(8,128)(2,1)S(1)} async-done(((bf16[32,24,384]{2,1,0:T(8,128)(2,1)}), bf16[32,24,384]{2,1,0:T(8,128)(2,1)S(1)}, u32[]{:S(2)}, u32[]{:S(2)}) %all-to-all-start) | async-done | bytes 589856 | tf_op jit(solution)/shard_map/all_to_all | solution.py:321
  27.3 0.0 copy-done.2
  27.3 1.6 %attend.1 = (bf16[768,128]{1,0:T(8,128)(2,1)}, bf16[192,256]{1,0:T(8,128)(2,1)S(1)}, bf16[192,256]{1,0:T(8,128)(2,1)S(1)}, bf16[192,256]{1,0:T(8,128)(2,1)S(1)}) custom-call(s32[4,4]{1,0:T(4,128)S(1)} %copy-done.2, bf16[768,384]{1,0:T(8,128)(2,1)S(1)} %bitcast.4, bf16[32,4096]{1,0:T(8,128)(2,1)S(1)} %collective-permute-done.after_ref.moved_ref), custom_call_target="tpu_custom_call" | custom-call | flops 150994944 | bytes 1343552 | tf_op jit(solution)/shard_map/attend/pallas_call | solution.py:279
  28.9 2.6 %all-to-all-start.1 = ((bf16[32,24,128]{2,1,0:T(8,128)(2,1)}), bf16[32,24,128]{2,1,0:T(8,128)(2,1)S(1)}, u32[]{:S(2)}, u32[]{:S(2)}) async-start(bf16[32,24,128]{2,1,0:T(8,128)(2,1)} %bitcast.8), calls=%async_computation.1 | async-start | bytes 393216 | tf_op jit(solution)/shard_map/all_to_all | solution.py:347
  31.5 1.3 %collective-permute-start.1 = (bf16[192,256]{1,0:T(8,128)(2,1)S(1)}, bf16[192,256]{1,0:T(8,128)(2,1)S(1)}, u32[]{:S(2)}, u32[]{:S(2)}) collective-permute-start(bf16[192,256]{1,0:T(8,128)(2,1)S(1)} %get-tuple-element.7), channel_id=1, source_target_pairs={{8,16},{16,8},{24,0},{9,17},{17,9},{25,1},{10,18},{18,10},{26,2},{... | collective-permute-start | bytes 294920 | tf_op jit(solution)/shard_map/ppermute | solution.py:351
  32.8 4.4 %collective-permute-start.2 = (bf16[192,256]{1,0:T(8,128)(2,1)S(1)}, bf16[192,256]{1,0:T(8,128)(2,1)S(1)}, u32[]{:S(2)}, u32[]{:S(2)}) collective-permute-start(bf16[192,256]{1,0:T(8,128)(2,1)S(1)} %get-tuple-element.8), channel_id=1, source_target_pairs={{0,16},{16,0},{24,8},{1,17},{17,1},{25,9},{2,18},{18,2},{26,10},{3... | collective-permute-start | bytes 294920 | tf_op jit(solution)/shard_map/ppermute | solution.py:351
  37.2 0.0 copy-start.1
  37.2 2.1 %collective-permute-start.3 = (bf16[192,256]{1,0:T(8,128)(2,1)S(1)}, bf16[192,256]{1,0:T(8,128)(2,1)S(1)}, u32[]{:S(2)}, u32[]{:S(2)}) collective-permute-start(bf16[192,256]{1,0:T(8,128)(2,1)S(1)} %get-tuple-element.9), channel_id=1, source_target_pairs={{0,8},{8,0},{24,16},{1,9},{9,1},{25,17},{2,10},{10,2},{26,18},{3,1... | collective-permute-start | bytes 294920 | tf_op jit(solution)/shard_map/ppermute | solution.py:351
  39.2 0.0 collective-permute-done.1.hand_ref
  39.3 0.8 %cache.1.after_ref.begun_hbm = bf16[1,2,192,512]{3,2,1,0:T(8,128)(2,1)} custom-call(bf16[768,384]{1,0:T(8,128)(2,1)S(1)} %bitcast.5, bf16[192,256]{1,0:T(8,128)(2,1)S(1)} %collective-permute-done.1.hand_ref), custom_call_target="tpu_custom_call" | custom-call | bytes 1081344 | tf_op jit(solution)/shard_map/cache/pallas_call | solution.py:279
  40.1 1.2 %all-to-all-done.1 = bf16[32,24,128]{2,1,0:T(8,128)(2,1)S(1)} async-done(((bf16[32,24,128]{2,1,0:T(8,128)(2,1)}), bf16[32,24,128]{2,1,0:T(8,128)(2,1)S(1)}, u32[]{:S(2)}, u32[]{:S(2)}) %all-to-all-start.1) | async-done | bytes 196640 | tf_op jit(solution)/shard_map/all_to_all | solution.py:347
  41.3 0.0 copy-done.1
  41.3 0.8 %update.1.after_ref = bf16[1,24,4096]{2,1,0:T(8,128)(2,1)} custom-call(bf16[768,128]{1,0:T(8,128)(2,1)S(1)} %bitcast.6, bf16[32,4096]{1,0:T(8,128)(2,1)S(1)} %collective-permute-done.after_ref.moved_ref, bf16[24,4096]{1,0:T(8,128)(2,1)S(1)} %copy-done.1, bf16[1,2,192,512]{3,2,1,0:T(8,128)(2,1)} %cache.1.after_ref.begun_hbm), custom_call_target="tpu_custom_call" | custom-call | bytes 1245184 | tf_op jit(solution)/shard_map/update/pallas_call | solution.py:279
  42.0 0.0 collective-permute-done.2.refs_0_
  42.0 0.0 collective-permute-done.3.refs_1_
  42.0 0.8 %cache_rest.1 = bf16[1,2,192,512]{3,2,1,0:T(8,128)(2,1)} custom-call(bf16[1,2,192,512]{3,2,1,0:T(8,128)(2,1)} %cache.1.after_ref.begun_hbm, bf16[1,24,4096]{2,1,0:T(8,128)(2,1)} %update.1.after_ref, bf16[192,256]{1,0:T(8,128)(2,1)S(1)} %collective-permute-done.2.refs_0_, ...), custom_call_target="tpu_custom_call", output_to_operand_aliasing={{}: (0, {})} | custom-call | bytes 1179648 | tf_op jit(solution)/shard_map/cache_rest/pallas_call | solution.py:279
Async XLA Ops:
  2.6 8.0 %copy-start = (bf16[1,24,4096]{2,1,0:T(8,128)(2,1)S(1)}, bf16[1,24,4096]{2,1,0:T(8,128)(2,1)}, u32[]{:S(2)}) copy-start(bf16[1,24,4096]{2,1,0:T(8,128)(2,1)} %h_ref.1) | copy-start | bytes 589828
  2.7 24.6 %all-to-all-start = ((bf16[32,24,384]{2,1,0:T(8,128)(2,1)}), bf16[32,24,384]{2,1,0:T(8,128)(2,1)S(1)}, u32[]{:S(2)}, u32[]{:S(2)}) async-start(bf16[32,24,384]{2,1,0:T(8,128)(2,1)} %bitcast.7), calls=%async_computation | async-start | bytes 1179648 | tf_op jit(solution)/shard_map/all_to_all | solution.py:321
  10.6 16.7 %copy-start.2 = (s32[4,4]{1,0:T(4,128)S(1)}, s32[4,4]{1,0:T(4,128)}, u32[]{:S(2)}) copy-start(s32[4,4]{1,0:T(4,128)} %pattern_ref.1) | copy-start | bytes 196
  11.7 3.4 %collective-permute-start = (bf16[32,4096]{1,0:T(8,128)(2,1)S(1)}, bf16[32,4096]{1,0:T(8,128)(2,1)S(1)}, u32[]{:S(2)}, u32[]{:S(2)}) collective-permute-start(bf16[32,4096]{1,0:T(8,128)(2,1)S(1)} %residual.1), channel_id=1, source_target_pairs={{8,0},{16,8},{24,16},{9,1},{17,9},{25,17},{10,2},{18,10},{26,18},{... | collective-permute-start | bytes 786440 | tf_op jit(solution)/shard_map/ppermute | solution.py:21
  28.9 12.4 %all-to-all-start.1 = ((bf16[32,24,128]{2,1,0:T(8,128)(2,1)}), bf16[32,24,128]{2,1,0:T(8,128)(2,1)S(1)}, u32[]{:S(2)}, u32[]{:S(2)}) async-start(bf16[32,24,128]{2,1,0:T(8,128)(2,1)} %bitcast.8), calls=%async_computation.1 | async-start | bytes 393216 | tf_op jit(solution)/shard_map/all_to_all | solution.py:347
  31.5 7.8 %collective-permute-start.1 = (bf16[192,256]{1,0:T(8,128)(2,1)S(1)}, bf16[192,256]{1,0:T(8,128)(2,1)S(1)}, u32[]{:S(2)}, u32[]{:S(2)}) collective-permute-start(bf16[192,256]{1,0:T(8,128)(2,1)S(1)} %get-tuple-element.7), channel_id=1, source_target_pairs={{8,16},{16,8},{24,0},{9,17},{17,9},{25,1},{10,18},{18,10},{26,2},{... | collective-permute-start | bytes 294920 | tf_op jit(solution)/shard_map/ppermute | solution.py:351
  32.8 9.2 %collective-permute-start.2 = (bf16[192,256]{1,0:T(8,128)(2,1)S(1)}, bf16[192,256]{1,0:T(8,128)(2,1)S(1)}, u32[]{:S(2)}, u32[]{:S(2)}) collective-permute-start(bf16[192,256]{1,0:T(8,128)(2,1)S(1)} %get-tuple-element.8), channel_id=1, source_target_pairs={{0,16},{16,0},{24,8},{1,17},{17,1},{25,9},{2,18},{18,2},{26,10},{3... | collective-permute-start | bytes 294920 | tf_op jit(solution)/shard_map/ppermute | solution.py:351
  37.2 4.1 %copy-start.1 = (bf16[24,4096]{1,0:T(8,128)(2,1)S(1)}, bf16[24,4096]{1,0:T(8,128)(2,1)}, u32[]{:S(2)}) copy-start(bf16[24,4096]{1,0:T(8,128)(2,1)} %fresh_ref.1) | copy-start | bytes 589828
  37.2 4.8 %collective-permute-start.3 = (bf16[192,256]{1,0:T(8,128)(2,1)S(1)}, bf16[192,256]{1,0:T(8,128)(2,1)S(1)}, u32[]{:S(2)}, u32[]{:S(2)}) collective-permute-start(bf16[192,256]{1,0:T(8,128)(2,1)S(1)} %get-tuple-element.9), channel_id=1, source_target_pairs={{0,8},{8,0},{24,16},{1,9},{9,1},{25,17},{2,10},{10,2},{26,18},{3,1... | collective-permute-start | bytes 294920 | tf_op jit(solution)/shard_map/ppermute | solution.py:351

commit v24 on v16

--- a/solution.py
+++ b/solution.py
@@ -25,16 +25,14 @@
     return (index + count // 2) % count
 
 
+def back_place(pair, pairs):
+    return pairs - 1 - pair
+
+
 def back_order(tm_count, seq_count):
-    ordered = sorted(range(seq_count), key=lambda index: mixed(index, seq_count))
-    half = tm_count // 2
-    return [
-        (high * half + low, ordered[pair + member])
-        for low in range(half)
-        for pair in range(0, seq_count, 2)
-        for high in range(tm_count // half)
-        for member in range(2)
-    ]
+    pairs = seq_count // 2
+    ordered = sorted(range(pairs), key=lambda pair: back_place(pair, pairs))
+    return [(tm, 2 * pair + member) for tm in range(tm_count) for pair in ordered for member in range(2)]
 
 
 def pack_kernel(seq_count, parts, q_hbm, k_hbm, v_hbm, out_hbm, held, block, in_sems, out_sems):
@@ -148,16 +146,15 @@
             chosen = jnp.where((lane >= start) & (lane < start + rows), flag, chosen)
         kept.append(chosen[:, : ends[-1]] > 0)
 
-    halves = groups // (groups // 2)
     pairs = seq_count // 2
     step = rows // pairs
 
     def keep(group, head, result):
         for place in (group - 1, groups - 1) if group == groups - 1 else (group - 1,):
-            low, high = place % (groups // 2), place // (groups // 2)
             for pair in range(pairs):
-                to = ((low * pairs + pair) * halves + high) * step
-                held[to : to + step, head : head + HD] = result[pair * step : (pair + 1) * step]
+                at = mixed(2 * pair, seq_count) // 2 * step
+                to = place * rows + back_place(pair, pairs) * step
+                held[to : to + step, head : head + HD] = result[at : at + step]
 
     def spread(row, fill):
         rest = across - row.shape[1]
@@ -233,46 +230,45 @@
         out_ref[0, :, :, lanes_of(distances(groups)[0], groups, here, wide)] = hand_ref[...]
 
 
-def cache_rest_kernel(groups, begun_hbm, after_ref, *refs):
-    *hand_refs, out_hbm, sems = refs
-    here = lax.axis_index("tm")
-
-    @pl.when(here < groups - 1)
-    def place():
-        copies = [
-            pltpu.make_async_copy(
-                block, out_hbm.at[0, :, :, lanes_of(distance, groups, here, block.shape[2])], sems.at[index]
-            )
-            for index, (distance, block) in enumerate(zip(distances(groups)[1:], hand_refs))
-        ]
-        for copy in copies:
-            copy.start()
-        for copy in copies:
-            copy.wait()
-
-
-def update_kernel(seq_count, tm_count, att_ref, moved_ref, fresh_ref, after_ref, out_ref):
-    tok = out_ref.shape[1]
+def finish_kernel(seq_count, tm_count, att_ref, moved_ref, fresh_ref, begun_hbm, *refs):
+    *hand_refs, out_hbm, cache_hbm, held, sem, sems = refs
+    tok = held.shape[1]
     wide = att_ref.shape[1]
     count = att_ref.shape[0] // tok
     order = back_order(tm_count, seq_count)
-    last = lax.axis_index("tm") == tm_count - 1
+    here = lax.axis_index("tm")
+    last = here == tm_count - 1
+    copies = [
+        pltpu.make_async_copy(
+            block, cache_hbm.at[0, :, :, lanes_of(distance, tm_count, here, block.shape[2])], sems.at[index]
+        )
+        for index, (distance, block) in enumerate(zip(distances(tm_count)[1:], hand_refs))
+    ]
 
     @pl.when(last)
     def take_fresh():
-        out_ref[0] = fresh_ref[...]
+        copy = pltpu.make_async_copy(fresh_ref, out_hbm.at[0], sem)
+        copy.start()
+        copy.wait()
 
     @pl.when(jnp.logical_not(last))
     def take_update():
+        for copy in copies:
+            copy.start()
         for pair in range(count // 2):
             rows = att_ref[2 * pair * tok : 2 * (pair + 1) * tok, :].astype(jnp.float32)
             for half in range(2):
-                source = 2 * pair + half
-                start = (order[source][1] * tm_count + order[source][0]) * wide
+                tm, seq = order[2 * pair + half]
+                start = (seq * tm_count + tm) * wide
                 moved = moved_ref[:, start : start + wide].astype(jnp.float32)
                 gate = (moved[tok : tok + 1] + moved[tok + 1 : tok + 2]) + moved[tok + 2 : tok + 3]
                 result = moved[:tok] + gate * rows[half * tok : (half + 1) * tok]
-                out_ref[0, :, start : start + wide] = result.astype(jnp.bfloat16)
+                held[0, :, start : start + wide] = result.astype(jnp.bfloat16)
+        copy = pltpu.make_async_copy(held, out_hbm, sem)
+        copy.start()
+        copy.wait()
+        for copy in copies:
+            copy.wait()
 
 
 def whole(space=VMEM):
@@ -367,21 +363,14 @@
         (exchanged, first),
     )
     begun = pltpu.with_memory_space_constraint(begun, HBM)
-    advanced = run(
-        functools.partial(update_kernel, seq_count, tm_count),
-        "update",
-        [jax.ShapeDtypeStruct((1, tok, width), kind)],
-        [whole()] * 3 + [whole(HBM)],
-        (returned, moved, fresh_latent, begun),
-    )
-    next_cache = run(
-        functools.partial(cache_rest_kernel, tm_count),
-        "cache_rest",
-        [HBM(begun.shape, kind)],
-        [whole(HBM)] * 2 + [whole()] * len(rest),
-        (begun, pltpu.with_memory_space_constraint(advanced, HBM), *rest),
-        scratch=[DMA((len(rest),))],
-        aliases={0: 0},
+    advanced, next_cache = run(
+        functools.partial(finish_kernel, seq_count, tm_count),
+        "finish",
+        [HBM((1, tok, width), kind), HBM(begun.shape, kind)],
+        [whole()] * 3 + [whole(HBM)] + [whole()] * len(rest),
+        (returned, moved, fresh_latent, begun, *rest),
+        scratch=[VMEM((1, tok, width), kind), DMA, DMA((len(rest),))],
+        aliases={3: 1},
     )
     return (advanced, next_cache)
 

time: 42.7 us -> 42.8 us (level)
  waiting for transfers between devices: 15 us -> 15.7 us
  Pallas kernels: 6.84 us -> 6.2 us
    ppermute x3, waiting for transfers between devices: 0.07 us -> 1.36 us  [spread_body(): lax.ppermute(hand, 'tm', [(i, j) for i, j in route if j < tm_count - 1])]
    pallas_call x6 -> x5, Pallas kernels: 6.84 us -> 6.2 us  [run(): pl.pallas_call(kernel, out_shape=outs, in_specs=specs, out_specs=[whole(g...]
    all_to_all x1, waiting for transfers between devices: 0.58 us -> 0.01 us  [spread_body(): returned = exchange(attended, axis_index_groups=[back])]
  transfers between devices with their start and end apart: 6 -> 6, of which waited for: 4 -> 3; matrix products, arithmetic and copies ran while one was open for 0% -> 0% of each run, Pallas kernels for 6% -> 4%
where the time goes in v24:
time: 42.8 us; the launch traced here: 42.3 us
  starting transfers between devices  19 us (44%)
  waiting for transfers between devices  15.7 us (37%)
  Pallas kernels  6.2 us (14%)
  between operations  1.39 us (3%)
    all_to_all x1, waiting for transfers between devices, spread_body(): exchanged = exchange(packed, axis_index_groups=[order])  12.2 us
    ppermute x3, starting transfers between devices, spread_body(): lax.ppermute(hand, 'tm', [(i, j) for i, j in route if j < tm_count - 1])  7.75 us
    all_to_all x1, starting transfers between devices, spread_body(): exchanged = exchange(packed, axis_index_groups=[order])  7.3 us
    pallas_call x5, Pallas kernels, run(): pl.pallas_call(kernel, out_shape=outs, in_specs=specs, out_specs=[whole(g...  6.2 us
    all_to_all x1, starting transfers between devices, spread_body(): returned = exchange(attended, axis_index_groups=[back])  2.68 us
    ppermute x1, waiting for transfers between devices, shifted(): return lax.ppermute(block, axis, route)  2.13 us
    ppermute x3, waiting for transfers between devices, spread_body(): lax.ppermute(hand, 'tm', [(i, j) for i, j in route if j < tm_count - 1])  1.36 us
    ppermute x1, starting transfers between devices, shifted(): return lax.ppermute(block, axis, route)  1.29 us
  transfers between devices with their start and end apart: 6, of which 3 were waited for; matrix products, arithmetic and copies ran while one was open for 0% of the time, Pallas kernels for 4%

profile of v24, /device:TPU:0, one launch (start us, length us, event | category | flops | bytes accessed | tf_op | source)
XLA Modules:
  0.0 42.3 jit_solution(18028326074359375675)
XLA Ops:
  0.6 2.0 %pack.1.after_ref = bf16[768,384]{1,0:T(8,128)(2,1)} custom-call(bf16[1,24,4096]{2,1,0:T(8,128)(2,1)} %q_hbm.1, bf16[1,24,4096]{2,1,0:T(8,128)(2,1)} %k_hbm.1, bf16[1,24,4096]{2,1,0:T(8,128)(2,1)} %v_hbm.1), custom_call_target="tpu_custom_call" | custom-call | bytes 1179648 | tf_op jit(solution)/shard_map/pack/pallas_call | solution.py:283
  2.6 0.0 copy-start
  2.6 7.3 %all-to-all-start = ((bf16[32,24,384]{2,1,0:T(8,128)(2,1)}), bf16[32,24,384]{2,1,0:T(8,128)(2,1)S(1)}, u32[]{:S(2)}, u32[]{:S(2)}) async-start(bf16[32,24,384]{2,1,0:T(8,128)(2,1)} %bitcast.7), calls=%async_computation | async-start | bytes 1179648 | tf_op jit(solution)/shard_map/all_to_all | solution.py:325
  10.6 0.0 copy-done
  10.6 0.0 copy-start.2
  10.6 1.0 %residual.1 = bf16[32,4096]{1,0:T(8,128)(2,1)S(1)} custom-call(s32[1]{0:T(128)S(6)} %copy.12.noise_ref, bf16[1,24,4096]{2,1,0:T(8,128)(2,1)S(1)} %copy-done, f32[50,4096]{1,0:T(8,128)} %gate_hbm.1, bf16[768,384]{1,0:T(8,128)(2,1)} %pack.1.after_ref), custom_call_target="tpu_custom_call" | custom-call | bytes 1867780 | tf_op jit(solution)/shard_map/residual/pallas_call | solution.py:283
  11.6 1.3 %collective-permute-start = (bf16[32,4096]{1,0:T(8,128)(2,1)S(1)}, bf16[32,4096]{1,0:T(8,128)(2,1)S(1)}, u32[]{:S(2)}, u32[]{:S(2)}) collective-permute-start(bf16[32,4096]{1,0:T(8,128)(2,1)S(1)} %residual.1), channel_id=1, source_target_pairs={{8,0},{16,8},{24,16},{9,1},{17,9},{25,17},{10,2},{18,10},{26,18},{... | collective-permute-start | bytes 786440 | tf_op jit(solution)/shard_map/ppermute | solution.py:21
  12.9 2.1 %collective-permute-done.after_ref.moved_ref = bf16[32,4096]{1,0:T(8,128)(2,1)S(1)} collective-permute-done((bf16[32,4096]{1,0:T(8,128)(2,1)S(1)}, bf16[32,4096]{1,0:T(8,128)(2,1)S(1)}, u32[]{:S(2)}, u32[]{:S(2)}) %collective-permute-start) | collective-permute-done | bytes 262176 | tf_op jit(solution)/shard_map/ppermute | solution.py:21
  15.1 12.2 %all-to-all-done = bf16[32,24,384]{2,1,0:T(8,128)(2,1)S(1)} async-done(((bf16[32,24,384]{2,1,0:T(8,128)(2,1)}), bf16[32,24,384]{2,1,0:T(8,128)(2,1)S(1)}, u32[]{:S(2)}, u32[]{:S(2)}) %all-to-all-start) | async-done | bytes 589856 | tf_op jit(solution)/shard_map/all_to_all | solution.py:325
  27.2 0.0 copy-done.2
  27.3 1.6 %attend.1 = (bf16[768,128]{1,0:T(8,128)(2,1)}, bf16[2,192,128]{2,1,0:T(8,128)(2,1)S(1)}, bf16[2,192,128]{2,1,0:T(8,128)(2,1)S(1)}, bf16[2,192,128]{2,1,0:T(8,128)(2,1)S(1)}) custom-call(s32[4,4]{1,0:T(4,128)S(1)} %copy-done.2, bf16[768,384]{1,0:T(8,128)(2,1)S(1)} %bitcast.4, bf16[32,4096]{1,0:T(8,128)(2,1)S(1)} %collective-permute-done.after_ref.moved_ref), custom_call_target="tpu_custom_call" | custom-call | flops 150994944 | bytes 1343552 | tf_op jit(solution)/shard_map/attend/pallas_call | solution.py:283
  28.8 2.7 %all-to-all-start.1 = ((bf16[32,24,128]{2,1,0:T(8,128)(2,1)}), bf16[32,24,128]{2,1,0:T(8,128)(2,1)S(1)}, u32[]{:S(2)}, u32[]{:S(2)}) async-start(bf16[32,24,128]{2,1,0:T(8,128)(2,1)} %bitcast.8), calls=%async_computation.1 | async-start | bytes 393216 | tf_op jit(solution)/shard_map/all_to_all | solution.py:351
  31.5 1.3 %collective-permute-start.1 = (bf16[2,192,128]{2,1,0:T(8,128)(2,1)S(1)}, bf16[2,192,128]{2,1,0:T(8,128)(2,1)S(1)}, u32[]{:S(2)}, u32[]{:S(2)}) collective-permute-start(bf16[2,192,128]{2,1,0:T(8,128)(2,1)S(1)} %get-tuple-element.7), channel_id=1, source_target_pairs={{8,16},{16,8},{24,0},{9,17},{17,9},{25,1},{10,18},{18,10},{26,2},{... | collective-permute-start | bytes 294920 | tf_op jit(solution)/shard_map/ppermute | solution.py:355
  32.8 4.4 %collective-permute-start.2 = (bf16[2,192,128]{2,1,0:T(8,128)(2,1)S(1)}, bf16[2,192,128]{2,1,0:T(8,128)(2,1)S(1)}, u32[]{:S(2)}, u32[]{:S(2)}) collective-permute-start(bf16[2,192,128]{2,1,0:T(8,128)(2,1)S(1)} %get-tuple-element.8), channel_id=1, source_target_pairs={{0,16},{16,0},{24,8},{1,17},{17,1},{25,9},{2,18},{18,2},{26,10},{3... | collective-permute-start | bytes 294920 | tf_op jit(solution)/shard_map/ppermute | solution.py:355
  37.2 0.0 copy-start.1
  37.3 2.1 %collective-permute-start.3 = (bf16[2,192,128]{2,1,0:T(8,128)(2,1)S(1)}, bf16[2,192,128]{2,1,0:T(8,128)(2,1)S(1)}, u32[]{:S(2)}, u32[]{:S(2)}) collective-permute-start(bf16[2,192,128]{2,1,0:T(8,128)(2,1)S(1)} %get-tuple-element.9), channel_id=1, source_target_pairs={{0,8},{8,0},{24,16},{1,9},{9,1},{25,17},{2,10},{10,2},{26,18},{3,1... | collective-permute-start | bytes 294920 | tf_op jit(solution)/shard_map/ppermute | solution.py:355
  39.3 0.0 collective-permute-done.1.hand_ref
  39.3 0.8 %cache.1.begun_hbm = bf16[1,2,192,512]{3,2,1,0:T(8,128)(2,1)} custom-call(bf16[768,384]{1,0:T(8,128)(2,1)S(1)} %bitcast.5, bf16[2,192,128]{2,1,0:T(8,128)(2,1)S(1)} %collective-permute-done.1.hand_ref), custom_call_target="tpu_custom_call" | custom-call | bytes 1081344 | tf_op jit(solution)/shard_map/cache/pallas_call | solution.py:283
  40.1 1.4 %collective-permute-done.2.refs_0_ = bf16[2,192,128]{2,1,0:T(8,128)(2,1)S(1)} collective-permute-done((bf16[2,192,128]{2,1,0:T(8,128)(2,1)S(1)}, bf16[2,192,128]{2,1,0:T(8,128)(2,1)S(1)}, u32[]{:S(2)}, u32[]{:S(2)}) %collective-permute-start.2) | collective-permute-done | bytes 98336 | tf_op jit(solution)/shard_map/ppermute | solution.py:355
  41.5 0.0 collective-permute-done.3.refs_1_
  41.5 0.0 all-to-all-done.1
  41.5 0.0 copy-done.1
  41.5 0.8 %finish.1 = (bf16[1,24,4096]{2,1,0:T(8,128)(2,1)}, bf16[1,2,192,512]{3,2,1,0:T(8,128)(2,1)}) custom-call(bf16[768,128]{1,0:T(8,128)(2,1)S(1)} %bitcast.6, bf16[32,4096]{1,0:T(8,128)(2,1)S(1)} %collective-permute-done.after_ref.moved_ref, bf16[24,4096]{1,0:T(8,128)(2,1)S(1)} %copy-done.1, ...), custom_call_target="tpu_custom_call", output_to_operand_aliasing={{1}: (3, {})} | custom-call | bytes 1835008 | tf_op jit(solution)/shard_map/finish/pallas_call | solution.py:283
Async XLA Ops:
  2.6 8.0 %copy-start = (bf16[1,24,4096]{2,1,0:T(8,128)(2,1)S(1)}, bf16[1,24,4096]{2,1,0:T(8,128)(2,1)}, u32[]{:S(2)}) copy-start(bf16[1,24,4096]{2,1,0:T(8,128)(2,1)} %h_ref.1) | copy-start | bytes 589828
  2.6 24.6 %all-to-all-start = ((bf16[32,24,384]{2,1,0:T(8,128)(2,1)}), bf16[32,24,384]{2,1,0:T(8,128)(2,1)S(1)}, u32[]{:S(2)}, u32[]{:S(2)}) async-start(bf16[32,24,384]{2,1,0:T(8,128)(2,1)} %bitcast.7), calls=%async_computation | async-start | bytes 1179648 | tf_op jit(solution)/shard_map/all_to_all | solution.py:325
  10.6 16.7 %copy-start.2 = (s32[4,4]{1,0:T(4,128)S(1)}, s32[4,4]{1,0:T(4,128)}, u32[]{:S(2)}) copy-start(s32[4,4]{1,0:T(4,128)} %pattern_ref.1) | copy-start | bytes 196
  11.6 3.4 %collective-permute-start = (bf16[32,4096]{1,0:T(8,128)(2,1)S(1)}, bf16[32,4096]{1,0:T(8,128)(2,1)S(1)}, u32[]{:S(2)}, u32[]{:S(2)}) collective-permute-start(bf16[32,4096]{1,0:T(8,128)(2,1)S(1)} %residual.1), channel_id=1, source_target_pairs={{8,0},{16,8},{24,16},{9,1},{17,9},{25,17},{10,2},{18,10},{26,18},{... | collective-permute-start | bytes 786440 | tf_op jit(solution)/shard_map/ppermute | solution.py:21
  28.8 12.6 %all-to-all-start.1 = ((bf16[32,24,128]{2,1,0:T(8,128)(2,1)}), bf16[32,24,128]{2,1,0:T(8,128)(2,1)S(1)}, u32[]{:S(2)}, u32[]{:S(2)}) async-start(bf16[32,24,128]{2,1,0:T(8,128)(2,1)} %bitcast.8), calls=%async_computation.1 | async-start | bytes 393216 | tf_op jit(solution)/shard_map/all_to_all | solution.py:351
  31.5 7.8 %collective-permute-start.1 = (bf16[2,192,128]{2,1,0:T(8,128)(2,1)S(1)}, bf16[2,192,128]{2,1,0:T(8,128)(2,1)S(1)}, u32[]{:S(2)}, u32[]{:S(2)}) collective-permute-start(bf16[2,192,128]{2,1,0:T(8,128)(2,1)S(1)} %get-tuple-element.7), channel_id=1, source_target_pairs={{8,16},{16,8},{24,0},{9,17},{17,9},{25,1},{10,18},{18,10},{26,2},{... | collective-permute-start | bytes 294920 | tf_op jit(solution)/shard_map/ppermute | solution.py:355
  32.8 8.7 %collective-permute-start.2 = (bf16[2,192,128]{2,1,0:T(8,128)(2,1)S(1)}, bf16[2,192,128]{2,1,0:T(8,128)(2,1)S(1)}, u32[]{:S(2)}, u32[]{:S(2)}) collective-permute-start(bf16[2,192,128]{2,1,0:T(8,128)(2,1)S(1)} %get-tuple-element.8), channel_id=1, source_target_pairs={{0,16},{16,0},{24,8},{1,17},{17,1},{25,9},{2,18},{18,2},{26,10},{3... | collective-permute-start | bytes 294920 | tf_op jit(solution)/shard_map/ppermute | solution.py:355
  37.2 4.3 %copy-start.1 = (bf16[24,4096]{1,0:T(8,128)(2,1)S(1)}, bf16[24,4096]{1,0:T(8,128)(2,1)}, u32[]{:S(2)}) copy-start(bf16[24,4096]{1,0:T(8,128)(2,1)} %fresh_ref.1) | copy-start | bytes 589828
  37.3 4.2 %collective-permute-start.3 = (bf16[2,192,128]{2,1,0:T(8,128)(2,1)S(1)}, bf16[2,192,128]{2,1,0:T(8,128)(2,1)S(1)}, u32[]{:S(2)}, u32[]{:S(2)}) collective-permute-start(bf16[2,192,128]{2,1,0:T(8,128)(2,1)S(1)} %get-tuple-element.9), channel_id=1, source_target_pairs={{0,8},{8,0},{24,16},{1,9},{9,1},{25,17},{2,10},{10,2},{26,18},{3,1... | collective-permute-start | bytes 294920 | tf_op jit(solution)/shard_map/ppermute | solution.py:355

commit v25 on v15

--- a/solution.py
+++ b/solution.py
@@ -23,6 +23,10 @@
 
 def mixed(index, count):
     return (index + count // 2) % count
+
+
+def turned(group, groups):
+    return (group + groups // 2) % groups
 
 
 def pack_kernel(seq_count, parts, q_hbm, k_hbm, v_hbm, out_hbm, held, block, in_sems, out_sems):
@@ -47,7 +51,7 @@
             copies[3 * part + place].wait()
         for tm in range(tm_count):
             for seq in range(part * members, (part + 1) * members, 2):
-                first = (tm * seq_count + mixed(seq, seq_count)) * tok
+                first = (turned(tm, tm_count) * seq_count + mixed(seq, seq_count)) * tok
                 for place in range(3):
                     rows = []
                     for member in (seq, seq + 1):
@@ -56,7 +60,7 @@
                     block[first : first + 2 * tok, place * wide : (place + 1) * wide] = jnp.concatenate(
                         rows, axis=0
                     ).astype(jnp.bfloat16)
-            first = (tm * seq_count + mixed(part * members, seq_count)) * tok
+            first = (turned(tm, tm_count) * seq_count + mixed(part * members, seq_count)) * tok
             rows = slice(first, first + members * tok)
             outs.append(
                 pltpu.make_async_copy(block.at[rows], out_hbm.at[rows], out_sems.at[part, tm])
@@ -105,12 +109,12 @@
     return range(groups - 1, 0, -1)
 
 
-def hand_over(group, x_ref, out_ref, lanes=slice(None)):
+def hand_over(group, groups, x_ref, out_ref, lanes=slice(None)):
     wide = x_ref.shape[1] // 3
     rows = out_ref.shape[1]
     half = rows // 2
     for part in range(2):
-        first = pl.multiple_of(group * rows + mixed(part, 2) * half, half)
+        first = pl.multiple_of(turned(group, groups) * rows + mixed(part, 2) * half, half)
         for kind in range(2):
             out_ref[kind, part * half : (part + 1) * half, lanes] = x_ref[
                 pl.ds(first, half), (kind + 1) * wide : (kind + 2) * wide
@@ -136,6 +140,10 @@
             chosen = jnp.where((lane >= start) & (lane < start + rows), flag, chosen)
         kept.append(chosen[:, : ends[-1]] > 0)
 
+    def take(group, first):
+        start = turned(group, groups) * rows
+        return x_ref[start : start + rows, first : first + HD]
+
     copies = []
 
     def send(group):
@@ -153,14 +161,15 @@
 
     for head in range(0, wide, HD):
         query = jnp.concatenate(
-            [x_ref[group * rows : (group + 1) * rows, head : head + HD] for group in range(groups - 1, 0, -1)],
-            axis=0,
+            [take(group, head) for group in range(groups - 1, 0, -1)], axis=0
         )
         query = jnp.transpose(query)
-        value = jnp.transpose(x_ref[:, 2 * wide + head : 2 * wide + head + HD])
+        value = jnp.transpose(
+            jnp.concatenate([take(group, 2 * wide + head) for group in range(groups)], axis=0)
+        )
         scores, highest = [], None
         for source in range(groups):
-            key = x_ref[source * rows : (source + 1) * rows, wide + head : wide + head + HD]
+            key = take(source, wide + head)
             scores.append(
                 jnp.dot(key, query[:, : ends[source]], preferred_element_type=jnp.float32)
             )
@@ -195,7 +204,7 @@
                     send(waiting)
                 waiting -= 1
     for distance, hand_ref in zip(distances(groups), hand_refs):
-        hand_over(lax.rem(partner(here, distance, groups) + 1, groups), x_ref, hand_ref)
+        hand_over(lax.rem(partner(here, distance, groups) + 1, groups), groups, x_ref, hand_ref)
     for copy in copies:
         copy.wait()
 
@@ -212,7 +221,7 @@
 
     @pl.when(here < groups - 1)
     def place():
-        hand_over(here + 1, x_ref, out_ref.at[0], lanes_of(0, groups, here, wide))
+        hand_over(here + 1, groups, x_ref, out_ref.at[0], lanes_of(0, groups, here, wide))
         out_ref[0, :, :, lanes_of(distances(groups)[0], groups, here, wide)] = hand_ref[...]
 
 
@@ -303,11 +312,12 @@
             DMA((parts, tm_count)),
         ],
     )
-    order = [tm * seq_count + mixed(s, seq_count) for tm in range(tm_count) for s in range(seq_count)]
+    back = [tm * seq_count + mixed(s, seq_count) for tm in range(tm_count) for s in range(seq_count)]
+    half = len(back) // 2
     exchange = functools.partial(
-        lax.all_to_all, axis_name=BOTH, split_axis=0, concat_axis=0, tiled=True, axis_index_groups=[order]
-    )
-    exchanged = exchange(packed)
+        lax.all_to_all, axis_name=BOTH, split_axis=0, concat_axis=0, tiled=True
+    )
+    exchanged = exchange(packed, axis_index_groups=[back[half:] + back[:half]])
 
     residual = run(
         residual_kernel,
@@ -333,7 +343,7 @@
         flops=2 * count * tok * count * tok * wide,
         scratch=[VMEM((tm_count - 1, group_tok, wide), kind), DMA((tm_count,))],
     )
-    returned = exchange(attended)
+    returned = exchange(attended, axis_index_groups=[back])
     handed = []
     for distance, hand in zip(distances(tm_count), hands):
         route = [(i, partner(i, distance, tm_count)) for i in range(tm_count)]
@@ -441,7 +451,7 @@
     tm_count, seq_count = lax.axis_size("tm"), lax.axis_size("seq")
     _, tok, width = queries.shape
     count = tm_count * seq_count
-    even = width % (count * HD) == 0 and tok % 8 == 0 and seq_count % 4 == 0 and tm_count > 2
+    even = width % (count * HD) == 0 and tok % 8 == 0 and seq_count % 4 == 0 and tm_count > 2 and tm_count % 2 == 0
     return (spread_body if even else gather_body)(queries, *others)
 
 

time: 42.7 us -> 42.7 us (level)
  no operation moved by 1% of the time
where the time goes in v25:
time: 42.7 us; the launch traced here: 42.3 us
  starting transfers between devices  19 us (44%)
  waiting for transfers between devices  15.1 us (35%)
  Pallas kernels  6.82 us (16%)
  between operations  1.38 us (3%)
    all_to_all x1, waiting for transfers between devices, spread_body(): exchanged = exchange(packed, axis_index_groups=[back[half:] + back[:half]])  12.2 us
    ppermute x3, starting transfers between devices, spread_body(): lax.ppermute(hand, 'tm', [(i, j) for i, j in route if j < tm_count - 1])  7.75 us
    all_to_all x1, starting transfers between devices, spread_body(): exchanged = exchange(packed, axis_index_groups=[back[half:] + back[:half]])  7.3 us
    pallas_call x6, Pallas kernels, run(): pl.pallas_call(kernel, out_shape=outs, in_specs=specs, out_specs=[whole(g...  6.82 us
    all_to_all x1, starting transfers between devices, spread_body(): returned = exchange(attended, axis_index_groups=[back])  2.68 us
    ppermute x1, waiting for transfers between devices, shifted(): return lax.ppermute(block, axis, route)  2.13 us
    ppermute x1, starting transfers between devices, shifted(): return lax.ppermute(block, axis, route)  1.29 us
  transfers between devices with their start and end apart: 6, of which 4 were waited for; matrix products, arithmetic and copies ran while one was open for 0% of the time, Pallas kernels for 6%

profile of v25, /device:TPU:0, one launch (start us, length us, event | category | flops | bytes accessed | tf_op | source)
XLA Modules:
  0.0 42.3 jit_solution(13442371622177405880)
XLA Ops:
  0.6 2.0 %pack.1.after_ref = bf16[768,384]{1,0:T(8,128)(2,1)} custom-call(bf16[1,24,4096]{2,1,0:T(8,128)(2,1)} %q_hbm.1, bf16[1,24,4096]{2,1,0:T(8,128)(2,1)} %k_hbm.1, bf16[1,24,4096]{2,1,0:T(8,128)(2,1)} %v_hbm.1), custom_call_target="tpu_custom_call" | custom-call | bytes 1179648 | tf_op jit(solution)/shard_map/pack/pallas_call | solution.py:278
  2.6 0.0 copy-start
  2.6 7.3 %all-to-all-start = ((bf16[32,24,384]{2,1,0:T(8,128)(2,1)}), bf16[32,24,384]{2,1,0:T(8,128)(2,1)S(1)}, u32[]{:S(2)}, u32[]{:S(2)}) async-start(bf16[32,24,384]{2,1,0:T(8,128)(2,1)} %bitcast.7), calls=%async_computation | async-start | bytes 1179648 | tf_op jit(solution)/shard_map/all_to_all | solution.py:320
  10.6 0.0 copy-done
  10.6 0.0 copy-start.2
  10.6 1.0 %residual.1 = bf16[32,4096]{1,0:T(8,128)(2,1)S(1)} custom-call(s32[1]{0:T(128)S(6)} %copy.12.noise_ref, bf16[1,24,4096]{2,1,0:T(8,128)(2,1)S(1)} %copy-done, f32[50,4096]{1,0:T(8,128)} %gate_hbm.1, bf16[768,384]{1,0:T(8,128)(2,1)} %pack.1.after_ref), custom_call_target="tpu_custom_call" | custom-call | bytes 1867780 | tf_op jit(solution)/shard_map/residual/pallas_call | solution.py:278
  11.6 1.3 %collective-permute-start = (bf16[32,4096]{1,0:T(8,128)(2,1)S(1)}, bf16[32,4096]{1,0:T(8,128)(2,1)S(1)}, u32[]{:S(2)}, u32[]{:S(2)}) collective-permute-start(bf16[32,4096]{1,0:T(8,128)(2,1)S(1)} %residual.1), channel_id=1, source_target_pairs={{8,0},{16,8},{24,16},{9,1},{17,9},{25,17},{10,2},{18,10},{26,18},{... | collective-permute-start | bytes 786440 | tf_op jit(solution)/shard_map/ppermute | solution.py:21
  12.9 2.1 %collective-permute-done.after_ref.moved_ref = bf16[32,4096]{1,0:T(8,128)(2,1)S(1)} collective-permute-done((bf16[32,4096]{1,0:T(8,128)(2,1)S(1)}, bf16[32,4096]{1,0:T(8,128)(2,1)S(1)}, u32[]{:S(2)}, u32[]{:S(2)}) %collective-permute-start) | collective-permute-done | bytes 262176 | tf_op jit(solution)/shard_map/ppermute | solution.py:21
  15.1 12.2 %all-to-all-done = bf16[32,24,384]{2,1,0:T(8,128)(2,1)S(1)} async-done(((bf16[32,24,384]{2,1,0:T(8,128)(2,1)}), bf16[32,24,384]{2,1,0:T(8,128)(2,1)S(1)}, u32[]{:S(2)}, u32[]{:S(2)}) %all-to-all-start) | async-done | bytes 589856 | tf_op jit(solution)/shard_map/all_to_all | solution.py:320
  27.3 0.0 copy-done.2
  27.3 1.6 %attend.1 = (bf16[768,128]{1,0:T(8,128)(2,1)}, bf16[2,192,128]{2,1,0:T(8,128)(2,1)S(1)}, bf16[2,192,128]{2,1,0:T(8,128)(2,1)S(1)}, bf16[2,192,128]{2,1,0:T(8,128)(2,1)S(1)}) custom-call(s32[4,4]{1,0:T(4,128)S(1)} %copy-done.2, bf16[768,384]{1,0:T(8,128)(2,1)S(1)} %bitcast.4, bf16[32,4096]{1,0:T(8,128)(2,1)S(1)} %collective-permute-done.after_ref.moved_ref), custom_call_target="tpu_custom_call" | custom-call | flops 150994944 | bytes 1343552 | tf_op jit(solution)/shard_map/attend/pallas_call | solution.py:278
  28.8 2.7 %all-to-all-start.1 = ((bf16[32,24,128]{2,1,0:T(8,128)(2,1)}), bf16[32,24,128]{2,1,0:T(8,128)(2,1)S(1)}, u32[]{:S(2)}, u32[]{:S(2)}) async-start(bf16[32,24,128]{2,1,0:T(8,128)(2,1)} %bitcast.8), calls=%async_computation.1 | async-start | bytes 393216 | tf_op jit(solution)/shard_map/all_to_all | solution.py:346
  31.5 1.3 %collective-permute-start.1 = (bf16[2,192,128]{2,1,0:T(8,128)(2,1)S(1)}, bf16[2,192,128]{2,1,0:T(8,128)(2,1)S(1)}, u32[]{:S(2)}, u32[]{:S(2)}) collective-permute-start(bf16[2,192,128]{2,1,0:T(8,128)(2,1)S(1)} %get-tuple-element.7), channel_id=1, source_target_pairs={{8,16},{16,8},{24,0},{9,17},{17,9},{25,1},{10,18},{18,10},{26,2},{... | collective-permute-start | bytes 294920 | tf_op jit(solution)/shard_map/ppermute | solution.py:350
  32.8 4.4 %collective-permute-start.2 = (bf16[2,192,128]{2,1,0:T(8,128)(2,1)S(1)}, bf16[2,192,128]{2,1,0:T(8,128)(2,1)S(1)}, u32[]{:S(2)}, u32[]{:S(2)}) collective-permute-start(bf16[2,192,128]{2,1,0:T(8,128)(2,1)S(1)} %get-tuple-element.8), channel_id=1, source_target_pairs={{0,16},{16,0},{24,8},{1,17},{17,1},{25,9},{2,18},{18,2},{26,10},{3... | collective-permute-start | bytes 294920 | tf_op jit(solution)/shard_map/ppermute | solution.py:350
  37.2 0.0 copy-start.1
  37.2 2.1 %collective-permute-start.3 = (bf16[2,192,128]{2,1,0:T(8,128)(2,1)S(1)}, bf16[2,192,128]{2,1,0:T(8,128)(2,1)S(1)}, u32[]{:S(2)}, u32[]{:S(2)}) collective-permute-start(bf16[2,192,128]{2,1,0:T(8,128)(2,1)S(1)} %get-tuple-element.9), channel_id=1, source_target_pairs={{0,8},{8,0},{24,16},{1,9},{9,1},{25,17},{2,10},{10,2},{26,18},{3,1... | collective-permute-start | bytes 294920 | tf_op jit(solution)/shard_map/ppermute | solution.py:350
  39.3 0.0 collective-permute-done.1.hand_ref
  39.3 0.8 %cache.1.after_ref.begun_hbm = bf16[1,2,192,512]{3,2,1,0:T(8,128)(2,1)} custom-call(bf16[768,384]{1,0:T(8,128)(2,1)S(1)} %bitcast.5, bf16[2,192,128]{2,1,0:T(8,128)(2,1)S(1)} %collective-permute-done.1.hand_ref), custom_call_target="tpu_custom_call" | custom-call | bytes 1081344 | tf_op jit(solution)/shard_map/cache/pallas_call | solution.py:278
  40.1 0.2 all-to-all-done.1
  40.4 0.0 copy-done.1
  40.4 0.8 %update.1.after_ref = bf16[1,24,4096]{2,1,0:T(8,128)(2,1)} custom-call(bf16[768,128]{1,0:T(8,128)(2,1)S(1)} %bitcast.6, bf16[32,4096]{1,0:T(8,128)(2,1)S(1)} %collective-permute-done.after_ref.moved_ref, bf16[24,4096]{1,0:T(8,128)(2,1)S(1)} %copy-done.1, bf16[1,2,192,512]{3,2,1,0:T(8,128)(2,1)} %cache.1.after_ref.begun_hbm), custom_call_target="tpu_custom_call" | custom-call | bytes 1245184 | tf_op jit(solution)/shard_map/update/pallas_call | solution.py:278
  41.2 0.4 %collective-permute-done.2.refs_0_ = bf16[2,192,128]{2,1,0:T(8,128)(2,1)S(1)} collective-permute-done((bf16[2,192,128]{2,1,0:T(8,128)(2,1)S(1)}, bf16[2,192,128]{2,1,0:T(8,128)(2,1)S(1)}, u32[]{:S(2)}, u32[]{:S(2)}) %collective-permute-start.2) | collective-permute-done | bytes 98336 | tf_op jit(solution)/shard_map/ppermute | solution.py:350
  41.6 0.0 collective-permute-done.3.refs_1_
  41.6 0.7 %cache_rest.1 = bf16[1,2,192,512]{3,2,1,0:T(8,128)(2,1)} custom-call(bf16[1,2,192,512]{3,2,1,0:T(8,128)(2,1)} %cache.1.after_ref.begun_hbm, bf16[1,24,4096]{2,1,0:T(8,128)(2,1)} %update.1.after_ref, bf16[2,192,128]{2,1,0:T(8,128)(2,1)S(1)} %collective-permute-done.2.refs_0_, ...), custom_call_target="tpu_custom_call", output_to_operand_aliasing={{}: (0, {})} | custom-call | bytes 1179648 | tf_op jit(solution)/shard_map/cache_rest/pallas_call | solution.py:278
Async XLA Ops:
  2.6 8.0 %copy-start = (bf16[1,24,4096]{2,1,0:T(8,128)(2,1)S(1)}, bf16[1,24,4096]{2,1,0:T(8,128)(2,1)}, u32[]{:S(2)}) copy-start(bf16[1,24,4096]{2,1,0:T(8,128)(2,1)} %h_ref.1) | copy-start | bytes 589828
  2.6 24.6 %all-to-all-start = ((bf16[32,24,384]{2,1,0:T(8,128)(2,1)}), bf16[32,24,384]{2,1,0:T(8,128)(2,1)S(1)}, u32[]{:S(2)}, u32[]{:S(2)}) async-start(bf16[32,24,384]{2,1,0:T(8,128)(2,1)} %bitcast.7), calls=%async_computation | async-start | bytes 1179648 | tf_op jit(solution)/shard_map/all_to_all | solution.py:320
  10.6 16.7 %copy-start.2 = (s32[4,4]{1,0:T(4,128)S(1)}, s32[4,4]{1,0:T(4,128)}, u32[]{:S(2)}) copy-start(s32[4,4]{1,0:T(4,128)} %pattern_ref.1) | copy-start | bytes 196
  11.6 3.4 %collective-permute-start = (bf16[32,4096]{1,0:T(8,128)(2,1)S(1)}, bf16[32,4096]{1,0:T(8,128)(2,1)S(1)}, u32[]{:S(2)}, u32[]{:S(2)}) collective-permute-start(bf16[32,4096]{1,0:T(8,128)(2,1)S(1)} %residual.1), channel_id=1, source_target_pairs={{8,0},{16,8},{24,16},{9,1},{17,9},{25,17},{10,2},{18,10},{26,18},{... | collective-permute-start | bytes 786440 | tf_op jit(solution)/shard_map/ppermute | solution.py:21
  28.8 11.6 %all-to-all-start.1 = ((bf16[32,24,128]{2,1,0:T(8,128)(2,1)}), bf16[32,24,128]{2,1,0:T(8,128)(2,1)S(1)}, u32[]{:S(2)}, u32[]{:S(2)}) async-start(bf16[32,24,128]{2,1,0:T(8,128)(2,1)} %bitcast.8), calls=%async_computation.1 | async-start | bytes 393216 | tf_op jit(solution)/shard_map/all_to_all | solution.py:346
  31.5 7.8 %collective-permute-start.1 = (bf16[2,192,128]{2,1,0:T(8,128)(2,1)S(1)}, bf16[2,192,128]{2,1,0:T(8,128)(2,1)S(1)}, u32[]{:S(2)}, u32[]{:S(2)}) collective-permute-start(bf16[2,192,128]{2,1,0:T(8,128)(2,1)S(1)} %get-tuple-element.7), channel_id=1, source_target_pairs={{8,16},{16,8},{24,0},{9,17},{17,9},{25,1},{10,18},{18,10},{26,2},{... | collective-permute-start | bytes 294920 | tf_op jit(solution)/shard_map/ppermute | solution.py:350
  32.8 8.8 %collective-permute-start.2 = (bf16[2,192,128]{2,1,0:T(8,128)(2,1)S(1)}, bf16[2,192,128]{2,1,0:T(8,128)(2,1)S(1)}, u32[]{:S(2)}, u32[]{:S(2)}) collective-permute-start(bf16[2,192,128]{2,1,0:T(8,128)(2,1)S(1)} %get-tuple-element.8), channel_id=1, source_target_pairs={{0,16},{16,0},{24,8},{1,17},{17,1},{25,9},{2,18},{18,2},{26,10},{3... | collective-permute-start | bytes 294920 | tf_op jit(solution)/shard_map/ppermute | solution.py:350
  37.2 3.2 %copy-start.1 = (bf16[24,4096]{1,0:T(8,128)(2,1)S(1)}, bf16[24,4096]{1,0:T(8,128)(2,1)}, u32[]{:S(2)}) copy-start(bf16[24,4096]{1,0:T(8,128)(2,1)} %fresh_ref.1) | copy-start | bytes 589828
  37.2 4.4 %collective-permute-start.3 = (bf16[2,192,128]{2,1,0:T(8,128)(2,1)S(1)}, bf16[2,192,128]{2,1,0:T(8,128)(2,1)S(1)}, u32[]{:S(2)}, u32[]{:S(2)}) collective-permute-start(bf16[2,192,128]{2,1,0:T(8,128)(2,1)S(1)} %get-tuple-element.9), channel_id=1, source_target_pairs={{0,8},{8,0},{24,16},{1,9},{9,1},{25,17},{2,10},{10,2},{26,18},{3,1... | collective-permute-start | bytes 294920 | tf_op jit(solution)/shard_map/ppermute | solution.py:350

commit v26 on v25

--- a/solution.py
+++ b/solution.py
@@ -25,8 +25,18 @@
     return (index + count // 2) % count
 
 
-def turned(group, groups):
-    return (group + groups // 2) % groups
+def pair_place(group, pair, pairs):
+    return pair + group % 2 * (pairs - 1 - 2 * pair)
+
+
+def out_order(tm_count, seq_count):
+    pairs = seq_count // 2
+    return [
+        (tm, 2 * pair_place(tm, pair, pairs) + member)
+        for tm in range(tm_count)
+        for pair in range(pairs)
+        for member in range(2)
+    ]
 
 
 def pack_kernel(seq_count, parts, q_hbm, k_hbm, v_hbm, out_hbm, held, block, in_sems, out_sems):
@@ -35,6 +45,7 @@
     count = out_hbm.shape[0] // tok
     tm_count = count // seq_count
     span, members = width // parts, seq_count // parts
+    order = out_order(tm_count, seq_count)
     copies = []
     for part in range(parts):
         columns = slice(part * span, (part + 1) * span)
@@ -51,7 +62,7 @@
             copies[3 * part + place].wait()
         for tm in range(tm_count):
             for seq in range(part * members, (part + 1) * members, 2):
-                first = (turned(tm, tm_count) * seq_count + mixed(seq, seq_count)) * tok
+                first = order.index((tm, seq)) * tok
                 for place in range(3):
                     rows = []
                     for member in (seq, seq + 1):
@@ -60,7 +71,7 @@
                     block[first : first + 2 * tok, place * wide : (place + 1) * wide] = jnp.concatenate(
                         rows, axis=0
                     ).astype(jnp.bfloat16)
-            first = (turned(tm, tm_count) * seq_count + mixed(part * members, seq_count)) * tok
+            first = order.index((tm, part * members)) * tok
             rows = slice(first, first + members * tok)
             outs.append(
                 pltpu.make_async_copy(block.at[rows], out_hbm.at[rows], out_sems.at[part, tm])
@@ -109,22 +120,24 @@
     return range(groups - 1, 0, -1)
 
 
-def hand_over(group, groups, x_ref, out_ref, lanes=slice(None)):
+def hand_over(group, seq_count, x_ref, out_ref, lanes=slice(None)):
     wide = x_ref.shape[1] // 3
-    rows = out_ref.shape[1]
-    half = rows // 2
-    for part in range(2):
-        first = pl.multiple_of(turned(group, groups) * rows + mixed(part, 2) * half, half)
+    pairs = seq_count // 2
+    step = out_ref.shape[1] // pairs
+    for pair in range(pairs):
+        first = pl.multiple_of((group * pairs + pair_place(group, pair, pairs)) * step, step)
         for kind in range(2):
-            out_ref[kind, part * half : (part + 1) * half, lanes] = x_ref[
-                pl.ds(first, half), (kind + 1) * wide : (kind + 2) * wide
+            out_ref[kind, pair * step : (pair + 1) * step, lanes] = x_ref[
+                pl.ds(first, step), (kind + 1) * wide : (kind + 2) * wide
             ]
 
 
-def attend_kernel(groups, pattern_ref, x_ref, after_ref, out_hbm, *refs):
+def attend_kernel(groups, seq_count, pattern_ref, x_ref, after_ref, out_hbm, *refs):
     *hand_refs, held, sems = refs
     wide = held.shape[2]
     rows = held.shape[1]
+    pairs = seq_count // 2
+    step = rows // pairs
     across = (groups - 1) * rows
     factor = math.log2(math.e) / math.sqrt(HD)
     here = lax.axis_index("tm")
@@ -141,8 +154,7 @@
         kept.append(chosen[:, : ends[-1]] > 0)
 
     def take(group, first):
-        start = turned(group, groups) * rows
-        return x_ref[start : start + rows, first : first + HD]
+        return x_ref[group * rows : (group + 1) * rows, first : first + HD]
 
     copies = []
 
@@ -198,13 +210,17 @@
                 left = result if left is None else jnp.concatenate([left, result], axis=0)
                 start = stop
             while left is not None and left.shape[0] >= rows:
-                held[waiting - 1, :, head : head + HD] = left[:rows].astype(jnp.bfloat16)
+                ready = left[:rows].astype(jnp.bfloat16)
+                for pair in range(pairs):
+                    at = pair_place(waiting, pair, pairs) * step
+                    to = mixed(2 * pair, seq_count) // 2 * step
+                    held[waiting - 1, to : to + step, head : head + HD] = ready[at : at + step]
                 left = left[rows:] if left.shape[0] > rows else None
                 if last:
                     send(waiting)
                 waiting -= 1
     for distance, hand_ref in zip(distances(groups), hand_refs):
-        hand_over(lax.rem(partner(here, distance, groups) + 1, groups), groups, x_ref, hand_ref)
+        hand_over(lax.rem(partner(here, distance, groups) + 1, groups), seq_count, x_ref, hand_ref)
     for copy in copies:
         copy.wait()
 
@@ -214,14 +230,14 @@
     return pl.ds(pl.multiple_of(source * wide, wide), wide)
 
 
-def cache_kernel(groups, x_ref, hand_ref, out_ref):
+def cache_kernel(groups, seq_count, x_ref, hand_ref, out_ref):
     wide = x_ref.shape[1] // 3
     here = lax.axis_index("tm")
     out_ref[...] = jnp.zeros_like(out_ref)
 
     @pl.when(here < groups - 1)
     def place():
-        hand_over(here + 1, groups, x_ref, out_ref.at[0], lanes_of(0, groups, here, wide))
+        hand_over(here + 1, seq_count, x_ref, out_ref.at[0], lanes_of(0, groups, here, wide))
         out_ref[0, :, :, lanes_of(distances(groups)[0], groups, here, wide)] = hand_ref[...]
 
 
@@ -297,7 +313,7 @@
     group_tok = tok * seq_count
     kind = queries.dtype
     DMA = pltpu.SemaphoreType.DMA
-    parts = 4 if seq_count % 8 == 0 else 2
+    parts = seq_count // 2
 
     packed = run(
         functools.partial(pack_kernel, seq_count, parts),
@@ -313,11 +329,11 @@
         ],
     )
     back = [tm * seq_count + mixed(s, seq_count) for tm in range(tm_count) for s in range(seq_count)]
-    half = len(back) // 2
+    out = [tm * seq_count + index for tm, index in out_order(tm_count, seq_count)]
     exchange = functools.partial(
         lax.all_to_all, axis_name=BOTH, split_axis=0, concat_axis=0, tiled=True
     )
-    exchanged = exchange(packed, axis_index_groups=[back[half:] + back[:half]])
+    exchanged = exchange(packed, axis_index_groups=[out])
 
     residual = run(
         residual_kernel,
@@ -335,7 +351,7 @@
     moved = shifted(residual, "tm", -1)
 
     attended, *hands = run(
-        functools.partial(attend_kernel, tm_count),
+        functools.partial(attend_kernel, tm_count, seq_count),
         "attend",
         [HBM((count * tok, wide), kind)] + [VMEM((2, group_tok, wide), kind)] * (tm_count - 1),
         [whole(), whole(), whole(pl.ANY)],
@@ -351,7 +367,7 @@
 
     first, *rest = handed
     begun = run(
-        functools.partial(cache_kernel, tm_count),
+        functools.partial(cache_kernel, tm_count, seq_count),
         "cache",
         [jax.ShapeDtypeStruct((1, 2, group_tok, tm_count * wide), kind)],
         [whole()] * 2,

time: 42.7 us -> 42.8 us (level)
  waiting for transfers between devices: 15.1 us -> 14.2 us
  starting transfers between devices: 19 us -> 19.9 us
    all_to_all x1, starting transfers between devices: 2.68 us -> 3.6 us  [spread_body(): returned = exchange(attended, axis_index_groups=[back])]
    all_to_all x1, waiting for transfers between devices: 12.2 us -> 11.3 us  [spread_body(): exchanged = exchange(packed, axis_index_groups=[out])]
where the time goes in v26:
time: 42.8 us; the launch traced here: 42.4 us
  starting transfers between devices  19.9 us (46%)
  waiting for transfers between devices  14.2 us (33%)
  Pallas kernels  6.85 us (16%)
  between operations  1.38 us (3%)
    all_to_all x1, waiting for transfers between devices, spread_body(): exchanged = exchange(packed, axis_index_groups=[out])  11.3 us
    ppermute x3, starting transfers between devices, spread_body(): lax.ppermute(hand, 'tm', [(i, j) for i, j in route if j < tm_count - 1])  7.75 us
    all_to_all x1, starting transfers between devices, spread_body(): exchanged = exchange(packed, axis_index_groups=[out])  7.3 us
    pallas_call x6, Pallas kernels, run(): pl.pallas_call(kernel, out_shape=outs, in_specs=specs, out_specs=[whole(g...  6.85 us
    all_to_all x1, starting transfers between devices, spread_body(): returned = exchange(attended, axis_index_groups=[back])  3.6 us
    ppermute x1, waiting for transfers between devices, shifted(): return lax.ppermute(block, axis, route)  2.13 us
    ppermute x1, starting transfers between devices, shifted(): return lax.ppermute(block, axis, route)  1.29 us
  transfers between devices with their start and end apart: 6, of which 4 were waited for; matrix products, arithmetic and copies ran while one was open for 0% of the time, Pallas kernels for 6%

profile of v26, /device:TPU:0, one launch (start us, length us, event | category | flops | bytes accessed | tf_op | source)
XLA Modules:
  0.0 42.4 jit_solution(112631410153095006)
XLA Ops:
  0.6 2.0 %pack.1.after_ref = bf16[768,384]{1,0:T(8,128)(2,1)} custom-call(bf16[1,24,4096]{2,1,0:T(8,128)(2,1)} %q_hbm.1, bf16[1,24,4096]{2,1,0:T(8,128)(2,1)} %k_hbm.1, bf16[1,24,4096]{2,1,0:T(8,128)(2,1)} %v_hbm.1), custom_call_target="tpu_custom_call" | custom-call | bytes 1179648 | tf_op jit(solution)/shard_map/pack/pallas_call | solution.py:294
  2.6 0.0 copy-start
  2.7 7.3 %all-to-all-start = ((bf16[32,24,384]{2,1,0:T(8,128)(2,1)}), bf16[32,24,384]{2,1,0:T(8,128)(2,1)S(1)}, u32[]{:S(2)}, u32[]{:S(2)}) async-start(bf16[32,24,384]{2,1,0:T(8,128)(2,1)} %bitcast.7), calls=%async_computation | async-start | bytes 1179648 | tf_op jit(solution)/shard_map/all_to_all | solution.py:336
  10.6 0.0 copy-done
  10.6 0.0 copy-start.2
  10.6 1.0 %residual.1 = bf16[32,4096]{1,0:T(8,128)(2,1)S(1)} custom-call(s32[1]{0:T(128)S(6)} %copy.12.noise_ref, bf16[1,24,4096]{2,1,0:T(8,128)(2,1)S(1)} %copy-done, f32[50,4096]{1,0:T(8,128)} %gate_hbm.1, bf16[768,384]{1,0:T(8,128)(2,1)} %pack.1.after_ref), custom_call_target="tpu_custom_call" | custom-call | bytes 1867780 | tf_op jit(solution)/shard_map/residual/pallas_call | solution.py:294
  11.7 1.3 %collective-permute-start = (bf16[32,4096]{1,0:T(8,128)(2,1)S(1)}, bf16[32,4096]{1,0:T(8,128)(2,1)S(1)}, u32[]{:S(2)}, u32[]{:S(2)}) collective-permute-start(bf16[32,4096]{1,0:T(8,128)(2,1)S(1)} %residual.1), channel_id=1, source_target_pairs={{8,0},{16,8},{24,16},{9,1},{17,9},{25,17},{10,2},{18,10},{26,18},{... | collective-permute-start | bytes 786440 | tf_op jit(solution)/shard_map/ppermute | solution.py:21
  13.0 2.1 %collective-permute-done.after_ref.moved_ref = bf16[32,4096]{1,0:T(8,128)(2,1)S(1)} collective-permute-done((bf16[32,4096]{1,0:T(8,128)(2,1)S(1)}, bf16[32,4096]{1,0:T(8,128)(2,1)S(1)}, u32[]{:S(2)}, u32[]{:S(2)}) %collective-permute-start) | collective-permute-done | bytes 262176 | tf_op jit(solution)/shard_map/ppermute | solution.py:21
  15.1 11.3 %all-to-all-done = bf16[32,24,384]{2,1,0:T(8,128)(2,1)S(1)} async-done(((bf16[32,24,384]{2,1,0:T(8,128)(2,1)}), bf16[32,24,384]{2,1,0:T(8,128)(2,1)S(1)}, u32[]{:S(2)}, u32[]{:S(2)}) %all-to-all-start) | async-done | bytes 589856 | tf_op jit(solution)/shard_map/all_to_all | solution.py:336
  26.4 0.0 copy-done.2
  26.4 1.6 %attend.1 = (bf16[768,128]{1,0:T(8,128)(2,1)}, bf16[2,192,128]{2,1,0:T(8,128)(2,1)S(1)}, bf16[2,192,128]{2,1,0:T(8,128)(2,1)S(1)}, bf16[2,192,128]{2,1,0:T(8,128)(2,1)S(1)}) custom-call(s32[4,4]{1,0:T(4,128)S(1)} %copy-done.2, bf16[768,384]{1,0:T(8,128)(2,1)S(1)} %bitcast.4, bf16[32,4096]{1,0:T(8,128)(2,1)S(1)} %collective-permute-done.after_ref.moved_ref), custom_call_target="tpu_custom_call" | custom-call | flops 150994944 | bytes 1343552 | tf_op jit(solution)/shard_map/attend/pallas_call | solution.py:294
  28.0 3.6 %all-to-all-start.1 = ((bf16[32,24,128]{2,1,0:T(8,128)(2,1)}), bf16[32,24,128]{2,1,0:T(8,128)(2,1)S(1)}, u32[]{:S(2)}, u32[]{:S(2)}) async-start(bf16[32,24,128]{2,1,0:T(8,128)(2,1)} %bitcast.8), calls=%async_computation.1 | async-start | bytes 393216 | tf_op jit(solution)/shard_map/all_to_all | solution.py:362
  31.6 1.3 %collective-permute-start.1 = (bf16[2,192,128]{2,1,0:T(8,128)(2,1)S(1)}, bf16[2,192,128]{2,1,0:T(8,128)(2,1)S(1)}, u32[]{:S(2)}, u32[]{:S(2)}) collective-permute-start(bf16[2,192,128]{2,1,0:T(8,128)(2,1)S(1)} %get-tuple-element.7), channel_id=1, source_target_pairs={{8,16},{16,8},{24,0},{9,17},{17,9},{25,1},{10,18},{18,10},{26,2},{... | collective-permute-start | bytes 294920 | tf_op jit(solution)/shard_map/ppermute | solution.py:366
  32.9 4.4 %collective-permute-start.2 = (bf16[2,192,128]{2,1,0:T(8,128)(2,1)S(1)}, bf16[2,192,128]{2,1,0:T(8,128)(2,1)S(1)}, u32[]{:S(2)}, u32[]{:S(2)}) collective-permute-start(bf16[2,192,128]{2,1,0:T(8,128)(2,1)S(1)} %get-tuple-element.8), channel_id=1, source_target_pairs={{0,16},{16,0},{24,8},{1,17},{17,1},{25,9},{2,18},{18,2},{26,10},{3... | collective-permute-start | bytes 294920 | tf_op jit(solution)/shard_map/ppermute | solution.py:366
  37.3 0.0 copy-start.1
  37.3 2.1 %collective-permute-start.3 = (bf16[2,192,128]{2,1,0:T(8,128)(2,1)S(1)}, bf16[2,192,128]{2,1,0:T(8,128)(2,1)S(1)}, u32[]{:S(2)}, u32[]{:S(2)}) collective-permute-start(bf16[2,192,128]{2,1,0:T(8,128)(2,1)S(1)} %get-tuple-element.9), channel_id=1, source_target_pairs={{0,8},{8,0},{24,16},{1,9},{9,1},{25,17},{2,10},{10,2},{26,18},{3,1... | collective-permute-start | bytes 294920 | tf_op jit(solution)/shard_map/ppermute | solution.py:366
  39.4 0.0 collective-permute-done.1.hand_ref
  39.4 0.8 %cache.1.after_ref.begun_hbm = bf16[1,2,192,512]{3,2,1,0:T(8,128)(2,1)} custom-call(bf16[768,384]{1,0:T(8,128)(2,1)S(1)} %bitcast.5, bf16[2,192,128]{2,1,0:T(8,128)(2,1)S(1)} %collective-permute-done.1.hand_ref), custom_call_target="tpu_custom_call" | custom-call | bytes 1081344 | tf_op jit(solution)/shard_map/cache/pallas_call | solution.py:294
  40.2 0.2 all-to-all-done.1
  40.5 0.0 copy-done.1
  40.5 0.8 %update.1.after_ref = bf16[1,24,4096]{2,1,0:T(8,128)(2,1)} custom-call(bf16[768,128]{1,0:T(8,128)(2,1)S(1)} %bitcast.6, bf16[32,4096]{1,0:T(8,128)(2,1)S(1)} %collective-permute-done.after_ref.moved_ref, bf16[24,4096]{1,0:T(8,128)(2,1)S(1)} %copy-done.1, bf16[1,2,192,512]{3,2,1,0:T(8,128)(2,1)} %cache.1.after_ref.begun_hbm), custom_call_target="tpu_custom_call" | custom-call | bytes 1245184 | tf_op jit(solution)/shard_map/update/pallas_call | solution.py:294
  41.2 0.4 %collective-permute-done.2.refs_0_ = bf16[2,192,128]{2,1,0:T(8,128)(2,1)S(1)} collective-permute-done((bf16[2,192,128]{2,1,0:T(8,128)(2,1)S(1)}, bf16[2,192,128]{2,1,0:T(8,128)(2,1)S(1)}, u32[]{:S(2)}, u32[]{:S(2)}) %collective-permute-start.2) | collective-permute-done | bytes 98336 | tf_op jit(solution)/shard_map/ppermute | solution.py:366
  41.7 0.0 collective-permute-done.3.refs_1_
  41.7 0.7 %cache_rest.1 = bf16[1,2,192,512]{3,2,1,0:T(8,128)(2,1)} custom-call(bf16[1,2,192,512]{3,2,1,0:T(8,128)(2,1)} %cache.1.after_ref.begun_hbm, bf16[1,24,4096]{2,1,0:T(8,128)(2,1)} %update.1.after_ref, bf16[2,192,128]{2,1,0:T(8,128)(2,1)S(1)} %collective-permute-done.2.refs_0_, ...), custom_call_target="tpu_custom_call", output_to_operand_aliasing={{}: (0, {})} | custom-call | bytes 1179648 | tf_op jit(solution)/shard_map/cache_rest/pallas_call | solution.py:294
Async XLA Ops:
  2.6 8.0 %copy-start = (bf16[1,24,4096]{2,1,0:T(8,128)(2,1)S(1)}, bf16[1,24,4096]{2,1,0:T(8,128)(2,1)}, u32[]{:S(2)}) copy-start(bf16[1,24,4096]{2,1,0:T(8,128)(2,1)} %h_ref.1) | copy-start | bytes 589828
  2.7 23.7 %all-to-all-start = ((bf16[32,24,384]{2,1,0:T(8,128)(2,1)}), bf16[32,24,384]{2,1,0:T(8,128)(2,1)S(1)}, u32[]{:S(2)}, u32[]{:S(2)}) async-start(bf16[32,24,384]{2,1,0:T(8,128)(2,1)} %bitcast.7), calls=%async_computation | async-start | bytes 1179648 | tf_op jit(solution)/shard_map/all_to_all | solution.py:336
  10.6 15.8 %copy-start.2 = (s32[4,4]{1,0:T(4,128)S(1)}, s32[4,4]{1,0:T(4,128)}, u32[]{:S(2)}) copy-start(s32[4,4]{1,0:T(4,128)} %pattern_ref.1) | copy-start | bytes 196
  11.7 3.4 %collective-permute-start = (bf16[32,4096]{1,0:T(8,128)(2,1)S(1)}, bf16[32,4096]{1,0:T(8,128)(2,1)S(1)}, u32[]{:S(2)}, u32[]{:S(2)}) collective-permute-start(bf16[32,4096]{1,0:T(8,128)(2,1)S(1)} %residual.1), channel_id=1, source_target_pairs={{8,0},{16,8},{24,16},{9,1},{17,9},{25,17},{10,2},{18,10},{26,18},{... | collective-permute-start | bytes 786440 | tf_op jit(solution)/shard_map/ppermute | solution.py:21
  28.0 12.5 %all-to-all-start.1 = ((bf16[32,24,128]{2,1,0:T(8,128)(2,1)}), bf16[32,24,128]{2,1,0:T(8,128)(2,1)S(1)}, u32[]{:S(2)}, u32[]{:S(2)}) async-start(bf16[32,24,128]{2,1,0:T(8,128)(2,1)} %bitcast.8), calls=%async_computation.1 | async-start | bytes 393216 | tf_op jit(solution)/shard_map/all_to_all | solution.py:362
  31.6 7.8 %collective-permute-start.1 = (bf16[2,192,128]{2,1,0:T(8,128)(2,1)S(1)}, bf16[2,192,128]{2,1,0:T(8,128)(2,1)S(1)}, u32[]{:S(2)}, u32[]{:S(2)}) collective-permute-start(bf16[2,192,128]{2,1,0:T(8,128)(2,1)S(1)} %get-tuple-element.7), channel_id=1, source_target_pairs={{8,16},{16,8},{24,0},{9,17},{17,9},{25,1},{10,18},{18,10},{26,2},{... | collective-permute-start | bytes 294920 | tf_op jit(solution)/shard_map/ppermute | solution.py:366
  32.9 8.8 %collective-permute-start.2 = (bf16[2,192,128]{2,1,0:T(8,128)(2,1)S(1)}, bf16[2,192,128]{2,1,0:T(8,128)(2,1)S(1)}, u32[]{:S(2)}, u32[]{:S(2)}) collective-permute-start(bf16[2,192,128]{2,1,0:T(8,128)(2,1)S(1)} %get-tuple-element.8), channel_id=1, source_target_pairs={{0,16},{16,0},{24,8},{1,17},{17,1},{25,9},{2,18},{18,2},{26,10},{3... | collective-permute-start | bytes 294920 | tf_op jit(solution)/shard_map/ppermute | solution.py:366
  37.3 3.2 %copy-start.1 = (bf16[24,4096]{1,0:T(8,128)(2,1)S(1)}, bf16[24,4096]{1,0:T(8,128)(2,1)}, u32[]{:S(2)}) copy-start(bf16[24,4096]{1,0:T(8,128)(2,1)} %fresh_ref.1) | copy-start | bytes 589828
  37.3 4.4 %collective-permute-start.3 = (bf16[2,192,128]{2,1,0:T(8,128)(2,1)S(1)}, bf16[2,192,128]{2,1,0:T(8,128)(2,1)S(1)}, u32[]{:S(2)}, u32[]{:S(2)}) collective-permute-start(bf16[2,192,128]{2,1,0:T(8,128)(2,1)S(1)} %get-tuple-element.9), channel_id=1, source_target_pairs={{0,8},{8,0},{24,16},{1,9},{9,1},{25,17},{2,10},{10,2},{26,18},{3,1... | collective-permute-start | bytes 294920 | tf_op jit(solution)/shard_map/ppermute | solution.py:366

commit v27 on v26

--- a/solution.py
+++ b/solution.py
@@ -26,7 +26,8 @@
 
 
 def pair_place(group, pair, pairs):
-    return pair + group % 2 * (pairs - 1 - 2 * pair)
+    place = (pair + pairs // 2) % pairs
+    return place + group % 2 * (pairs - 1 - 2 * place)
 
 
 def out_order(tm_count, seq_count):

time: 42.8 us -> 42.8 us (level)
  waiting for transfers between devices: 14.2 us -> 15.3 us
  starting transfers between devices: 19.9 us -> 18.8 us
    all_to_all x1, starting transfers between devices: 3.6 us -> 2.6 us  [spread_body(): returned = exchange(attended, axis_index_groups=[back])]
    all_to_all x1, waiting for transfers between devices: 11.3 us -> 12.2 us  [spread_body(): exchanged = exchange(packed, axis_index_groups=[out])]
  transfers between devices with their start and end apart: 6 -> 6, of which waited for: 4 -> 5; matrix products, arithmetic and copies ran while one was open for 0% -> 0% of each run, Pallas kernels for 6% -> 6%
where the time goes in v27:
time: 42.8 us; the launch traced here: 42.3 us
  starting transfers between devices  18.8 us (44%)
  waiting for transfers between devices  15.3 us (36%)
  Pallas kernels  6.82 us (16%)
  between operations  1.38 us (3%)
    all_to_all x1, waiting for transfers between devices, spread_body(): exchanged = exchange(packed, axis_index_groups=[out])  12.2 us
    ppermute x3, starting transfers between devices, spread_body(): lax.ppermute(hand, 'tm', [(i, j) for i, j in route if j < tm_count - 1])  7.61 us
    all_to_all x1, starting transfers between devices, spread_body(): exchanged = exchange(packed, axis_index_groups=[out])  7.3 us
    pallas_call x6, Pallas kernels, run(): pl.pallas_call(kernel, out_shape=outs, in_specs=specs, out_specs=[whole(g...  6.82 us
    all_to_all x1, starting transfers between devices, spread_body(): returned = exchange(attended, axis_index_groups=[back])  2.6 us
    ppermute x1, waiting for transfers between devices, shifted(): return lax.ppermute(block, axis, route)  2.13 us
    ppermute x1, starting transfers between devices, shifted(): return lax.ppermute(block, axis, route)  1.29 us
  transfers between devices with their start and end apart: 6, of which 5 were waited for; matrix products, arithmetic and copies ran while one was open for 0% of the time, Pallas kernels for 6%

profile of v27, /device:TPU:0, one launch (start us, length us, event | category | flops | bytes accessed | tf_op | source)
XLA Modules:
  0.0 42.3 jit_solution(2692810624936187792)
XLA Ops:
  0.6 2.0 %pack.1.after_ref = bf16[768,384]{1,0:T(8,128)(2,1)} custom-call(bf16[1,24,4096]{2,1,0:T(8,128)(2,1)} %q_hbm.1, bf16[1,24,4096]{2,1,0:T(8,128)(2,1)} %k_hbm.1, bf16[1,24,4096]{2,1,0:T(8,128)(2,1)} %v_hbm.1), custom_call_target="tpu_custom_call" | custom-call | bytes 1179648 | tf_op jit(solution)/shard_map/pack/pallas_call | solution.py:295
  2.6 0.0 copy-start
  2.6 7.3 %all-to-all-start = ((bf16[32,24,384]{2,1,0:T(8,128)(2,1)}), bf16[32,24,384]{2,1,0:T(8,128)(2,1)S(1)}, u32[]{:S(2)}, u32[]{:S(2)}) async-start(bf16[32,24,384]{2,1,0:T(8,128)(2,1)} %bitcast.7), calls=%async_computation | async-start | bytes 1179648 | tf_op jit(solution)/shard_map/all_to_all | solution.py:337
  10.6 0.0 copy-done
  10.6 0.0 copy-start.2
  10.6 1.0 %residual.1 = bf16[32,4096]{1,0:T(8,128)(2,1)S(1)} custom-call(s32[1]{0:T(128)S(6)} %copy.12.noise_ref, bf16[1,24,4096]{2,1,0:T(8,128)(2,1)S(1)} %copy-done, f32[50,4096]{1,0:T(8,128)} %gate_hbm.1, bf16[768,384]{1,0:T(8,128)(2,1)} %pack.1.after_ref), custom_call_target="tpu_custom_call" | custom-call | bytes 1867780 | tf_op jit(solution)/shard_map/residual/pallas_call | solution.py:295
  11.6 1.3 %collective-permute-start = (bf16[32,4096]{1,0:T(8,128)(2,1)S(1)}, bf16[32,4096]{1,0:T(8,128)(2,1)S(1)}, u32[]{:S(2)}, u32[]{:S(2)}) collective-permute-start(bf16[32,4096]{1,0:T(8,128)(2,1)S(1)} %residual.1), channel_id=1, source_target_pairs={{8,0},{16,8},{24,16},{9,1},{17,9},{25,17},{10,2},{18,10},{26,18},{... | collective-permute-start | bytes 786440 | tf_op jit(solution)/shard_map/ppermute | solution.py:21
  12.9 2.1 %collective-permute-done.after_ref.moved_ref = bf16[32,4096]{1,0:T(8,128)(2,1)S(1)} collective-permute-done((bf16[32,4096]{1,0:T(8,128)(2,1)S(1)}, bf16[32,4096]{1,0:T(8,128)(2,1)S(1)}, u32[]{:S(2)}, u32[]{:S(2)}) %collective-permute-start) | collective-permute-done | bytes 262176 | tf_op jit(solution)/shard_map/ppermute | solution.py:21
  15.1 12.2 %all-to-all-done = bf16[32,24,384]{2,1,0:T(8,128)(2,1)S(1)} async-done(((bf16[32,24,384]{2,1,0:T(8,128)(2,1)}), bf16[32,24,384]{2,1,0:T(8,128)(2,1)S(1)}, u32[]{:S(2)}, u32[]{:S(2)}) %all-to-all-start) | async-done | bytes 589856 | tf_op jit(solution)/shard_map/all_to_all | solution.py:337
  27.2 0.0 copy-done.2
  27.2 1.6 %attend.1 = (bf16[768,128]{1,0:T(8,128)(2,1)}, bf16[2,192,128]{2,1,0:T(8,128)(2,1)S(1)}, bf16[2,192,128]{2,1,0:T(8,128)(2,1)S(1)}, bf16[2,192,128]{2,1,0:T(8,128)(2,1)S(1)}) custom-call(s32[4,4]{1,0:T(4,128)S(1)} %copy-done.2, bf16[768,384]{1,0:T(8,128)(2,1)S(1)} %bitcast.4, bf16[32,4096]{1,0:T(8,128)(2,1)S(1)} %collective-permute-done.after_ref.moved_ref), custom_call_target="tpu_custom_call" | custom-call | flops 150994944 | bytes 1343552 | tf_op jit(solution)/shard_map/attend/pallas_call | solution.py:295
  28.8 2.6 %all-to-all-start.1 = ((bf16[32,24,128]{2,1,0:T(8,128)(2,1)}), bf16[32,24,128]{2,1,0:T(8,128)(2,1)S(1)}, u32[]{:S(2)}, u32[]{:S(2)}) async-start(bf16[32,24,128]{2,1,0:T(8,128)(2,1)} %bitcast.8), calls=%async_computation.1 | async-start | bytes 393216 | tf_op jit(solution)/shard_map/all_to_all | solution.py:363
  31.4 1.3 %collective-permute-start.1 = (bf16[2,192,128]{2,1,0:T(8,128)(2,1)S(1)}, bf16[2,192,128]{2,1,0:T(8,128)(2,1)S(1)}, u32[]{:S(2)}, u32[]{:S(2)}) collective-permute-start(bf16[2,192,128]{2,1,0:T(8,128)(2,1)S(1)} %get-tuple-element.7), channel_id=1, source_target_pairs={{8,16},{16,8},{24,0},{9,17},{17,9},{25,1},{10,18},{18,10},{26,2},{... | collective-permute-start | bytes 294920 | tf_op jit(solution)/shard_map/ppermute | solution.py:367
  32.7 4.3 %collective-permute-start.2 = (bf16[2,192,128]{2,1,0:T(8,128)(2,1)S(1)}, bf16[2,192,128]{2,1,0:T(8,128)(2,1)S(1)}, u32[]{:S(2)}, u32[]{:S(2)}) collective-permute-start(bf16[2,192,128]{2,1,0:T(8,128)(2,1)S(1)} %get-tuple-element.8), channel_id=1, source_target_pairs={{0,16},{16,0},{24,8},{1,17},{17,1},{25,9},{2,18},{18,2},{26,10},{3... | collective-permute-start | bytes 294920 | tf_op jit(solution)/shard_map/ppermute | solution.py:367
  37.0 0.0 copy-start.1
  37.0 2.1 %collective-permute-start.3 = (bf16[2,192,128]{2,1,0:T(8,128)(2,1)S(1)}, bf16[2,192,128]{2,1,0:T(8,128)(2,1)S(1)}, u32[]{:S(2)}, u32[]{:S(2)}) collective-permute-start(bf16[2,192,128]{2,1,0:T(8,128)(2,1)S(1)} %get-tuple-element.9), channel_id=1, source_target_pairs={{0,8},{8,0},{24,16},{1,9},{9,1},{25,17},{2,10},{10,2},{26,18},{3,1... | collective-permute-start | bytes 294920 | tf_op jit(solution)/shard_map/ppermute | solution.py:367
  39.1 0.2 collective-permute-done.1.hand_ref
  39.3 0.8 %cache.1.after_ref.begun_hbm = bf16[1,2,192,512]{3,2,1,0:T(8,128)(2,1)} custom-call(bf16[768,384]{1,0:T(8,128)(2,1)S(1)} %bitcast.5, bf16[2,192,128]{2,1,0:T(8,128)(2,1)S(1)} %collective-permute-done.1.hand_ref), custom_call_target="tpu_custom_call" | custom-call | bytes 1081344 | tf_op jit(solution)/shard_map/cache/pallas_call | solution.py:295
  40.1 0.2 all-to-all-done.1
  40.3 0.0 copy-done.1
  40.3 0.8 %update.1.after_ref = bf16[1,24,4096]{2,1,0:T(8,128)(2,1)} custom-call(bf16[768,128]{1,0:T(8,128)(2,1)S(1)} %bitcast.6, bf16[32,4096]{1,0:T(8,128)(2,1)S(1)} %collective-permute-done.after_ref.moved_ref, bf16[24,4096]{1,0:T(8,128)(2,1)S(1)} %copy-done.1, bf16[1,2,192,512]{3,2,1,0:T(8,128)(2,1)} %cache.1.after_ref.begun_hbm), custom_call_target="tpu_custom_call" | custom-call | bytes 1245184 | tf_op jit(solution)/shard_map/update/pallas_call | solution.py:295
  41.1 0.6 %collective-permute-done.2.refs_0_ = bf16[2,192,128]{2,1,0:T(8,128)(2,1)S(1)} collective-permute-done((bf16[2,192,128]{2,1,0:T(8,128)(2,1)S(1)}, bf16[2,192,128]{2,1,0:T(8,128)(2,1)S(1)}, u32[]{:S(2)}, u32[]{:S(2)}) %collective-permute-start.2) | collective-permute-done | bytes 98336 | tf_op jit(solution)/shard_map/ppermute | solution.py:367
  41.6 0.0 collective-permute-done.3.refs_1_
  41.6 0.7 %cache_rest.1 = bf16[1,2,192,512]{3,2,1,0:T(8,128)(2,1)} custom-call(bf16[1,2,192,512]{3,2,1,0:T(8,128)(2,1)} %cache.1.after_ref.begun_hbm, bf16[1,24,4096]{2,1,0:T(8,128)(2,1)} %update.1.after_ref, bf16[2,192,128]{2,1,0:T(8,128)(2,1)S(1)} %collective-permute-done.2.refs_0_, ...), custom_call_target="tpu_custom_call", output_to_operand_aliasing={{}: (0, {})} | custom-call | bytes 1179648 | tf_op jit(solution)/shard_map/cache_rest/pallas_call | solution.py:295
Async XLA Ops:
  2.6 8.0 %copy-start = (bf16[1,24,4096]{2,1,0:T(8,128)(2,1)S(1)}, bf16[1,24,4096]{2,1,0:T(8,128)(2,1)}, u32[]{:S(2)}) copy-start(bf16[1,24,4096]{2,1,0:T(8,128)(2,1)} %h_ref.1) | copy-start | bytes 589828
  2.6 24.6 %all-to-all-start = ((bf16[32,24,384]{2,1,0:T(8,128)(2,1)}), bf16[32,24,384]{2,1,0:T(8,128)(2,1)S(1)}, u32[]{:S(2)}, u32[]{:S(2)}) async-start(bf16[32,24,384]{2,1,0:T(8,128)(2,1)} %bitcast.7), calls=%async_computation | async-start | bytes 1179648 | tf_op jit(solution)/shard_map/all_to_all | solution.py:337
  10.6 16.7 %copy-start.2 = (s32[4,4]{1,0:T(4,128)S(1)}, s32[4,4]{1,0:T(4,128)}, u32[]{:S(2)}) copy-start(s32[4,4]{1,0:T(4,128)} %pattern_ref.1) | copy-start | bytes 196
  11.6 3.4 %collective-permute-start = (bf16[32,4096]{1,0:T(8,128)(2,1)S(1)}, bf16[32,4096]{1,0:T(8,128)(2,1)S(1)}, u32[]{:S(2)}, u32[]{:S(2)}) collective-permute-start(bf16[32,4096]{1,0:T(8,128)(2,1)S(1)} %residual.1), channel_id=1, source_target_pairs={{8,0},{16,8},{24,16},{9,1},{17,9},{25,17},{10,2},{18,10},{26,18},{... | collective-permute-start | bytes 786440 | tf_op jit(solution)/shard_map/ppermute | solution.py:21
  28.8 11.5 %all-to-all-start.1 = ((bf16[32,24,128]{2,1,0:T(8,128)(2,1)}), bf16[32,24,128]{2,1,0:T(8,128)(2,1)S(1)}, u32[]{:S(2)}, u32[]{:S(2)}) async-start(bf16[32,24,128]{2,1,0:T(8,128)(2,1)} %bitcast.8), calls=%async_computation.1 | async-start | bytes 393216 | tf_op jit(solution)/shard_map/all_to_all | solution.py:363
  31.4 7.9 %collective-permute-start.1 = (bf16[2,192,128]{2,1,0:T(8,128)(2,1)S(1)}, bf16[2,192,128]{2,1,0:T(8,128)(2,1)S(1)}, u32[]{:S(2)}, u32[]{:S(2)}) collective-permute-start(bf16[2,192,128]{2,1,0:T(8,128)(2,1)S(1)} %get-tuple-element.7), channel_id=1, source_target_pairs={{8,16},{16,8},{24,0},{9,17},{17,9},{25,1},{10,18},{18,10},{26,2},{... | collective-permute-start | bytes 294920 | tf_op jit(solution)/shard_map/ppermute | solution.py:367
  32.7 8.9 %collective-permute-start.2 = (bf16[2,192,128]{2,1,0:T(8,128)(2,1)S(1)}, bf16[2,192,128]{2,1,0:T(8,128)(2,1)S(1)}, u32[]{:S(2)}, u32[]{:S(2)}) collective-permute-start(bf16[2,192,128]{2,1,0:T(8,128)(2,1)S(1)} %get-tuple-element.8), channel_id=1, source_target_pairs={{0,16},{16,0},{24,8},{1,17},{17,1},{25,9},{2,18},{18,2},{26,10},{3... | collective-permute-start | bytes 294920 | tf_op jit(solution)/shard_map/ppermute | solution.py:367
  37.0 3.3 %copy-start.1 = (bf16[24,4096]{1,0:T(8,128)(2,1)S(1)}, bf16[24,4096]{1,0:T(8,128)(2,1)}, u32[]{:S(2)}) copy-start(bf16[24,4096]{1,0:T(8,128)(2,1)} %fresh_ref.1) | copy-start | bytes 589828
  37.0 4.6 %collective-permute-start.3 = (bf16[2,192,128]{2,1,0:T(8,128)(2,1)S(1)}, bf16[2,192,128]{2,1,0:T(8,128)(2,1)S(1)}, u32[]{:S(2)}, u32[]{:S(2)}) collective-permute-start(bf16[2,192,128]{2,1,0:T(8,128)(2,1)S(1)} %get-tuple-element.9), channel_id=1, source_target_pairs={{0,8},{8,0},{24,16},{1,9},{9,1},{25,17},{2,10},{10,2},{26,18},{3,1... | collective-permute-start | bytes 294920 | tf_op jit(solution)/shard_map/ppermute | solution.py:367

commit v28 on v27

--- a/solution.py
+++ b/solution.py
@@ -27,7 +27,7 @@
 
 def pair_place(group, pair, pairs):
     place = (pair + pairs // 2) % pairs
-    return place + group % 2 * (pairs - 1 - 2 * place)
+    return place + group // 2 % 2 * (pairs - 1 - 2 * place)
 
 
 def out_order(tm_count, seq_count):

time: 42.8 us -> 42.6 us (level)
  transfers between devices with their start and end apart: 6 -> 6, of which waited for: 5 -> 4; matrix products, arithmetic and copies ran while one was open for 0% -> 0% of each run, Pallas kernels for 6% -> 6%
where the time goes in v28:
time: 42.6 us; the launch traced here: 42.1 us
  starting transfers between devices  19.1 us (45%)
  waiting for transfers between devices  14.9 us (35%)
  Pallas kernels  6.82 us (16%)
  between operations  1.38 us (3%)
    all_to_all x1, waiting for transfers between devices, spread_body(): exchanged = exchange(packed, axis_index_groups=[out])  12 us
    ppermute x3, starting transfers between devices, spread_body(): lax.ppermute(hand, 'tm', [(i, j) for i, j in route if j < tm_count - 1])  7.75 us
    all_to_all x1, starting transfers between devices, spread_body(): exchanged = exchange(packed, axis_index_groups=[out])  7.3 us
    pallas_call x6, Pallas kernels, run(): pl.pallas_call(kernel, out_shape=outs, in_specs=specs, out_specs=[whole(g...  6.82 us
    all_to_all x1, starting transfers between devices, spread_body(): returned = exchange(attended, axis_index_groups=[back])  2.71 us
    ppermute x1, waiting for transfers between devices, shifted(): return lax.ppermute(block, axis, route)  2.13 us
    ppermute x1, starting transfers between devices, shifted(): return lax.ppermute(block, axis, route)  1.29 us
  transfers between devices with their start and end apart: 6, of which 4 were waited for; matrix products, arithmetic and copies ran while one was open for 0% of the time, Pallas kernels for 6%

profile of v28, /device:TPU:0, one launch (start us, length us, event | category | flops | bytes accessed | tf_op | source)
XLA Modules:
  0.0 42.1 jit_solution(12771704409409659698)
XLA Ops:
  0.6 2.0 %pack.1.after_ref = bf16[768,384]{1,0:T(8,128)(2,1)} custom-call(bf16[1,24,4096]{2,1,0:T(8,128)(2,1)} %q_hbm.1, bf16[1,24,4096]{2,1,0:T(8,128)(2,1)} %k_hbm.1, bf16[1,24,4096]{2,1,0:T(8,128)(2,1)} %v_hbm.1), custom_call_target="tpu_custom_call" | custom-call | bytes 1179648 | tf_op jit(solution)/shard_map/pack/pallas_call | solution.py:295
  2.6 0.0 copy-start
  2.6 7.3 %all-to-all-start = ((bf16[32,24,384]{2,1,0:T(8,128)(2,1)}), bf16[32,24,384]{2,1,0:T(8,128)(2,1)S(1)}, u32[]{:S(2)}, u32[]{:S(2)}) async-start(bf16[32,24,384]{2,1,0:T(8,128)(2,1)} %bitcast.7), calls=%async_computation | async-start | bytes 1179648 | tf_op jit(solution)/shard_map/all_to_all | solution.py:337
  10.6 0.0 copy-done
  10.6 0.0 copy-start.2
  10.6 1.0 %residual.1 = bf16[32,4096]{1,0:T(8,128)(2,1)S(1)} custom-call(s32[1]{0:T(128)S(6)} %copy.12.noise_ref, bf16[1,24,4096]{2,1,0:T(8,128)(2,1)S(1)} %copy-done, f32[50,4096]{1,0:T(8,128)} %gate_hbm.1, bf16[768,384]{1,0:T(8,128)(2,1)} %pack.1.after_ref), custom_call_target="tpu_custom_call" | custom-call | bytes 1867780 | tf_op jit(solution)/shard_map/residual/pallas_call | solution.py:295
  11.6 1.3 %collective-permute-start = (bf16[32,4096]{1,0:T(8,128)(2,1)S(1)}, bf16[32,4096]{1,0:T(8,128)(2,1)S(1)}, u32[]{:S(2)}, u32[]{:S(2)}) collective-permute-start(bf16[32,4096]{1,0:T(8,128)(2,1)S(1)} %residual.1), channel_id=1, source_target_pairs={{8,0},{16,8},{24,16},{9,1},{17,9},{25,17},{10,2},{18,10},{26,18},{... | collective-permute-start | bytes 786440 | tf_op jit(solution)/shard_map/ppermute | solution.py:21
  12.9 2.1 %collective-permute-done.after_ref.moved_ref = bf16[32,4096]{1,0:T(8,128)(2,1)S(1)} collective-permute-done((bf16[32,4096]{1,0:T(8,128)(2,1)S(1)}, bf16[32,4096]{1,0:T(8,128)(2,1)S(1)}, u32[]{:S(2)}, u32[]{:S(2)}) %collective-permute-start) | collective-permute-done | bytes 262176 | tf_op jit(solution)/shard_map/ppermute | solution.py:21
  15.1 12.0 %all-to-all-done = bf16[32,24,384]{2,1,0:T(8,128)(2,1)S(1)} async-done(((bf16[32,24,384]{2,1,0:T(8,128)(2,1)}), bf16[32,24,384]{2,1,0:T(8,128)(2,1)S(1)}, u32[]{:S(2)}, u32[]{:S(2)}) %all-to-all-start) | async-done | bytes 589856 | tf_op jit(solution)/shard_map/all_to_all | solution.py:337
  27.1 0.0 copy-done.2
  27.1 1.6 %attend.1 = (bf16[768,128]{1,0:T(8,128)(2,1)}, bf16[2,192,128]{2,1,0:T(8,128)(2,1)S(1)}, bf16[2,192,128]{2,1,0:T(8,128)(2,1)S(1)}, bf16[2,192,128]{2,1,0:T(8,128)(2,1)S(1)}) custom-call(s32[4,4]{1,0:T(4,128)S(1)} %copy-done.2, bf16[768,384]{1,0:T(8,128)(2,1)S(1)} %bitcast.4, bf16[32,4096]{1,0:T(8,128)(2,1)S(1)} %collective-permute-done.after_ref.moved_ref), custom_call_target="tpu_custom_call" | custom-call | flops 150994944 | bytes 1343552 | tf_op jit(solution)/shard_map/attend/pallas_call | solution.py:295
  28.6 2.7 %all-to-all-start.1 = ((bf16[32,24,128]{2,1,0:T(8,128)(2,1)}), bf16[32,24,128]{2,1,0:T(8,128)(2,1)S(1)}, u32[]{:S(2)}, u32[]{:S(2)}) async-start(bf16[32,24,128]{2,1,0:T(8,128)(2,1)} %bitcast.8), calls=%async_computation.1 | async-start | bytes 393216 | tf_op jit(solution)/shard_map/all_to_all | solution.py:363
  31.4 1.3 %collective-permute-start.1 = (bf16[2,192,128]{2,1,0:T(8,128)(2,1)S(1)}, bf16[2,192,128]{2,1,0:T(8,128)(2,1)S(1)}, u32[]{:S(2)}, u32[]{:S(2)}) collective-permute-start(bf16[2,192,128]{2,1,0:T(8,128)(2,1)S(1)} %get-tuple-element.7), channel_id=1, source_target_pairs={{8,16},{16,8},{24,0},{9,17},{17,9},{25,1},{10,18},{18,10},{26,2},{... | collective-permute-start | bytes 294920 | tf_op jit(solution)/shard_map/ppermute | solution.py:367
  32.7 4.4 %collective-permute-start.2 = (bf16[2,192,128]{2,1,0:T(8,128)(2,1)S(1)}, bf16[2,192,128]{2,1,0:T(8,128)(2,1)S(1)}, u32[]{:S(2)}, u32[]{:S(2)}) collective-permute-start(bf16[2,192,128]{2,1,0:T(8,128)(2,1)S(1)} %get-tuple-element.8), channel_id=1, source_target_pairs={{0,16},{16,0},{24,8},{1,17},{17,1},{25,9},{2,18},{18,2},{26,10},{3... | collective-permute-start | bytes 294920 | tf_op jit(solution)/shard_map/ppermute | solution.py:367
  37.1 0.0 copy-start.1
  37.1 2.1 %collective-permute-start.3 = (bf16[2,192,128]{2,1,0:T(8,128)(2,1)S(1)}, bf16[2,192,128]{2,1,0:T(8,128)(2,1)S(1)}, u32[]{:S(2)}, u32[]{:S(2)}) collective-permute-start(bf16[2,192,128]{2,1,0:T(8,128)(2,1)S(1)} %get-tuple-element.9), channel_id=1, source_target_pairs={{0,8},{8,0},{24,16},{1,9},{9,1},{25,17},{2,10},{10,2},{26,18},{3,1... | collective-permute-start | bytes 294920 | tf_op jit(solution)/shard_map/ppermute | solution.py:367
  39.1 0.0 collective-permute-done.1.hand_ref
  39.2 0.8 %cache.1.after_ref.begun_hbm = bf16[1,2,192,512]{3,2,1,0:T(8,128)(2,1)} custom-call(bf16[768,384]{1,0:T(8,128)(2,1)S(1)} %bitcast.5, bf16[2,192,128]{2,1,0:T(8,128)(2,1)S(1)} %collective-permute-done.1.hand_ref), custom_call_target="tpu_custom_call" | custom-call | bytes 1081344 | tf_op jit(solution)/shard_map/cache/pallas_call | solution.py:295
  40.0 0.2 all-to-all-done.1
  40.2 0.0 copy-done.1
  40.2 0.8 %update.1.after_ref = bf16[1,24,4096]{2,1,0:T(8,128)(2,1)} custom-call(bf16[768,128]{1,0:T(8,128)(2,1)S(1)} %bitcast.6, bf16[32,4096]{1,0:T(8,128)(2,1)S(1)} %collective-permute-done.after_ref.moved_ref, bf16[24,4096]{1,0:T(8,128)(2,1)S(1)} %copy-done.1, bf16[1,2,192,512]{3,2,1,0:T(8,128)(2,1)} %cache.1.after_ref.begun_hbm), custom_call_target="tpu_custom_call" | custom-call | bytes 1245184 | tf_op jit(solution)/shard_map/update/pallas_call | solution.py:295
  41.0 0.4 %collective-permute-done.2.refs_0_ = bf16[2,192,128]{2,1,0:T(8,128)(2,1)S(1)} collective-permute-done((bf16[2,192,128]{2,1,0:T(8,128)(2,1)S(1)}, bf16[2,192,128]{2,1,0:T(8,128)(2,1)S(1)}, u32[]{:S(2)}, u32[]{:S(2)}) %collective-permute-start.2) | collective-permute-done | bytes 98336 | tf_op jit(solution)/shard_map/ppermute | solution.py:367
  41.5 0.0 collective-permute-done.3.refs_1_
  41.5 0.7 %cache_rest.1 = bf16[1,2,192,512]{3,2,1,0:T(8,128)(2,1)} custom-call(bf16[1,2,192,512]{3,2,1,0:T(8,128)(2,1)} %cache.1.after_ref.begun_hbm, bf16[1,24,4096]{2,1,0:T(8,128)(2,1)} %update.1.after_ref, bf16[2,192,128]{2,1,0:T(8,128)(2,1)S(1)} %collective-permute-done.2.refs_0_, ...), custom_call_target="tpu_custom_call", output_to_operand_aliasing={{}: (0, {})} | custom-call | bytes 1179648 | tf_op jit(solution)/shard_map/cache_rest/pallas_call | solution.py:295
Async XLA Ops:
  2.6 8.0 %copy-start = (bf16[1,24,4096]{2,1,0:T(8,128)(2,1)S(1)}, bf16[1,24,4096]{2,1,0:T(8,128)(2,1)}, u32[]{:S(2)}) copy-start(bf16[1,24,4096]{2,1,0:T(8,128)(2,1)} %h_ref.1) | copy-start | bytes 589828
  2.6 24.4 %all-to-all-start = ((bf16[32,24,384]{2,1,0:T(8,128)(2,1)}), bf16[32,24,384]{2,1,0:T(8,128)(2,1)S(1)}, u32[]{:S(2)}, u32[]{:S(2)}) async-start(bf16[32,24,384]{2,1,0:T(8,128)(2,1)} %bitcast.7), calls=%async_computation | async-start | bytes 1179648 | tf_op jit(solution)/shard_map/all_to_all | solution.py:337
  10.6 16.5 %copy-start.2 = (s32[4,4]{1,0:T(4,128)S(1)}, s32[4,4]{1,0:T(4,128)}, u32[]{:S(2)}) copy-start(s32[4,4]{1,0:T(4,128)} %pattern_ref.1) | copy-start | bytes 196
  11.6 3.4 %collective-permute-start = (bf16[32,4096]{1,0:T(8,128)(2,1)S(1)}, bf16[32,4096]{1,0:T(8,128)(2,1)S(1)}, u32[]{:S(2)}, u32[]{:S(2)}) collective-permute-start(bf16[32,4096]{1,0:T(8,128)(2,1)S(1)} %residual.1), channel_id=1, source_target_pairs={{8,0},{16,8},{24,16},{9,1},{17,9},{25,17},{10,2},{18,10},{26,18},{... | collective-permute-start | bytes 786440 | tf_op jit(solution)/shard_map/ppermute | solution.py:21
  28.6 11.6 %all-to-all-start.1 = ((bf16[32,24,128]{2,1,0:T(8,128)(2,1)}), bf16[32,24,128]{2,1,0:T(8,128)(2,1)S(1)}, u32[]{:S(2)}, u32[]{:S(2)}) async-start(bf16[32,24,128]{2,1,0:T(8,128)(2,1)} %bitcast.8), calls=%async_computation.1 | async-start | bytes 393216 | tf_op jit(solution)/shard_map/all_to_all | solution.py:363
  31.4 7.8 %collective-permute-start.1 = (bf16[2,192,128]{2,1,0:T(8,128)(2,1)S(1)}, bf16[2,192,128]{2,1,0:T(8,128)(2,1)S(1)}, u32[]{:S(2)}, u32[]{:S(2)}) collective-permute-start(bf16[2,192,128]{2,1,0:T(8,128)(2,1)S(1)} %get-tuple-element.7), channel_id=1, source_target_pairs={{8,16},{16,8},{24,0},{9,17},{17,9},{25,1},{10,18},{18,10},{26,2},{... | collective-permute-start | bytes 294920 | tf_op jit(solution)/shard_map/ppermute | solution.py:367
  32.7 8.8 %collective-permute-start.2 = (bf16[2,192,128]{2,1,0:T(8,128)(2,1)S(1)}, bf16[2,192,128]{2,1,0:T(8,128)(2,1)S(1)}, u32[]{:S(2)}, u32[]{:S(2)}) collective-permute-start(bf16[2,192,128]{2,1,0:T(8,128)(2,1)S(1)} %get-tuple-element.8), channel_id=1, source_target_pairs={{0,16},{16,0},{24,8},{1,17},{17,1},{25,9},{2,18},{18,2},{26,10},{3... | collective-permute-start | bytes 294920 | tf_op jit(solution)/shard_map/ppermute | solution.py:367
  37.1 3.2 %copy-start.1 = (bf16[24,4096]{1,0:T(8,128)(2,1)S(1)}, bf16[24,4096]{1,0:T(8,128)(2,1)}, u32[]{:S(2)}) copy-start(bf16[24,4096]{1,0:T(8,128)(2,1)} %fresh_ref.1) | copy-start | bytes 589828
  37.1 4.4 %collective-permute-start.3 = (bf16[2,192,128]{2,1,0:T(8,128)(2,1)S(1)}, bf16[2,192,128]{2,1,0:T(8,128)(2,1)S(1)}, u32[]{:S(2)}, u32[]{:S(2)}) collective-permute-start(bf16[2,192,128]{2,1,0:T(8,128)(2,1)S(1)} %get-tuple-element.9), channel_id=1, source_target_pairs={{0,8},{8,0},{24,16},{1,9},{9,1},{25,17},{2,10},{10,2},{26,18},{3,1... | collective-permute-start | bytes 294920 | tf_op jit(solution)/shard_map/ppermute | solution.py:367

commit v29 on v28

--- a/solution.py
+++ b/solution.py
@@ -19,10 +19,6 @@
     devices = range(lax.axis_size(axis))
     route = [(i - distance, i) for i in devices if i - distance in devices]
     return lax.ppermute(block, axis, route)
-
-
-def mixed(index, count):
-    return (index + count // 2) % count
 
 
 def pair_place(group, pair, pairs):
@@ -214,7 +210,7 @@
                 ready = left[:rows].astype(jnp.bfloat16)
                 for pair in range(pairs):
                     at = pair_place(waiting, pair, pairs) * step
-                    to = mixed(2 * pair, seq_count) // 2 * step
+                    to = pair_place(waiting - 1, pair, pairs) * step
                     held[waiting - 1, to : to + step, head : head + HD] = ready[at : at + step]
                 left = left[rows:] if left.shape[0] > rows else None
                 if last:
@@ -264,6 +260,7 @@
     tok = out_ref.shape[1]
     wide = att_ref.shape[1]
     count = att_ref.shape[0] // tok
+    order = out_order(tm_count, seq_count)
     last = lax.axis_index("tm") == tm_count - 1
 
     @pl.when(last)
@@ -276,7 +273,8 @@
             rows = att_ref[2 * pair * tok : 2 * (pair + 1) * tok, :].astype(jnp.float32)
             for half in range(2):
                 source = 2 * pair + half
-                start = (mixed(source % seq_count, seq_count) * tm_count + source // seq_count) * wide
+                tm, seq = order[source]
+                start = (seq * tm_count + tm) * wide
                 moved = moved_ref[:, start : start + wide].astype(jnp.float32)
                 gate = (moved[tok : tok + 1] + moved[tok + 1 : tok + 2]) + moved[tok + 2 : tok + 3]
                 result = moved[:tok] + gate * rows[half * tok : (half + 1) * tok]
@@ -329,7 +327,6 @@
             DMA((parts, tm_count)),
         ],
     )
-    back = [tm * seq_count + mixed(s, seq_count) for tm in range(tm_count) for s in range(seq_count)]
     out = [tm * seq_count + index for tm, index in out_order(tm_count, seq_count)]
     exchange = functools.partial(
         lax.all_to_all, axis_name=BOTH, split_axis=0, concat_axis=0, tiled=True
@@ -360,7 +357,7 @@
         flops=2 * count * tok * count * tok * wide,
         scratch=[VMEM((tm_count - 1, group_tok, wide), kind), DMA((tm_count,))],
     )
-    returned = exchange(attended, axis_index_groups=[back])
+    returned = exchange(attended, axis_index_groups=[out])
     handed = []
     for distance, hand in zip(distances(tm_count), hands):
         route = [(i, partner(i, distance, tm_count)) for i in range(tm_count)]

time: 42.6 us -> 42.4 us (level)
    ppermute x3, waiting for transfers between devices: 0.49 us -> 0.01 us  [spread_body(): lax.ppermute(hand, 'tm', [(i, j) for i, j in route if j < tm_count - 1])]
  transfers between devices with their start and end apart: 6 -> 6, of which waited for: 4 -> 3; matrix products, arithmetic and copies ran while one was open for 0% -> 0% of each run, Pallas kernels for 6% -> 6%
where the time goes in v29:
time: 42.4 us; the launch traced here: 42 us
  starting transfers between devices  19.1 us (45%)
  waiting for transfers between devices  14.7 us (35%)
  Pallas kernels  6.83 us (16%)
  between operations  1.39 us (3%)
    all_to_all x1, waiting for transfers between devices, spread_body(): exchanged = exchange(packed, axis_index_groups=[out])  12 us
    ppermute x3, starting transfers between devices, spread_body(): lax.ppermute(hand, 'tm', [(i, j) for i, j in route if j < tm_count - 1])  7.75 us
    all_to_all x1, starting transfers between devices, spread_body(): exchanged = exchange(packed, axis_index_groups=[out])  7.3 us
    pallas_call x6, Pallas kernels, run(): pl.pallas_call(kernel, out_shape=outs, in_specs=specs, out_specs=[whole(g...  6.83 us
    all_to_all x1, starting transfers between devices, spread_body(): returned = exchange(attended, axis_index_groups=[out])  2.71 us
    ppermute x1, waiting for transfers between devices, shifted(): return lax.ppermute(block, axis, route)  2.13 us
    ppermute x1, starting transfers between devices, shifted(): return lax.ppermute(block, axis, route)  1.29 us
  transfers between devices with their start and end apart: 6, of which 3 were waited for; matrix products, arithmetic and copies ran while one was open for 0% of the time, Pallas kernels for 6%

profile of v29, /device:TPU:0, one launch (start us, length us, event | category | flops | bytes accessed | tf_op | source)
XLA Modules:
  0.0 42.0 jit_solution(14579727589721711603)
XLA Ops:
  0.6 2.0 %pack.1.after_ref = bf16[768,384]{1,0:T(8,128)(2,1)} custom-call(bf16[1,24,4096]{2,1,0:T(8,128)(2,1)} %q_hbm.1, bf16[1,24,4096]{2,1,0:T(8,128)(2,1)} %k_hbm.1, bf16[1,24,4096]{2,1,0:T(8,128)(2,1)} %v_hbm.1), custom_call_target="tpu_custom_call" | custom-call | bytes 1179648 | tf_op jit(solution)/shard_map/pack/pallas_call | solution.py:293
  2.6 0.0 copy-start
  2.6 7.3 %all-to-all-start = ((bf16[32,24,384]{2,1,0:T(8,128)(2,1)}), bf16[32,24,384]{2,1,0:T(8,128)(2,1)S(1)}, u32[]{:S(2)}, u32[]{:S(2)}) async-start(bf16[32,24,384]{2,1,0:T(8,128)(2,1)} %bitcast.7), calls=%async_computation | async-start | bytes 1179648 | tf_op jit(solution)/shard_map/all_to_all | solution.py:334
  10.6 0.0 copy-done
  10.6 0.0 copy-start.2
  10.6 1.0 %residual.1 = bf16[32,4096]{1,0:T(8,128)(2,1)S(1)} custom-call(s32[1]{0:T(128)S(6)} %copy.12.noise_ref, bf16[1,24,4096]{2,1,0:T(8,128)(2,1)S(1)} %copy-done, f32[50,4096]{1,0:T(8,128)} %gate_hbm.1, bf16[768,384]{1,0:T(8,128)(2,1)} %pack.1.after_ref), custom_call_target="tpu_custom_call" | custom-call | bytes 1867780 | tf_op jit(solution)/shard_map/residual/pallas_call | solution.py:293
  11.6 1.3 %collective-permute-start = (bf16[32,4096]{1,0:T(8,128)(2,1)S(1)}, bf16[32,4096]{1,0:T(8,128)(2,1)S(1)}, u32[]{:S(2)}, u32[]{:S(2)}) collective-permute-start(bf16[32,4096]{1,0:T(8,128)(2,1)S(1)} %residual.1), channel_id=1, source_target_pairs={{8,0},{16,8},{24,16},{9,1},{17,9},{25,17},{10,2},{18,10},{26,18},{... | collective-permute-start | bytes 786440 | tf_op jit(solution)/shard_map/ppermute | solution.py:21
  12.9 2.1 %collective-permute-done.after_ref.moved_ref = bf16[32,4096]{1,0:T(8,128)(2,1)S(1)} collective-permute-done((bf16[32,4096]{1,0:T(8,128)(2,1)S(1)}, bf16[32,4096]{1,0:T(8,128)(2,1)S(1)}, u32[]{:S(2)}, u32[]{:S(2)}) %collective-permute-start) | collective-permute-done | bytes 262176 | tf_op jit(solution)/shard_map/ppermute | solution.py:21
  15.1 12.0 %all-to-all-done = bf16[32,24,384]{2,1,0:T(8,128)(2,1)S(1)} async-done(((bf16[32,24,384]{2,1,0:T(8,128)(2,1)}), bf16[32,24,384]{2,1,0:T(8,128)(2,1)S(1)}, u32[]{:S(2)}, u32[]{:S(2)}) %all-to-all-start) | async-done | bytes 589856 | tf_op jit(solution)/shard_map/all_to_all | solution.py:334
  27.1 0.0 copy-done.2
  27.1 1.6 %attend.1 = (bf16[768,128]{1,0:T(8,128)(2,1)}, bf16[2,192,128]{2,1,0:T(8,128)(2,1)S(1)}, bf16[2,192,128]{2,1,0:T(8,128)(2,1)S(1)}, bf16[2,192,128]{2,1,0:T(8,128)(2,1)S(1)}) custom-call(s32[4,4]{1,0:T(4,128)S(1)} %copy-done.2, bf16[768,384]{1,0:T(8,128)(2,1)S(1)} %bitcast.4, bf16[32,4096]{1,0:T(8,128)(2,1)S(1)} %collective-permute-done.after_ref.moved_ref), custom_call_target="tpu_custom_call" | custom-call | flops 150994944 | bytes 1343552 | tf_op jit(solution)/shard_map/attend/pallas_call | solution.py:293
  28.6 2.7 %all-to-all-start.1 = ((bf16[32,24,128]{2,1,0:T(8,128)(2,1)}), bf16[32,24,128]{2,1,0:T(8,128)(2,1)S(1)}, u32[]{:S(2)}, u32[]{:S(2)}) async-start(bf16[32,24,128]{2,1,0:T(8,128)(2,1)} %bitcast.8), calls=%async_computation.1 | async-start | bytes 393216 | tf_op jit(solution)/shard_map/all_to_all | solution.py:360
  31.4 1.3 %collective-permute-start.1 = (bf16[2,192,128]{2,1,0:T(8,128)(2,1)S(1)}, bf16[2,192,128]{2,1,0:T(8,128)(2,1)S(1)}, u32[]{:S(2)}, u32[]{:S(2)}) collective-permute-start(bf16[2,192,128]{2,1,0:T(8,128)(2,1)S(1)} %get-tuple-element.7), channel_id=1, source_target_pairs={{8,16},{16,8},{24,0},{9,17},{17,9},{25,1},{10,18},{18,10},{26,2},{... | collective-permute-start | bytes 294920 | tf_op jit(solution)/shard_map/ppermute | solution.py:364
  32.7 4.4 %collective-permute-start.2 = (bf16[2,192,128]{2,1,0:T(8,128)(2,1)S(1)}, bf16[2,192,128]{2,1,0:T(8,128)(2,1)S(1)}, u32[]{:S(2)}, u32[]{:S(2)}) collective-permute-start(bf16[2,192,128]{2,1,0:T(8,128)(2,1)S(1)} %get-tuple-element.8), channel_id=1, source_target_pairs={{0,16},{16,0},{24,8},{1,17},{17,1},{25,9},{2,18},{18,2},{26,10},{3... | collective-permute-start | bytes 294920 | tf_op jit(solution)/shard_map/ppermute | solution.py:364
  37.1 0.0 copy-start.1
  37.1 2.1 %collective-permute-start.3 = (bf16[2,192,128]{2,1,0:T(8,128)(2,1)S(1)}, bf16[2,192,128]{2,1,0:T(8,128)(2,1)S(1)}, u32[]{:S(2)}, u32[]{:S(2)}) collective-permute-start(bf16[2,192,128]{2,1,0:T(8,128)(2,1)S(1)} %get-tuple-element.9), channel_id=1, source_target_pairs={{0,8},{8,0},{24,16},{1,9},{9,1},{25,17},{2,10},{10,2},{26,18},{3,1... | collective-permute-start | bytes 294920 | tf_op jit(solution)/shard_map/ppermute | solution.py:364
  39.1 0.0 collective-permute-done.1.hand_ref
  39.1 0.8 %cache.1.after_ref.begun_hbm = bf16[1,2,192,512]{3,2,1,0:T(8,128)(2,1)} custom-call(bf16[768,384]{1,0:T(8,128)(2,1)S(1)} %bitcast.5, bf16[2,192,128]{2,1,0:T(8,128)(2,1)S(1)} %collective-permute-done.1.hand_ref), custom_call_target="tpu_custom_call" | custom-call | bytes 1081344 | tf_op jit(solution)/shard_map/cache/pallas_call | solution.py:293
  40.0 0.5 %all-to-all-done.1 = bf16[32,24,128]{2,1,0:T(8,128)(2,1)S(1)} async-done(((bf16[32,24,128]{2,1,0:T(8,128)(2,1)}), bf16[32,24,128]{2,1,0:T(8,128)(2,1)S(1)}, u32[]{:S(2)}, u32[]{:S(2)}) %all-to-all-start.1) | async-done | bytes 196640 | tf_op jit(solution)/shard_map/all_to_all | solution.py:360
  40.5 0.0 copy-done.1
  40.5 0.8 %update.1.after_ref = bf16[1,24,4096]{2,1,0:T(8,128)(2,1)} custom-call(bf16[768,128]{1,0:T(8,128)(2,1)S(1)} %bitcast.6, bf16[32,4096]{1,0:T(8,128)(2,1)S(1)} %collective-permute-done.after_ref.moved_ref, bf16[24,4096]{1,0:T(8,128)(2,1)S(1)} %copy-done.1, bf16[1,2,192,512]{3,2,1,0:T(8,128)(2,1)} %cache.1.after_ref.begun_hbm), custom_call_target="tpu_custom_call" | custom-call | bytes 1245184 | tf_op jit(solution)/shard_map/update/pallas_call | solution.py:293
  41.3 0.0 collective-permute-done.2.refs_0_
  41.3 0.0 collective-permute-done.3.refs_1_
  41.3 0.7 %cache_rest.1 = bf16[1,2,192,512]{3,2,1,0:T(8,128)(2,1)} custom-call(bf16[1,2,192,512]{3,2,1,0:T(8,128)(2,1)} %cache.1.after_ref.begun_hbm, bf16[1,24,4096]{2,1,0:T(8,128)(2,1)} %update.1.after_ref, bf16[2,192,128]{2,1,0:T(8,128)(2,1)S(1)} %collective-permute-done.2.refs_0_, ...), custom_call_target="tpu_custom_call", output_to_operand_aliasing={{}: (0, {})} | custom-call | bytes 1179648 | tf_op jit(solution)/shard_map/cache_rest/pallas_call | solution.py:293
Async XLA Ops:
  2.6 8.0 %copy-start = (bf16[1,24,4096]{2,1,0:T(8,128)(2,1)S(1)}, bf16[1,24,4096]{2,1,0:T(8,128)(2,1)}, u32[]{:S(2)}) copy-start(bf16[1,24,4096]{2,1,0:T(8,128)(2,1)} %h_ref.1) | copy-start | bytes 589828
  2.6 24.4 %all-to-all-start = ((bf16[32,24,384]{2,1,0:T(8,128)(2,1)}), bf16[32,24,384]{2,1,0:T(8,128)(2,1)S(1)}, u32[]{:S(2)}, u32[]{:S(2)}) async-start(bf16[32,24,384]{2,1,0:T(8,128)(2,1)} %bitcast.7), calls=%async_computation | async-start | bytes 1179648 | tf_op jit(solution)/shard_map/all_to_all | solution.py:334
  10.6 16.5 %copy-start.2 = (s32[4,4]{1,0:T(4,128)S(1)}, s32[4,4]{1,0:T(4,128)}, u32[]{:S(2)}) copy-start(s32[4,4]{1,0:T(4,128)} %pattern_ref.1) | copy-start | bytes 196
  11.6 3.4 %collective-permute-start = (bf16[32,4096]{1,0:T(8,128)(2,1)S(1)}, bf16[32,4096]{1,0:T(8,128)(2,1)S(1)}, u32[]{:S(2)}, u32[]{:S(2)}) collective-permute-start(bf16[32,4096]{1,0:T(8,128)(2,1)S(1)} %residual.1), channel_id=1, source_target_pairs={{8,0},{16,8},{24,16},{9,1},{17,9},{25,17},{10,2},{18,10},{26,18},{... | collective-permute-start | bytes 786440 | tf_op jit(solution)/shard_map/ppermute | solution.py:21
  28.6 11.9 %all-to-all-start.1 = ((bf16[32,24,128]{2,1,0:T(8,128)(2,1)}), bf16[32,24,128]{2,1,0:T(8,128)(2,1)S(1)}, u32[]{:S(2)}, u32[]{:S(2)}) async-start(bf16[32,24,128]{2,1,0:T(8,128)(2,1)} %bitcast.8), calls=%async_computation.1 | async-start | bytes 393216 | tf_op jit(solution)/shard_map/all_to_all | solution.py:360
  31.4 7.8 %collective-permute-start.1 = (bf16[2,192,128]{2,1,0:T(8,128)(2,1)S(1)}, bf16[2,192,128]{2,1,0:T(8,128)(2,1)S(1)}, u32[]{:S(2)}, u32[]{:S(2)}) collective-permute-start(bf16[2,192,128]{2,1,0:T(8,128)(2,1)S(1)} %get-tuple-element.7), channel_id=1, source_target_pairs={{8,16},{16,8},{24,0},{9,17},{17,9},{25,1},{10,18},{18,10},{26,2},{... | collective-permute-start | bytes 294920 | tf_op jit(solution)/shard_map/ppermute | solution.py:364
  32.7 8.6 %collective-permute-start.2 = (bf16[2,192,128]{2,1,0:T(8,128)(2,1)S(1)}, bf16[2,192,128]{2,1,0:T(8,128)(2,1)S(1)}, u32[]{:S(2)}, u32[]{:S(2)}) collective-permute-start(bf16[2,192,128]{2,1,0:T(8,128)(2,1)S(1)} %get-tuple-element.8), channel_id=1, source_target_pairs={{0,16},{16,0},{24,8},{1,17},{17,1},{25,9},{2,18},{18,2},{26,10},{3... | collective-permute-start | bytes 294920 | tf_op jit(solution)/shard_map/ppermute | solution.py:364
  37.1 3.4 %copy-start.1 = (bf16[24,4096]{1,0:T(8,128)(2,1)S(1)}, bf16[24,4096]{1,0:T(8,128)(2,1)}, u32[]{:S(2)}) copy-start(bf16[24,4096]{1,0:T(8,128)(2,1)} %fresh_ref.1) | copy-start | bytes 589828
  37.1 4.2 %collective-permute-start.3 = (bf16[2,192,128]{2,1,0:T(8,128)(2,1)S(1)}, bf16[2,192,128]{2,1,0:T(8,128)(2,1)S(1)}, u32[]{:S(2)}, u32[]{:S(2)}) collective-permute-start(bf16[2,192,128]{2,1,0:T(8,128)(2,1)S(1)} %get-tuple-element.9), channel_id=1, source_target_pairs={{0,8},{8,0},{24,16},{1,9},{9,1},{25,17},{2,10},{10,2},{26,18},{3,1... | collective-permute-start | bytes 294920 | tf_op jit(solution)/shard_map/ppermute | solution.py:364

commit v30 on v29

--- a/solution.py
+++ b/solution.py
@@ -238,47 +238,45 @@
         out_ref[0, :, :, lanes_of(distances(groups)[0], groups, here, wide)] = hand_ref[...]
 
 
-def cache_rest_kernel(groups, begun_hbm, after_ref, *refs):
-    *hand_refs, out_hbm, sems = refs
-    here = lax.axis_index("tm")
-
-    @pl.when(here < groups - 1)
-    def place():
-        copies = [
-            pltpu.make_async_copy(
-                block, out_hbm.at[0, :, :, lanes_of(distance, groups, here, block.shape[2])], sems.at[index]
-            )
-            for index, (distance, block) in enumerate(zip(distances(groups)[1:], hand_refs))
-        ]
-        for copy in copies:
-            copy.start()
-        for copy in copies:
-            copy.wait()
-
-
-def update_kernel(seq_count, tm_count, att_ref, moved_ref, fresh_ref, after_ref, out_ref):
-    tok = out_ref.shape[1]
+def finish_kernel(seq_count, tm_count, att_ref, moved_ref, fresh_ref, begun_hbm, *refs):
+    *hand_refs, out_hbm, cache_hbm, held, sem, sems = refs
+    tok = held.shape[1]
     wide = att_ref.shape[1]
     count = att_ref.shape[0] // tok
     order = out_order(tm_count, seq_count)
-    last = lax.axis_index("tm") == tm_count - 1
+    here = lax.axis_index("tm")
+    last = here == tm_count - 1
+    copies = [
+        pltpu.make_async_copy(
+            block, cache_hbm.at[0, :, :, lanes_of(distance, tm_count, here, block.shape[2])], sems.at[index]
+        )
+        for index, (distance, block) in enumerate(zip(distances(tm_count)[1:], hand_refs))
+    ]
 
     @pl.when(last)
     def take_fresh():
-        out_ref[0] = fresh_ref[...]
+        copy = pltpu.make_async_copy(fresh_ref, out_hbm.at[0], sem)
+        copy.start()
+        copy.wait()
 
     @pl.when(jnp.logical_not(last))
     def take_update():
+        for copy in copies:
+            copy.start()
         for pair in range(count // 2):
             rows = att_ref[2 * pair * tok : 2 * (pair + 1) * tok, :].astype(jnp.float32)
             for half in range(2):
-                source = 2 * pair + half
-                tm, seq = order[source]
+                tm, seq = order[2 * pair + half]
                 start = (seq * tm_count + tm) * wide
                 moved = moved_ref[:, start : start + wide].astype(jnp.float32)
                 gate = (moved[tok : tok + 1] + moved[tok + 1 : tok + 2]) + moved[tok + 2 : tok + 3]
                 result = moved[:tok] + gate * rows[half * tok : (half + 1) * tok]
-                out_ref[0, :, start : start + wide] = result.astype(jnp.bfloat16)
+                held[0, :, start : start + wide] = result.astype(jnp.bfloat16)
+        copy = pltpu.make_async_copy(held, out_hbm, sem)
+        copy.start()
+        copy.wait()
+        for copy in copies:
+            copy.wait()
 
 
 def whole(space=VMEM):
@@ -372,21 +370,14 @@
         (exchanged, first),
     )
     begun = pltpu.with_memory_space_constraint(begun, HBM)
-    advanced = run(
-        functools.partial(update_kernel, seq_count, tm_count),
-        "update",
-        [jax.ShapeDtypeStruct((1, tok, width), kind)],
-        [whole()] * 3 + [whole(HBM)],
-        (returned, moved, fresh_latent, begun),
-    )
-    next_cache = run(
-        functools.partial(cache_rest_kernel, tm_count),
-        "cache_rest",
-        [HBM(begun.shape, kind)],
-        [whole(HBM)] * 2 + [whole()] * len(rest),
-        (begun, pltpu.with_memory_space_constraint(advanced, HBM), *rest),
-        scratch=[DMA((len(rest),))],
-        aliases={0: 0},
+    advanced, next_cache = run(
+        functools.partial(finish_kernel, seq_count, tm_count),
+        "finish",
+        [HBM((1, tok, width), kind), HBM(begun.shape, kind)],
+        [whole()] * 3 + [whole(HBM)] + [whole()] * len(rest),
+        (returned, moved, fresh_latent, begun, *rest),
+        scratch=[VMEM((1, tok, width), kind), DMA, DMA((len(rest),))],
+        aliases={3: 1},
     )
     return (advanced, next_cache)
 

time: 42.4 us -> 42.3 us (level)
  Pallas kernels: 6.83 us -> 6.18 us
  waiting for transfers between devices: 14.7 us -> 15.2 us
    ppermute x3, waiting for transfers between devices: 0.01 us -> 1.06 us  [spread_body(): lax.ppermute(hand, 'tm', [(i, j) for i, j in route if j < tm_count - 1])]
    pallas_call x6 -> x5, Pallas kernels: 6.83 us -> 6.18 us  [run(): pl.pallas_call(kernel, out_shape=outs, in_specs=specs, out_specs=[whole(g...]
    all_to_all x1, waiting for transfers between devices: 0.53 us -> 0.01 us  [spread_body(): returned = exchange(attended, axis_index_groups=[out])]
  transfers between devices with their start and end apart: 6 -> 6, of which waited for: 3 -> 3; matrix products, arithmetic and copies ran while one was open for 0% -> 0% of each run, Pallas kernels for 6% -> 4%
where the time goes in v30:
time: 42.3 us; the launch traced here: 41.9 us
  starting transfers between devices  19.1 us (45%)
  waiting for transfers between devices  15.2 us (36%)
  Pallas kernels  6.18 us (15%)
  between operations  1.39 us (3%)
    all_to_all x1, waiting for transfers between devices, spread_body(): exchanged = exchange(packed, axis_index_groups=[out])  12 us
    ppermute x3, starting transfers between devices, spread_body(): lax.ppermute(hand, 'tm', [(i, j) for i, j in route if j < tm_count - 1])  7.75 us
    all_to_all x1, starting transfers between devices, spread_body(): exchanged = exchange(packed, axis_index_groups=[out])  7.3 us
    pallas_call x5, Pallas kernels, run(): pl.pallas_call(kernel, out_shape=outs, in_specs=specs, out_specs=[whole(g...  6.18 us
    all_to_all x1, starting transfers between devices, spread_body(): returned = exchange(attended, axis_index_groups=[out])  2.71 us
    ppermute x1, waiting for transfers between devices, shifted(): return lax.ppermute(block, axis, route)  2.13 us
    ppermute x1, starting transfers between devices, shifted(): return lax.ppermute(block, axis, route)  1.29 us
    ppermute x3, waiting for transfers between devices, spread_body(): lax.ppermute(hand, 'tm', [(i, j) for i, j in route if j < tm_count - 1])  1.06 us
  transfers between devices with their start and end apart: 6, of which 3 were waited for; matrix products, arithmetic and copies ran while one was open for 0% of the time, Pallas kernels for 4%

profile of v30, /device:TPU:0, one launch (start us, length us, event | category | flops | bytes accessed | tf_op | source)
XLA Modules:
  0.0 41.9 jit_solution(7765685069899602368)
XLA Ops:
  0.6 2.0 %pack.1.after_ref = bf16[768,384]{1,0:T(8,128)(2,1)} custom-call(bf16[1,24,4096]{2,1,0:T(8,128)(2,1)} %q_hbm.1, bf16[1,24,4096]{2,1,0:T(8,128)(2,1)} %k_hbm.1, bf16[1,24,4096]{2,1,0:T(8,128)(2,1)} %v_hbm.1), custom_call_target="tpu_custom_call" | custom-call | bytes 1179648 | tf_op jit(solution)/shard_map/pack/pallas_call | solution.py:291
  2.6 0.0 copy-start
  2.6 7.3 %all-to-all-start = ((bf16[32,24,384]{2,1,0:T(8,128)(2,1)}), bf16[32,24,384]{2,1,0:T(8,128)(2,1)S(1)}, u32[]{:S(2)}, u32[]{:S(2)}) async-start(bf16[32,24,384]{2,1,0:T(8,128)(2,1)} %bitcast.7), calls=%async_computation | async-start | bytes 1179648 | tf_op jit(solution)/shard_map/all_to_all | solution.py:332
  10.6 0.0 copy-done
  10.6 0.0 copy-start.2
  10.6 1.0 %residual.1 = bf16[32,4096]{1,0:T(8,128)(2,1)S(1)} custom-call(s32[1]{0:T(128)S(6)} %copy.12.noise_ref, bf16[1,24,4096]{2,1,0:T(8,128)(2,1)S(1)} %copy-done, f32[50,4096]{1,0:T(8,128)} %gate_hbm.1, bf16[768,384]{1,0:T(8,128)(2,1)} %pack.1.after_ref), custom_call_target="tpu_custom_call" | custom-call | bytes 1867780 | tf_op jit(solution)/shard_map/residual/pallas_call | solution.py:291
  11.6 1.3 %collective-permute-start = (bf16[32,4096]{1,0:T(8,128)(2,1)S(1)}, bf16[32,4096]{1,0:T(8,128)(2,1)S(1)}, u32[]{:S(2)}, u32[]{:S(2)}) collective-permute-start(bf16[32,4096]{1,0:T(8,128)(2,1)S(1)} %residual.1), channel_id=1, source_target_pairs={{8,0},{16,8},{24,16},{9,1},{17,9},{25,17},{10,2},{18,10},{26,18},{... | collective-permute-start | bytes 786440 | tf_op jit(solution)/shard_map/ppermute | solution.py:21
  12.9 2.1 %collective-permute-done.after_ref.moved_ref = bf16[32,4096]{1,0:T(8,128)(2,1)S(1)} collective-permute-done((bf16[32,4096]{1,0:T(8,128)(2,1)S(1)}, bf16[32,4096]{1,0:T(8,128)(2,1)S(1)}, u32[]{:S(2)}, u32[]{:S(2)}) %collective-permute-start) | collective-permute-done | bytes 262176 | tf_op jit(solution)/shard_map/ppermute | solution.py:21
  15.1 12.0 %all-to-all-done = bf16[32,24,384]{2,1,0:T(8,128)(2,1)S(1)} async-done(((bf16[32,24,384]{2,1,0:T(8,128)(2,1)}), bf16[32,24,384]{2,1,0:T(8,128)(2,1)S(1)}, u32[]{:S(2)}, u32[]{:S(2)}) %all-to-all-start) | async-done | bytes 589856 | tf_op jit(solution)/shard_map/all_to_all | solution.py:332
  27.1 0.0 copy-done.2
  27.1 1.6 %attend.1 = (bf16[768,128]{1,0:T(8,128)(2,1)}, bf16[2,192,128]{2,1,0:T(8,128)(2,1)S(1)}, bf16[2,192,128]{2,1,0:T(8,128)(2,1)S(1)}, bf16[2,192,128]{2,1,0:T(8,128)(2,1)S(1)}) custom-call(s32[4,4]{1,0:T(4,128)S(1)} %copy-done.2, bf16[768,384]{1,0:T(8,128)(2,1)S(1)} %bitcast.4, bf16[32,4096]{1,0:T(8,128)(2,1)S(1)} %collective-permute-done.after_ref.moved_ref), custom_call_target="tpu_custom_call" | custom-call | flops 150994944 | bytes 1343552 | tf_op jit(solution)/shard_map/attend/pallas_call | solution.py:291
  28.6 2.7 %all-to-all-start.1 = ((bf16[32,24,128]{2,1,0:T(8,128)(2,1)}), bf16[32,24,128]{2,1,0:T(8,128)(2,1)S(1)}, u32[]{:S(2)}, u32[]{:S(2)}) async-start(bf16[32,24,128]{2,1,0:T(8,128)(2,1)} %bitcast.8), calls=%async_computation.1 | async-start | bytes 393216 | tf_op jit(solution)/shard_map/all_to_all | solution.py:358
  31.4 1.3 %collective-permute-start.1 = (bf16[2,192,128]{2,1,0:T(8,128)(2,1)S(1)}, bf16[2,192,128]{2,1,0:T(8,128)(2,1)S(1)}, u32[]{:S(2)}, u32[]{:S(2)}) collective-permute-start(bf16[2,192,128]{2,1,0:T(8,128)(2,1)S(1)} %get-tuple-element.7), channel_id=1, source_target_pairs={{8,16},{16,8},{24,0},{9,17},{17,9},{25,1},{10,18},{18,10},{26,2},{... | collective-permute-start | bytes 294920 | tf_op jit(solution)/shard_map/ppermute | solution.py:362
  32.7 4.4 %collective-permute-start.2 = (bf16[2,192,128]{2,1,0:T(8,128)(2,1)S(1)}, bf16[2,192,128]{2,1,0:T(8,128)(2,1)S(1)}, u32[]{:S(2)}, u32[]{:S(2)}) collective-permute-start(bf16[2,192,128]{2,1,0:T(8,128)(2,1)S(1)} %get-tuple-element.8), channel_id=1, source_target_pairs={{0,16},{16,0},{24,8},{1,17},{17,1},{25,9},{2,18},{18,2},{26,10},{3... | collective-permute-start | bytes 294920 | tf_op jit(solution)/shard_map/ppermute | solution.py:362
  37.1 0.0 copy-start.1
  37.1 2.1 %collective-permute-start.3 = (bf16[2,192,128]{2,1,0:T(8,128)(2,1)S(1)}, bf16[2,192,128]{2,1,0:T(8,128)(2,1)S(1)}, u32[]{:S(2)}, u32[]{:S(2)}) collective-permute-start(bf16[2,192,128]{2,1,0:T(8,128)(2,1)S(1)} %get-tuple-element.9), channel_id=1, source_target_pairs={{0,8},{8,0},{24,16},{1,9},{9,1},{25,17},{2,10},{10,2},{26,18},{3,1... | collective-permute-start | bytes 294920 | tf_op jit(solution)/shard_map/ppermute | solution.py:362
  39.1 0.0 collective-permute-done.1.hand_ref
  39.1 0.8 %cache.1.begun_hbm = bf16[1,2,192,512]{3,2,1,0:T(8,128)(2,1)} custom-call(bf16[768,384]{1,0:T(8,128)(2,1)S(1)} %bitcast.5, bf16[2,192,128]{2,1,0:T(8,128)(2,1)S(1)} %collective-permute-done.1.hand_ref), custom_call_target="tpu_custom_call" | custom-call | bytes 1081344 | tf_op jit(solution)/shard_map/cache/pallas_call | solution.py:291
  40.0 1.1 %collective-permute-done.2.refs_0_ = bf16[2,192,128]{2,1,0:T(8,128)(2,1)S(1)} collective-permute-done((bf16[2,192,128]{2,1,0:T(8,128)(2,1)S(1)}, bf16[2,192,128]{2,1,0:T(8,128)(2,1)S(1)}, u32[]{:S(2)}, u32[]{:S(2)}) %collective-permute-start.2) | collective-permute-done | bytes 98336 | tf_op jit(solution)/shard_map/ppermute | solution.py:362
  41.0 0.0 collective-permute-done.3.refs_1_
  41.0 0.0 all-to-all-done.1
  41.0 0.0 copy-done.1
  41.0 0.8 %finish.1 = (bf16[1,24,4096]{2,1,0:T(8,128)(2,1)}, bf16[1,2,192,512]{3,2,1,0:T(8,128)(2,1)}) custom-call(bf16[768,128]{1,0:T(8,128)(2,1)S(1)} %bitcast.6, bf16[32,4096]{1,0:T(8,128)(2,1)S(1)} %collective-permute-done.after_ref.moved_ref, bf16[24,4096]{1,0:T(8,128)(2,1)S(1)} %copy-done.1, ...), custom_call_target="tpu_custom_call", output_to_operand_aliasing={{1}: (3, {})} | custom-call | bytes 1835008 | tf_op jit(solution)/shard_map/finish/pallas_call | solution.py:291
Async XLA Ops:
  2.6 8.0 %copy-start = (bf16[1,24,4096]{2,1,0:T(8,128)(2,1)S(1)}, bf16[1,24,4096]{2,1,0:T(8,128)(2,1)}, u32[]{:S(2)}) copy-start(bf16[1,24,4096]{2,1,0:T(8,128)(2,1)} %h_ref.1) | copy-start | bytes 589828
  2.6 24.4 %all-to-all-start = ((bf16[32,24,384]{2,1,0:T(8,128)(2,1)}), bf16[32,24,384]{2,1,0:T(8,128)(2,1)S(1)}, u32[]{:S(2)}, u32[]{:S(2)}) async-start(bf16[32,24,384]{2,1,0:T(8,128)(2,1)} %bitcast.7), calls=%async_computation | async-start | bytes 1179648 | tf_op jit(solution)/shard_map/all_to_all | solution.py:332
  10.6 16.5 %copy-start.2 = (s32[4,4]{1,0:T(4,128)S(1)}, s32[4,4]{1,0:T(4,128)}, u32[]{:S(2)}) copy-start(s32[4,4]{1,0:T(4,128)} %pattern_ref.1) | copy-start | bytes 196
  11.6 3.4 %collective-permute-start = (bf16[32,4096]{1,0:T(8,128)(2,1)S(1)}, bf16[32,4096]{1,0:T(8,128)(2,1)S(1)}, u32[]{:S(2)}, u32[]{:S(2)}) collective-permute-start(bf16[32,4096]{1,0:T(8,128)(2,1)S(1)} %residual.1), channel_id=1, source_target_pairs={{8,0},{16,8},{24,16},{9,1},{17,9},{25,17},{10,2},{18,10},{26,18},{... | collective-permute-start | bytes 786440 | tf_op jit(solution)/shard_map/ppermute | solution.py:21
  28.6 12.4 %all-to-all-start.1 = ((bf16[32,24,128]{2,1,0:T(8,128)(2,1)}), bf16[32,24,128]{2,1,0:T(8,128)(2,1)S(1)}, u32[]{:S(2)}, u32[]{:S(2)}) async-start(bf16[32,24,128]{2,1,0:T(8,128)(2,1)} %bitcast.8), calls=%async_computation.1 | async-start | bytes 393216 | tf_op jit(solution)/shard_map/all_to_all | solution.py:358
  31.4 7.8 %collective-permute-start.1 = (bf16[2,192,128]{2,1,0:T(8,128)(2,1)S(1)}, bf16[2,192,128]{2,1,0:T(8,128)(2,1)S(1)}, u32[]{:S(2)}, u32[]{:S(2)}) collective-permute-start(bf16[2,192,128]{2,1,0:T(8,128)(2,1)S(1)} %get-tuple-element.7), channel_id=1, source_target_pairs={{8,16},{16,8},{24,0},{9,17},{17,9},{25,1},{10,18},{18,10},{26,2},{... | collective-permute-start | bytes 294920 | tf_op jit(solution)/shard_map/ppermute | solution.py:362
  32.7 8.4 %collective-permute-start.2 = (bf16[2,192,128]{2,1,0:T(8,128)(2,1)S(1)}, bf16[2,192,128]{2,1,0:T(8,128)(2,1)S(1)}, u32[]{:S(2)}, u32[]{:S(2)}) collective-permute-start(bf16[2,192,128]{2,1,0:T(8,128)(2,1)S(1)} %get-tuple-element.8), channel_id=1, source_target_pairs={{0,16},{16,0},{24,8},{1,17},{17,1},{25,9},{2,18},{18,2},{26,10},{3... | collective-permute-start | bytes 294920 | tf_op jit(solution)/shard_map/ppermute | solution.py:362
  37.1 4.0 %copy-start.1 = (bf16[24,4096]{1,0:T(8,128)(2,1)S(1)}, bf16[24,4096]{1,0:T(8,128)(2,1)}, u32[]{:S(2)}) copy-start(bf16[24,4096]{1,0:T(8,128)(2,1)} %fresh_ref.1) | copy-start | bytes 589828
  37.1 4.0 %collective-permute-start.3 = (bf16[2,192,128]{2,1,0:T(8,128)(2,1)S(1)}, bf16[2,192,128]{2,1,0:T(8,128)(2,1)S(1)}, u32[]{:S(2)}, u32[]{:S(2)}) collective-permute-start(bf16[2,192,128]{2,1,0:T(8,128)(2,1)S(1)} %get-tuple-element.9), channel_id=1, source_target_pairs={{0,8},{8,0},{24,16},{1,9},{9,1},{25,17},{2,10},{10,2},{26,18},{3,1... | collective-permute-start | bytes 294920 | tf_op jit(solution)/shard_map/ppermute | solution.py:362

commit v31 on v30

--- a/solution.py
+++ b/solution.py
@@ -114,7 +114,7 @@
 
 
 def distances(groups):
-    return range(groups - 1, 0, -1)
+    return sorted(range(1, groups), key=lambda distance: (distance < groups // 2, distance))
 
 
 def hand_over(group, seq_count, x_ref, out_ref, lanes=slice(None)):

time: 42.3 us -> 42.8 us (1.012)
  no operation moved by 1% of the time
where the time goes in v31:
time: 42.8 us; the launch traced here: 42.4 us
  starting transfers between devices  19.3 us (45%)
  waiting for transfers between devices  15.5 us (36%)
  Pallas kernels  6.18 us (14%)
  between operations  1.39 us (3%)
    all_to_all x1, waiting for transfers between devices, spread_body(): exchanged = exchange(packed, axis_index_groups=[out])  12 us
    ppermute x3, starting transfers between devices, spread_body(): lax.ppermute(hand, 'tm', [(i, j) for i, j in route if j < tm_count - 1])  8 us
    all_to_all x1, starting transfers between devices, spread_body(): exchanged = exchange(packed, axis_index_groups=[out])  7.3 us
    pallas_call x5, Pallas kernels, run(): pl.pallas_call(kernel, out_shape=outs, in_specs=specs, out_specs=[whole(g...  6.18 us
    all_to_all x1, starting transfers between devices, spread_body(): returned = exchange(attended, axis_index_groups=[out])  2.71 us
    ppermute x1, waiting for transfers between devices, shifted(): return lax.ppermute(block, axis, route)  2.13 us
    ppermute x3, waiting for transfers between devices, spread_body(): lax.ppermute(hand, 'tm', [(i, j) for i, j in route if j < tm_count - 1])  1.33 us
    ppermute x1, starting transfers between devices, shifted(): return lax.ppermute(block, axis, route)  1.29 us
  transfers between devices with their start and end apart: 6, of which 3 were waited for; matrix products, arithmetic and copies ran while one was open for 0% of the time, Pallas kernels for 4%

profile of v31, /device:TPU:0, one launch (start us, length us, event | category | flops | bytes accessed | tf_op | source)
XLA Modules:
  0.0 42.4 jit_solution(12933203768123408789)
XLA Ops:
  0.6 2.0 %pack.1.after_ref = bf16[768,384]{1,0:T(8,128)(2,1)} custom-call(bf16[1,24,4096]{2,1,0:T(8,128)(2,1)} %q_hbm.1, bf16[1,24,4096]{2,1,0:T(8,128)(2,1)} %k_hbm.1, bf16[1,24,4096]{2,1,0:T(8,128)(2,1)} %v_hbm.1), custom_call_target="tpu_custom_call" | custom-call | bytes 1179648 | tf_op jit(solution)/shard_map/pack/pallas_call | solution.py:291
  2.6 0.0 copy-start
  2.6 7.3 %all-to-all-start = ((bf16[32,24,384]{2,1,0:T(8,128)(2,1)}), bf16[32,24,384]{2,1,0:T(8,128)(2,1)S(1)}, u32[]{:S(2)}, u32[]{:S(2)}) async-start(bf16[32,24,384]{2,1,0:T(8,128)(2,1)} %bitcast.7), calls=%async_computation | async-start | bytes 1179648 | tf_op jit(solution)/shard_map/all_to_all | solution.py:332
  10.6 0.0 copy-done
  10.6 0.0 copy-start.2
  10.6 1.0 %residual.1 = bf16[32,4096]{1,0:T(8,128)(2,1)S(1)} custom-call(s32[1]{0:T(128)S(6)} %copy.12.noise_ref, bf16[1,24,4096]{2,1,0:T(8,128)(2,1)S(1)} %copy-done, f32[50,4096]{1,0:T(8,128)} %gate_hbm.1, bf16[768,384]{1,0:T(8,128)(2,1)} %pack.1.after_ref), custom_call_target="tpu_custom_call" | custom-call | bytes 1867780 | tf_op jit(solution)/shard_map/residual/pallas_call | solution.py:291
  11.6 1.3 %collective-permute-start = (bf16[32,4096]{1,0:T(8,128)(2,1)S(1)}, bf16[32,4096]{1,0:T(8,128)(2,1)S(1)}, u32[]{:S(2)}, u32[]{:S(2)}) collective-permute-start(bf16[32,4096]{1,0:T(8,128)(2,1)S(1)} %residual.1), channel_id=1, source_target_pairs={{8,0},{16,8},{24,16},{9,1},{17,9},{25,17},{10,2},{18,10},{26,18},{... | collective-permute-start | bytes 786440 | tf_op jit(solution)/shard_map/ppermute | solution.py:21
  12.9 2.1 %collective-permute-done.after_ref.moved_ref = bf16[32,4096]{1,0:T(8,128)(2,1)S(1)} collective-permute-done((bf16[32,4096]{1,0:T(8,128)(2,1)S(1)}, bf16[32,4096]{1,0:T(8,128)(2,1)S(1)}, u32[]{:S(2)}, u32[]{:S(2)}) %collective-permute-start) | collective-permute-done | bytes 262176 | tf_op jit(solution)/shard_map/ppermute | solution.py:21
  15.1 12.0 %all-to-all-done = bf16[32,24,384]{2,1,0:T(8,128)(2,1)S(1)} async-done(((bf16[32,24,384]{2,1,0:T(8,128)(2,1)}), bf16[32,24,384]{2,1,0:T(8,128)(2,1)S(1)}, u32[]{:S(2)}, u32[]{:S(2)}) %all-to-all-start) | async-done | bytes 589856 | tf_op jit(solution)/shard_map/all_to_all | solution.py:332
  27.1 0.0 copy-done.2
  27.1 1.6 %attend.1 = (bf16[768,128]{1,0:T(8,128)(2,1)}, bf16[2,192,128]{2,1,0:T(8,128)(2,1)S(1)}, bf16[2,192,128]{2,1,0:T(8,128)(2,1)S(1)}, bf16[2,192,128]{2,1,0:T(8,128)(2,1)S(1)}) custom-call(s32[4,4]{1,0:T(4,128)S(1)} %copy-done.2, bf16[768,384]{1,0:T(8,128)(2,1)S(1)} %bitcast.4, bf16[32,4096]{1,0:T(8,128)(2,1)S(1)} %collective-permute-done.after_ref.moved_ref), custom_call_target="tpu_custom_call" | custom-call | flops 150994944 | bytes 1343552 | tf_op jit(solution)/shard_map/attend/pallas_call | solution.py:291
  28.6 2.7 %all-to-all-start.1 = ((bf16[32,24,128]{2,1,0:T(8,128)(2,1)}), bf16[32,24,128]{2,1,0:T(8,128)(2,1)S(1)}, u32[]{:S(2)}, u32[]{:S(2)}) async-start(bf16[32,24,128]{2,1,0:T(8,128)(2,1)} %bitcast.8), calls=%async_computation.1 | async-start | bytes 393216 | tf_op jit(solution)/shard_map/all_to_all | solution.py:358
  31.4 3.7 %collective-permute-start.1 = (bf16[2,192,128]{2,1,0:T(8,128)(2,1)S(1)}, bf16[2,192,128]{2,1,0:T(8,128)(2,1)S(1)}, u32[]{:S(2)}, u32[]{:S(2)}) collective-permute-start(bf16[2,192,128]{2,1,0:T(8,128)(2,1)S(1)} %get-tuple-element.7), channel_id=1, source_target_pairs={{0,16},{16,0},{24,8},{1,17},{17,1},{25,9},{2,18},{18,2},{26,10},{3... | collective-permute-start | bytes 294920 | tf_op jit(solution)/shard_map/ppermute | solution.py:362
  35.0 1.3 %collective-permute-start.2 = (bf16[2,192,128]{2,1,0:T(8,128)(2,1)S(1)}, bf16[2,192,128]{2,1,0:T(8,128)(2,1)S(1)}, u32[]{:S(2)}, u32[]{:S(2)}) collective-permute-start(bf16[2,192,128]{2,1,0:T(8,128)(2,1)S(1)} %get-tuple-element.8), channel_id=1, source_target_pairs={{8,16},{16,8},{24,0},{9,17},{17,9},{25,1},{10,18},{18,10},{26,2},{... | collective-permute-start | bytes 294920 | tf_op jit(solution)/shard_map/ppermute | solution.py:362
  36.3 0.0 copy-start.1
  36.4 3.0 %collective-permute-start.3 = (bf16[2,192,128]{2,1,0:T(8,128)(2,1)S(1)}, bf16[2,192,128]{2,1,0:T(8,128)(2,1)S(1)}, u32[]{:S(2)}, u32[]{:S(2)}) collective-permute-start(bf16[2,192,128]{2,1,0:T(8,128)(2,1)S(1)} %get-tuple-element.9), channel_id=1, source_target_pairs={{0,8},{8,0},{24,16},{1,9},{9,1},{25,17},{2,10},{10,2},{26,18},{3,1... | collective-permute-start | bytes 294920 | tf_op jit(solution)/shard_map/ppermute | solution.py:362
  39.4 0.0 collective-permute-done.1.hand_ref
  39.4 0.8 %cache.1.begun_hbm = bf16[1,2,192,512]{3,2,1,0:T(8,128)(2,1)} custom-call(bf16[768,384]{1,0:T(8,128)(2,1)S(1)} %bitcast.5, bf16[2,192,128]{2,1,0:T(8,128)(2,1)S(1)} %collective-permute-done.1.hand_ref), custom_call_target="tpu_custom_call" | custom-call | bytes 1081344 | tf_op jit(solution)/shard_map/cache/pallas_call | solution.py:291
  40.2 1.3 %collective-permute-done.2.refs_0_ = bf16[2,192,128]{2,1,0:T(8,128)(2,1)S(1)} collective-permute-done((bf16[2,192,128]{2,1,0:T(8,128)(2,1)S(1)}, bf16[2,192,128]{2,1,0:T(8,128)(2,1)S(1)}, u32[]{:S(2)}, u32[]{:S(2)}) %collective-permute-start.2) | collective-permute-done | bytes 98336 | tf_op jit(solution)/shard_map/ppermute | solution.py:362
  41.5 0.0 collective-permute-done.3.refs_1_
  41.6 0.0 all-to-all-done.1
  41.6 0.0 copy-done.1
  41.6 0.8 %finish.1 = (bf16[1,24,4096]{2,1,0:T(8,128)(2,1)}, bf16[1,2,192,512]{3,2,1,0:T(8,128)(2,1)}) custom-call(bf16[768,128]{1,0:T(8,128)(2,1)S(1)} %bitcast.6, bf16[32,4096]{1,0:T(8,128)(2,1)S(1)} %collective-permute-done.after_ref.moved_ref, bf16[24,4096]{1,0:T(8,128)(2,1)S(1)} %copy-done.1, ...), custom_call_target="tpu_custom_call", output_to_operand_aliasing={{1}: (3, {})} | custom-call | bytes 1835008 | tf_op jit(solution)/shard_map/finish/pallas_call | solution.py:291
Async XLA Ops:
  2.6 8.0 %copy-start = (bf16[1,24,4096]{2,1,0:T(8,128)(2,1)S(1)}, bf16[1,24,4096]{2,1,0:T(8,128)(2,1)}, u32[]{:S(2)}) copy-start(bf16[1,24,4096]{2,1,0:T(8,128)(2,1)} %h_ref.1) | copy-start | bytes 589828
  2.6 24.4 %all-to-all-start = ((bf16[32,24,384]{2,1,0:T(8,128)(2,1)}), bf16[32,24,384]{2,1,0:T(8,128)(2,1)S(1)}, u32[]{:S(2)}, u32[]{:S(2)}) async-start(bf16[32,24,384]{2,1,0:T(8,128)(2,1)} %bitcast.7), calls=%async_computation | async-start | bytes 1179648 | tf_op jit(solution)/shard_map/all_to_all | solution.py:332
  10.6 16.5 %copy-start.2 = (s32[4,4]{1,0:T(4,128)S(1)}, s32[4,4]{1,0:T(4,128)}, u32[]{:S(2)}) copy-start(s32[4,4]{1,0:T(4,128)} %pattern_ref.1) | copy-start | bytes 196
  11.6 3.4 %collective-permute-start = (bf16[32,4096]{1,0:T(8,128)(2,1)S(1)}, bf16[32,4096]{1,0:T(8,128)(2,1)S(1)}, u32[]{:S(2)}, u32[]{:S(2)}) collective-permute-start(bf16[32,4096]{1,0:T(8,128)(2,1)S(1)} %residual.1), channel_id=1, source_target_pairs={{8,0},{16,8},{24,16},{9,1},{17,9},{25,17},{10,2},{18,10},{26,18},{... | collective-permute-start | bytes 786440 | tf_op jit(solution)/shard_map/ppermute | solution.py:21
  28.6 12.9 %all-to-all-start.1 = ((bf16[32,24,128]{2,1,0:T(8,128)(2,1)}), bf16[32,24,128]{2,1,0:T(8,128)(2,1)S(1)}, u32[]{:S(2)}, u32[]{:S(2)}) async-start(bf16[32,24,128]{2,1,0:T(8,128)(2,1)} %bitcast.8), calls=%async_computation.1 | async-start | bytes 393216 | tf_op jit(solution)/shard_map/all_to_all | solution.py:358
  31.4 8.0 %collective-permute-start.1 = (bf16[2,192,128]{2,1,0:T(8,128)(2,1)S(1)}, bf16[2,192,128]{2,1,0:T(8,128)(2,1)S(1)}, u32[]{:S(2)}, u32[]{:S(2)}) collective-permute-start(bf16[2,192,128]{2,1,0:T(8,128)(2,1)S(1)} %get-tuple-element.7), channel_id=1, source_target_pairs={{0,16},{16,0},{24,8},{1,17},{17,1},{25,9},{2,18},{18,2},{26,10},{3... | collective-permute-start | bytes 294920 | tf_op jit(solution)/shard_map/ppermute | solution.py:362
  35.0 6.5 %collective-permute-start.2 = (bf16[2,192,128]{2,1,0:T(8,128)(2,1)S(1)}, bf16[2,192,128]{2,1,0:T(8,128)(2,1)S(1)}, u32[]{:S(2)}, u32[]{:S(2)}) collective-permute-start(bf16[2,192,128]{2,1,0:T(8,128)(2,1)S(1)} %get-tuple-element.8), channel_id=1, source_target_pairs={{8,16},{16,8},{24,0},{9,17},{17,9},{25,1},{10,18},{18,10},{26,2},{... | collective-permute-start | bytes 294920 | tf_op jit(solution)/shard_map/ppermute | solution.py:362
  36.3 5.2 %copy-start.1 = (bf16[24,4096]{1,0:T(8,128)(2,1)S(1)}, bf16[24,4096]{1,0:T(8,128)(2,1)}, u32[]{:S(2)}) copy-start(bf16[24,4096]{1,0:T(8,128)(2,1)} %fresh_ref.1) | copy-start | bytes 589828
  36.4 5.2 %collective-permute-start.3 = (bf16[2,192,128]{2,1,0:T(8,128)(2,1)S(1)}, bf16[2,192,128]{2,1,0:T(8,128)(2,1)S(1)}, u32[]{:S(2)}, u32[]{:S(2)}) collective-permute-start(bf16[2,192,128]{2,1,0:T(8,128)(2,1)S(1)} %get-tuple-element.9), channel_id=1, source_target_pairs={{0,8},{8,0},{24,16},{1,9},{9,1},{25,17},{2,10},{10,2},{26,18},{3,1... | collective-permute-start | bytes 294920 | tf_op jit(solution)/shard_map/ppermute | solution.py:362

commit v32 on v29

--- a/solution.py
+++ b/solution.py
@@ -22,8 +22,7 @@
 
 
 def pair_place(group, pair, pairs):
-    place = (pair + pairs // 2) % pairs
-    return place + group // 2 % 2 * (pairs - 1 - 2 * place)
+    return pair + group // 2 % 2 * (pairs - 1 - 2 * pair)
 
 
 def out_order(tm_count, seq_count):

time: 42.4 us -> 42.7 us (level)
  waiting for transfers between devices: 14.7 us -> 15.2 us
where the time goes in v32:
time: 42.7 us; the launch traced here: 42.2 us
  starting transfers between devices  18.8 us (44%)
  waiting for transfers between devices  15.2 us (36%)
  Pallas kernels  6.84 us (16%)
  between operations  1.39 us (3%)
    all_to_all x1, waiting for transfers between devices, spread_body(): exchanged = exchange(packed, axis_index_groups=[out])  12.4 us
    ppermute x3, starting transfers between devices, spread_body(): lax.ppermute(hand, 'tm', [(i, j) for i, j in route if j < tm_count - 1])  7.61 us
    all_to_all x1, starting transfers between devices, spread_body(): exchanged = exchange(packed, axis_index_groups=[out])  7.3 us
    pallas_call x6, Pallas kernels, run(): pl.pallas_call(kernel, out_shape=outs, in_specs=specs, out_specs=[whole(g...  6.84 us
    all_to_all x1, starting transfers between devices, spread_body(): returned = exchange(attended, axis_index_groups=[out])  2.6 us
    ppermute x1, waiting for transfers between devices, shifted(): return lax.ppermute(block, axis, route)  2.13 us
    ppermute x1, starting transfers between devices, shifted(): return lax.ppermute(block, axis, route)  1.29 us
  transfers between devices with their start and end apart: 6, of which 3 were waited for; matrix products, arithmetic and copies ran while one was open for 0% of the time, Pallas kernels for 6%

profile of v32, /device:TPU:0, one launch (start us, length us, event | category | flops | bytes accessed | tf_op | source)
XLA Modules:
  0.0 42.2 jit_solution(16843129107921805994)
XLA Ops:
  0.6 2.0 %pack.1.after_ref = bf16[768,384]{1,0:T(8,128)(2,1)} custom-call(bf16[1,24,4096]{2,1,0:T(8,128)(2,1)} %q_hbm.1, bf16[1,24,4096]{2,1,0:T(8,128)(2,1)} %k_hbm.1, bf16[1,24,4096]{2,1,0:T(8,128)(2,1)} %v_hbm.1), custom_call_target="tpu_custom_call" | custom-call | bytes 1179648 | tf_op jit(solution)/shard_map/pack/pallas_call | solution.py:292
  2.6 0.0 copy-start
  2.6 7.3 %all-to-all-start = ((bf16[32,24,384]{2,1,0:T(8,128)(2,1)}), bf16[32,24,384]{2,1,0:T(8,128)(2,1)S(1)}, u32[]{:S(2)}, u32[]{:S(2)}) async-start(bf16[32,24,384]{2,1,0:T(8,128)(2,1)} %bitcast.7), calls=%async_computation | async-start | bytes 1179648 | tf_op jit(solution)/shard_map/all_to_all | solution.py:333
  10.6 0.0 copy-done
  10.6 0.0 copy-start.2
  10.6 1.0 %residual.1 = bf16[32,4096]{1,0:T(8,128)(2,1)S(1)} custom-call(s32[1]{0:T(128)S(6)} %copy.12.noise_ref, bf16[1,24,4096]{2,1,0:T(8,128)(2,1)S(1)} %copy-done, f32[50,4096]{1,0:T(8,128)} %gate_hbm.1, bf16[768,384]{1,0:T(8,128)(2,1)} %pack.1.after_ref), custom_call_target="tpu_custom_call" | custom-call | bytes 1867780 | tf_op jit(solution)/shard_map/residual/pallas_call | solution.py:292
  11.6 1.3 %collective-permute-start = (bf16[32,4096]{1,0:T(8,128)(2,1)S(1)}, bf16[32,4096]{1,0:T(8,128)(2,1)S(1)}, u32[]{:S(2)}, u32[]{:S(2)}) collective-permute-start(bf16[32,4096]{1,0:T(8,128)(2,1)S(1)} %residual.1), channel_id=1, source_target_pairs={{8,0},{16,8},{24,16},{9,1},{17,9},{25,17},{10,2},{18,10},{26,18},{... | collective-permute-start | bytes 786440 | tf_op jit(solution)/shard_map/ppermute | solution.py:21
  12.9 2.1 %collective-permute-done.after_ref.moved_ref = bf16[32,4096]{1,0:T(8,128)(2,1)S(1)} collective-permute-done((bf16[32,4096]{1,0:T(8,128)(2,1)S(1)}, bf16[32,4096]{1,0:T(8,128)(2,1)S(1)}, u32[]{:S(2)}, u32[]{:S(2)}) %collective-permute-start) | collective-permute-done | bytes 262176 | tf_op jit(solution)/shard_map/ppermute | solution.py:21
  15.1 12.4 %all-to-all-done = bf16[32,24,384]{2,1,0:T(8,128)(2,1)S(1)} async-done(((bf16[32,24,384]{2,1,0:T(8,128)(2,1)}), bf16[32,24,384]{2,1,0:T(8,128)(2,1)S(1)}, u32[]{:S(2)}, u32[]{:S(2)}) %all-to-all-start) | async-done | bytes 589856 | tf_op jit(solution)/shard_map/all_to_all | solution.py:333
  27.5 0.0 copy-done.2
  27.5 1.6 %attend.1 = (bf16[768,128]{1,0:T(8,128)(2,1)}, bf16[2,192,128]{2,1,0:T(8,128)(2,1)S(1)}, bf16[2,192,128]{2,1,0:T(8,128)(2,1)S(1)}, bf16[2,192,128]{2,1,0:T(8,128)(2,1)S(1)}) custom-call(s32[4,4]{1,0:T(4,128)S(1)} %copy-done.2, bf16[768,384]{1,0:T(8,128)(2,1)S(1)} %bitcast.4, bf16[32,4096]{1,0:T(8,128)(2,1)S(1)} %collective-permute-done.after_ref.moved_ref), custom_call_target="tpu_custom_call" | custom-call | flops 150994944 | bytes 1343552 | tf_op jit(solution)/shard_map/attend/pallas_call | solution.py:292
  29.0 2.6 %all-to-all-start.1 = ((bf16[32,24,128]{2,1,0:T(8,128)(2,1)}), bf16[32,24,128]{2,1,0:T(8,128)(2,1)S(1)}, u32[]{:S(2)}, u32[]{:S(2)}) async-start(bf16[32,24,128]{2,1,0:T(8,128)(2,1)} %bitcast.8), calls=%async_computation.1 | async-start | bytes 393216 | tf_op jit(solution)/shard_map/all_to_all | solution.py:359
  31.7 1.3 %collective-permute-start.1 = (bf16[2,192,128]{2,1,0:T(8,128)(2,1)S(1)}, bf16[2,192,128]{2,1,0:T(8,128)(2,1)S(1)}, u32[]{:S(2)}, u32[]{:S(2)}) collective-permute-start(bf16[2,192,128]{2,1,0:T(8,128)(2,1)S(1)} %get-tuple-element.7), channel_id=1, source_target_pairs={{8,16},{16,8},{24,0},{9,17},{17,9},{25,1},{10,18},{18,10},{26,2},{... | collective-permute-start | bytes 294920 | tf_op jit(solution)/shard_map/ppermute | solution.py:363
  33.0 4.3 %collective-permute-start.2 = (bf16[2,192,128]{2,1,0:T(8,128)(2,1)S(1)}, bf16[2,192,128]{2,1,0:T(8,128)(2,1)S(1)}, u32[]{:S(2)}, u32[]{:S(2)}) collective-permute-start(bf16[2,192,128]{2,1,0:T(8,128)(2,1)S(1)} %get-tuple-element.8), channel_id=1, source_target_pairs={{0,16},{16,0},{24,8},{1,17},{17,1},{25,9},{2,18},{18,2},{26,10},{3... | collective-permute-start | bytes 294920 | tf_op jit(solution)/shard_map/ppermute | solution.py:363
  37.2 0.0 copy-start.1
  37.2 2.1 %collective-permute-start.3 = (bf16[2,192,128]{2,1,0:T(8,128)(2,1)S(1)}, bf16[2,192,128]{2,1,0:T(8,128)(2,1)S(1)}, u32[]{:S(2)}, u32[]{:S(2)}) collective-permute-start(bf16[2,192,128]{2,1,0:T(8,128)(2,1)S(1)} %get-tuple-element.9), channel_id=1, source_target_pairs={{0,8},{8,0},{24,16},{1,9},{9,1},{25,17},{2,10},{10,2},{26,18},{3,1... | collective-permute-start | bytes 294920 | tf_op jit(solution)/shard_map/ppermute | solution.py:363
  39.3 0.0 collective-permute-done.1.hand_ref
  39.3 0.8 %cache.1.after_ref.begun_hbm = bf16[1,2,192,512]{3,2,1,0:T(8,128)(2,1)} custom-call(bf16[768,384]{1,0:T(8,128)(2,1)S(1)} %bitcast.5, bf16[2,192,128]{2,1,0:T(8,128)(2,1)S(1)} %collective-permute-done.1.hand_ref), custom_call_target="tpu_custom_call" | custom-call | bytes 1081344 | tf_op jit(solution)/shard_map/cache/pallas_call | solution.py:292
  40.1 0.6 %all-to-all-done.1 = bf16[32,24,128]{2,1,0:T(8,128)(2,1)S(1)} async-done(((bf16[32,24,128]{2,1,0:T(8,128)(2,1)}), bf16[32,24,128]{2,1,0:T(8,128)(2,1)S(1)}, u32[]{:S(2)}, u32[]{:S(2)}) %all-to-all-start.1) | async-done | bytes 196640 | tf_op jit(solution)/shard_map/all_to_all | solution.py:359
  40.7 0.0 copy-done.1
  40.7 0.8 %update.1.after_ref = bf16[1,24,4096]{2,1,0:T(8,128)(2,1)} custom-call(bf16[768,128]{1,0:T(8,128)(2,1)S(1)} %bitcast.6, bf16[32,4096]{1,0:T(8,128)(2,1)S(1)} %collective-permute-done.after_ref.moved_ref, bf16[24,4096]{1,0:T(8,128)(2,1)S(1)} %copy-done.1, bf16[1,2,192,512]{3,2,1,0:T(8,128)(2,1)} %cache.1.after_ref.begun_hbm), custom_call_target="tpu_custom_call" | custom-call | bytes 1245184 | tf_op jit(solution)/shard_map/update/pallas_call | solution.py:292
  41.5 0.0 collective-permute-done.2.refs_0_
  41.5 0.0 collective-permute-done.3.refs_1_
  41.5 0.7 %cache_rest.1 = bf16[1,2,192,512]{3,2,1,0:T(8,128)(2,1)} custom-call(bf16[1,2,192,512]{3,2,1,0:T(8,128)(2,1)} %cache.1.after_ref.begun_hbm, bf16[1,24,4096]{2,1,0:T(8,128)(2,1)} %update.1.after_ref, bf16[2,192,128]{2,1,0:T(8,128)(2,1)S(1)} %collective-permute-done.2.refs_0_, ...), custom_call_target="tpu_custom_call", output_to_operand_aliasing={{}: (0, {})} | custom-call | bytes 1179648 | tf_op jit(solution)/shard_map/cache_rest/pallas_call | solution.py:292
Async XLA Ops:
  2.6 8.0 %copy-start = (bf16[1,24,4096]{2,1,0:T(8,128)(2,1)S(1)}, bf16[1,24,4096]{2,1,0:T(8,128)(2,1)}, u32[]{:S(2)}) copy-start(bf16[1,24,4096]{2,1,0:T(8,128)(2,1)} %h_ref.1) | copy-start | bytes 589828
  2.6 24.8 %all-to-all-start = ((bf16[32,24,384]{2,1,0:T(8,128)(2,1)}), bf16[32,24,384]{2,1,0:T(8,128)(2,1)S(1)}, u32[]{:S(2)}, u32[]{:S(2)}) async-start(bf16[32,24,384]{2,1,0:T(8,128)(2,1)} %bitcast.7), calls=%async_computation | async-start | bytes 1179648 | tf_op jit(solution)/shard_map/all_to_all | solution.py:333
  10.6 16.9 %copy-start.2 = (s32[4,4]{1,0:T(4,128)S(1)}, s32[4,4]{1,0:T(4,128)}, u32[]{:S(2)}) copy-start(s32[4,4]{1,0:T(4,128)} %pattern_ref.1) | copy-start | bytes 196
  11.6 3.4 %collective-permute-start = (bf16[32,4096]{1,0:T(8,128)(2,1)S(1)}, bf16[32,4096]{1,0:T(8,128)(2,1)S(1)}, u32[]{:S(2)}, u32[]{:S(2)}) collective-permute-start(bf16[32,4096]{1,0:T(8,128)(2,1)S(1)} %residual.1), channel_id=1, source_target_pairs={{8,0},{16,8},{24,16},{9,1},{17,9},{25,17},{10,2},{18,10},{26,18},{... | collective-permute-start | bytes 786440 | tf_op jit(solution)/shard_map/ppermute | solution.py:21
  29.0 11.7 %all-to-all-start.1 = ((bf16[32,24,128]{2,1,0:T(8,128)(2,1)}), bf16[32,24,128]{2,1,0:T(8,128)(2,1)S(1)}, u32[]{:S(2)}, u32[]{:S(2)}) async-start(bf16[32,24,128]{2,1,0:T(8,128)(2,1)} %bitcast.8), calls=%async_computation.1 | async-start | bytes 393216 | tf_op jit(solution)/shard_map/all_to_all | solution.py:359
  31.7 7.7 %collective-permute-start.1 = (bf16[2,192,128]{2,1,0:T(8,128)(2,1)S(1)}, bf16[2,192,128]{2,1,0:T(8,128)(2,1)S(1)}, u32[]{:S(2)}, u32[]{:S(2)}) collective-permute-start(bf16[2,192,128]{2,1,0:T(8,128)(2,1)S(1)} %get-tuple-element.7), channel_id=1, source_target_pairs={{8,16},{16,8},{24,0},{9,17},{17,9},{25,1},{10,18},{18,10},{26,2},{... | collective-permute-start | bytes 294920 | tf_op jit(solution)/shard_map/ppermute | solution.py:363
  33.0 8.6 %collective-permute-start.2 = (bf16[2,192,128]{2,1,0:T(8,128)(2,1)S(1)}, bf16[2,192,128]{2,1,0:T(8,128)(2,1)S(1)}, u32[]{:S(2)}, u32[]{:S(2)}) collective-permute-start(bf16[2,192,128]{2,1,0:T(8,128)(2,1)S(1)} %get-tuple-element.8), channel_id=1, source_target_pairs={{0,16},{16,0},{24,8},{1,17},{17,1},{25,9},{2,18},{18,2},{26,10},{3... | collective-permute-start | bytes 294920 | tf_op jit(solution)/shard_map/ppermute | solution.py:363
  37.2 3.5 %copy-start.1 = (bf16[24,4096]{1,0:T(8,128)(2,1)S(1)}, bf16[24,4096]{1,0:T(8,128)(2,1)}, u32[]{:S(2)}) copy-start(bf16[24,4096]{1,0:T(8,128)(2,1)} %fresh_ref.1) | copy-start | bytes 589828
  37.2 4.3 %collective-permute-start.3 = (bf16[2,192,128]{2,1,0:T(8,128)(2,1)S(1)}, bf16[2,192,128]{2,1,0:T(8,128)(2,1)S(1)}, u32[]{:S(2)}, u32[]{:S(2)}) collective-permute-start(bf16[2,192,128]{2,1,0:T(8,128)(2,1)S(1)} %get-tuple-element.9), channel_id=1, source_target_pairs={{0,8},{8,0},{24,16},{1,9},{9,1},{25,17},{2,10},{10,2},{26,18},{3,1... | collective-permute-start | bytes 294920 | tf_op jit(solution)/shard_map/ppermute | solution.py:363
